TPU v7x, 32 devices: a whole 2x2x4 slice. The times are simulated.
32 devices in a mesh: grp: 2 (over y), blk: 16 (over z, x, core).
Axes of the slice: x: 2, y: 2, z: 4, core: 2. Of those that a mesh axis runs over, the one named last changes fastest.
Arguments:
- activations: bfloat16 [2, 4096, 256], P(None, ('grp', 'blk')), parts along dimension 1, may hold values from -6 to 6
- out_grads: bfloat16 [2, 4096, 256], P(None, ('grp', 'blk')), parts along dimension 1, may hold values from -6 to 6
- lengths: int32 [64], P(('grp', 'blk')), parts along dimension 0, may hold values from 8 to 64
- layer_ids: int32 [4], P('grp'), parts along dimension 0, may hold values from 0 to 15, as said below
- flagged: int32 [64], P('grp'), parts along dimension 0, may hold values from 0 to 31, each once
- act_factor: float32 [16, 256, 256], replicated, as said below
- grad_factor: float32 [16, 256, 256], replicated, as said below
Outputs:
- influence: float32 [64, 32], P(('grp', 'blk')), parts along dimension 0
There are 2 independent parts, one for each index of `grp`. A program takes and returns all parts, laid end to end along the dimension named above; an argument that names none is the same for every part. Nothing has to cross between parts.
Inputs may be any that keep to these rules, and one draw needn't show every extreme that they name: `act_factor`: each stored factor is symmetric. `grad_factor`: each stored factor is symmetric. `layer_ids`: indices of stored layers.
All inputs are finite; a program needn't handle non-finite values.
Results may differ from a plain program's by a relative error of at most 0.0007.
Values may be sent and summed in bfloat16 or wider, within the bound.
No kernel may reach another device: no remote copies, remote signals or barrier semaphores. Data moves between devices by JAX's collectives and lax.ppermute only.
A program may use at most 128 MiB of HBM per device.

v0:
```python
import jax
import jax.numpy as jnp
from jax import lax
from jax.sharding import PartitionSpec as P


def tile_scores(white_acts, white_grads, remote_acts, remote_grads, seq_len):
    gram_acts = jnp.einsum(
        "lqr,lkr->lqk", white_acts, remote_acts, preferred_element_type=jnp.float32
    )
    gram_grads = jnp.einsum(
        "lqr,lkr->lqk", white_grads, remote_grads, preferred_element_type=jnp.float32
    )
    pair = jnp.sum(gram_acts * gram_grads, axis=0)
    rows = pair.shape[0] // seq_len
    columns = pair.shape[1] // seq_len
    width = white_acts.shape[2]
    return pair.reshape(rows, seq_len, columns, seq_len).sum(axis=(1, 3)) * (
        1.0 / (width * seq_len)
    )


def shards(activations, out_grads, lengths, layer_ids, flagged, act_factor, grad_factor):
    tok_rows = activations.shape[1]
    seq_count = lengths.shape[0]
    seq_len = tok_rows // seq_count
    slots = jnp.arange(tok_rows) % seq_len
    keep = (slots < jnp.repeat(lengths, seq_len)).astype(jnp.bfloat16)
    masked_acts = activations * keep[None, :, None]
    masked_grads = out_grads * keep[None, :, None]
    picked_act = jnp.take(act_factor, layer_ids, axis=0)
    picked_grad = jnp.take(grad_factor, layer_ids, axis=0)
    white_acts = jnp.einsum(
        "ltr,lrs->lts", masked_acts.astype(jnp.float32), picked_act, precision=lax.Precision.HIGHEST
    ).astype(jnp.bfloat16)
    white_grads = jnp.einsum(
        "ltr,lrs->lts",
        masked_grads.astype(jnp.float32),
        picked_grad,
        precision=lax.Precision.HIGHEST,
    ).astype(jnp.bfloat16)
    part_scores = tile_scores(
        white_acts,
        white_grads,
        lax.all_gather(masked_acts, "blk", axis=1, tiled=True),
        lax.all_gather(masked_grads, "blk", axis=1, tiled=True),
        seq_len,
    )
    return jnp.take(part_scores, flagged, axis=1)


def solution(mesh):
    in_specs = (
        P(None, ("grp", "blk"), None),
        P(None, ("grp", "blk"), None),
        P(("grp", "blk")),
        P("grp"),
        P("grp"),
        P(),
        P(),
    )
    out_specs = P(("grp", "blk"), None)
    return jax.shard_map(shards, mesh=mesh, in_specs=in_specs, out_specs=out_specs, check_vma=False)
```

profile of v0, /device:TPU:0, one launch (start us, length us, event | category | flops | bytes accessed | tf_op | source)
XLA Modules:
  0.0 107.9 jit_solution(582894465063444471)
XLA Ops:
  6.5 0.0 copy-start.2
  6.5 0.0 copy-start.3
  6.5 0.0 all-gather.3.cloned.1.call-start
  6.5 0.7 broadcast_in_dim.27
  7.3 0.1 reshape.31
  7.4 1.8 %broadcast_multiply_fusion = (bf16[2,128,256]{2,1,0:T(8,128)(2,1)}, bf16[2,128,256]{2,1,0:T(8,128)(2,1)}) fusion(bf16[2,128,256]{2,1,0:T(8,128)(2,1)} %param.10, bf16[128]{0:T(256)(128)(2,1)S(1)} %compare_convert_fusion, bf16[2,128,256]{2,1,0:T(8,128)(2,1)} %param.9), kind=kLoop, calls=%fused_computation.13 | loop fusion | flops 131072 | bytes 524544 | tf_op jit(solution)/shard_map/mul | solution.py:30
  9.1 0.0 copy-start.1
  9.1 0.0 copy-start
  9.1 0.0 all-gather.3.cloned.1.call-update
  9.2 0.0 all-gather.5.cloned.1.call-start
  9.2 0.7 all-gather.5.cloned.1.call-update
  9.9 0.7 compare_select_fusion
  10.6 2.8 %gather_fusion.1 = f32[2,256,256]{2,1,0:T(8,128)S(1)} fusion(f32[16,256,256]{2,1,0:T(8,128)} %param.14, s32[1024]{0:T(1024)S(1)} %pad_clamp_fusion.1), kind=kCustom, calls=%fused_computation.clone | custom fusion | bytes 1048584 | tf_op jit(solution)/shard_map/jit(_take)/gather | solution.py:31
  13.4 2.8 %gather_fusion.2 = f32[2,256,256]{2,1,0:T(8,128)S(1)} fusion(f32[16,256,256]{2,1,0:T(8,128)} %param.15, s32[1024]{0:T(1024)S(1)} %pad_clamp_fusion.1), kind=kCustom, calls=%fused_computation.1.clone | custom fusion | bytes 1048584 | tf_op jit(solution)/shard_map/jit(_take)/gather | solution.py:32
  16.1 0.0 copy-done.3
  16.2 0.0 copy-done.2
  16.2 0.0 copy-done.1
  16.2 0.4 convolution_convert_fusion.1
  16.7 0.0 copy-done
  16.7 0.4 convolution_convert_fusion
  17.1 36.6 %all-gather.3.cloned.1.call-done = bf16[2,2048,256]{2,1,0:T(8,128)(2,1)} async-done(((bf16[2,128,256]{2,1,0:T(8,128)(2,1)}), bf16[2,2048,256]{2,1,0:T(8,128)(2,1)}) %all-gather.3.cloned.1.call-update) | async-done | bytes 2097168 | tf_op jit(solution)/shard_map/all_gather | solution.py:45
  53.7 2.4 %fusion.9 = f32[2,128,2048]{2,1,0:T(8,128)S(1)} fusion(bf16[2,128,256]{2,1,0:T(8,128)(2,1)S(1)} %convolution_convert_fusion.1, bf16[2,2048,256]{2,1,0:T(8,128)(2,1)} %all-gather.3.cloned.1.call-done), kind=kOutput, calls=%fused_computation.27 | convolution fusion | flops 268435456 | bytes 4325376 | tf_op jit(solution)/shard_map/lqr,lkr->lqk/dot_general | solution.py:8
  56.1 40.0 %all-gather.5.cloned.1.call-done = bf16[2,2048,256]{2,1,0:T(8,128)(2,1)} async-done(((bf16[2,128,256]{2,1,0:T(8,128)(2,1)}), bf16[2,2048,256]{2,1,0:T(8,128)(2,1)}) %all-gather.5.cloned.1.call-update) | async-done | bytes 2097168 | tf_op jit(solution)/shard_map/all_gather | solution.py:46
  96.0 2.5 %fusion = f32[128,2048]{1,0:T(8,128)S(1)} fusion(f32[2,128,2048]{2,1,0:T(8,128)S(1)} %fusion.9, bf16[2,128,256]{2,1,0:T(8,128)(2,1)S(1)} %convolution_convert_fusion, bf16[2,2048,256]{2,1,0:T(8,128)(2,1)} %all-gather.5.cloned.1.call-done), kind=kOutput, calls=%fused_computation.4 | convolution fusion | flops 269221888 | bytes 5373952 | tf_op jit(solution)/shard_map/lqr,lkr->lqk/dot_general | solution.py:11
  98.5 0.8 reshape.32
  99.4 0.3 reduce_sum.19
  99.7 0.1 copy.11
  99.7 0.6 gather_fusion
  100.3 0.1 select_bitcast_fusion
  100.4 0.6 copy.12
  (7 shorter events, 0.0 us)
Async XLA Ops:
  6.5 9.6 %copy-start.2 = (s32[2]{0:T(128)S(1)}, s32[2]{0:T(128)}, u32[]{:S(2)}) copy-start(s32[2]{0:T(128)} %param.12) | copy-start | bytes 28
  6.5 9.6 %copy-start.3 = (s32[32]{0:T(128)S(1)}, s32[32]{0:T(128)}, u32[]{:S(2)}) copy-start(s32[32]{0:T(128)} %param.13) | copy-start | bytes 388
  6.5 47.1 %all-gather.3.cloned.1.call-start = ((), (), s32[]{:S(2)}) async-start(), calls=%async_computation | async-start | bytes 2228224 | tf_op jit(solution)/shard_map/all_gather | solution.py:45
  9.1 7.1 %copy-start.1 = (bf16[2,128,256]{2,1,0:T(8,128)(2,1)S(1)}, bf16[2,128,256]{2,1,0:T(8,128)(2,1)}, u32[]{:S(2)}) copy-start(bf16[2,128,256]{2,1,0:T(8,128)(2,1)} %get-tuple-element.7) | copy-start | bytes 393220
  9.1 7.5 %copy-start = (bf16[2,128,256]{2,1,0:T(8,128)(2,1)S(1)}, bf16[2,128,256]{2,1,0:T(8,128)(2,1)}, u32[]{:S(2)}) copy-start(bf16[2,128,256]{2,1,0:T(8,128)(2,1)} %get-tuple-element.6) | copy-start | bytes 393220
  9.2 86.9 %all-gather.5.cloned.1.call-start = ((), (), s32[]{:S(2)}) async-start(), calls=%async_computation.1 | async-start | bytes 2228224 | tf_op jit(solution)/shard_map/all_gather | solution.py:46
Sparse Core Ops, SparseCore 0:
  9.5 44.0 all-gather.2
  55.9 40.1 all-gather.4
where the time goes:
time: 108 us
  waiting for transfers between devices  77.2 us (71%)
  between operations  13.5 us (12%)
  local copies, waits for them, and re-layouts  8.52 us (8%)
  matrix products  5.76 us (5%)
  other arithmetic  2.81 us (3%)
    all_gather x1, waiting for transfers between devices, shards(): lax.all_gather(masked_grads, 'blk', axis=1, tiled=True)  40 us
    all_gather x1, waiting for transfers between devices, shards(): lax.all_gather(masked_acts, 'blk', axis=1, tiled=True)  36.6 us
    gather x1, local copies, waits for them, and re-layouts, shards(): picked_grad = jnp.take(grad_factor, layer_ids, axis=0)  2.77 us
    gather x1, local copies, waits for them, and re-layouts, shards(): picked_act = jnp.take(act_factor, layer_ids, axis=0)  2.77 us
    dot_general x1, matrix products, tile_scores(): jnp.einsum('lqr,lkr->lqk', white_grads, remote_grads, preferred_element_t...  2.49 us
    dot_general x1, matrix products, tile_scores(): jnp.einsum('lqr,lkr->lqk', white_acts, remote_acts, preferred_element_typ...  2.4 us
  transfers between devices with their start and end apart: 2, of which 2 were waited for; matrix products, arithmetic and copies ran while one was open for 9% of the time, Pallas kernels for 0%

commit v1 on v0

--- a/solution.py
+++ b/solution.py
@@ -1,7 +1,13 @@
+import functools
+
 import jax
 import jax.numpy as jnp
 from jax import lax
+from jax.experimental import pallas as pl
+from jax.experimental.pallas import tpu as pltpu
 from jax.sharding import PartitionSpec as P
+
+HIGHEST = lax.Precision.HIGHEST
 
 
 def tile_scores(white_acts, white_grads, remote_acts, remote_grads, seq_len):
@@ -20,7 +26,7 @@
     )
 
 
-def shards(activations, out_grads, lengths, layer_ids, flagged, act_factor, grad_factor):
+def gathered(activations, out_grads, lengths, layer_ids, flagged, act_factor, grad_factor):
     tok_rows = activations.shape[1]
     seq_count = lengths.shape[0]
     seq_len = tok_rows // seq_count
@@ -31,13 +37,10 @@
     picked_act = jnp.take(act_factor, layer_ids, axis=0)
     picked_grad = jnp.take(grad_factor, layer_ids, axis=0)
     white_acts = jnp.einsum(
-        "ltr,lrs->lts", masked_acts.astype(jnp.float32), picked_act, precision=lax.Precision.HIGHEST
+        "ltr,lrs->lts", masked_acts.astype(jnp.float32), picked_act, precision=HIGHEST
     ).astype(jnp.bfloat16)
     white_grads = jnp.einsum(
-        "ltr,lrs->lts",
-        masked_grads.astype(jnp.float32),
-        picked_grad,
-        precision=lax.Precision.HIGHEST,
+        "ltr,lrs->lts", masked_grads.astype(jnp.float32), picked_grad, precision=HIGHEST
     ).astype(jnp.bfloat16)
     part_scores = tile_scores(
         white_acts,
@@ -47,6 +50,145 @@
         seq_len,
     )
     return jnp.take(part_scores, flagged, axis=1)
+
+
+def z_near(d):
+    return d ^ 4 ^ ((d >> 1) & 1)
+
+
+def prep_kernel(seq_len, lens, acts, grads, own, away):
+    half = lax.axis_index("blk") // 8
+    row = lax.broadcasted_iota(jnp.int32, (acts.shape[1], 1), 0)
+    bound = jnp.zeros_like(row)
+    for s in range(lens.shape[0]):
+        bound = jnp.where(row // seq_len == s, lens[s] + s * seq_len, bound)
+    keep = row < bound
+    for index, src in enumerate((acts, grads)):
+        for layer, dst in ((half, own), (1 - half, away)):
+            x = src[layer]
+            dst[index] = jnp.where(keep, x, jnp.zeros_like(x))
+
+
+def prep(activations, out_grads, lengths, seq_len):
+    unit = jax.ShapeDtypeStruct((2,) + activations.shape[1:], activations.dtype)
+    vmem = pl.BlockSpec(memory_space=pltpu.VMEM)
+    return pl.pallas_call(
+        functools.partial(prep_kernel, seq_len),
+        out_shape=(unit, unit),
+        in_specs=[pl.BlockSpec(memory_space=pltpu.SMEM), vmem, vmem],
+        out_specs=(vmem, vmem),
+        name="mask_units",
+    )(lengths, activations, out_grads)
+
+
+def whiten(x, factor):
+    total = None
+    rest = factor
+    for _ in range(3):
+        term = rest.astype(jnp.bfloat16)
+        rest = rest - term.astype(jnp.float32)
+        part = jnp.dot(x, term, preferred_element_type=jnp.float32)
+        total = part if total is None else total + part
+    return total.astype(jnp.bfloat16)
+
+
+def score_kernel(seq_len, layer_ids, flagged, act_f, grad_f, *refs):
+    units, out = refs[:8], refs[8]
+    rank = units[0].shape[2]
+    d = lax.axis_index("blk")
+    f32 = jnp.float32
+    toks = [
+        [jnp.concatenate([units[2 * i][w], units[2 * i + 1][w]], axis=0) for w in range(2)]
+        for i in range(4)
+    ]
+    factors = (act_f[0], grad_f[0])
+    white = [[whiten(toks[i][w], factors[w]) for w in range(2)] for i in range(3)]
+    rows = toks[0][0].shape[0]
+    seqs = rows // seq_len
+    zeros = jnp.zeros((seqs, rows), f32)
+    sums = []
+    for i in range(4):
+        line = []
+        for j in range(4):
+            if i < 3 and (j > i or i == 0) and not (i == 1 and j < 2):
+                grams = [
+                    lax.dot_general(
+                        white[i][w], toks[j][w], (((1,), (1,)), ((), ())), preferred_element_type=f32
+                    )
+                    for w in range(2)
+                ]
+                pair = grams[0] * grams[1]
+                line.append(pair.reshape(seqs, seq_len, rows).sum(axis=1))
+            else:
+                line.append(zeros)
+        sums.append(jnp.concatenate(line, axis=1))
+    sums = jnp.concatenate(sums, axis=0)
+    n = 4 * seqs
+    tok = lax.broadcasted_iota(jnp.int32, (4 * rows, n), 0)
+    col = lax.broadcasted_iota(jnp.int32, (4 * rows, n), 1)
+    fold = jnp.where(tok // seq_len == col, 1.0 / (rank * seq_len), 0.0).astype(f32)
+    local = jnp.dot(sums, fold, precision=HIGHEST, preferred_element_type=f32)
+    r = lax.broadcasted_iota(jnp.int32, (n, n), 0) // seqs
+    c = lax.broadcasted_iota(jnp.int32, (n, n), 1) // seqs
+    diagonal = jnp.where((r == 2) & (c == 3), local, 0.0)
+    place = lax.broadcasted_iota(jnp.int32, (n, flagged.shape[1]), 0)
+    per = seqs // 2
+    spot = place // per
+    slot = spot // 2
+    owner = jnp.where(slot == 0, d, jnp.where(slot == 1, d ^ 1, jnp.where(slot == 2, d ^ 2, z_near(d))))
+    owner = owner ^ (8 * (spot % 2))
+    seq = owner * per + place % per
+    pick = jnp.where(seq == flagged[...], 1.0, 0.0).astype(f32)
+    picked = jnp.dot(local, pick, precision=HIGHEST, preferred_element_type=f32)
+    picked = picked + lax.dot_general(
+        diagonal, pick, (((0,), (0,)), ((), ())), precision=HIGHEST, preferred_element_type=f32
+    )
+    out[...] = jnp.zeros_like(out)
+    for i, base in enumerate((d, d ^ 1, d ^ 2, z_near(d))):
+        for j in range(2):
+            at = (2 * i + j) * per
+            out[base ^ (8 * j)] = picked[at : at + per]
+
+
+def score(units, layer_ids, flagged, act_factor, grad_factor, seq_len, size):
+    rank = units[0].shape[2]
+    per = units[0].shape[1] // seq_len
+    vmem = pl.BlockSpec(memory_space=pltpu.VMEM)
+    factor = pl.BlockSpec(
+        (1, rank, rank), lambda i, ids: (ids[lax.axis_index("blk") // 8], 0, 0)
+    )
+    return pl.pallas_call(
+        functools.partial(score_kernel, seq_len),
+        out_shape=jax.ShapeDtypeStruct((size, per, flagged.shape[0]), jnp.float32),
+        grid_spec=pltpu.PrefetchScalarGridSpec(
+            num_scalar_prefetch=1,
+            grid=(1,),
+            in_specs=[pl.BlockSpec((1, flagged.shape[0]), lambda i, ids: (0, 0)), factor, factor] + [vmem] * 8,
+            out_specs=vmem,
+        ),
+        compiler_params=pltpu.CompilerParams(vmem_limit_bytes=48 * 1024 * 1024),
+        name="pair_scores",
+    )(layer_ids, flagged.reshape(1, -1), act_factor, grad_factor, *units)
+
+
+def paired(activations, out_grads, lengths, layer_ids, flagged, act_factor, grad_factor):
+    size = 16
+    seq_len = activations.shape[1] // lengths.shape[0]
+    own, away = prep(activations, out_grads, lengths, seq_len)
+
+    def send(x, to):
+        return lax.ppermute(x, "blk", [(d, to(d)) for d in range(size)])
+
+    ways = (lambda d: d ^ 1, lambda d: d ^ 2, z_near)
+    opposite = send(away, lambda d: d ^ 8)
+    near = [send(own, to) for to in ways]
+    far = [send(opposite, to) for to in ways]
+    units = [own, opposite]
+    for a, b in zip(near, far):
+        units += [a, b]
+    parts = score(units, layer_ids, flagged, act_factor, grad_factor, seq_len, size)
+    back = lax.all_to_all(parts, "blk", 0, 0, tiled=True)
+    return jnp.sum(back, axis=0)
 
 
 def solution(mesh):
@@ -60,4 +202,5 @@
         P(),
     )
     out_specs = P(("grp", "blk"), None)
+    shards = paired if mesh.shape["blk"] == 16 else gathered
     return jax.shard_map(shards, mesh=mesh, in_specs=in_specs, out_specs=out_specs, check_vma=False)

time: 108 us -> 39 us (0.36)
  waiting for transfers between devices: 77.2 us -> 7.65 us
  between operations: 13.5 us -> 0.01 us
  blocking collectives: 0 us -> 12.1 us
  starting transfers between devices: 0.04 us -> 8.99 us
  matrix products: 5.76 us -> 0 us
  Pallas kernels: 0 us -> 4.97 us
  local copies, waits for them, and re-layouts: 8.52 us -> 4.4 us
  other arithmetic: 2.81 us -> 0.59 us
    all_gather x2 -> x0, waiting for transfers between devices: 76.5 us -> none  [the longest x1 40 us: shards(): lax.all_gather(masked_grads, 'blk', axis=1, tiled=True)]
    all_to_all x0 -> x1, blocking collectives: none -> 12.1 us  [paired(): back = lax.all_to_all(parts, 'blk', 0, 0, tiled=True)]
    ppermute x0 -> x7, starting transfers between devices: none -> 8.99 us  [send(): return lax.ppermute(x, 'blk', [(d, to(d)) for d in range(size)])]
    ppermute x0 -> x7, waiting for transfers between devices: none -> 7.65 us  [send(): return lax.ppermute(x, 'blk', [(d, to(d)) for d in range(size)])]
    gather x3 -> x0, local copies, waits for them, and re-layouts: 6.11 us -> none  [the longest x1 2.77 us: shards(): picked_grad = jnp.take(grad_factor, layer_ids, axis=0)]
    dot_general x4 -> x0, matrix products: 5.76 us -> none  [the longest x1 2.49 us: tile_scores(): jnp.einsum('lqr,lkr->lqk', white_grads, remote_grads, preferred_element_t...]
    pallas_call x0 -> x2, Pallas kernels: none -> 4.97 us  [the longest x1 3.27 us: score(): pl.pallas_call(functools.partial(score_kernel, seq_len), out_shape=jax.Sh...]
    unnamed x8, local copies, waits for them, and re-layouts: 0.01 us -> 4.4 us
  transfers between devices with their start and end apart: 2 -> 7, of which waited for: 2 -> 3; matrix products, arithmetic and copies ran while one was open for 9% -> 0% of each run, Pallas kernels for 0% -> 0%
where the time goes in v1:
time: 39 us; the launch traced here: 38.8 us
  blocking collectives  12.1 us (31%)
  starting transfers between devices  8.99 us (23%)
  waiting for transfers between devices  7.65 us (20%)
  Pallas kernels  4.97 us (13%)
  local copies, waits for them, and re-layouts  4.4 us (11%)
  other arithmetic  0.59 us (2%)
    all_to_all x1, blocking collectives, paired(): back = lax.all_to_all(parts, 'blk', 0, 0, tiled=True)  12.1 us
    ppermute x7, starting transfers between devices, send(): return lax.ppermute(x, 'blk', [(d, to(d)) for d in range(size)])  8.99 us
    ppermute x7, waiting for transfers between devices, send(): return lax.ppermute(x, 'blk', [(d, to(d)) for d in range(size)])  7.65 us
    unnamed x8, local copies, waits for them, and re-layouts  4.4 us
    pallas_call x1, Pallas kernels, score(): pl.pallas_call(functools.partial(score_kernel, seq_len), out_shape=jax.Sh...  3.27 us
    pallas_call x1, Pallas kernels, prep(): pl.pallas_call(functools.partial(prep_kernel, seq_len), out_shape=(unit,...  1.71 us
  transfers between devices with their start and end apart: 7, of which 3 were waited for; matrix products, arithmetic and copies ran while one was open for 0% of the time, Pallas kernels for 0%

profile of v1, /device:TPU:0, one launch (start us, length us, event | category | flops | bytes accessed | tf_op | source)
XLA Modules:
  0.0 38.8 jit_solution(4234068494696127712)
XLA Ops:
  0.0 1.7 %mask_units.1 = (bf16[2,128,256]{2,1,0:T(8,128)(2,1)}, bf16[2,128,256]{2,1,0:T(8,128)(2,1)}) custom-call(s32[2]{0:T(128)} %lens.1, bf16[2,128,256]{2,1,0:T(8,128)(2,1)} %acts.1, bf16[2,128,256]{2,1,0:T(8,128)(2,1)} %grads.1), custom_call_target="tpu_custom_call" | custom-call | tf_op jit(solution)/shard_map/mask_units/pallas_call | solution.py:75
  1.7 4.0 %collective-permute-start = (bf16[2,128,256]{2,1,0:T(8,128)(2,1)}, bf16[2,128,256]{2,1,0:T(8,128)(2,1)S(1)}, u32[]{:S(2)}, u32[]{:S(2)}) collective-permute-start(bf16[2,128,256]{2,1,0:T(8,128)(2,1)} %get-tuple-element.8), channel_id=1, source_target_pairs={{0,8},{1,9},{2,10},{3,11},{4,12},{5,13},{6,14},{7,15},{8,0},{9,1},... | collective-permute-start | bytes 393224 | tf_op jit(solution)/shard_map/ppermute | solution.py:180
  5.7 1.6 %collective-permute-start.5 = (bf16[2,128,256]{2,1,0:T(8,128)(2,1)}, bf16[2,128,256]{2,1,0:T(8,128)(2,1)S(1)}, u32[]{:S(2)}, u32[]{:S(2)}) collective-permute-start(bf16[2,128,256]{2,1,0:T(8,128)(2,1)} %get-tuple-element.7.refs_0_), channel_id=1, source_target_pairs={{0,4},{1,5},{2,7},{3,6},{4,0},{5,1},{6,3},{7,2},{8,12},{9,13},{10,... | collective-permute-start | bytes 393224 | tf_op jit(solution)/shard_map/ppermute | solution.py:180
  7.3 0.7 %collective-permute-start.3 = (bf16[2,128,256]{2,1,0:T(8,128)(2,1)}, bf16[2,128,256]{2,1,0:T(8,128)(2,1)S(1)}, u32[]{:S(2)}, u32[]{:S(2)}) collective-permute-start(bf16[2,128,256]{2,1,0:T(8,128)(2,1)} %get-tuple-element.7.refs_0_), channel_id=1, source_target_pairs={{0,2},{1,3},{2,0},{3,1},{4,6},{5,7},{6,4},{7,5},{8,10},{9,11},{10,... | collective-permute-start | bytes 393224 | tf_op jit(solution)/shard_map/ppermute | solution.py:180
  8.0 0.7 %collective-permute-start.1 = (bf16[2,128,256]{2,1,0:T(8,128)(2,1)}, bf16[2,128,256]{2,1,0:T(8,128)(2,1)S(1)}, u32[]{:S(2)}, u32[]{:S(2)}) collective-permute-start(bf16[2,128,256]{2,1,0:T(8,128)(2,1)} %get-tuple-element.7.refs_0_), channel_id=1, source_target_pairs={{0,1},{1,0},{2,3},{3,2},{4,5},{5,4},{6,7},{7,6},{8,9},{9,8},{10,11... | collective-permute-start | bytes 393224 | tf_op jit(solution)/shard_map/ppermute | solution.py:180
  8.6 3.7 %collective-permute-done.refs_1_ = bf16[2,128,256]{2,1,0:T(8,128)(2,1)S(1)} collective-permute-done((bf16[2,128,256]{2,1,0:T(8,128)(2,1)}, bf16[2,128,256]{2,1,0:T(8,128)(2,1)S(1)}, u32[]{:S(2)}, u32[]{:S(2)}) %collective-permute-start) | collective-permute-done | bytes 131104 | tf_op jit(solution)/shard_map/ppermute | solution.py:180
  12.4 0.7 %collective-permute-start.6 = (bf16[2,128,256]{2,1,0:T(8,128)(2,1)S(1)}, bf16[2,128,256]{2,1,0:T(8,128)(2,1)S(1)}, u32[]{:S(2)}, u32[]{:S(2)}) collective-permute-start(bf16[2,128,256]{2,1,0:T(8,128)(2,1)S(1)} %collective-permute-done.refs_1_), channel_id=1, source_target_pairs={{0,4},{1,5},{2,7},{3,6},{4,0},{5,1},{6,3},{7,2},{8,12},{9,13},{10,... | collective-permute-start | bytes 393224 | tf_op jit(solution)/shard_map/ppermute | solution.py:180
  13.1 1.1 %collective-permute-start.4 = (bf16[2,128,256]{2,1,0:T(8,128)(2,1)S(1)}, bf16[2,128,256]{2,1,0:T(8,128)(2,1)S(1)}, u32[]{:S(2)}, u32[]{:S(2)}) collective-permute-start(bf16[2,128,256]{2,1,0:T(8,128)(2,1)S(1)} %collective-permute-done.refs_1_), channel_id=1, source_target_pairs={{0,2},{1,3},{2,0},{3,1},{4,6},{5,7},{6,4},{7,5},{8,10},{9,11},{10,... | collective-permute-start | bytes 393224 | tf_op jit(solution)/shard_map/ppermute | solution.py:180
  14.2 0.0 collective-permute-done.5.refs_6_
  14.2 0.2 collective-permute-start.2
  14.4 0.0 collective-permute-done.3.refs_4_
  14.4 0.0 collective-permute-done.1.refs_2_
  14.4 2.9 %collective-permute-done.6.refs_7_ = bf16[2,128,256]{2,1,0:T(8,128)(2,1)S(1)} collective-permute-done((bf16[2,128,256]{2,1,0:T(8,128)(2,1)S(1)}, bf16[2,128,256]{2,1,0:T(8,128)(2,1)S(1)}, u32[]{:S(2)}, u32[]{:S(2)}) %collective-permute-start.6) | collective-permute-done | bytes 131104 | tf_op jit(solution)/shard_map/ppermute | solution.py:180
  17.3 1.0 %collective-permute-done.4.refs_5_ = bf16[2,128,256]{2,1,0:T(8,128)(2,1)S(1)} collective-permute-done((bf16[2,128,256]{2,1,0:T(8,128)(2,1)S(1)}, bf16[2,128,256]{2,1,0:T(8,128)(2,1)S(1)}, u32[]{:S(2)}, u32[]{:S(2)}) %collective-permute-start.4) | collective-permute-done | bytes 131104 | tf_op jit(solution)/shard_map/ppermute | solution.py:180
  18.4 0.0 collective-permute-done.2.refs_3_
  18.4 0.0 copy-start
  18.4 2.2 %copy-done = f32[16,256,256]{2,1,0:T(8,128)S(1)} copy-done((f32[16,256,256]{2,1,0:T(8,128)S(1)}, f32[16,256,256]{2,1,0:T(8,128)}, u32[]{:S(2)}) %copy-start) | copy-done | bytes 4194328
  20.5 0.0 copy-start.1
  20.5 0.9 %copy-done.1 = bf16[2,128,256]{2,1,0:T(8,128)(2,1)S(1)} copy-done((bf16[2,128,256]{2,1,0:T(8,128)(2,1)S(1)}, bf16[2,128,256]{2,1,0:T(8,128)(2,1)}, u32[]{:S(2)}) %copy-start.1) | copy-done | bytes 131096
  21.5 0.0 copy-start.2
  21.5 0.7 %copy-done.2 = s32[2]{0:T(128)S(1)} copy-done((s32[2]{0:T(128)S(1)}, s32[2]{0:T(128)}, u32[]{:S(2)}) %copy-start.2) | copy-done | bytes 32
  22.1 0.0 copy-start.3
  22.1 0.7 %copy-done.3 = s32[32]{0:T(128)S(1)} copy-done((s32[32]{0:T(128)S(1)}, s32[32]{0:T(128)}, u32[]{:S(2)}) %copy-start.3) | copy-done | bytes 152
  22.8 3.3 %pair_scores.1 = f32[16,2,32]{2,1,0:T(2,128)S(1)} custom-call(s32[2]{0:T(128)S(1)} %copy-done.2, s32[1,32]{1,0:T(1,128)S(1)} %bitcast.1, f32[16,256,256]{2,1,0:T(8,128)S(1)} %copy-done, f32[16,256,256]{2,1,0:T(8,128)} %grad_f.1, bf16[2,128,256]{2,1,0:T(8,128)(2,1)S(1)} %copy-done.1, bf16[2,128,256]{2,1,0:T(8,128)(2,1)S(1)} %collective-permute-done.refs_1_, ...), custom_call_target="tpu_custom_call" | custom-call | tf_op jit(solution)/shard_map/pair_scores/pallas_call | solution.py:160
  26.0 12.1 %all_to_all.5 = f32[16,2,32]{2,1,0:T(2,128)S(1)} all-to-all(f32[16,2,32]{2,1,0:T(2,128)S(1)} %pair_scores.1), channel_id=1, replica_groups=mesh['grp'=2,'blk'=16] {'blk'}, dimensions={0} | all-to-all | bytes 8192 | tf_op jit(solution)/shard_map/all_to_all | solution.py:190
  38.2 0.6 %reduce_sum.9 = f32[2,32]{1,0:T(2,128)} reduce(f32[16,2,32]{2,1,0:T(2,128)S(1)} %all_to_all.5, f32[]{:T(128)} %constant.0.clone.1), dimensions={0}, to_apply=%region_0.0 | reduce | flops 960 | bytes 4356 | tf_op jit(solution)/shard_map/reduce_sum | solution.py:191
Async XLA Ops:
  1.7 10.7 %collective-permute-start = (bf16[2,128,256]{2,1,0:T(8,128)(2,1)}, bf16[2,128,256]{2,1,0:T(8,128)(2,1)S(1)}, u32[]{:S(2)}, u32[]{:S(2)}) collective-permute-start(bf16[2,128,256]{2,1,0:T(8,128)(2,1)} %get-tuple-element.8), channel_id=1, source_target_pairs={{0,8},{1,9},{2,10},{3,11},{4,12},{5,13},{6,14},{7,15},{8,0},{9,1},... | collective-permute-start | bytes 393224 | tf_op jit(solution)/shard_map/ppermute | solution.py:180
  5.7 8.5 %collective-permute-start.5 = (bf16[2,128,256]{2,1,0:T(8,128)(2,1)}, bf16[2,128,256]{2,1,0:T(8,128)(2,1)S(1)}, u32[]{:S(2)}, u32[]{:S(2)}) collective-permute-start(bf16[2,128,256]{2,1,0:T(8,128)(2,1)} %get-tuple-element.7.refs_0_), channel_id=1, source_target_pairs={{0,4},{1,5},{2,7},{3,6},{4,0},{5,1},{6,3},{7,2},{8,12},{9,13},{10,... | collective-permute-start | bytes 393224 | tf_op jit(solution)/shard_map/ppermute | solution.py:180
  7.3 7.1 %collective-permute-start.3 = (bf16[2,128,256]{2,1,0:T(8,128)(2,1)}, bf16[2,128,256]{2,1,0:T(8,128)(2,1)S(1)}, u32[]{:S(2)}, u32[]{:S(2)}) collective-permute-start(bf16[2,128,256]{2,1,0:T(8,128)(2,1)} %get-tuple-element.7.refs_0_), channel_id=1, source_target_pairs={{0,2},{1,3},{2,0},{3,1},{4,6},{5,7},{6,4},{7,5},{8,10},{9,11},{10,... | collective-permute-start | bytes 393224 | tf_op jit(solution)/shard_map/ppermute | solution.py:180
  8.0 6.5 %collective-permute-start.1 = (bf16[2,128,256]{2,1,0:T(8,128)(2,1)}, bf16[2,128,256]{2,1,0:T(8,128)(2,1)S(1)}, u32[]{:S(2)}, u32[]{:S(2)}) collective-permute-start(bf16[2,128,256]{2,1,0:T(8,128)(2,1)} %get-tuple-element.7.refs_0_), channel_id=1, source_target_pairs={{0,1},{1,0},{2,3},{3,2},{4,5},{5,4},{6,7},{7,6},{8,9},{9,8},{10,11... | collective-permute-start | bytes 393224 | tf_op jit(solution)/shard_map/ppermute | solution.py:180
  12.4 5.0 %collective-permute-start.6 = (bf16[2,128,256]{2,1,0:T(8,128)(2,1)S(1)}, bf16[2,128,256]{2,1,0:T(8,128)(2,1)S(1)}, u32[]{:S(2)}, u32[]{:S(2)}) collective-permute-start(bf16[2,128,256]{2,1,0:T(8,128)(2,1)S(1)} %collective-permute-done.refs_1_), channel_id=1, source_target_pairs={{0,4},{1,5},{2,7},{3,6},{4,0},{5,1},{6,3},{7,2},{8,12},{9,13},{10,... | collective-permute-start | bytes 393224 | tf_op jit(solution)/shard_map/ppermute | solution.py:180
  13.1 5.3 %collective-permute-start.4 = (bf16[2,128,256]{2,1,0:T(8,128)(2,1)S(1)}, bf16[2,128,256]{2,1,0:T(8,128)(2,1)S(1)}, u32[]{:S(2)}, u32[]{:S(2)}) collective-permute-start(bf16[2,128,256]{2,1,0:T(8,128)(2,1)S(1)} %collective-permute-done.refs_1_), channel_id=1, source_target_pairs={{0,2},{1,3},{2,0},{3,1},{4,6},{5,7},{6,4},{7,5},{8,10},{9,11},{10,... | collective-permute-start | bytes 393224 | tf_op jit(solution)/shard_map/ppermute | solution.py:180
  14.2 4.2 %collective-permute-start.2 = (bf16[2,128,256]{2,1,0:T(8,128)(2,1)S(1)}, bf16[2,128,256]{2,1,0:T(8,128)(2,1)S(1)}, u32[]{:S(2)}, u32[]{:S(2)}) collective-permute-start(bf16[2,128,256]{2,1,0:T(8,128)(2,1)S(1)} %collective-permute-done.refs_1_), channel_id=1, source_target_pairs={{0,1},{1,0},{2,3},{3,2},{4,5},{5,4},{6,7},{7,6},{8,9},{9,8},{10,11... | collective-permute-start | bytes 393224 | tf_op jit(solution)/shard_map/ppermute | solution.py:180
  18.4 2.2 %copy-start = (f32[16,256,256]{2,1,0:T(8,128)S(1)}, f32[16,256,256]{2,1,0:T(8,128)}, u32[]{:S(2)}) copy-start(f32[16,256,256]{2,1,0:T(8,128)} %act_f.1) | copy-start | bytes 12582916
  20.5 0.9 %copy-start.1 = (bf16[2,128,256]{2,1,0:T(8,128)(2,1)S(1)}, bf16[2,128,256]{2,1,0:T(8,128)(2,1)}, u32[]{:S(2)}) copy-start(bf16[2,128,256]{2,1,0:T(8,128)(2,1)} %get-tuple-element.7.refs_0_) | copy-start | bytes 393220
  21.5 0.7 %copy-start.2 = (s32[2]{0:T(128)S(1)}, s32[2]{0:T(128)}, u32[]{:S(2)}) copy-start(s32[2]{0:T(128)} %layer_ids.1) | copy-start | bytes 28
  22.1 0.7 %copy-start.3 = (s32[32]{0:T(128)S(1)}, s32[32]{0:T(128)}, u32[]{:S(2)}) copy-start(s32[32]{0:T(128)} %param.11) | copy-start | bytes 388

commit v2 on v0

--- a/solution.py
+++ b/solution.py
@@ -1,7 +1,13 @@
+import functools
+
 import jax
 import jax.numpy as jnp
 from jax import lax
+from jax.experimental import pallas as pl
+from jax.experimental.pallas import tpu as pltpu
 from jax.sharding import PartitionSpec as P
+
+HIGHEST = lax.Precision.HIGHEST
 
 
 def tile_scores(white_acts, white_grads, remote_acts, remote_grads, seq_len):
@@ -20,7 +26,7 @@
     )
 
 
-def shards(activations, out_grads, lengths, layer_ids, flagged, act_factor, grad_factor):
+def gathered(activations, out_grads, lengths, layer_ids, flagged, act_factor, grad_factor):
     tok_rows = activations.shape[1]
     seq_count = lengths.shape[0]
     seq_len = tok_rows // seq_count
@@ -31,13 +37,10 @@
     picked_act = jnp.take(act_factor, layer_ids, axis=0)
     picked_grad = jnp.take(grad_factor, layer_ids, axis=0)
     white_acts = jnp.einsum(
-        "ltr,lrs->lts", masked_acts.astype(jnp.float32), picked_act, precision=lax.Precision.HIGHEST
+        "ltr,lrs->lts", masked_acts.astype(jnp.float32), picked_act, precision=HIGHEST
     ).astype(jnp.bfloat16)
     white_grads = jnp.einsum(
-        "ltr,lrs->lts",
-        masked_grads.astype(jnp.float32),
-        picked_grad,
-        precision=lax.Precision.HIGHEST,
+        "ltr,lrs->lts", masked_grads.astype(jnp.float32), picked_grad, precision=HIGHEST
     ).astype(jnp.bfloat16)
     part_scores = tile_scores(
         white_acts,
@@ -47,6 +50,169 @@
         seq_len,
     )
     return jnp.take(part_scores, flagged, axis=1)
+
+
+def z_near(d):
+    return d ^ 4 ^ ((d >> 1) & 1)
+
+
+def prep_kernel(seq_len, lens, acts, grads, own, away):
+    half = lax.axis_index("blk") // 8
+    row = lax.broadcasted_iota(jnp.int32, (acts.shape[1], 1), 0)
+    bound = jnp.zeros_like(row)
+    for s in range(lens.shape[0]):
+        bound = jnp.where(row // seq_len == s, lens[s] + s * seq_len, bound)
+    keep = row < bound
+    for index, src in enumerate((acts, grads)):
+        for layer, dst in ((half, own), (1 - half, away)):
+            x = src[layer]
+            dst[index] = jnp.where(keep, x, jnp.zeros_like(x))
+
+
+def prep(activations, out_grads, lengths, seq_len):
+    unit = jax.ShapeDtypeStruct((2,) + activations.shape[1:], activations.dtype)
+    vmem = pl.BlockSpec(memory_space=pltpu.VMEM)
+    return pl.pallas_call(
+        functools.partial(prep_kernel, seq_len),
+        out_shape=(unit, unit),
+        in_specs=[pl.BlockSpec(memory_space=pltpu.SMEM), vmem, vmem],
+        out_specs=(vmem, vmem),
+        compiler_params=pltpu.CompilerParams(vmem_limit_bytes=59 * 1024 * 1024),
+        name="mask_units",
+    )(lengths, activations, out_grads)
+
+
+def setup_kernel(seq_len, per, layer_ids, flagged, act_f, grad_f, terms, pick, factor, sems):
+    d = lax.axis_index("blk")
+    layer = layer_ids[d // 8]
+    copies = [
+        pltpu.make_async_copy(src.at[layer], factor.at[i], sems.at[i])
+        for i, src in enumerate((act_f, grad_f))
+    ]
+    for copy in copies:
+        copy.start()
+    token = lax.broadcasted_iota(jnp.int32, pick.shape, 0)
+    spot = token // (seq_len * per)
+    slot = spot // 2
+    owner = jnp.where(
+        slot == 0, d, jnp.where(slot == 1, d ^ 1, jnp.where(slot == 2, d ^ 2, z_near(d)))
+    )
+    owner = owner ^ (8 * (spot % 2))
+    seq = owner * per + token // seq_len % per
+    scale = 1.0 / (factor.shape[1] * seq_len)
+    pick[...] = jnp.where(seq == flagged[...], scale, 0.0).astype(pick.dtype)
+    for i, copy in enumerate(copies):
+        copy.wait()
+        rest = factor[i]
+        for n in range(3):
+            term = rest.astype(jnp.bfloat16)
+            terms[i, n] = term
+            rest = rest - term.astype(jnp.float32)
+
+
+def setup(layer_ids, flagged, act_factor, grad_factor, seq_len, per):
+    rank = act_factor.shape[1]
+    vmem = pl.BlockSpec(memory_space=pltpu.VMEM)
+    hbm = pl.BlockSpec(memory_space=pltpu.HBM)
+    return pl.pallas_call(
+        functools.partial(setup_kernel, seq_len, per),
+        out_shape=(
+            jax.ShapeDtypeStruct((2, 3, rank, rank), jnp.bfloat16),
+            jax.ShapeDtypeStruct((8 * per * seq_len, flagged.shape[0]), jnp.bfloat16),
+        ),
+        in_specs=[pl.BlockSpec(memory_space=pltpu.SMEM), vmem, hbm, hbm],
+        out_specs=(vmem, vmem),
+        scratch_shapes=[pltpu.VMEM((2, rank, rank), jnp.float32), pltpu.SemaphoreType.DMA((2,))],
+        compiler_params=pltpu.CompilerParams(vmem_limit_bytes=59 * 1024 * 1024),
+        cost_estimate=pl.CostEstimate(flops=10**9, bytes_accessed=2 * 10**6, transcendentals=0),
+        name="factor_terms",
+    )(layer_ids, flagged.reshape(1, -1), act_factor, grad_factor)
+
+
+def whiten(x, terms):
+    total = jnp.dot(x, terms[0], preferred_element_type=jnp.float32)
+    for n in (1, 2):
+        total = total + jnp.dot(x, terms[n], preferred_element_type=jnp.float32)
+    return total.astype(jnp.bfloat16)
+
+
+def score_kernel(seq_len, terms, pick, *refs):
+    units, outs = refs[:8], refs[8:]
+    f32 = jnp.float32
+    toks = [
+        [jnp.concatenate([units[2 * i][w], units[2 * i + 1][w]], axis=0) for w in range(2)]
+        for i in range(4)
+    ]
+    white = [[whiten(toks[i][w], terms.at[w]) for w in range(2)] for i in range(3)]
+    rows = toks[0][0].shape[0]
+    seqs = rows // seq_len
+
+    def block(left, right):
+        grams = [
+            lax.dot_general(a, b, (((1,), (1,)), ((), ())), preferred_element_type=f32)
+            for a, b in zip(left, right)
+        ]
+        return (grams[0] * grams[1]).reshape(seqs, seq_len, rows).sum(axis=1)
+
+    zeros = jnp.zeros((seqs, rows), f32)
+    lines = [
+        [block(white[0], toks[j]) for j in range(4)],
+        [zeros, zeros] + [block(white[1], toks[j]) for j in (2, 3)],
+        [zeros, zeros, zeros, block(white[2], toks[3])],
+        [zeros, zeros, block(toks[3], white[2]), zeros],
+    ]
+    rest = jnp.concatenate([jnp.concatenate(line, axis=1) for line in lines], axis=0)
+    n = rest.shape[0]
+    parts = []
+    for _ in range(3):
+        part = rest.astype(jnp.bfloat16)
+        parts.append(part)
+        rest = rest - part.astype(f32)
+    picked = jnp.dot(jnp.concatenate(parts, axis=0), pick[...], preferred_element_type=f32)
+    picked = picked[:n] + picked[n : 2 * n] + picked[2 * n :]
+    per = n // 8
+    for i, out in enumerate(outs):
+        out[...] = picked[i * per : (i + 1) * per]
+
+
+def score(units, terms, pick, seq_len):
+    per = units[0].shape[1] // seq_len
+    vmem = pl.BlockSpec(memory_space=pltpu.VMEM)
+    return pl.pallas_call(
+        functools.partial(score_kernel, seq_len),
+        out_shape=[jax.ShapeDtypeStruct((per, pick.shape[1]), jnp.float32)] * 8,
+        in_specs=[vmem] * 10,
+        out_specs=[vmem] * 8,
+        compiler_params=pltpu.CompilerParams(vmem_limit_bytes=40 * 1024 * 1024),
+        cost_estimate=pl.CostEstimate(flops=2 * 10**9, bytes_accessed=2 * 10**6, transcendentals=0),
+        name="pair_scores",
+    )(terms, pick, *units)
+
+
+def paired(activations, out_grads, lengths, layer_ids, flagged, act_factor, grad_factor):
+    size = 16
+    per = lengths.shape[0]
+    seq_len = activations.shape[1] // per
+    own, away = prep(activations, out_grads, lengths, seq_len)
+
+    def send(x, to):
+        return lax.ppermute(x, "blk", [(d, to(d)) for d in range(size)])
+
+    ways = (lambda d: d ^ 1, lambda d: d ^ 2, z_near)
+    opposite = send(away, lambda d: d ^ 8)
+    near = [send(own, to) for to in ways]
+    terms, pick = setup(layer_ids, flagged, act_factor, grad_factor, seq_len, per)
+    opposite, terms, pick = lax.optimization_barrier((opposite, terms, pick))
+    far = [send(opposite, to) for to in ways]
+    units = [own, opposite]
+    for a, b in zip(near, far):
+        units += [a, b]
+    parts = score(units, terms, pick, seq_len)
+    total = parts[0] + send(parts[1], lambda d: d ^ 8)
+    for i, to in enumerate(ways):
+        total = total + send(parts[2 * i + 2], to)
+        total = total + send(parts[2 * i + 3], lambda d, to=to: to(d) ^ 8)
+    return total
 
 
 def solution(mesh):
@@ -60,4 +226,5 @@
         P(),
     )
     out_specs = P(("grp", "blk"), None)
+    shards = paired if mesh.shape["blk"] == 16 else gathered
     return jax.shard_map(shards, mesh=mesh, in_specs=in_specs, out_specs=out_specs, check_vma=False)

time: 108 us -> 36.1 us (0.33)
  waiting for transfers between devices: 77.2 us -> 8.59 us
  starting transfers between devices: 0.04 us -> 18.6 us
  between operations: 13.5 us -> 0.04 us
  local copies, waits for them, and re-layouts: 8.52 us -> 2.09 us
  Pallas kernels: 0 us -> 6.02 us
  matrix products: 5.76 us -> 0 us
  other arithmetic: 2.81 us -> 0.57 us
    all_gather x2 -> x0, waiting for transfers between devices: 76.5 us -> none  [the longest x1 40 us: shards(): lax.all_gather(masked_grads, 'blk', axis=1, tiled=True)]
    ppermute x0 -> x14, starting transfers between devices: none -> 18.6 us  [send(): return lax.ppermute(x, 'blk', [(d, to(d)) for d in range(size)])]
    ppermute x0 -> x14, waiting for transfers between devices: none -> 8.59 us  [send(): return lax.ppermute(x, 'blk', [(d, to(d)) for d in range(size)])]
    gather x3 -> x0, local copies, waits for them, and re-layouts: 6.11 us -> none  [the longest x1 2.77 us: shards(): picked_grad = jnp.take(grad_factor, layer_ids, axis=0)]
    pallas_call x0 -> x3, Pallas kernels: none -> 6.02 us  [the longest x1 2.83 us: setup(): pl.pallas_call(functools.partial(setup_kernel, seq_len, per), out_shape=(...]
    dot_general x4 -> x0, matrix products: 5.76 us -> none  [the longest x1 2.49 us: tile_scores(): jnp.einsum('lqr,lkr->lqk', white_grads, remote_grads, preferred_element_t...]
    unnamed x8 -> x6, local copies, waits for them, and re-layouts: 0.01 us -> 2.09 us
    mul x2 -> x0, other arithmetic: 1.76 us -> none  [the longest x1 1.75 us: shards(): masked_grads = out_grads * keep[None, :, None]]
  transfers between devices with their start and end apart: 2 -> 14, of which waited for: 2 -> 6; matrix products, arithmetic and copies ran while one was open for 9% -> 0% of each run, Pallas kernels for 0% -> 8%
where the time goes in v2:
time: 36.1 us; the launch traced here: 35.9 us
  starting transfers between devices  18.6 us (52%)
  waiting for transfers between devices  8.59 us (24%)
  Pallas kernels  6.02 us (17%)
  local copies, waits for them, and re-layouts  2.09 us (6%)
  other arithmetic  0.57 us (2%)
    ppermute x14, starting transfers between devices, send(): return lax.ppermute(x, 'blk', [(d, to(d)) for d in range(size)])  18.6 us
    ppermute x14, waiting for transfers between devices, send(): return lax.ppermute(x, 'blk', [(d, to(d)) for d in range(size)])  8.59 us
    pallas_call x1, Pallas kernels, setup(): pl.pallas_call(functools.partial(setup_kernel, seq_len, per), out_shape=(...  2.83 us
    unnamed x6, local copies, waits for them, and re-layouts  2.09 us
    pallas_call x1, Pallas kernels, prep(): pl.pallas_call(functools.partial(prep_kernel, seq_len), out_shape=(unit,...  1.73 us
    pallas_call x1, Pallas kernels, score(): pl.pallas_call(functools.partial(score_kernel, seq_len), out_shape=[jax.S...  1.46 us
  transfers between devices with their start and end apart: 14, of which 6 were waited for; matrix products, arithmetic and copies ran while one was open for 0% of the time, Pallas kernels for 8%

profile of v2, /device:TPU:0, one launch (start us, length us, event | category | flops | bytes accessed | tf_op | source)
XLA Modules:
  0.0 35.9 jit_solution(7328979689776054407)
XLA Ops:
  0.0 1.7 %mask_units.1 = (bf16[2,128,256]{2,1,0:T(8,128)(2,1)}, bf16[2,128,256]{2,1,0:T(8,128)(2,1)}) custom-call(s32[2]{0:T(128)} %lens.1, bf16[2,128,256]{2,1,0:T(8,128)(2,1)} %acts.1, bf16[2,128,256]{2,1,0:T(8,128)(2,1)} %grads.1), custom_call_target="tpu_custom_call" | custom-call | tf_op jit(solution)/shard_map/mask_units/pallas_call | solution.py:75
  1.7 4.0 %collective-permute-start = (bf16[2,128,256]{2,1,0:T(8,128)(2,1)}, bf16[2,128,256]{2,1,0:T(8,128)(2,1)S(1)}, u32[]{:S(2)}, u32[]{:S(2)}) collective-permute-start(bf16[2,128,256]{2,1,0:T(8,128)(2,1)} %get-tuple-element.20), channel_id=1, source_target_pairs={{0,8},{1,9},{2,10},{3,11},{4,12},{5,13},{6,14},{7,15},{8,0},{9,1},... | collective-permute-start | bytes 393224 | tf_op jit(solution)/shard_map/ppermute | solution.py:199
  5.8 1.6 %collective-permute-start.5 = (bf16[2,128,256]{2,1,0:T(8,128)(2,1)}, bf16[2,128,256]{2,1,0:T(8,128)(2,1)S(1)}, u32[]{:S(2)}, u32[]{:S(2)}) collective-permute-start(bf16[2,128,256]{2,1,0:T(8,128)(2,1)} %get-tuple-element.25.refs_0_), channel_id=1, source_target_pairs={{0,4},{1,5},{2,7},{3,6},{4,0},{5,1},{6,3},{7,2},{8,12},{9,13},{10,... | collective-permute-start | bytes 393224 | tf_op jit(solution)/shard_map/ppermute | solution.py:199
  7.3 0.7 %collective-permute-start.3 = (bf16[2,128,256]{2,1,0:T(8,128)(2,1)}, bf16[2,128,256]{2,1,0:T(8,128)(2,1)S(1)}, u32[]{:S(2)}, u32[]{:S(2)}) collective-permute-start(bf16[2,128,256]{2,1,0:T(8,128)(2,1)} %get-tuple-element.25.refs_0_), channel_id=1, source_target_pairs={{0,2},{1,3},{2,0},{3,1},{4,6},{5,7},{6,4},{7,5},{8,10},{9,11},{10,... | collective-permute-start | bytes 393224 | tf_op jit(solution)/shard_map/ppermute | solution.py:199
  8.0 0.7 %collective-permute-start.1 = (bf16[2,128,256]{2,1,0:T(8,128)(2,1)}, bf16[2,128,256]{2,1,0:T(8,128)(2,1)S(1)}, u32[]{:S(2)}, u32[]{:S(2)}) collective-permute-start(bf16[2,128,256]{2,1,0:T(8,128)(2,1)} %get-tuple-element.25.refs_0_), channel_id=1, source_target_pairs={{0,1},{1,0},{2,3},{3,2},{4,5},{5,4},{6,7},{7,6},{8,9},{9,8},{10,11... | collective-permute-start | bytes 393224 | tf_op jit(solution)/shard_map/ppermute | solution.py:199
  8.7 2.8 %factor_terms.1 = (bf16[2,3,256,256]{3,2,1,0:T(8,128)(2,1)}, bf16[1024,32]{1,0:T(8,128)(2,1)}) custom-call(s32[2]{0:T(128)} %layer_ids.1, s32[1,32]{1,0:T(1,128)} %bitcast.1, f32[16,256,256]{2,1,0:T(8,128)} %act_f.1, f32[16,256,256]{2,1,0:T(8,128)} %grad_f.1), custom_call_target="tpu_custom_call" | custom-call | flops 1000000000 | bytes 2000000 | tf_op jit(solution)/shard_map/factor_terms/pallas_call | solution.py:117
  11.5 0.9 %collective-permute-done.refs_1_ = bf16[2,128,256]{2,1,0:T(8,128)(2,1)S(1)} collective-permute-done((bf16[2,128,256]{2,1,0:T(8,128)(2,1)}, bf16[2,128,256]{2,1,0:T(8,128)(2,1)S(1)}, u32[]{:S(2)}, u32[]{:S(2)}) %collective-permute-start) | collective-permute-done | bytes 131104 | tf_op jit(solution)/shard_map/ppermute | solution.py:199
  12.4 0.7 %collective-permute-start.6 = (bf16[2,128,256]{2,1,0:T(8,128)(2,1)S(1)}, bf16[2,128,256]{2,1,0:T(8,128)(2,1)S(1)}, u32[]{:S(2)}, u32[]{:S(2)}) collective-permute-start(bf16[2,128,256]{2,1,0:T(8,128)(2,1)S(1)} %collective-permute-done.refs_1_), channel_id=1, source_target_pairs={{0,4},{1,5},{2,7},{3,6},{4,0},{5,1},{6,3},{7,2},{8,12},{9,13},{10,... | collective-permute-start | bytes 393224 | tf_op jit(solution)/shard_map/ppermute | solution.py:199
  13.1 1.1 %collective-permute-start.4 = (bf16[2,128,256]{2,1,0:T(8,128)(2,1)S(1)}, bf16[2,128,256]{2,1,0:T(8,128)(2,1)S(1)}, u32[]{:S(2)}, u32[]{:S(2)}) collective-permute-start(bf16[2,128,256]{2,1,0:T(8,128)(2,1)S(1)} %collective-permute-done.refs_1_), channel_id=1, source_target_pairs={{0,2},{1,3},{2,0},{3,1},{4,6},{5,7},{6,4},{7,5},{8,10},{9,11},{10,... | collective-permute-start | bytes 393224 | tf_op jit(solution)/shard_map/ppermute | solution.py:199
  14.2 0.0 collective-permute-done.5.refs_6_
  14.2 0.2 collective-permute-start.2
  14.4 0.0 collective-permute-done.3.refs_4_
  14.4 0.0 collective-permute-done.1.refs_2_
  14.4 2.9 %collective-permute-done.6.refs_7_ = bf16[2,128,256]{2,1,0:T(8,128)(2,1)S(1)} collective-permute-done((bf16[2,128,256]{2,1,0:T(8,128)(2,1)S(1)}, bf16[2,128,256]{2,1,0:T(8,128)(2,1)S(1)}, u32[]{:S(2)}, u32[]{:S(2)}) %collective-permute-start.6) | collective-permute-done | bytes 131104 | tf_op jit(solution)/shard_map/ppermute | solution.py:199
  17.4 1.0 %collective-permute-done.4.refs_5_ = bf16[2,128,256]{2,1,0:T(8,128)(2,1)S(1)} collective-permute-done((bf16[2,128,256]{2,1,0:T(8,128)(2,1)S(1)}, bf16[2,128,256]{2,1,0:T(8,128)(2,1)S(1)}, u32[]{:S(2)}, u32[]{:S(2)}) %collective-permute-start.4) | collective-permute-done | bytes 131104 | tf_op jit(solution)/shard_map/ppermute | solution.py:199
  18.4 0.0 collective-permute-done.2.refs_3_
  18.4 1.1 %copy-done = bf16[2,3,256,256]{3,2,1,0:T(8,128)(2,1)S(1)} copy-done((bf16[2,3,256,256]{3,2,1,0:T(8,128)(2,1)S(1)}, bf16[2,3,256,256]{3,2,1,0:T(8,128)(2,1)}, u32[]{:S(2)}) %copy-start) | copy-done | bytes 786456
  19.5 0.9 %copy-done.1 = bf16[1024,32]{1,0:T(8,128)(2,1)S(1)} copy-done((bf16[1024,32]{1,0:T(8,128)(2,1)S(1)}, bf16[1024,32]{1,0:T(8,128)(2,1)}, u32[]{:S(2)}) %copy-start.1) | copy-done | bytes 65560
  20.5 1.5 %pair_scores.1 = (f32[2,32]{1,0:T(2,128)S(1)}, f32[2,32]{1,0:T(2,128)S(1)}, f32[2,32]{1,0:T(2,128)S(1)}, f32[2,32]{1,0:T(2,128)S(1)}, f32[2,32]{1,0:T(2,128)S(1)...) custom-call(bf16[2,3,256,256]{3,2,1,0:T(8,128)(2,1)S(1)} %copy-done, ...), custom_call_target="tpu_custom_call" | custom-call | flops 2000000000 | bytes 2000000 | tf_op jit(solution)/shard_map/pair_scores/pallas_call | solution.py:181
  21.9 3.3 %collective-permute-start.7 = (f32[2,32]{1,0:T(2,128)S(1)}, f32[2,32]{1,0:T(2,128)S(1)}, u32[]{:S(2)}, u32[]{:S(2)}) collective-permute-start(f32[2,32]{1,0:T(2,128)S(1)} %get-tuple-element.28), channel_id=1, source_target_pairs={{0,8},{1,9},{2,10},{3,11},{4,12},{5,13},{6,14},{7,15},{8,0},{9,1},... | collective-permute-start | bytes 776 | tf_op jit(solution)/shard_map/ppermute | solution.py:199
  25.3 0.2 collective-permute-start.9
  25.5 1.7 %collective-permute-start.10 = (f32[2,32]{1,0:T(2,128)S(1)}, f32[2,32]{1,0:T(2,128)S(1)}, u32[]{:S(2)}, u32[]{:S(2)}) collective-permute-start(f32[2,32]{1,0:T(2,128)S(1)} %get-tuple-element.31), channel_id=1, source_target_pairs={{0,2},{1,3},{2,0},{3,1},{4,6},{5,7},{6,4},{7,5},{8,10},{9,11},{10,... | collective-permute-start | bytes 776 | tf_op jit(solution)/shard_map/ppermute | solution.py:199
  27.2 2.6 %collective-permute-start.11 = (f32[2,32]{1,0:T(2,128)S(1)}, f32[2,32]{1,0:T(2,128)S(1)}, u32[]{:S(2)}, u32[]{:S(2)}) collective-permute-start(f32[2,32]{1,0:T(2,128)S(1)} %get-tuple-element.32), channel_id=1, source_target_pairs={{0,10},{1,11},{2,8},{3,9},{4,14},{5,15},{6,12},{7,13},{8,2},{9,3},... | collective-permute-start | bytes 776 | tf_op jit(solution)/shard_map/ppermute | solution.py:199
  29.8 0.2 collective-permute-start.12
  29.9 0.0 collective-permute-done.8
  29.9 1.6 %collective-permute-start.13 = (f32[2,32]{1,0:T(2,128)S(1)}, f32[2,32]{1,0:T(2,128)S(1)}, u32[]{:S(2)}, u32[]{:S(2)}) collective-permute-start(f32[2,32]{1,0:T(2,128)S(1)} %get-tuple-element.34), channel_id=1, source_target_pairs={{0,12},{1,13},{2,15},{3,14},{4,8},{5,9},{6,11},{7,10},{8,4},{9,5},... | collective-permute-start | bytes 776 | tf_op jit(solution)/shard_map/ppermute | solution.py:199
  31.5 0.0 collective-permute-done.9
  31.5 0.0 collective-permute-done.10
  31.5 1.1 %collective-permute-done.11 = f32[2,32]{1,0:T(2,128)S(1)} collective-permute-done((f32[2,32]{1,0:T(2,128)S(1)}, f32[2,32]{1,0:T(2,128)S(1)}, u32[]{:S(2)}, u32[]{:S(2)}) %collective-permute-start.11) | collective-permute-done | bytes 288 | tf_op jit(solution)/shard_map/ppermute | solution.py:199
  32.6 0.8 %collective-permute-done.12 = f32[2,32]{1,0:T(2,128)S(1)} collective-permute-done((f32[2,32]{1,0:T(2,128)S(1)}, f32[2,32]{1,0:T(2,128)S(1)}, u32[]{:S(2)}, u32[]{:S(2)}) %collective-permute-start.12) | collective-permute-done | bytes 288 | tf_op jit(solution)/shard_map/ppermute | solution.py:199
  33.4 2.0 %collective-permute-done.13 = f32[2,32]{1,0:T(2,128)S(1)} collective-permute-done((f32[2,32]{1,0:T(2,128)S(1)}, f32[2,32]{1,0:T(2,128)S(1)}, u32[]{:S(2)}, u32[]{:S(2)}) %collective-permute-start.13) | collective-permute-done | bytes 288 | tf_op jit(solution)/shard_map/ppermute | solution.py:199
  35.3 0.6 %add_add_fusion = f32[2,32]{1,0:T(2,128)} fusion(f32[2,32]{1,0:T(2,128)S(1)} %collective-permute-done.13, f32[2,32]{1,0:T(2,128)S(1)} %collective-permute-done.12, f32[2,32]{1,0:T(2,128)S(1)} %collective-permute-done.11, f32[2,32]{1,0:T(2,128)S(1)} %collective-permute-done.10, f32[2,32]{1,0:T(2,128)S(1)} %collective-permute-done.9, ...), kind=kLoop, calls=%fused_computation | loop fusion | flops 448 | bytes 2304 | tf_op jit(solution)/shard_map/add | solution.py:214
  (6 shorter events, 0.0 us)
Async XLA Ops:
  1.7 10.7 %collective-permute-start = (bf16[2,128,256]{2,1,0:T(8,128)(2,1)}, bf16[2,128,256]{2,1,0:T(8,128)(2,1)S(1)}, u32[]{:S(2)}, u32[]{:S(2)}) collective-permute-start(bf16[2,128,256]{2,1,0:T(8,128)(2,1)} %get-tuple-element.20), channel_id=1, source_target_pairs={{0,8},{1,9},{2,10},{3,11},{4,12},{5,13},{6,14},{7,15},{8,0},{9,1},... | collective-permute-start | bytes 393224 | tf_op jit(solution)/shard_map/ppermute | solution.py:199
  5.8 8.5 %collective-permute-start.5 = (bf16[2,128,256]{2,1,0:T(8,128)(2,1)}, bf16[2,128,256]{2,1,0:T(8,128)(2,1)S(1)}, u32[]{:S(2)}, u32[]{:S(2)}) collective-permute-start(bf16[2,128,256]{2,1,0:T(8,128)(2,1)} %get-tuple-element.25.refs_0_), channel_id=1, source_target_pairs={{0,4},{1,5},{2,7},{3,6},{4,0},{5,1},{6,3},{7,2},{8,12},{9,13},{10,... | collective-permute-start | bytes 393224 | tf_op jit(solution)/shard_map/ppermute | solution.py:199
  7.3 7.1 %collective-permute-start.3 = (bf16[2,128,256]{2,1,0:T(8,128)(2,1)}, bf16[2,128,256]{2,1,0:T(8,128)(2,1)S(1)}, u32[]{:S(2)}, u32[]{:S(2)}) collective-permute-start(bf16[2,128,256]{2,1,0:T(8,128)(2,1)} %get-tuple-element.25.refs_0_), channel_id=1, source_target_pairs={{0,2},{1,3},{2,0},{3,1},{4,6},{5,7},{6,4},{7,5},{8,10},{9,11},{10,... | collective-permute-start | bytes 393224 | tf_op jit(solution)/shard_map/ppermute | solution.py:199
  8.0 6.5 %collective-permute-start.1 = (bf16[2,128,256]{2,1,0:T(8,128)(2,1)}, bf16[2,128,256]{2,1,0:T(8,128)(2,1)S(1)}, u32[]{:S(2)}, u32[]{:S(2)}) collective-permute-start(bf16[2,128,256]{2,1,0:T(8,128)(2,1)} %get-tuple-element.25.refs_0_), channel_id=1, source_target_pairs={{0,1},{1,0},{2,3},{3,2},{4,5},{5,4},{6,7},{7,6},{8,9},{9,8},{10,11... | collective-permute-start | bytes 393224 | tf_op jit(solution)/shard_map/ppermute | solution.py:199
  8.7 9.7 %copy-start.2 = (bf16[2,128,256]{2,1,0:T(8,128)(2,1)S(1)}, bf16[2,128,256]{2,1,0:T(8,128)(2,1)}, u32[]{:S(2)}) copy-start(bf16[2,128,256]{2,1,0:T(8,128)(2,1)} %get-tuple-element.25.refs_0_) | copy-start | bytes 393220
  12.4 5.0 %collective-permute-start.6 = (bf16[2,128,256]{2,1,0:T(8,128)(2,1)S(1)}, bf16[2,128,256]{2,1,0:T(8,128)(2,1)S(1)}, u32[]{:S(2)}, u32[]{:S(2)}) collective-permute-start(bf16[2,128,256]{2,1,0:T(8,128)(2,1)S(1)} %collective-permute-done.refs_1_), channel_id=1, source_target_pairs={{0,4},{1,5},{2,7},{3,6},{4,0},{5,1},{6,3},{7,2},{8,12},{9,13},{10,... | collective-permute-start | bytes 393224 | tf_op jit(solution)/shard_map/ppermute | solution.py:199
  13.1 5.3 %collective-permute-start.4 = (bf16[2,128,256]{2,1,0:T(8,128)(2,1)S(1)}, bf16[2,128,256]{2,1,0:T(8,128)(2,1)S(1)}, u32[]{:S(2)}, u32[]{:S(2)}) collective-permute-start(bf16[2,128,256]{2,1,0:T(8,128)(2,1)S(1)} %collective-permute-done.refs_1_), channel_id=1, source_target_pairs={{0,2},{1,3},{2,0},{3,1},{4,6},{5,7},{6,4},{7,5},{8,10},{9,11},{10,... | collective-permute-start | bytes 393224 | tf_op jit(solution)/shard_map/ppermute | solution.py:199
  14.2 4.2 %collective-permute-start.2 = (bf16[2,128,256]{2,1,0:T(8,128)(2,1)S(1)}, bf16[2,128,256]{2,1,0:T(8,128)(2,1)S(1)}, u32[]{:S(2)}, u32[]{:S(2)}) collective-permute-start(bf16[2,128,256]{2,1,0:T(8,128)(2,1)S(1)} %collective-permute-done.refs_1_), channel_id=1, source_target_pairs={{0,1},{1,0},{2,3},{3,2},{4,5},{5,4},{6,7},{7,6},{8,9},{9,8},{10,11... | collective-permute-start | bytes 393224 | tf_op jit(solution)/shard_map/ppermute | solution.py:199
  18.4 1.1 %copy-start = (bf16[2,3,256,256]{3,2,1,0:T(8,128)(2,1)S(1)}, bf16[2,3,256,256]{3,2,1,0:T(8,128)(2,1)}, u32[]{:S(2)}) copy-start(bf16[2,3,256,256]{3,2,1,0:T(8,128)(2,1)} %get-tuple-element.23.terms) | copy-start | bytes 2359300
  19.5 0.9 %copy-start.1 = (bf16[1024,32]{1,0:T(8,128)(2,1)S(1)}, bf16[1024,32]{1,0:T(8,128)(2,1)}, u32[]{:S(2)}) copy-start(bf16[1024,32]{1,0:T(8,128)(2,1)} %get-tuple-element.24.pick) | copy-start | bytes 196612
  21.9 7.8 %collective-permute-start.7 = (f32[2,32]{1,0:T(2,128)S(1)}, f32[2,32]{1,0:T(2,128)S(1)}, u32[]{:S(2)}, u32[]{:S(2)}) collective-permute-start(f32[2,32]{1,0:T(2,128)S(1)} %get-tuple-element.28), channel_id=1, source_target_pairs={{0,8},{1,9},{2,10},{3,11},{4,12},{5,13},{6,14},{7,15},{8,0},{9,1},... | collective-permute-start | bytes 776 | tf_op jit(solution)/shard_map/ppermute | solution.py:199
  25.3 4.7 %collective-permute-start.8 = (f32[2,32]{1,0:T(2,128)S(1)}, f32[2,32]{1,0:T(2,128)S(1)}, u32[]{:S(2)}, u32[]{:S(2)}) collective-permute-start(f32[2,32]{1,0:T(2,128)S(1)} %get-tuple-element.29), channel_id=1, source_target_pairs={{0,1},{1,0},{2,3},{3,2},{4,5},{5,4},{6,7},{7,6},{8,9},{9,8},{10,11... | collective-permute-start | bytes 776 | tf_op jit(solution)/shard_map/ppermute | solution.py:199
  25.3 6.3 %collective-permute-start.9 = (f32[2,32]{1,0:T(2,128)S(1)}, f32[2,32]{1,0:T(2,128)S(1)}, u32[]{:S(2)}, u32[]{:S(2)}) collective-permute-start(f32[2,32]{1,0:T(2,128)S(1)} %get-tuple-element.30), channel_id=1, source_target_pairs={{0,9},{1,8},{2,11},{3,10},{4,13},{5,12},{6,15},{7,14},{8,1},{9,0},... | collective-permute-start | bytes 776 | tf_op jit(solution)/shard_map/ppermute | solution.py:199
  25.5 6.1 %collective-permute-start.10 = (f32[2,32]{1,0:T(2,128)S(1)}, f32[2,32]{1,0:T(2,128)S(1)}, u32[]{:S(2)}, u32[]{:S(2)}) collective-permute-start(f32[2,32]{1,0:T(2,128)S(1)} %get-tuple-element.31), channel_id=1, source_target_pairs={{0,2},{1,3},{2,0},{3,1},{4,6},{5,7},{6,4},{7,5},{8,10},{9,11},{10,... | collective-permute-start | bytes 776 | tf_op jit(solution)/shard_map/ppermute | solution.py:199
  27.2 5.4 %collective-permute-start.11 = (f32[2,32]{1,0:T(2,128)S(1)}, f32[2,32]{1,0:T(2,128)S(1)}, u32[]{:S(2)}, u32[]{:S(2)}) collective-permute-start(f32[2,32]{1,0:T(2,128)S(1)} %get-tuple-element.32), channel_id=1, source_target_pairs={{0,10},{1,11},{2,8},{3,9},{4,14},{5,15},{6,12},{7,13},{8,2},{9,3},... | collective-permute-start | bytes 776 | tf_op jit(solution)/shard_map/ppermute | solution.py:199
  29.8 3.6 %collective-permute-start.12 = (f32[2,32]{1,0:T(2,128)S(1)}, f32[2,32]{1,0:T(2,128)S(1)}, u32[]{:S(2)}, u32[]{:S(2)}) collective-permute-start(f32[2,32]{1,0:T(2,128)S(1)} %get-tuple-element.33), channel_id=1, source_target_pairs={{0,4},{1,5},{2,7},{3,6},{4,0},{5,1},{6,3},{7,2},{8,12},{9,13},{10,... | collective-permute-start | bytes 776 | tf_op jit(solution)/shard_map/ppermute | solution.py:199
  29.9 5.4 %collective-permute-start.13 = (f32[2,32]{1,0:T(2,128)S(1)}, f32[2,32]{1,0:T(2,128)S(1)}, u32[]{:S(2)}, u32[]{:S(2)}) collective-permute-start(f32[2,32]{1,0:T(2,128)S(1)} %get-tuple-element.34), channel_id=1, source_target_pairs={{0,12},{1,13},{2,15},{3,14},{4,8},{5,9},{6,11},{7,10},{8,4},{9,5},... | collective-permute-start | bytes 776 | tf_op jit(solution)/shard_map/ppermute | solution.py:199

commit v3 on v2

--- a/solution.py
+++ b/solution.py
@@ -123,7 +123,7 @@
         in_specs=[pl.BlockSpec(memory_space=pltpu.SMEM), vmem, hbm, hbm],
         out_specs=(vmem, vmem),
         scratch_shapes=[pltpu.VMEM((2, rank, rank), jnp.float32), pltpu.SemaphoreType.DMA((2,))],
-        compiler_params=pltpu.CompilerParams(vmem_limit_bytes=59 * 1024 * 1024),
+        compiler_params=pltpu.CompilerParams(vmem_limit_bytes=51 * 1024 * 1024),
         cost_estimate=pl.CostEstimate(flops=10**9, bytes_accessed=2 * 10**6, transcendentals=0),
         name="factor_terms",
     )(layer_ids, flagged.reshape(1, -1), act_factor, grad_factor)
@@ -143,7 +143,7 @@
         [jnp.concatenate([units[2 * i][w], units[2 * i + 1][w]], axis=0) for w in range(2)]
         for i in range(4)
     ]
-    white = [[whiten(toks[i][w], terms.at[w]) for w in range(2)] for i in range(3)]
+    white = {i: [whiten(toks[i][w], terms.at[w]) for w in range(2)] for i in (0, 2, 3)}
     rows = toks[0][0].shape[0]
     seqs = rows // seq_len
 
@@ -157,9 +157,8 @@
     zeros = jnp.zeros((seqs, rows), f32)
     lines = [
         [block(white[0], toks[j]) for j in range(4)],
-        [zeros, zeros] + [block(white[1], toks[j]) for j in (2, 3)],
-        [zeros, zeros, zeros, block(white[2], toks[3])],
-        [zeros, zeros, block(toks[3], white[2]), zeros],
+        [zeros, block(white[2], toks[1]), zeros, block(white[2], toks[3])],
+        [zeros, block(white[3], toks[1]), block(white[3], toks[2]), zeros],
     ]
     rest = jnp.concatenate([jnp.concatenate(line, axis=1) for line in lines], axis=0)
     n = rest.shape[0]
@@ -170,19 +169,18 @@
         rest = rest - part.astype(f32)
     picked = jnp.dot(jnp.concatenate(parts, axis=0), pick[...], preferred_element_type=f32)
     picked = picked[:n] + picked[n : 2 * n] + picked[2 * n :]
-    per = n // 8
     for i, out in enumerate(outs):
-        out[...] = picked[i * per : (i + 1) * per]
+        out[...] = picked[i * seqs : (i + 1) * seqs]
 
 
 def score(units, terms, pick, seq_len):
-    per = units[0].shape[1] // seq_len
+    seqs = 2 * units[0].shape[1] // seq_len
     vmem = pl.BlockSpec(memory_space=pltpu.VMEM)
     return pl.pallas_call(
         functools.partial(score_kernel, seq_len),
-        out_shape=[jax.ShapeDtypeStruct((per, pick.shape[1]), jnp.float32)] * 8,
+        out_shape=[jax.ShapeDtypeStruct((seqs, pick.shape[1]), jnp.float32)] * 3,
         in_specs=[vmem] * 10,
-        out_specs=[vmem] * 8,
+        out_specs=[vmem] * 3,
         compiler_params=pltpu.CompilerParams(vmem_limit_bytes=40 * 1024 * 1024),
         cost_estimate=pl.CostEstimate(flops=2 * 10**9, bytes_accessed=2 * 10**6, transcendentals=0),
         name="pair_scores",
@@ -207,12 +205,9 @@
     units = [own, opposite]
     for a, b in zip(near, far):
         units += [a, b]
-    parts = score(units, terms, pick, seq_len)
-    total = parts[0] + send(parts[1], lambda d: d ^ 8)
-    for i, to in enumerate(ways):
-        total = total + send(parts[2 * i + 2], to)
-        total = total + send(parts[2 * i + 3], lambda d, to=to: to(d) ^ 8)
-    return total
+    mine, by_x, by_z = score(units, terms, pick, seq_len)
+    half_sum = mine + send(by_x, lambda d: d ^ 2) + send(by_z, z_near)
+    return half_sum[:per] + send(half_sum[per:], lambda d: d ^ 8)
 
 
 def solution(mesh):

time: 36.1 us -> 30.9 us (0.86)
  starting transfers between devices: 18.6 us -> 14.6 us
  Pallas kernels: 6.02 us -> 4.85 us
  waiting for transfers between devices: 8.59 us -> 9.37 us
  local copies, waits for them, and re-layouts: 2.09 us -> 1.32 us
    ppermute x14 -> x10, starting transfers between devices: 18.6 us -> 14.6 us  [send(): return lax.ppermute(x, 'blk', [(d, to(d)) for d in range(size)])]
    pallas_call x1, Pallas kernels: 2.83 us -> 1.67 us  [setup(): pl.pallas_call(functools.partial(setup_kernel, seq_len, per), out_shape=(...]
    unnamed x6, local copies, waits for them, and re-layouts: 2.09 us -> 1.31 us
    ppermute x14 -> x10, waiting for transfers between devices: 8.59 us -> 9.37 us  [send(): return lax.ppermute(x, 'blk', [(d, to(d)) for d in range(size)])]
  transfers between devices with their start and end apart: 14 -> 10, of which waited for: 6 -> 6; matrix products, arithmetic and copies ran while one was open for 0% -> 0% of each run, Pallas kernels for 8% -> 5%
where the time goes in v3:
time: 30.9 us; the launch traced here: 30.7 us
  starting transfers between devices  14.6 us (47%)
  waiting for transfers between devices  9.37 us (30%)
  Pallas kernels  4.85 us (16%)
  local copies, waits for them, and re-layouts  1.32 us (4%)
  other arithmetic  0.57 us (2%)
    ppermute x10, starting transfers between devices, send(): return lax.ppermute(x, 'blk', [(d, to(d)) for d in range(size)])  14.6 us
    ppermute x10, waiting for transfers between devices, send(): return lax.ppermute(x, 'blk', [(d, to(d)) for d in range(size)])  9.37 us
    pallas_call x1, Pallas kernels, prep(): pl.pallas_call(functools.partial(prep_kernel, seq_len), out_shape=(unit,...  1.71 us
    pallas_call x1, Pallas kernels, setup(): pl.pallas_call(functools.partial(setup_kernel, seq_len, per), out_shape=(...  1.67 us
    pallas_call x1, Pallas kernels, score(): pl.pallas_call(functools.partial(score_kernel, seq_len), out_shape=[jax.S...  1.47 us
    unnamed x6, local copies, waits for them, and re-layouts  1.31 us
  transfers between devices with their start and end apart: 10, of which 6 were waited for; matrix products, arithmetic and copies ran while one was open for 0% of the time, Pallas kernels for 5%

profile of v3, /device:TPU:0, one launch (start us, length us, event | category | flops | bytes accessed | tf_op | source)
XLA Modules:
  0.0 30.7 jit_solution(15614529632417783039)
XLA Ops:
  0.0 1.7 %mask_units.1 = (bf16[2,128,256]{2,1,0:T(8,128)(2,1)}, bf16[2,128,256]{2,1,0:T(8,128)(2,1)}) custom-call(s32[2]{0:T(128)} %lens.1, bf16[2,128,256]{2,1,0:T(8,128)(2,1)} %acts.1, bf16[2,128,256]{2,1,0:T(8,128)(2,1)} %grads.1), custom_call_target="tpu_custom_call" | custom-call | tf_op jit(solution)/shard_map/mask_units/pallas_call | solution.py:75
  1.7 4.0 %collective-permute-start = (bf16[2,128,256]{2,1,0:T(8,128)(2,1)}, bf16[2,128,256]{2,1,0:T(8,128)(2,1)S(1)}, u32[]{:S(2)}, u32[]{:S(2)}) collective-permute-start(bf16[2,128,256]{2,1,0:T(8,128)(2,1)} %get-tuple-element.15), channel_id=1, source_target_pairs={{0,8},{1,9},{2,10},{3,11},{4,12},{5,13},{6,14},{7,15},{8,0},{9,1},... | collective-permute-start | bytes 393224 | tf_op jit(solution)/shard_map/ppermute | solution.py:197
  5.7 1.6 %collective-permute-start.5 = (bf16[2,128,256]{2,1,0:T(8,128)(2,1)}, bf16[2,128,256]{2,1,0:T(8,128)(2,1)S(1)}, u32[]{:S(2)}, u32[]{:S(2)}) collective-permute-start(bf16[2,128,256]{2,1,0:T(8,128)(2,1)} %get-tuple-element.20.refs_0_), channel_id=1, source_target_pairs={{0,4},{1,5},{2,7},{3,6},{4,0},{5,1},{6,3},{7,2},{8,12},{9,13},{10,... | collective-permute-start | bytes 393224 | tf_op jit(solution)/shard_map/ppermute | solution.py:197
  7.3 0.7 %collective-permute-start.3 = (bf16[2,128,256]{2,1,0:T(8,128)(2,1)}, bf16[2,128,256]{2,1,0:T(8,128)(2,1)S(1)}, u32[]{:S(2)}, u32[]{:S(2)}) collective-permute-start(bf16[2,128,256]{2,1,0:T(8,128)(2,1)} %get-tuple-element.20.refs_0_), channel_id=1, source_target_pairs={{0,2},{1,3},{2,0},{3,1},{4,6},{5,7},{6,4},{7,5},{8,10},{9,11},{10,... | collective-permute-start | bytes 393224 | tf_op jit(solution)/shard_map/ppermute | solution.py:197
  8.0 0.7 %collective-permute-start.1 = (bf16[2,128,256]{2,1,0:T(8,128)(2,1)}, bf16[2,128,256]{2,1,0:T(8,128)(2,1)S(1)}, u32[]{:S(2)}, u32[]{:S(2)}) collective-permute-start(bf16[2,128,256]{2,1,0:T(8,128)(2,1)} %get-tuple-element.20.refs_0_), channel_id=1, source_target_pairs={{0,1},{1,0},{2,3},{3,2},{4,5},{5,4},{6,7},{7,6},{8,9},{9,8},{10,11... | collective-permute-start | bytes 393224 | tf_op jit(solution)/shard_map/ppermute | solution.py:197
  8.6 0.0 copy-start
  8.7 0.7 %copy-done = s32[2]{0:T(128)S(1)} copy-done((s32[2]{0:T(128)S(1)}, s32[2]{0:T(128)}, u32[]{:S(2)}) %copy-start) | copy-done | bytes 32
  9.3 0.0 copy-start.1
  9.3 0.7 %copy-done.1 = s32[32]{0:T(128)S(1)} copy-done((s32[32]{0:T(128)S(1)}, s32[32]{0:T(128)}, u32[]{:S(2)}) %copy-start.1) | copy-done | bytes 152
  10.0 0.0 copy-start.2
  10.0 1.7 %factor_terms.1 = (bf16[2,3,256,256]{3,2,1,0:T(8,128)(2,1)S(1)}, bf16[1024,32]{1,0:T(8,128)(2,1)S(1)}) custom-call(s32[2]{0:T(128)S(1)} %copy-done, s32[1,32]{1,0:T(1,128)S(1)} %bitcast.1, f32[16,256,256]{2,1,0:T(8,128)} %act_f.1, f32[16,256,256]{2,1,0:T(8,128)} %grad_f.1), custom_call_target="tpu_custom_call" | custom-call | flops 1000000000 | bytes 2000000 | tf_op jit(solution)/shard_map/factor_terms/pallas_call | solution.py:117
  11.6 0.7 %collective-permute-done.refs_1_ = bf16[2,128,256]{2,1,0:T(8,128)(2,1)S(1)} collective-permute-done((bf16[2,128,256]{2,1,0:T(8,128)(2,1)}, bf16[2,128,256]{2,1,0:T(8,128)(2,1)S(1)}, u32[]{:S(2)}, u32[]{:S(2)}) %collective-permute-start) | collective-permute-done | bytes 131104 | tf_op jit(solution)/shard_map/ppermute | solution.py:197
  12.4 0.7 %collective-permute-start.6 = (bf16[2,128,256]{2,1,0:T(8,128)(2,1)S(1)}, bf16[2,128,256]{2,1,0:T(8,128)(2,1)S(1)}, u32[]{:S(2)}, u32[]{:S(2)}) collective-permute-start(bf16[2,128,256]{2,1,0:T(8,128)(2,1)S(1)} %collective-permute-done.refs_1_), channel_id=1, source_target_pairs={{0,4},{1,5},{2,7},{3,6},{4,0},{5,1},{6,3},{7,2},{8,12},{9,13},{10,... | collective-permute-start | bytes 393224 | tf_op jit(solution)/shard_map/ppermute | solution.py:197
  13.1 1.1 %collective-permute-start.4 = (bf16[2,128,256]{2,1,0:T(8,128)(2,1)S(1)}, bf16[2,128,256]{2,1,0:T(8,128)(2,1)S(1)}, u32[]{:S(2)}, u32[]{:S(2)}) collective-permute-start(bf16[2,128,256]{2,1,0:T(8,128)(2,1)S(1)} %collective-permute-done.refs_1_), channel_id=1, source_target_pairs={{0,2},{1,3},{2,0},{3,1},{4,6},{5,7},{6,4},{7,5},{8,10},{9,11},{10,... | collective-permute-start | bytes 393224 | tf_op jit(solution)/shard_map/ppermute | solution.py:197
  14.2 0.0 collective-permute-done.5.refs_6_
  14.2 0.2 collective-permute-start.2
  14.4 0.0 collective-permute-done.3.refs_4_
  14.4 0.0 collective-permute-done.1.refs_2_
  14.4 2.9 %collective-permute-done.6.refs_7_ = bf16[2,128,256]{2,1,0:T(8,128)(2,1)S(1)} collective-permute-done((bf16[2,128,256]{2,1,0:T(8,128)(2,1)S(1)}, bf16[2,128,256]{2,1,0:T(8,128)(2,1)S(1)}, u32[]{:S(2)}, u32[]{:S(2)}) %collective-permute-start.6) | collective-permute-done | bytes 131104 | tf_op jit(solution)/shard_map/ppermute | solution.py:197
  17.3 1.0 %collective-permute-done.4.refs_5_ = bf16[2,128,256]{2,1,0:T(8,128)(2,1)S(1)} collective-permute-done((bf16[2,128,256]{2,1,0:T(8,128)(2,1)S(1)}, bf16[2,128,256]{2,1,0:T(8,128)(2,1)S(1)}, u32[]{:S(2)}, u32[]{:S(2)}) %collective-permute-start.4) | collective-permute-done | bytes 131104 | tf_op jit(solution)/shard_map/ppermute | solution.py:197
  18.4 0.0 collective-permute-done.2.refs_3_
  18.4 0.0 copy-done.2
  18.4 1.5 %pair_scores.1 = (f32[4,32]{1,0:T(4,128)S(1)}, f32[4,32]{1,0:T(4,128)S(1)}, f32[4,32]{1,0:T(4,128)S(1)}) custom-call(bf16[2,3,256,256]{3,2,1,0:T(8,128)(2,1)S(1)} %get-tuple-element.18.terms, bf16[1024,32]{1,0:T(8,128)(2,1)S(1)} %get-tuple-element.19.pick, bf16[2,128,256]{2,1,0:T(8,128)(2,1)S(1)} %copy-done.2, ...), custom_call_target="tpu_custom_call" | custom-call | flops 2000000000 | bytes 2000000 | tf_op jit(solution)/shard_map/pair_scores/pallas_call | solution.py:179
  19.8 1.8 %collective-permute-start.7 = (f32[4,32]{1,0:T(4,128)S(1)}, f32[4,32]{1,0:T(4,128)S(1)}, u32[]{:S(2)}, u32[]{:S(2)}) collective-permute-start(f32[4,32]{1,0:T(4,128)S(1)} %get-tuple-element.23), channel_id=1, source_target_pairs={{0,2},{1,3},{2,0},{3,1},{4,6},{5,7},{6,4},{7,5},{8,10},{9,11},{10,... | collective-permute-start | bytes 1544 | tf_op jit(solution)/shard_map/ppermute | solution.py:197
  21.7 0.4 %collective-permute-start.8 = (f32[4,32]{1,0:T(4,128)S(1)}, f32[4,32]{1,0:T(4,128)S(1)}, u32[]{:S(2)}, u32[]{:S(2)}) collective-permute-start(f32[4,32]{1,0:T(4,128)S(1)} %get-tuple-element.24), channel_id=1, source_target_pairs={{0,4},{1,5},{2,7},{3,6},{4,0},{5,1},{6,3},{7,2},{8,12},{9,13},{10,... | collective-permute-start | bytes 1544 | tf_op jit(solution)/shard_map/ppermute | solution.py:197
  22.1 1.4 %collective-permute-done.7 = f32[4,32]{1,0:T(4,128)S(1)} collective-permute-done((f32[4,32]{1,0:T(4,128)S(1)}, f32[4,32]{1,0:T(4,128)S(1)}, u32[]{:S(2)}, u32[]{:S(2)}) %collective-permute-start.7) | collective-permute-done | bytes 544 | tf_op jit(solution)/shard_map/ppermute | solution.py:197
  23.5 1.7 %collective-permute-done.8 = f32[4,32]{1,0:T(4,128)S(1)} collective-permute-done((f32[4,32]{1,0:T(4,128)S(1)}, f32[4,32]{1,0:T(4,128)S(1)}, u32[]{:S(2)}, u32[]{:S(2)}) %collective-permute-start.8) | collective-permute-done | bytes 544 | tf_op jit(solution)/shard_map/ppermute | solution.py:197
  25.2 3.3 %collective-permute-start.9 = (f32[2,32]{1,0:T(2,128)S(1)}, f32[2,32]{1,0:T(2,128)S(1)}, u32[]{:S(2)}, u32[]{:S(2)}) collective-permute-start(f32[2,32]{1,0:T(2,128)S(1)} %slice.7), channel_id=1, source_target_pairs={{0,8},{1,9},{2,10},{3,11},{4,12},{5,13},{6,14},{7,15},{8,0},{9,1},... | collective-permute-start | bytes 776 | tf_op jit(solution)/shard_map/ppermute | solution.py:197
  28.6 1.5 %collective-permute-done.9 = f32[2,32]{1,0:T(2,128)S(1)} collective-permute-done((f32[2,32]{1,0:T(2,128)S(1)}, f32[2,32]{1,0:T(2,128)S(1)}, u32[]{:S(2)}, u32[]{:S(2)}) %collective-permute-start.9) | collective-permute-done | bytes 288 | tf_op jit(solution)/shard_map/ppermute | solution.py:197
  30.1 0.6 %slice_add_fusion = f32[2,32]{1,0:T(2,128)} fusion(f32[2,32]{1,0:T(2,128)S(1)} %collective-permute-done.9, f32[4,32]{1,0:T(4,128)S(1)} %add_add_fusion), kind=kLoop, calls=%fused_computation.1 | loop fusion | flops 64 | bytes 768 | tf_op jit(solution)/shard_map/add | solution.py:210
  (2 shorter events, 0.0 us)
Async XLA Ops:
  1.7 10.7 %collective-permute-start = (bf16[2,128,256]{2,1,0:T(8,128)(2,1)}, bf16[2,128,256]{2,1,0:T(8,128)(2,1)S(1)}, u32[]{:S(2)}, u32[]{:S(2)}) collective-permute-start(bf16[2,128,256]{2,1,0:T(8,128)(2,1)} %get-tuple-element.15), channel_id=1, source_target_pairs={{0,8},{1,9},{2,10},{3,11},{4,12},{5,13},{6,14},{7,15},{8,0},{9,1},... | collective-permute-start | bytes 393224 | tf_op jit(solution)/shard_map/ppermute | solution.py:197
  5.7 8.5 %collective-permute-start.5 = (bf16[2,128,256]{2,1,0:T(8,128)(2,1)}, bf16[2,128,256]{2,1,0:T(8,128)(2,1)S(1)}, u32[]{:S(2)}, u32[]{:S(2)}) collective-permute-start(bf16[2,128,256]{2,1,0:T(8,128)(2,1)} %get-tuple-element.20.refs_0_), channel_id=1, source_target_pairs={{0,4},{1,5},{2,7},{3,6},{4,0},{5,1},{6,3},{7,2},{8,12},{9,13},{10,... | collective-permute-start | bytes 393224 | tf_op jit(solution)/shard_map/ppermute | solution.py:197
  7.3 7.1 %collective-permute-start.3 = (bf16[2,128,256]{2,1,0:T(8,128)(2,1)}, bf16[2,128,256]{2,1,0:T(8,128)(2,1)S(1)}, u32[]{:S(2)}, u32[]{:S(2)}) collective-permute-start(bf16[2,128,256]{2,1,0:T(8,128)(2,1)} %get-tuple-element.20.refs_0_), channel_id=1, source_target_pairs={{0,2},{1,3},{2,0},{3,1},{4,6},{5,7},{6,4},{7,5},{8,10},{9,11},{10,... | collective-permute-start | bytes 393224 | tf_op jit(solution)/shard_map/ppermute | solution.py:197
  8.0 6.5 %collective-permute-start.1 = (bf16[2,128,256]{2,1,0:T(8,128)(2,1)}, bf16[2,128,256]{2,1,0:T(8,128)(2,1)S(1)}, u32[]{:S(2)}, u32[]{:S(2)}) collective-permute-start(bf16[2,128,256]{2,1,0:T(8,128)(2,1)} %get-tuple-element.20.refs_0_), channel_id=1, source_target_pairs={{0,1},{1,0},{2,3},{3,2},{4,5},{5,4},{6,7},{7,6},{8,9},{9,8},{10,11... | collective-permute-start | bytes 393224 | tf_op jit(solution)/shard_map/ppermute | solution.py:197
  8.6 0.7 %copy-start = (s32[2]{0:T(128)S(1)}, s32[2]{0:T(128)}, u32[]{:S(2)}) copy-start(s32[2]{0:T(128)} %layer_ids.1) | copy-start | bytes 28
  9.3 0.7 %copy-start.1 = (s32[32]{0:T(128)S(1)}, s32[32]{0:T(128)}, u32[]{:S(2)}) copy-start(s32[32]{0:T(128)} %param.11) | copy-start | bytes 388
  10.0 8.4 %copy-start.2 = (bf16[2,128,256]{2,1,0:T(8,128)(2,1)S(1)}, bf16[2,128,256]{2,1,0:T(8,128)(2,1)}, u32[]{:S(2)}) copy-start(bf16[2,128,256]{2,1,0:T(8,128)(2,1)} %get-tuple-element.20.refs_0_) | copy-start | bytes 393220
  12.4 5.0 %collective-permute-start.6 = (bf16[2,128,256]{2,1,0:T(8,128)(2,1)S(1)}, bf16[2,128,256]{2,1,0:T(8,128)(2,1)S(1)}, u32[]{:S(2)}, u32[]{:S(2)}) collective-permute-start(bf16[2,128,256]{2,1,0:T(8,128)(2,1)S(1)} %collective-permute-done.refs_1_), channel_id=1, source_target_pairs={{0,4},{1,5},{2,7},{3,6},{4,0},{5,1},{6,3},{7,2},{8,12},{9,13},{10,... | collective-permute-start | bytes 393224 | tf_op jit(solution)/shard_map/ppermute | solution.py:197
  13.1 5.3 %collective-permute-start.4 = (bf16[2,128,256]{2,1,0:T(8,128)(2,1)S(1)}, bf16[2,128,256]{2,1,0:T(8,128)(2,1)S(1)}, u32[]{:S(2)}, u32[]{:S(2)}) collective-permute-start(bf16[2,128,256]{2,1,0:T(8,128)(2,1)S(1)} %collective-permute-done.refs_1_), channel_id=1, source_target_pairs={{0,2},{1,3},{2,0},{3,1},{4,6},{5,7},{6,4},{7,5},{8,10},{9,11},{10,... | collective-permute-start | bytes 393224 | tf_op jit(solution)/shard_map/ppermute | solution.py:197
  14.2 4.2 %collective-permute-start.2 = (bf16[2,128,256]{2,1,0:T(8,128)(2,1)S(1)}, bf16[2,128,256]{2,1,0:T(8,128)(2,1)S(1)}, u32[]{:S(2)}, u32[]{:S(2)}) collective-permute-start(bf16[2,128,256]{2,1,0:T(8,128)(2,1)S(1)} %collective-permute-done.refs_1_), channel_id=1, source_target_pairs={{0,1},{1,0},{2,3},{3,2},{4,5},{5,4},{6,7},{7,6},{8,9},{9,8},{10,11... | collective-permute-start | bytes 393224 | tf_op jit(solution)/shard_map/ppermute | solution.py:197
  19.8 3.7 %collective-permute-start.7 = (f32[4,32]{1,0:T(4,128)S(1)}, f32[4,32]{1,0:T(4,128)S(1)}, u32[]{:S(2)}, u32[]{:S(2)}) collective-permute-start(f32[4,32]{1,0:T(4,128)S(1)} %get-tuple-element.23), channel_id=1, source_target_pairs={{0,2},{1,3},{2,0},{3,1},{4,6},{5,7},{6,4},{7,5},{8,10},{9,11},{10,... | collective-permute-start | bytes 1544 | tf_op jit(solution)/shard_map/ppermute | solution.py:197
  21.7 3.6 %collective-permute-start.8 = (f32[4,32]{1,0:T(4,128)S(1)}, f32[4,32]{1,0:T(4,128)S(1)}, u32[]{:S(2)}, u32[]{:S(2)}) collective-permute-start(f32[4,32]{1,0:T(4,128)S(1)} %get-tuple-element.24), channel_id=1, source_target_pairs={{0,4},{1,5},{2,7},{3,6},{4,0},{5,1},{6,3},{7,2},{8,12},{9,13},{10,... | collective-permute-start | bytes 1544 | tf_op jit(solution)/shard_map/ppermute | solution.py:197
  25.2 4.9 %collective-permute-start.9 = (f32[2,32]{1,0:T(2,128)S(1)}, f32[2,32]{1,0:T(2,128)S(1)}, u32[]{:S(2)}, u32[]{:S(2)}) collective-permute-start(f32[2,32]{1,0:T(2,128)S(1)} %slice.7), channel_id=1, source_target_pairs={{0,8},{1,9},{2,10},{3,11},{4,12},{5,13},{6,14},{7,15},{8,0},{9,1},... | collective-permute-start | bytes 776 | tf_op jit(solution)/shard_map/ppermute | solution.py:197

commit v4 on v3

--- a/solution.py
+++ b/solution.py
@@ -137,7 +137,7 @@
 
 
 def score_kernel(seq_len, terms, pick, *refs):
-    units, outs = refs[:8], refs[8:]
+    units, out = refs[:8], refs[8]
     f32 = jnp.float32
     toks = [
         [jnp.concatenate([units[2 * i][w], units[2 * i + 1][w]], axis=0) for w in range(2)]
@@ -169,18 +169,23 @@
         rest = rest - part.astype(f32)
     picked = jnp.dot(jnp.concatenate(parts, axis=0), pick[...], preferred_element_type=f32)
     picked = picked[:n] + picked[n : 2 * n] + picked[2 * n :]
-    for i, out in enumerate(outs):
-        out[...] = picked[i * seqs : (i + 1) * seqs]
-
-
-def score(units, terms, pick, seq_len):
-    seqs = 2 * units[0].shape[1] // seq_len
+    d = lax.axis_index("blk")
+    per = seqs // 2
+    out[...] = jnp.zeros_like(out)
+    for i, owner in enumerate((d, d ^ 2, z_near(d))):
+        at = i * seqs
+        out[owner] = picked[at : at + per]
+        out[owner ^ 8] = picked[at + per : at + seqs]
+
+
+def score(units, terms, pick, seq_len, size):
+    per = units[0].shape[1] // seq_len
     vmem = pl.BlockSpec(memory_space=pltpu.VMEM)
     return pl.pallas_call(
         functools.partial(score_kernel, seq_len),
-        out_shape=[jax.ShapeDtypeStruct((seqs, pick.shape[1]), jnp.float32)] * 3,
+        out_shape=jax.ShapeDtypeStruct((size, per, pick.shape[1]), jnp.float32),
         in_specs=[vmem] * 10,
-        out_specs=[vmem] * 3,
+        out_specs=vmem,
         compiler_params=pltpu.CompilerParams(vmem_limit_bytes=40 * 1024 * 1024),
         cost_estimate=pl.CostEstimate(flops=2 * 10**9, bytes_accessed=2 * 10**6, transcendentals=0),
         name="pair_scores",
@@ -205,9 +210,8 @@
     units = [own, opposite]
     for a, b in zip(near, far):
         units += [a, b]
-    mine, by_x, by_z = score(units, terms, pick, seq_len)
-    half_sum = mine + send(by_x, lambda d: d ^ 2) + send(by_z, z_near)
-    return half_sum[:per] + send(half_sum[per:], lambda d: d ^ 8)
+    total = lax.psum(score(units, terms, pick, seq_len, size), "blk")
+    return lax.dynamic_index_in_dim(total, lax.axis_index("blk"), 0, keepdims=False)
 
 
 def solution(mesh):

time: 30.9 us -> 82.3 us (2.66)
  blocking collectives: 0 us -> 60.6 us
  starting transfers between devices: 14.6 us -> 9.38 us
  waiting for transfers between devices: 9.37 us -> 5.46 us
    psum x0 -> x1, blocking collectives: none -> 60.6 us  [paired(): total = lax.psum(score(units, terms, pick, seq_len, size), 'blk')]
    ppermute x10 -> x7, starting transfers between devices: 14.6 us -> 9.38 us  [send(): return lax.ppermute(x, 'blk', [(d, to(d)) for d in range(size)])]
    ppermute x10 -> x7, waiting for transfers between devices: 9.37 us -> 5.46 us  [send(): return lax.ppermute(x, 'blk', [(d, to(d)) for d in range(size)])]
  transfers between devices with their start and end apart: 10 -> 7, of which waited for: 6 -> 3; matrix products, arithmetic and copies ran while one was open for 0% -> 0% of each run, Pallas kernels for 5% -> 2%
where the time goes in v4:
time: 82.3 us; the launch traced here: 82.1 us
  blocking collectives  60.6 us (74%)
  starting transfers between devices  9.38 us (11%)
  waiting for transfers between devices  5.46 us (7%)
  Pallas kernels  4.84 us (6%)
  local copies, waits for them, and re-layouts  1.88 us (2%)
    psum x1, blocking collectives, paired(): total = lax.psum(score(units, terms, pick, seq_len, size), 'blk')  60.6 us
    ppermute x7, starting transfers between devices, send(): return lax.ppermute(x, 'blk', [(d, to(d)) for d in range(size)])  9.38 us
    ppermute x7, waiting for transfers between devices, send(): return lax.ppermute(x, 'blk', [(d, to(d)) for d in range(size)])  5.46 us
    pallas_call x1, Pallas kernels, prep(): pl.pallas_call(functools.partial(prep_kernel, seq_len), out_shape=(unit,...  1.71 us
    pallas_call x1, Pallas kernels, setup(): pl.pallas_call(functools.partial(setup_kernel, seq_len, per), out_shape=(...  1.67 us
  transfers between devices with their start and end apart: 7, of which 3 were waited for; matrix products, arithmetic and copies ran while one was open for 0% of the time, Pallas kernels for 2%

profile of v4, /device:TPU:0, one launch (start us, length us, event | category | flops | bytes accessed | tf_op | source)
XLA Modules:
  0.0 82.1 jit_solution(17002384888948291000)
XLA Ops:
  0.0 1.7 %mask_units.1 = (bf16[2,128,256]{2,1,0:T(8,128)(2,1)}, bf16[2,128,256]{2,1,0:T(8,128)(2,1)}) custom-call(s32[2]{0:T(128)} %lens.1, bf16[2,128,256]{2,1,0:T(8,128)(2,1)} %acts.1, bf16[2,128,256]{2,1,0:T(8,128)(2,1)} %grads.1), custom_call_target="tpu_custom_call" | custom-call | tf_op jit(solution)/shard_map/mask_units/pallas_call | solution.py:75
  1.7 4.0 %collective-permute-start = (bf16[2,128,256]{2,1,0:T(8,128)(2,1)}, bf16[2,128,256]{2,1,0:T(8,128)(2,1)S(1)}, u32[]{:S(2)}, u32[]{:S(2)}) collective-permute-start(bf16[2,128,256]{2,1,0:T(8,128)(2,1)} %get-tuple-element.12), channel_id=1, source_target_pairs={{0,8},{1,9},{2,10},{3,11},{4,12},{5,13},{6,14},{7,15},{8,0},{9,1},... | collective-permute-start | bytes 393224 | tf_op jit(solution)/shard_map/ppermute | solution.py:202
  5.7 0.0 collective-permute-start.1
  5.7 1.5 %collective-permute-start.3 = (bf16[2,128,256]{2,1,0:T(8,128)(2,1)}, bf16[2,128,256]{2,1,0:T(8,128)(2,1)S(1)}, u32[]{:S(2)}, u32[]{:S(2)}) collective-permute-start(bf16[2,128,256]{2,1,0:T(8,128)(2,1)} %get-tuple-element.17.refs_0_), channel_id=1, source_target_pairs={{0,2},{1,3},{2,0},{3,1},{4,6},{5,7},{6,4},{7,5},{8,10},{9,11},{10,... | collective-permute-start | bytes 393224 | tf_op jit(solution)/shard_map/ppermute | solution.py:202
  7.2 1.6 %collective-permute-start.5 = (bf16[2,128,256]{2,1,0:T(8,128)(2,1)}, bf16[2,128,256]{2,1,0:T(8,128)(2,1)S(1)}, u32[]{:S(2)}, u32[]{:S(2)}) collective-permute-start(bf16[2,128,256]{2,1,0:T(8,128)(2,1)} %get-tuple-element.17.refs_0_), channel_id=1, source_target_pairs={{0,4},{1,5},{2,7},{3,6},{4,0},{5,1},{6,3},{7,2},{8,12},{9,13},{10,... | collective-permute-start | bytes 393224 | tf_op jit(solution)/shard_map/ppermute | solution.py:202
  8.8 0.0 copy-start
  8.8 0.7 copy-done
  9.5 0.0 copy-start.1
  9.5 0.7 copy-done.1
  10.1 0.0 copy-start.2
  10.1 1.7 %factor_terms.1 = (bf16[2,3,256,256]{3,2,1,0:T(8,128)(2,1)S(1)}, bf16[1024,32]{1,0:T(8,128)(2,1)S(1)}) custom-call(s32[2]{0:T(128)S(1)} %copy-done, s32[1,32]{1,0:T(1,128)S(1)} %bitcast.3, f32[16,256,256]{2,1,0:T(8,128)} %act_f.1, f32[16,256,256]{2,1,0:T(8,128)} %grad_f.1), custom_call_target="tpu_custom_call" | custom-call | flops 1000000000 | bytes 2000000 | tf_op jit(solution)/shard_map/factor_terms/pallas_call | solution.py:117
  11.8 0.6 collective-permute-done.refs_1_
  12.4 0.0 collective-permute-start.2
  12.4 1.5 %collective-permute-start.4 = (bf16[2,128,256]{2,1,0:T(8,128)(2,1)S(1)}, bf16[2,128,256]{2,1,0:T(8,128)(2,1)S(1)}, u32[]{:S(2)}, u32[]{:S(2)}) collective-permute-start(bf16[2,128,256]{2,1,0:T(8,128)(2,1)S(1)} %collective-permute-done.refs_1_), channel_id=1, source_target_pairs={{0,2},{1,3},{2,0},{3,1},{4,6},{5,7},{6,4},{7,5},{8,10},{9,11},{10,... | collective-permute-start | bytes 393224 | tf_op jit(solution)/shard_map/ppermute | solution.py:202
  13.9 0.0 collective-permute-done.1.refs_2_
  13.9 0.7 collective-permute-start.6
  14.6 0.0 collective-permute-done.3.refs_4_
  14.6 0.0 collective-permute-done.5.refs_6_
  14.7 0.0 collective-permute-done.2.refs_3_
  14.7 3.6 %collective-permute-done.4.refs_5_ = bf16[2,128,256]{2,1,0:T(8,128)(2,1)S(1)} collective-permute-done((bf16[2,128,256]{2,1,0:T(8,128)(2,1)S(1)}, bf16[2,128,256]{2,1,0:T(8,128)(2,1)S(1)}, u32[]{:S(2)}, u32[]{:S(2)}) %collective-permute-start.4) | collective-permute-done | bytes 131104 | tf_op jit(solution)/shard_map/ppermute | solution.py:202
  18.3 1.3 %collective-permute-done.6.refs_7_ = bf16[2,128,256]{2,1,0:T(8,128)(2,1)S(1)} collective-permute-done((bf16[2,128,256]{2,1,0:T(8,128)(2,1)S(1)}, bf16[2,128,256]{2,1,0:T(8,128)(2,1)S(1)}, u32[]{:S(2)}, u32[]{:S(2)}) %collective-permute-start.6) | collective-permute-done | bytes 131104 | tf_op jit(solution)/shard_map/ppermute | solution.py:202
  19.5 0.0 copy-done.2
  19.5 1.5 %pair_scores.1 = f32[16,2,32]{2,1,0:T(2,128)S(1)} custom-call(bf16[2,3,256,256]{3,2,1,0:T(8,128)(2,1)S(1)} %get-tuple-element.15.terms, bf16[1024,32]{1,0:T(8,128)(2,1)S(1)} %get-tuple-element.16.pick, bf16[2,128,256]{2,1,0:T(8,128)(2,1)S(1)} %copy-done.2, bf16[2,128,256]{2,1,0:T(8,128)(2,1)S(1)} %collective-permute-done.refs_1_, ...), custom_call_target="tpu_custom_call" | custom-call | flops 2000000000 | bytes 2000000 | tf_op jit(solution)/shard_map/pair_scores/pallas_call | solution.py:184
  21.0 60.6 %psum.7 = f32[16,2,32]{2,1,0:T(2,128)S(1)} all-reduce(f32[16,2,32]{2,1,0:T(2,128)S(1)} %pair_scores.1), channel_id=1, replica_groups=mesh['grp'=2,'blk'=16] {'blk'}, use_global_device_ids=true, to_apply=%region_0.0 | all-reduce | flops 1024 | bytes 8192 | tf_op jit(solution)/shard_map/psum | solution.py:213
  81.6 0.6 dynamic-slice_bitcast_fusion
Async XLA Ops:
  1.7 10.7 %collective-permute-start = (bf16[2,128,256]{2,1,0:T(8,128)(2,1)}, bf16[2,128,256]{2,1,0:T(8,128)(2,1)S(1)}, u32[]{:S(2)}, u32[]{:S(2)}) collective-permute-start(bf16[2,128,256]{2,1,0:T(8,128)(2,1)} %get-tuple-element.12), channel_id=1, source_target_pairs={{0,8},{1,9},{2,10},{3,11},{4,12},{5,13},{6,14},{7,15},{8,0},{9,1},... | collective-permute-start | bytes 393224 | tf_op jit(solution)/shard_map/ppermute | solution.py:202
  5.7 8.2 %collective-permute-start.1 = (bf16[2,128,256]{2,1,0:T(8,128)(2,1)}, bf16[2,128,256]{2,1,0:T(8,128)(2,1)S(1)}, u32[]{:S(2)}, u32[]{:S(2)}) collective-permute-start(bf16[2,128,256]{2,1,0:T(8,128)(2,1)} %get-tuple-element.17.refs_0_), channel_id=1, source_target_pairs={{0,1},{1,0},{2,3},{3,2},{4,5},{5,4},{6,7},{7,6},{8,9},{9,8},{10,11... | collective-permute-start | bytes 393224 | tf_op jit(solution)/shard_map/ppermute | solution.py:202
  5.7 8.9 %collective-permute-start.3 = (bf16[2,128,256]{2,1,0:T(8,128)(2,1)}, bf16[2,128,256]{2,1,0:T(8,128)(2,1)S(1)}, u32[]{:S(2)}, u32[]{:S(2)}) collective-permute-start(bf16[2,128,256]{2,1,0:T(8,128)(2,1)} %get-tuple-element.17.refs_0_), channel_id=1, source_target_pairs={{0,2},{1,3},{2,0},{3,1},{4,6},{5,7},{6,4},{7,5},{8,10},{9,11},{10,... | collective-permute-start | bytes 393224 | tf_op jit(solution)/shard_map/ppermute | solution.py:202
  7.2 7.4 %collective-permute-start.5 = (bf16[2,128,256]{2,1,0:T(8,128)(2,1)}, bf16[2,128,256]{2,1,0:T(8,128)(2,1)S(1)}, u32[]{:S(2)}, u32[]{:S(2)}) collective-permute-start(bf16[2,128,256]{2,1,0:T(8,128)(2,1)} %get-tuple-element.17.refs_0_), channel_id=1, source_target_pairs={{0,4},{1,5},{2,7},{3,6},{4,0},{5,1},{6,3},{7,2},{8,12},{9,13},{10,... | collective-permute-start | bytes 393224 | tf_op jit(solution)/shard_map/ppermute | solution.py:202
  8.8 0.7 copy-start
  9.5 0.7 copy-start.1
  10.1 9.4 %copy-start.2 = (bf16[2,128,256]{2,1,0:T(8,128)(2,1)S(1)}, bf16[2,128,256]{2,1,0:T(8,128)(2,1)}, u32[]{:S(2)}) copy-start(bf16[2,128,256]{2,1,0:T(8,128)(2,1)} %get-tuple-element.17.refs_0_) | copy-start | bytes 393220
  12.4 2.3 %collective-permute-start.2 = (bf16[2,128,256]{2,1,0:T(8,128)(2,1)S(1)}, bf16[2,128,256]{2,1,0:T(8,128)(2,1)S(1)}, u32[]{:S(2)}, u32[]{:S(2)}) collective-permute-start(bf16[2,128,256]{2,1,0:T(8,128)(2,1)S(1)} %collective-permute-done.refs_1_), channel_id=1, source_target_pairs={{0,1},{1,0},{2,3},{3,2},{4,5},{5,4},{6,7},{7,6},{8,9},{9,8},{10,11... | collective-permute-start | bytes 393224 | tf_op jit(solution)/shard_map/ppermute | solution.py:202
  12.4 5.9 %collective-permute-start.4 = (bf16[2,128,256]{2,1,0:T(8,128)(2,1)S(1)}, bf16[2,128,256]{2,1,0:T(8,128)(2,1)S(1)}, u32[]{:S(2)}, u32[]{:S(2)}) collective-permute-start(bf16[2,128,256]{2,1,0:T(8,128)(2,1)S(1)} %collective-permute-done.refs_1_), channel_id=1, source_target_pairs={{0,2},{1,3},{2,0},{3,1},{4,6},{5,7},{6,4},{7,5},{8,10},{9,11},{10,... | collective-permute-start | bytes 393224 | tf_op jit(solution)/shard_map/ppermute | solution.py:202
  13.9 5.6 %collective-permute-start.6 = (bf16[2,128,256]{2,1,0:T(8,128)(2,1)S(1)}, bf16[2,128,256]{2,1,0:T(8,128)(2,1)S(1)}, u32[]{:S(2)}, u32[]{:S(2)}) collective-permute-start(bf16[2,128,256]{2,1,0:T(8,128)(2,1)S(1)} %collective-permute-done.refs_1_), channel_id=1, source_target_pairs={{0,4},{1,5},{2,7},{3,6},{4,0},{5,1},{6,3},{7,2},{8,12},{9,13},{10,... | collective-permute-start | bytes 393224 | tf_op jit(solution)/shard_map/ppermute | solution.py:202

commit v5 on v0

--- a/solution.py
+++ b/solution.py
@@ -1,7 +1,13 @@
+import functools
+
 import jax
 import jax.numpy as jnp
 from jax import lax
+from jax.experimental import pallas as pl
+from jax.experimental.pallas import tpu as pltpu
 from jax.sharding import PartitionSpec as P
+
+HIGHEST = lax.Precision.HIGHEST
 
 
 def tile_scores(white_acts, white_grads, remote_acts, remote_grads, seq_len):
@@ -20,7 +26,7 @@
     )
 
 
-def shards(activations, out_grads, lengths, layer_ids, flagged, act_factor, grad_factor):
+def gathered(activations, out_grads, lengths, layer_ids, flagged, act_factor, grad_factor):
     tok_rows = activations.shape[1]
     seq_count = lengths.shape[0]
     seq_len = tok_rows // seq_count
@@ -31,13 +37,10 @@
     picked_act = jnp.take(act_factor, layer_ids, axis=0)
     picked_grad = jnp.take(grad_factor, layer_ids, axis=0)
     white_acts = jnp.einsum(
-        "ltr,lrs->lts", masked_acts.astype(jnp.float32), picked_act, precision=lax.Precision.HIGHEST
+        "ltr,lrs->lts", masked_acts.astype(jnp.float32), picked_act, precision=HIGHEST
     ).astype(jnp.bfloat16)
     white_grads = jnp.einsum(
-        "ltr,lrs->lts",
-        masked_grads.astype(jnp.float32),
-        picked_grad,
-        precision=lax.Precision.HIGHEST,
+        "ltr,lrs->lts", masked_grads.astype(jnp.float32), picked_grad, precision=HIGHEST
     ).astype(jnp.bfloat16)
     part_scores = tile_scores(
         white_acts,
@@ -47,6 +50,244 @@
         seq_len,
     )
     return jnp.take(part_scores, flagged, axis=1)
+
+
+def z_near(d):
+    return d ^ 4 ^ ((d >> 1) & 1)
+
+
+def mask_kernel(seq_len, pieces, lens, acts, grads, *refs):
+    outs, bufs, sems = refs[: len(pieces)], refs[len(pieces) : -1], refs[-1]
+    half = lax.axis_index("blk") // 8
+    copies = []
+    for n, (kept, first, buf) in enumerate(zip(*zip(*pieces), bufs)):
+        layer = half if kept else 1 - half
+        for w, src in enumerate((acts, grads)):
+            rows = pl.ds(first, buf.shape[1])
+            copies.append(pltpu.make_async_copy(src.at[layer, rows], buf.at[w], sems.at[n, w]))
+            copies[-1].start()
+    for n, (piece, buf, out) in enumerate(zip(pieces, bufs, outs)):
+        row = lax.broadcasted_iota(jnp.int32, (buf.shape[1], 1), 0)
+        bound = jnp.zeros_like(row)
+        for s in range(buf.shape[1] // seq_len):
+            bound = jnp.where(row // seq_len == s, lens[piece[1] // seq_len + s] + s * seq_len, bound)
+        for w in range(2):
+            copies[2 * n + w].wait()
+            x = buf[w]
+            out[w] = jnp.where(row < bound, x, jnp.zeros_like(x))
+
+
+def masked(activations, out_grads, lengths, seq_len, pieces):
+    rank = activations.shape[2]
+    shapes = [(2, rows, rank) for _, _, rows in pieces]
+    vmem = pl.BlockSpec(memory_space=pltpu.VMEM)
+    hbm = pl.BlockSpec(memory_space=pltpu.HBM)
+    return pl.pallas_call(
+        functools.partial(mask_kernel, seq_len, [piece[:2] for piece in pieces]),
+        out_shape=[jax.ShapeDtypeStruct(shape, activations.dtype) for shape in shapes],
+        in_specs=[pl.BlockSpec(memory_space=pltpu.SMEM), hbm, hbm],
+        out_specs=[vmem] * len(pieces),
+        scratch_shapes=[pltpu.VMEM(shape, activations.dtype) for shape in shapes]
+        + [pltpu.SemaphoreType.DMA((len(pieces), 2))],
+        compiler_params=pltpu.CompilerParams(vmem_limit_bytes=59 * 1024 * 1024),
+        cost_estimate=pl.CostEstimate(flops=10**9, bytes_accessed=10**6, transcendentals=0),
+        name="masked",
+    )(lengths, activations, out_grads)
+
+
+def whiten(x, terms):
+    total = jnp.dot(x, terms[0], preferred_element_type=jnp.float32)
+    for n in (1, 2):
+        total = total + jnp.dot(x, terms[n], preferred_element_type=jnp.float32)
+    return total.astype(jnp.bfloat16)
+
+
+def stack(*arrays):
+    return jnp.concatenate(arrays, axis=0)
+
+
+def block(seq_len, left, right):
+    grams = [
+        lax.dot_general(a, b, (((1,), (1,)), ((), ())), preferred_element_type=jnp.float32)
+        for a, b in zip(left, right)
+    ]
+    rows, columns = grams[0].shape
+    return (grams[0] * grams[1]).reshape(rows // seq_len, seq_len, columns).sum(axis=1)
+
+
+def pick_columns(sums, pick):
+    rest, terms = sums, []
+    for _ in range(3):
+        terms.append(rest.astype(jnp.bfloat16))
+        rest = rest - terms[-1].astype(jnp.float32)
+    n = sums.shape[0]
+    out = jnp.dot(stack(*terms), pick[...], preferred_element_type=jnp.float32)
+    return out[:n] + out[n : 2 * n] + out[2 * n :]
+
+
+def early_kernel(
+    seq_len, per, layer_ids, flagged, act_f, grad_f, u0, u1, u2, u3, v,
+    terms, white, pick, sums, factor, sems,
+):
+    d = lax.axis_index("blk")
+    layer = layer_ids[d // 8]
+    copies = [
+        pltpu.make_async_copy(src.at[layer], factor.at[i], sems.at[i])
+        for i, src in enumerate((act_f, grad_f))
+    ]
+    for copy in copies:
+        copy.start()
+    token = lax.broadcasted_iota(jnp.int32, pick.shape, 0)
+    spot = token // (seq_len * per)
+    slot = spot // 2
+    owner = jnp.where(
+        slot == 0, d, jnp.where(slot == 1, d ^ 1, jnp.where(slot == 2, d ^ 2, z_near(d)))
+    )
+    owner = owner ^ (8 * (spot % 2))
+    seq = owner * per + token // seq_len % per
+    scale = 1.0 / (factor.shape[1] * seq_len)
+    pick[...] = jnp.where(seq == flagged[...], scale, 0.0).astype(pick.dtype)
+    n = u0.shape[1]
+    mine, x, z = [], [], []
+    for w in range(2):
+        copies[w].wait()
+        rest = factor[w]
+        for t in range(3):
+            term = rest.astype(jnp.bfloat16)
+            terms[w, t] = term
+            rest = rest - term.astype(jnp.float32)
+        rows = whiten(stack(u0[w], v[w], u2[w], u3[w]), terms.at[w])
+        white[w] = rows
+        mine.append(rows[: 2 * n])
+        x.append(rows[2 * n : 3 * n])
+        z.append(rows[3 * n :])
+    tok = [[u[w] for w in range(2)] for u in (u0, u1, u2, u3)]
+    own = [stack(u0[w], v[w]) for w in range(2)]
+    sums[...] = jnp.zeros_like(sums)
+    r = 2 * per
+    sums[0:r, 0 : 2 * n] = block(seq_len, mine, own)
+    for slot in (1, 2, 3):
+        at = 2 * n * slot
+        sums[0:r, at : at + n] = block(seq_len, mine, tok[slot])
+    for row, left, slots in ((r, x, (1, 3)), (2 * r, z, (1, 2))):
+        for slot in slots:
+            at = 2 * n * slot
+            sums[row : row + per, at : at + n] = block(seq_len, left, tok[slot])
+
+
+def return_kernel(seq_len, per, terms, white, pick, sums, u1, u2, u3, *refs):
+    v, outs = refs[:3], refs[3:]
+    n = u1.shape[1]
+    late = [[v[i][w] for w in range(2)] for i in range(3)]
+    tok = [[u[w] for w in range(2)] for u in (u1, u2, u3)]
+    both = [[stack(tok[i][w], late[i][w]) for w in range(2)] for i in range(3)]
+    fresh = [whiten(stack(late[1][w], late[2][w]), terms.at[w]) for w in range(2)]
+    zeros = jnp.zeros((per, n), jnp.float32)
+    wide = jnp.zeros((per, 2 * n), jnp.float32)
+    lines = []
+    for i, other in ((1, 2), (2, 1)):
+        early = [white[w, (i + 1) * n : (i + 2) * n] for w in range(2)]
+        got = block(seq_len, early, [stack(late[0][w], late[other][w]) for w in range(2)])
+        cols = {1: jnp.concatenate([zeros, got[:, :n]], axis=1)}
+        cols[other + 1] = jnp.concatenate([zeros, got[:, n:]], axis=1)
+        lines.append(jnp.concatenate([cols.get(slot, wide) for slot in range(4)], axis=1))
+        new = [fresh[w][(i - 1) * n : i * n] for w in range(2)]
+        cols = {1: block(seq_len, new, both[0]), other + 1: block(seq_len, new, both[other])}
+        lines.append(jnp.concatenate([cols.get(slot, wide) for slot in range(4)], axis=1))
+    r = 2 * per
+    picked = pick_columns(sums[r:, :] + stack(*lines), pick)
+    for i, out in enumerate(outs):
+        out[...] = picked[i * r : (i + 1) * r]
+
+
+def own_kernel(seq_len, per, white, pick, sums, *refs):
+    v, out = refs[:3], refs[3]
+    n = v[0].shape[1]
+    r = 2 * per
+    mine = [white[w, : 2 * n] for w in range(2)]
+    line = [jnp.zeros((r, 2 * n), jnp.float32)]
+    for i in range(3):
+        right = [v[i][w] for w in range(2)]
+        line += [jnp.zeros((r, n), jnp.float32), block(seq_len, mine, right)]
+    out[...] = pick_columns(sums[:r, :] + jnp.concatenate(line, axis=1), pick)
+
+
+def call(kernel, name, flops, limit, operands, specs, out_shape, scratch=()):
+    vmem = pl.BlockSpec(memory_space=pltpu.VMEM)
+    return pl.pallas_call(
+        kernel,
+        out_shape=out_shape,
+        in_specs=specs + [vmem] * (len(operands) - len(specs)),
+        out_specs=jax.tree.map(lambda _: vmem, out_shape),
+        scratch_shapes=scratch,
+        compiler_params=pltpu.CompilerParams(vmem_limit_bytes=limit * 1024 * 1024),
+        cost_estimate=pl.CostEstimate(flops=flops, bytes_accessed=10**6, transcendentals=0),
+        name=name,
+    )(*operands)
+
+
+def paired(activations, out_grads, lengths, layer_ids, flagged, act_factor, grad_factor):
+    size = 16
+    per = lengths.shape[0]
+    tokens, rank = activations.shape[1:]
+    seq_len = tokens // per
+    f32, bf16 = jnp.float32, jnp.bfloat16
+
+    def send(x, to):
+        return lax.ppermute(x, "blk", [(d, to(d)) for d in range(size)])
+
+    def opposite(d):
+        return d ^ 8
+
+    ways = (lambda d: d ^ 1, lambda d: d ^ 2, z_near)
+    data = (activations, out_grads, lengths, seq_len)
+    (away,) = masked(*data, [(False, 0, tokens)])
+    v = send(away, opposite)
+    away, *data = lax.optimization_barrier((away, *data[:3]))
+    (own,) = masked(*data, seq_len, [(True, 0, tokens)])
+    u = [own] + [send(own, to) for to in ways[::-1]][::-1]
+    late = [send(v, to) for to in ways[::-1]][::-1]
+
+    shape = jax.ShapeDtypeStruct
+    columns = flagged.shape[0]
+    hbm = pl.BlockSpec(memory_space=pltpu.HBM)
+    vmem = pl.BlockSpec(memory_space=pltpu.VMEM)
+    terms, white, pick, sums = call(
+        functools.partial(early_kernel, seq_len, per),
+        "early_pairs",
+        10**9,
+        51,
+        (layer_ids, flagged.reshape(1, -1), act_factor, grad_factor, *u, v),
+        [pl.BlockSpec(memory_space=pltpu.SMEM), vmem, hbm, hbm],
+        (
+            shape((2, 3, rank, rank), bf16),
+            shape((2, 4 * tokens, rank), bf16),
+            shape((8 * tokens, columns), bf16),
+            shape((6 * per, 8 * tokens), f32),
+        ),
+        [pltpu.VMEM((2, rank, rank), f32), pltpu.SemaphoreType.DMA((2,))],
+    )
+    rows = shape((2 * per, columns), f32)
+    by_x, by_z = call(
+        functools.partial(return_kernel, seq_len, per),
+        "return_rows",
+        10**9,
+        40,
+        (terms, white, pick, sums, *u[1:], *late),
+        [],
+        (rows, rows),
+    )
+    mine = call(
+        functools.partial(own_kernel, seq_len, per),
+        "own_rows",
+        10**9,
+        40,
+        (white, pick, sums, *late),
+        [],
+        rows,
+    )
+    half_sum = mine + send(by_x, lambda d: d ^ 2) + send(by_z, z_near)
+    return half_sum[:per] + send(half_sum[per:], opposite)
 
 
 def solution(mesh):
@@ -60,4 +301,5 @@
         P(),
     )
     out_specs = P(("grp", "blk"), None)
+    shards = paired if mesh.shape["blk"] == 16 else gathered
     return jax.shard_map(shards, mesh=mesh, in_specs=in_specs, out_specs=out_specs, check_vma=False)

time: 108 us -> 31.7 us (0.29)
  waiting for transfers between devices: 77.2 us -> 6.64 us
  starting transfers between devices: 0.04 us -> 14.1 us
  between operations: 13.5 us -> 0.06 us
  Pallas kernels: 0 us -> 9.13 us
  local copies, waits for them, and re-layouts: 8.52 us -> 0.92 us
  matrix products: 5.76 us -> 0 us
  other arithmetic: 2.81 us -> 0.57 us
    all_gather x2 -> x0, waiting for transfers between devices: 76.5 us -> none  [the longest x1 40 us: shards(): lax.all_gather(masked_grads, 'blk', axis=1, tiled=True)]
    ppermute x0 -> x10, starting transfers between devices: none -> 14.1 us  [send(): return lax.ppermute(x, 'blk', [(d, to(d)) for d in range(size)])]
    pallas_call x0 -> x5, Pallas kernels: none -> 9.13 us  [the longest x2 4.57 us: masked(): pl.pallas_call(functools.partial(mask_kernel, seq_len, [piece[:2] for pie...]
    ppermute x0 -> x10, waiting for transfers between devices: none -> 6.64 us  [send(): return lax.ppermute(x, 'blk', [(d, to(d)) for d in range(size)])]
    gather x3 -> x0, local copies, waits for them, and re-layouts: 6.11 us -> none  [the longest x1 2.77 us: shards(): picked_grad = jnp.take(grad_factor, layer_ids, axis=0)]
    dot_general x4 -> x0, matrix products: 5.76 us -> none  [the longest x1 2.49 us: tile_scores(): jnp.einsum('lqr,lkr->lqk', white_grads, remote_grads, preferred_element_t...]
    mul x2 -> x0, other arithmetic: 1.76 us -> none  [the longest x1 1.75 us: shards(): masked_grads = out_grads * keep[None, :, None]]
  transfers between devices with their start and end apart: 2 -> 10, of which waited for: 2 -> 6; matrix products, arithmetic and copies ran while one was open for 9% -> 0% of each run, Pallas kernels for 0% -> 18%
where the time goes in v5:
time: 31.7 us; the launch traced here: 31.4 us
  starting transfers between devices  14.1 us (44%)
  Pallas kernels  9.13 us (29%)
  waiting for transfers between devices  6.64 us (21%)
  local copies, waits for them, and re-layouts  0.92 us (3%)
  other arithmetic  0.57 us (2%)
    ppermute x10, starting transfers between devices, send(): return lax.ppermute(x, 'blk', [(d, to(d)) for d in range(size)])  14.1 us
    ppermute x10, waiting for transfers between devices, send(): return lax.ppermute(x, 'blk', [(d, to(d)) for d in range(size)])  6.64 us
    pallas_call x2, Pallas kernels, masked(): pl.pallas_call(functools.partial(mask_kernel, seq_len, [piece[:2] for pie...  4.57 us
    pallas_call x3, Pallas kernels, call(): pl.pallas_call(kernel, out_shape=out_shape, in_specs=specs + [vmem] * (le...  4.56 us
    unnamed x6, local copies, waits for them, and re-layouts  0.91 us
  transfers between devices with their start and end apart: 10, of which 6 were waited for; matrix products, arithmetic and copies ran while one was open for 0% of the time, Pallas kernels for 18%

profile of v5, /device:TPU:0, one launch (start us, length us, event | category | flops | bytes accessed | tf_op | source)
XLA Modules:
  0.0 31.4 jit_solution(5134790017880046754)
XLA Ops:
  0.0 0.0 copy-start.1
  0.0 0.0 copy-start.2
  0.0 2.4 %masked.2 = bf16[2,128,256]{2,1,0:T(8,128)(2,1)} custom-call(s32[2]{0:T(128)} %lens.2, bf16[2,128,256]{2,1,0:T(8,128)(2,1)} %acts.2, bf16[2,128,256]{2,1,0:T(8,128)(2,1)} %grads.2), custom_call_target="tpu_custom_call" | custom-call | flops 1000000000 | bytes 1000000 | tf_op jit(solution)/shard_map/masked/pallas_call | solution.py:85
  2.4 4.1 %collective-permute-start.3 = (bf16[2,128,256]{2,1,0:T(8,128)(2,1)}, bf16[2,128,256]{2,1,0:T(8,128)(2,1)S(1)}, u32[]{:S(2)}, u32[]{:S(2)}) collective-permute-start(bf16[2,128,256]{2,1,0:T(8,128)(2,1)} %masked.2), channel_id=1, source_target_pairs={{0,8},{1,9},{2,10},{3,11},{4,12},{5,13},{6,14},{7,15},{8,0},{9,1},... | collective-permute-start | bytes 393224 | tf_op jit(solution)/shard_map/ppermute | solution.py:237
  6.5 2.2 %masked.3.u0 = bf16[2,128,256]{2,1,0:T(8,128)(2,1)} custom-call(s32[2]{0:T(128)} %lens.2, bf16[2,128,256]{2,1,0:T(8,128)(2,1)} %acts.2, bf16[2,128,256]{2,1,0:T(8,128)(2,1)} %grads.2), custom_call_target="tpu_custom_call" | custom-call | flops 1000000000 | bytes 1000000 | tf_op jit(solution)/shard_map/masked/pallas_call | solution.py:85
  8.7 0.1 collective-permute-start
  8.8 1.6 %collective-permute-start.1 = (bf16[2,128,256]{2,1,0:T(8,128)(2,1)}, bf16[2,128,256]{2,1,0:T(8,128)(2,1)S(1)}, u32[]{:S(2)}, u32[]{:S(2)}) collective-permute-start(bf16[2,128,256]{2,1,0:T(8,128)(2,1)} %masked.3.u0), channel_id=1, source_target_pairs={{0,2},{1,3},{2,0},{3,1},{4,6},{5,7},{6,4},{7,5},{8,10},{9,11},{10,... | collective-permute-start | bytes 393224 | tf_op jit(solution)/shard_map/ppermute | solution.py:237
  10.3 1.6 %collective-permute-start.2 = (bf16[2,128,256]{2,1,0:T(8,128)(2,1)}, bf16[2,128,256]{2,1,0:T(8,128)(2,1)S(1)}, u32[]{:S(2)}, u32[]{:S(2)}) collective-permute-start(bf16[2,128,256]{2,1,0:T(8,128)(2,1)} %masked.3.u0), channel_id=1, source_target_pairs={{0,4},{1,5},{2,7},{3,6},{4,0},{5,1},{6,3},{7,2},{8,12},{9,13},{10,... | collective-permute-start | bytes 393224 | tf_op jit(solution)/shard_map/ppermute | solution.py:237
  11.9 1.1 %collective-permute-done.3.v = bf16[2,128,256]{2,1,0:T(8,128)(2,1)S(1)} collective-permute-done((bf16[2,128,256]{2,1,0:T(8,128)(2,1)}, bf16[2,128,256]{2,1,0:T(8,128)(2,1)S(1)}, u32[]{:S(2)}, u32[]{:S(2)}) %collective-permute-start.3) | collective-permute-done | bytes 131104 | tf_op jit(solution)/shard_map/ppermute | solution.py:237
  13.0 0.0 collective-permute-start.4
  13.0 1.6 %collective-permute-start.5 = (bf16[2,128,256]{2,1,0:T(8,128)(2,1)S(1)}, bf16[2,128,256]{2,1,0:T(8,128)(2,1)S(1)}, u32[]{:S(2)}, u32[]{:S(2)}) collective-permute-start(bf16[2,128,256]{2,1,0:T(8,128)(2,1)S(1)} %collective-permute-done.3.v), channel_id=1, source_target_pairs={{0,2},{1,3},{2,0},{3,1},{4,6},{5,7},{6,4},{7,5},{8,10},{9,11},{10,... | collective-permute-start | bytes 393224 | tf_op jit(solution)/shard_map/ppermute | solution.py:237
  14.6 0.0 collective-permute-done.u1
  14.6 0.8 %collective-permute-start.6 = (bf16[2,128,256]{2,1,0:T(8,128)(2,1)S(1)}, bf16[2,128,256]{2,1,0:T(8,128)(2,1)S(1)}, u32[]{:S(2)}, u32[]{:S(2)}) collective-permute-start(bf16[2,128,256]{2,1,0:T(8,128)(2,1)S(1)} %collective-permute-done.3.v), channel_id=1, source_target_pairs={{0,4},{1,5},{2,7},{3,6},{4,0},{5,1},{6,3},{7,2},{8,12},{9,13},{10,... | collective-permute-start | bytes 393224 | tf_op jit(solution)/shard_map/ppermute | solution.py:237
  15.4 0.0 collective-permute-done.1.u2
  15.4 0.7 %collective-permute-done.2.u3 = bf16[2,128,256]{2,1,0:T(8,128)(2,1)S(1)} collective-permute-done((bf16[2,128,256]{2,1,0:T(8,128)(2,1)}, bf16[2,128,256]{2,1,0:T(8,128)(2,1)S(1)}, u32[]{:S(2)}, u32[]{:S(2)}) %collective-permute-start.2) | collective-permute-done | bytes 131104 | tf_op jit(solution)/shard_map/ppermute | solution.py:237
  16.1 0.0 copy-done.1
  16.1 0.0 copy-done.2
  16.1 0.0 copy-start
  16.1 0.9 %copy-done = bf16[2,128,256]{2,1,0:T(8,128)(2,1)S(1)} copy-done((bf16[2,128,256]{2,1,0:T(8,128)(2,1)S(1)}, bf16[2,128,256]{2,1,0:T(8,128)(2,1)}, u32[]{:S(2)}) %copy-start) | copy-done | bytes 131096
  17.0 3.1 %early_pairs.1 = (bf16[2,3,256,256]{3,2,1,0:T(8,128)(2,1)S(1)}, bf16[2,512,256]{2,1,0:T(8,128)(2,1)S(1)}, bf16[1024,32]{1,0:T(8,128)(2,1)S(1)}, f32[12,1024]{1,0:T(8,128)S(1)}) custom-call(s32[2]{0:T(128)S(1)} %copy-done.1, s32[1,32]{1,0:T(1,128)S(1)} %bitcast.1, f32[16,256,256]{2,1,0:T(8,128)} %act_f.1, f32[16,256,256]{2,1,0:T(8,128)} %grad_f.1, ...), custom_call_target="tpu_custom_call" | custom-call | flops 1000000000 | bytes 1000000 | tf_op jit(solution)/shard_map/early_pairs/pallas_call | solution.py:217
  20.1 0.0 collective-permute-done.4.refs_0_
  20.1 0.0 collective-permute-done.5.refs_1_
  20.1 0.1 collective-permute-done.6.refs_2_
  20.2 1.0 %return_rows.1 = (f32[4,32]{1,0:T(4,128)S(1)}, f32[4,32]{1,0:T(4,128)S(1)}) custom-call(bf16[2,3,256,256]{3,2,1,0:T(8,128)(2,1)S(1)} %get-tuple-element.20.terms, bf16[2,512,256]{2,1,0:T(8,128)(2,1)S(1)} %get-tuple-element.17.white, bf16[1024,32]{1,0:T(8,128)(2,1)S(1)} %get-tuple-element.18.pick, f32[12,1024]{1,0:T(8,128)S(1)} %get-tuple-element.19.sums, ...), custom_call_target="tpu_custom_call" | custom-call | flops 1000000000 | bytes 1000000 | tf_op jit(solution)/shard_map/return_rows/pallas_call | solution.py:217
  21.2 1.6 %collective-permute-start.8 = (f32[4,32]{1,0:T(4,128)S(1)}, f32[4,32]{1,0:T(4,128)S(1)}, u32[]{:S(2)}, u32[]{:S(2)}) collective-permute-start(f32[4,32]{1,0:T(4,128)S(1)} %get-tuple-element.22), channel_id=1, source_target_pairs={{0,4},{1,5},{2,7},{3,6},{4,0},{5,1},{6,3},{7,2},{8,12},{9,13},{10,... | collective-permute-start | bytes 1544 | tf_op jit(solution)/shard_map/ppermute | solution.py:237
  22.7 0.2 collective-permute-start.7
  23.0 0.5 %own_rows.1 = f32[4,32]{1,0:T(4,128)S(1)} custom-call(bf16[2,512,256]{2,1,0:T(8,128)(2,1)S(1)} %get-tuple-element.17.white, bf16[1024,32]{1,0:T(8,128)(2,1)S(1)} %get-tuple-element.18.pick, f32[12,1024]{1,0:T(8,128)S(1)} %get-tuple-element.19.sums, bf16[2,128,256]{2,1,0:T(8,128)(2,1)S(1)} %collective-permute-done.4.refs_0_, ...), custom_call_target="tpu_custom_call" | custom-call | flops 1000000000 | bytes 1000000 | tf_op jit(solution)/shard_map/own_rows/pallas_call | solution.py:217
  23.5 1.3 %collective-permute-done.8 = f32[4,32]{1,0:T(4,128)S(1)} collective-permute-done((f32[4,32]{1,0:T(4,128)S(1)}, f32[4,32]{1,0:T(4,128)S(1)}, u32[]{:S(2)}, u32[]{:S(2)}) %collective-permute-start.8) | collective-permute-done | bytes 544 | tf_op jit(solution)/shard_map/ppermute | solution.py:237
  24.8 1.5 %collective-permute-done.7 = f32[4,32]{1,0:T(4,128)S(1)} collective-permute-done((f32[4,32]{1,0:T(4,128)S(1)}, f32[4,32]{1,0:T(4,128)S(1)}, u32[]{:S(2)}, u32[]{:S(2)}) %collective-permute-start.7) | collective-permute-done | bytes 544 | tf_op jit(solution)/shard_map/ppermute | solution.py:237
  26.3 2.6 %collective-permute-start.9 = (f32[2,32]{1,0:T(2,128)S(1)}, f32[2,32]{1,0:T(2,128)S(1)}, u32[]{:S(2)}, u32[]{:S(2)}) collective-permute-start(f32[2,32]{1,0:T(2,128)S(1)} %slice.7), channel_id=1, source_target_pairs={{0,8},{1,9},{2,10},{3,11},{4,12},{5,13},{6,14},{7,15},{8,0},{9,1},... | collective-permute-start | bytes 776 | tf_op jit(solution)/shard_map/ppermute | solution.py:237
  29.0 1.9 %collective-permute-done.9 = f32[2,32]{1,0:T(2,128)S(1)} collective-permute-done((f32[2,32]{1,0:T(2,128)S(1)}, f32[2,32]{1,0:T(2,128)S(1)}, u32[]{:S(2)}, u32[]{:S(2)}) %collective-permute-start.9) | collective-permute-done | bytes 288 | tf_op jit(solution)/shard_map/ppermute | solution.py:237
  30.9 0.6 %slice_add_fusion = f32[2,32]{1,0:T(2,128)} fusion(f32[2,32]{1,0:T(2,128)S(1)} %collective-permute-done.9, f32[4,32]{1,0:T(4,128)S(1)} %add_add_fusion), kind=kLoop, calls=%fused_computation.1 | loop fusion | flops 64 | bytes 768 | tf_op jit(solution)/shard_map/add | solution.py:290
  (2 shorter events, 0.0 us)
Async XLA Ops:
  0.0 16.1 %copy-start.1 = (s32[2]{0:T(128)S(1)}, s32[2]{0:T(128)}, u32[]{:S(2)}) copy-start(s32[2]{0:T(128)} %layer_ids.1) | copy-start | bytes 28
  0.0 16.1 %copy-start.2 = (s32[32]{0:T(128)S(1)}, s32[32]{0:T(128)}, u32[]{:S(2)}) copy-start(s32[32]{0:T(128)} %param.11) | copy-start | bytes 388
  2.4 10.6 %collective-permute-start.3 = (bf16[2,128,256]{2,1,0:T(8,128)(2,1)}, bf16[2,128,256]{2,1,0:T(8,128)(2,1)S(1)}, u32[]{:S(2)}, u32[]{:S(2)}) collective-permute-start(bf16[2,128,256]{2,1,0:T(8,128)(2,1)} %masked.2), channel_id=1, source_target_pairs={{0,8},{1,9},{2,10},{3,11},{4,12},{5,13},{6,14},{7,15},{8,0},{9,1},... | collective-permute-start | bytes 393224 | tf_op jit(solution)/shard_map/ppermute | solution.py:237
  8.7 5.9 %collective-permute-start = (bf16[2,128,256]{2,1,0:T(8,128)(2,1)}, bf16[2,128,256]{2,1,0:T(8,128)(2,1)S(1)}, u32[]{:S(2)}, u32[]{:S(2)}) collective-permute-start(bf16[2,128,256]{2,1,0:T(8,128)(2,1)} %masked.3.u0), channel_id=1, source_target_pairs={{0,1},{1,0},{2,3},{3,2},{4,5},{5,4},{6,7},{7,6},{8,9},{9,8},{10,11... | collective-permute-start | bytes 393224 | tf_op jit(solution)/shard_map/ppermute | solution.py:237
  8.8 6.6 %collective-permute-start.1 = (bf16[2,128,256]{2,1,0:T(8,128)(2,1)}, bf16[2,128,256]{2,1,0:T(8,128)(2,1)S(1)}, u32[]{:S(2)}, u32[]{:S(2)}) collective-permute-start(bf16[2,128,256]{2,1,0:T(8,128)(2,1)} %masked.3.u0), channel_id=1, source_target_pairs={{0,2},{1,3},{2,0},{3,1},{4,6},{5,7},{6,4},{7,5},{8,10},{9,11},{10,... | collective-permute-start | bytes 393224 | tf_op jit(solution)/shard_map/ppermute | solution.py:237
  10.3 5.8 %collective-permute-start.2 = (bf16[2,128,256]{2,1,0:T(8,128)(2,1)}, bf16[2,128,256]{2,1,0:T(8,128)(2,1)S(1)}, u32[]{:S(2)}, u32[]{:S(2)}) collective-permute-start(bf16[2,128,256]{2,1,0:T(8,128)(2,1)} %masked.3.u0), channel_id=1, source_target_pairs={{0,4},{1,5},{2,7},{3,6},{4,0},{5,1},{6,3},{7,2},{8,12},{9,13},{10,... | collective-permute-start | bytes 393224 | tf_op jit(solution)/shard_map/ppermute | solution.py:237
  13.0 7.1 %collective-permute-start.4 = (bf16[2,128,256]{2,1,0:T(8,128)(2,1)S(1)}, bf16[2,128,256]{2,1,0:T(8,128)(2,1)S(1)}, u32[]{:S(2)}, u32[]{:S(2)}) collective-permute-start(bf16[2,128,256]{2,1,0:T(8,128)(2,1)S(1)} %collective-permute-done.3.v), channel_id=1, source_target_pairs={{0,1},{1,0},{2,3},{3,2},{4,5},{5,4},{6,7},{7,6},{8,9},{9,8},{10,11... | collective-permute-start | bytes 393224 | tf_op jit(solution)/shard_map/ppermute | solution.py:237
  13.0 7.2 %collective-permute-start.5 = (bf16[2,128,256]{2,1,0:T(8,128)(2,1)S(1)}, bf16[2,128,256]{2,1,0:T(8,128)(2,1)S(1)}, u32[]{:S(2)}, u32[]{:S(2)}) collective-permute-start(bf16[2,128,256]{2,1,0:T(8,128)(2,1)S(1)} %collective-permute-done.3.v), channel_id=1, source_target_pairs={{0,2},{1,3},{2,0},{3,1},{4,6},{5,7},{6,4},{7,5},{8,10},{9,11},{10,... | collective-permute-start | bytes 393224 | tf_op jit(solution)/shard_map/ppermute | solution.py:237
  14.6 5.6 %collective-permute-start.6 = (bf16[2,128,256]{2,1,0:T(8,128)(2,1)S(1)}, bf16[2,128,256]{2,1,0:T(8,128)(2,1)S(1)}, u32[]{:S(2)}, u32[]{:S(2)}) collective-permute-start(bf16[2,128,256]{2,1,0:T(8,128)(2,1)S(1)} %collective-permute-done.3.v), channel_id=1, source_target_pairs={{0,4},{1,5},{2,7},{3,6},{4,0},{5,1},{6,3},{7,2},{8,12},{9,13},{10,... | collective-permute-start | bytes 393224 | tf_op jit(solution)/shard_map/ppermute | solution.py:237
  16.1 0.9 %copy-start = (bf16[2,128,256]{2,1,0:T(8,128)(2,1)S(1)}, bf16[2,128,256]{2,1,0:T(8,128)(2,1)}, u32[]{:S(2)}) copy-start(bf16[2,128,256]{2,1,0:T(8,128)(2,1)} %masked.3.u0) | copy-start | bytes 393220
  21.2 3.6 %collective-permute-start.8 = (f32[4,32]{1,0:T(4,128)S(1)}, f32[4,32]{1,0:T(4,128)S(1)}, u32[]{:S(2)}, u32[]{:S(2)}) collective-permute-start(f32[4,32]{1,0:T(4,128)S(1)} %get-tuple-element.22), channel_id=1, source_target_pairs={{0,4},{1,5},{2,7},{3,6},{4,0},{5,1},{6,3},{7,2},{8,12},{9,13},{10,... | collective-permute-start | bytes 1544 | tf_op jit(solution)/shard_map/ppermute | solution.py:237
  22.7 3.6 %collective-permute-start.7 = (f32[4,32]{1,0:T(4,128)S(1)}, f32[4,32]{1,0:T(4,128)S(1)}, u32[]{:S(2)}, u32[]{:S(2)}) collective-permute-start(f32[4,32]{1,0:T(4,128)S(1)} %get-tuple-element.21), channel_id=1, source_target_pairs={{0,2},{1,3},{2,0},{3,1},{4,6},{5,7},{6,4},{7,5},{8,10},{9,11},{10,... | collective-permute-start | bytes 1544 | tf_op jit(solution)/shard_map/ppermute | solution.py:237
  26.3 4.5 %collective-permute-start.9 = (f32[2,32]{1,0:T(2,128)S(1)}, f32[2,32]{1,0:T(2,128)S(1)}, u32[]{:S(2)}, u32[]{:S(2)}) collective-permute-start(f32[2,32]{1,0:T(2,128)S(1)} %slice.7), channel_id=1, source_target_pairs={{0,8},{1,9},{2,10},{3,11},{4,12},{5,13},{6,14},{7,15},{8,0},{9,1},... | collective-permute-start | bytes 776 | tf_op jit(solution)/shard_map/ppermute | solution.py:237

commit v6 on v5

--- a/solution.py
+++ b/solution.py
@@ -56,39 +56,31 @@
     return d ^ 4 ^ ((d >> 1) & 1)
 
 
-def mask_kernel(seq_len, pieces, lens, acts, grads, *refs):
-    outs, bufs, sems = refs[: len(pieces)], refs[len(pieces) : -1], refs[-1]
-    half = lax.axis_index("blk") // 8
-    copies = []
-    for n, (kept, first, buf) in enumerate(zip(*zip(*pieces), bufs)):
-        layer = half if kept else 1 - half
-        for w, src in enumerate((acts, grads)):
-            rows = pl.ds(first, buf.shape[1])
-            copies.append(pltpu.make_async_copy(src.at[layer, rows], buf.at[w], sems.at[n, w]))
-            copies[-1].start()
-    for n, (piece, buf, out) in enumerate(zip(pieces, bufs, outs)):
-        row = lax.broadcasted_iota(jnp.int32, (buf.shape[1], 1), 0)
-        bound = jnp.zeros_like(row)
-        for s in range(buf.shape[1] // seq_len):
-            bound = jnp.where(row // seq_len == s, lens[piece[1] // seq_len + s] + s * seq_len, bound)
-        for w in range(2):
-            copies[2 * n + w].wait()
-            x = buf[w]
-            out[w] = jnp.where(row < bound, x, jnp.zeros_like(x))
-
-
-def masked(activations, out_grads, lengths, seq_len, pieces):
-    rank = activations.shape[2]
-    shapes = [(2, rows, rank) for _, _, rows in pieces]
-    vmem = pl.BlockSpec(memory_space=pltpu.VMEM)
-    hbm = pl.BlockSpec(memory_space=pltpu.HBM)
+def mask_kernel(seq_len, lens, acts, grads, out):
+    tokens = acts.shape[1]
+    row = lax.broadcasted_iota(jnp.int32, (tokens, 1), 0)
+    bound = jnp.zeros_like(row)
+    for s in range(tokens // seq_len):
+        bound = jnp.where(row // seq_len == s, lens[s] + s * seq_len, bound)
+    for w, src in enumerate((acts, grads)):
+        x = src[0]
+        out[w] = jnp.where(row < bound, x, jnp.zeros_like(x))
+
+
+def masked(activations, out_grads, lengths, seq_len, kept):
+    tokens, rank = activations.shape[1:]
+
+    def layer(i):
+        half = lax.axis_index("blk") // 8
+        return (half if kept else 1 - half, 0, 0)
+
+    data = pl.BlockSpec((1, tokens, rank), layer)
     return pl.pallas_call(
-        functools.partial(mask_kernel, seq_len, [piece[:2] for piece in pieces]),
-        out_shape=[jax.ShapeDtypeStruct(shape, activations.dtype) for shape in shapes],
-        in_specs=[pl.BlockSpec(memory_space=pltpu.SMEM), hbm, hbm],
-        out_specs=[vmem] * len(pieces),
-        scratch_shapes=[pltpu.VMEM(shape, activations.dtype) for shape in shapes]
-        + [pltpu.SemaphoreType.DMA((len(pieces), 2))],
+        functools.partial(mask_kernel, seq_len),
+        grid=(1,),
+        out_shape=jax.ShapeDtypeStruct((2, tokens, rank), activations.dtype),
+        in_specs=[pl.BlockSpec(memory_space=pltpu.SMEM), data, data],
+        out_specs=pl.BlockSpec((2, tokens, rank), lambda i: (0, 0, 0)),
         compiler_params=pltpu.CompilerParams(vmem_limit_bytes=59 * 1024 * 1024),
         cost_estimate=pl.CostEstimate(flops=10**9, bytes_accessed=10**6, transcendentals=0),
         name="masked",
@@ -125,10 +117,7 @@
     return out[:n] + out[n : 2 * n] + out[2 * n :]
 
 
-def early_kernel(
-    seq_len, per, layer_ids, flagged, act_f, grad_f, u0, u1, u2, u3, v,
-    terms, white, pick, sums, factor, sems,
-):
+def setup_kernel(seq_len, per, layer_ids, flagged, act_f, grad_f, terms, pick, factor, sems):
     d = lax.axis_index("blk")
     layer = layer_ids[d // 8]
     copies = [
@@ -147,15 +136,19 @@
     seq = owner * per + token // seq_len % per
     scale = 1.0 / (factor.shape[1] * seq_len)
     pick[...] = jnp.where(seq == flagged[...], scale, 0.0).astype(pick.dtype)
-    n = u0.shape[1]
-    mine, x, z = [], [], []
-    for w in range(2):
-        copies[w].wait()
+    for w, copy in enumerate(copies):
+        copy.wait()
         rest = factor[w]
         for t in range(3):
             term = rest.astype(jnp.bfloat16)
             terms[w, t] = term
             rest = rest - term.astype(jnp.float32)
+
+
+def early_kernel(seq_len, per, terms, u0, v, u3, u2, u1, white, sums):
+    n = u0.shape[1]
+    mine, x, z = [], [], []
+    for w in range(2):
         rows = whiten(stack(u0[w], v[w], u2[w], u3[w]), terms.at[w])
         white[w] = rows
         mine.append(rows[: 2 * n])
@@ -175,8 +168,8 @@
             sums[row : row + per, at : at + n] = block(seq_len, left, tok[slot])
 
 
-def return_kernel(seq_len, per, terms, white, pick, sums, u1, u2, u3, *refs):
-    v, outs = refs[:3], refs[3:]
+def return_kernel(seq_len, per, terms, white, pick, sums, u3, u2, u1, v3, v2, v1, *outs):
+    v = (v1, v2, v3)
     n = u1.shape[1]
     late = [[v[i][w] for w in range(2)] for i in range(3)]
     tok = [[u[w] for w in range(2)] for u in (u1, u2, u3)]
@@ -200,8 +193,8 @@
         out[...] = picked[i * r : (i + 1) * r]
 
 
-def own_kernel(seq_len, per, white, pick, sums, *refs):
-    v, out = refs[:3], refs[3]
+def own_kernel(seq_len, per, white, pick, sums, v3, v2, v1, out):
+    v = (v1, v2, v3)
     n = v[0].shape[1]
     r = 2 * per
     mine = [white[w, : 2 * n] for w in range(2)]
@@ -239,33 +232,38 @@
     def opposite(d):
         return d ^ 8
 
-    ways = (lambda d: d ^ 1, lambda d: d ^ 2, z_near)
-    data = (activations, out_grads, lengths, seq_len)
-    (away,) = masked(*data, [(False, 0, tokens)])
+    ways = (z_near, lambda d: d ^ 2, lambda d: d ^ 1)
+    data = (activations, out_grads, lengths)
+    away = masked(*data, seq_len, False)
     v = send(away, opposite)
-    away, *data = lax.optimization_barrier((away, *data[:3]))
-    (own,) = masked(*data, seq_len, [(True, 0, tokens)])
-    u = [own] + [send(own, to) for to in ways[::-1]][::-1]
-    late = [send(v, to) for to in ways[::-1]][::-1]
+    away, *data = lax.optimization_barrier((away, *data))
+    own = masked(*data, seq_len, True)
+    near = [send(own, to) for to in ways]
 
     shape = jax.ShapeDtypeStruct
     columns = flagged.shape[0]
     hbm = pl.BlockSpec(memory_space=pltpu.HBM)
     vmem = pl.BlockSpec(memory_space=pltpu.VMEM)
-    terms, white, pick, sums = call(
+    terms, pick = call(
+        functools.partial(setup_kernel, seq_len, per),
+        "factor_terms",
+        10**9,
+        51,
+        (layer_ids, flagged.reshape(1, -1), act_factor, grad_factor),
+        [pl.BlockSpec(memory_space=pltpu.SMEM), vmem, hbm, hbm],
+        (shape((2, 3, rank, rank), bf16), shape((8 * tokens, columns), bf16)),
+        [pltpu.VMEM((2, rank, rank), f32), pltpu.SemaphoreType.DMA((2,))],
+    )
+    v, terms, pick = lax.optimization_barrier((v, terms, pick))
+    late = [send(v, to) for to in ways]
+    white, sums = call(
         functools.partial(early_kernel, seq_len, per),
         "early_pairs",
         10**9,
-        51,
-        (layer_ids, flagged.reshape(1, -1), act_factor, grad_factor, *u, v),
-        [pl.BlockSpec(memory_space=pltpu.SMEM), vmem, hbm, hbm],
-        (
-            shape((2, 3, rank, rank), bf16),
-            shape((2, 4 * tokens, rank), bf16),
-            shape((8 * tokens, columns), bf16),
-            shape((6 * per, 8 * tokens), f32),
-        ),
-        [pltpu.VMEM((2, rank, rank), f32), pltpu.SemaphoreType.DMA((2,))],
+        40,
+        (terms, own, v, *near),
+        [],
+        (shape((2, 4 * tokens, rank), bf16), shape((6 * per, 8 * tokens), f32)),
     )
     rows = shape((2 * per, columns), f32)
     by_x, by_z = call(
@@ -273,7 +271,7 @@
         "return_rows",
         10**9,
         40,
-        (terms, white, pick, sums, *u[1:], *late),
+        (terms, white, pick, sums, *near, *late),
         [],
         (rows, rows),
     )

time: 31.7 us -> 29.5 us (0.931)
  Pallas kernels: 9.13 us -> 7.26 us
  waiting for transfers between devices: 6.64 us -> 7.92 us
  local copies, waits for them, and re-layouts: 0.92 us -> 0.02 us
  starting transfers between devices: 14.1 us -> 13.5 us
    pallas_call x2, Pallas kernels: 4.57 us -> 3.13 us  [masked(): pl.pallas_call(functools.partial(mask_kernel, seq_len), grid=(1,), out_sh...]
    ppermute x10, waiting for transfers between devices: 6.64 us -> 7.92 us  [send(): return lax.ppermute(x, 'blk', [(d, to(d)) for d in range(size)])]
    unnamed x6, local copies, waits for them, and re-layouts: 0.91 us -> 0.01 us
    ppermute x10, starting transfers between devices: 14.1 us -> 13.5 us  [send(): return lax.ppermute(x, 'blk', [(d, to(d)) for d in range(size)])]
    pallas_call x3 -> x4, Pallas kernels: 4.56 us -> 4.13 us  [call(): pl.pallas_call(kernel, out_shape=out_shape, in_specs=specs + [vmem] * (le...]
  transfers between devices with their start and end apart: 10 -> 10, of which waited for: 6 -> 6; matrix products, arithmetic and copies ran while one was open for 0% -> 0% of each run, Pallas kernels for 18% -> 16%
where the time goes in v6:
time: 29.5 us; the launch traced here: 29.3 us
  starting transfers between devices  13.5 us (46%)
  waiting for transfers between devices  7.92 us (27%)
  Pallas kernels  7.26 us (25%)
  other arithmetic  0.57 us (2%)
    ppermute x10, starting transfers between devices, send(): return lax.ppermute(x, 'blk', [(d, to(d)) for d in range(size)])  13.5 us
    ppermute x10, waiting for transfers between devices, send(): return lax.ppermute(x, 'blk', [(d, to(d)) for d in range(size)])  7.92 us
    pallas_call x4, Pallas kernels, call(): pl.pallas_call(kernel, out_shape=out_shape, in_specs=specs + [vmem] * (le...  4.13 us
    pallas_call x2, Pallas kernels, masked(): pl.pallas_call(functools.partial(mask_kernel, seq_len), grid=(1,), out_sh...  3.13 us
  transfers between devices with their start and end apart: 10, of which 6 were waited for; matrix products, arithmetic and copies ran while one was open for 0% of the time, Pallas kernels for 16%

profile of v6, /device:TPU:0, one launch (start us, length us, event | category | flops | bytes accessed | tf_op | source)
XLA Modules:
  0.0 29.3 jit_solution(6101221804057591126)
XLA Ops:
  0.0 0.0 copy-start
  0.0 0.0 copy-start.1
  0.0 1.6 %masked.2 = bf16[2,128,256]{2,1,0:T(8,128)(2,1)} custom-call(s32[2]{0:T(128)} %lens.2, bf16[2,128,256]{2,1,0:T(8,128)(2,1)} %acts.2, bf16[2,128,256]{2,1,0:T(8,128)(2,1)} %grads.2), custom_call_target="tpu_custom_call" | custom-call | flops 1000000000 | bytes 1000000 | tf_op jit(solution)/shard_map/masked/pallas_call | solution.py:78
  1.6 4.0 %collective-permute-start = (bf16[2,128,256]{2,1,0:T(8,128)(2,1)}, bf16[2,128,256]{2,1,0:T(8,128)(2,1)S(1)}, u32[]{:S(2)}, u32[]{:S(2)}) collective-permute-start(bf16[2,128,256]{2,1,0:T(8,128)(2,1)} %masked.2), channel_id=1, source_target_pairs={{0,8},{1,9},{2,10},{3,11},{4,12},{5,13},{6,14},{7,15},{8,0},{9,1},... | collective-permute-start | bytes 393224 | tf_op jit(solution)/shard_map/ppermute | solution.py:230
  5.6 1.6 %masked.3.u0 = bf16[2,128,256]{2,1,0:T(8,128)(2,1)} custom-call(s32[2]{0:T(128)} %lens.2, bf16[2,128,256]{2,1,0:T(8,128)(2,1)} %acts.2, bf16[2,128,256]{2,1,0:T(8,128)(2,1)} %grads.2), custom_call_target="tpu_custom_call" | custom-call | flops 1000000000 | bytes 1000000 | tf_op jit(solution)/shard_map/masked/pallas_call | solution.py:78
  7.2 1.6 %collective-permute-start.1 = (bf16[2,128,256]{2,1,0:T(8,128)(2,1)}, bf16[2,128,256]{2,1,0:T(8,128)(2,1)S(1)}, u32[]{:S(2)}, u32[]{:S(2)}) collective-permute-start(bf16[2,128,256]{2,1,0:T(8,128)(2,1)} %masked.3.u0), channel_id=1, source_target_pairs={{0,4},{1,5},{2,7},{3,6},{4,0},{5,1},{6,3},{7,2},{8,12},{9,13},{10,... | collective-permute-start | bytes 393224 | tf_op jit(solution)/shard_map/ppermute | solution.py:230
  8.8 0.7 %collective-permute-start.2 = (bf16[2,128,256]{2,1,0:T(8,128)(2,1)}, bf16[2,128,256]{2,1,0:T(8,128)(2,1)S(1)}, u32[]{:S(2)}, u32[]{:S(2)}) collective-permute-start(bf16[2,128,256]{2,1,0:T(8,128)(2,1)} %masked.3.u0), channel_id=1, source_target_pairs={{0,2},{1,3},{2,0},{3,1},{4,6},{5,7},{6,4},{7,5},{8,10},{9,11},{10,... | collective-permute-start | bytes 393224 | tf_op jit(solution)/shard_map/ppermute | solution.py:230
  9.4 0.7 %collective-permute-start.3 = (bf16[2,128,256]{2,1,0:T(8,128)(2,1)}, bf16[2,128,256]{2,1,0:T(8,128)(2,1)S(1)}, u32[]{:S(2)}, u32[]{:S(2)}) collective-permute-start(bf16[2,128,256]{2,1,0:T(8,128)(2,1)} %masked.3.u0), channel_id=1, source_target_pairs={{0,1},{1,0},{2,3},{3,2},{4,5},{5,4},{6,7},{7,6},{8,9},{9,8},{10,11... | collective-permute-start | bytes 393224 | tf_op jit(solution)/shard_map/ppermute | solution.py:230
  10.1 0.0 copy-done
  10.1 0.0 copy-done.1
  10.1 1.7 %factor_terms.1 = (bf16[2,3,256,256]{3,2,1,0:T(8,128)(2,1)S(1)}, bf16[1024,32]{1,0:T(8,128)(2,1)S(1)}) custom-call(s32[2]{0:T(128)S(1)} %copy-done, s32[1,32]{1,0:T(1,128)S(1)} %bitcast.1, f32[16,256,256]{2,1,0:T(8,128)} %act_f.1, f32[16,256,256]{2,1,0:T(8,128)} %grad_f.1), custom_call_target="tpu_custom_call" | custom-call | flops 1000000000 | bytes 1000000 | tf_op jit(solution)/shard_map/factor_terms/pallas_call | solution.py:210
  11.8 0.5 %collective-permute-done.v = bf16[2,128,256]{2,1,0:T(8,128)(2,1)S(1)} collective-permute-done((bf16[2,128,256]{2,1,0:T(8,128)(2,1)}, bf16[2,128,256]{2,1,0:T(8,128)(2,1)S(1)}, u32[]{:S(2)}, u32[]{:S(2)}) %collective-permute-start) | collective-permute-done | bytes 131104 | tf_op jit(solution)/shard_map/ppermute | solution.py:230
  12.2 0.8 %collective-permute-start.4 = (bf16[2,128,256]{2,1,0:T(8,128)(2,1)S(1)}, bf16[2,128,256]{2,1,0:T(8,128)(2,1)S(1)}, u32[]{:S(2)}, u32[]{:S(2)}) collective-permute-start(bf16[2,128,256]{2,1,0:T(8,128)(2,1)S(1)} %collective-permute-done.v), channel_id=1, source_target_pairs={{0,4},{1,5},{2,7},{3,6},{4,0},{5,1},{6,3},{7,2},{8,12},{9,13},{10,... | collective-permute-start | bytes 393224 | tf_op jit(solution)/shard_map/ppermute | solution.py:230
  13.0 1.1 %collective-permute-start.5 = (bf16[2,128,256]{2,1,0:T(8,128)(2,1)S(1)}, bf16[2,128,256]{2,1,0:T(8,128)(2,1)S(1)}, u32[]{:S(2)}, u32[]{:S(2)}) collective-permute-start(bf16[2,128,256]{2,1,0:T(8,128)(2,1)S(1)} %collective-permute-done.v), channel_id=1, source_target_pairs={{0,2},{1,3},{2,0},{3,1},{4,6},{5,7},{6,4},{7,5},{8,10},{9,11},{10,... | collective-permute-start | bytes 393224 | tf_op jit(solution)/shard_map/ppermute | solution.py:230
  14.1 0.0 collective-permute-done.1.u3
  14.1 0.2 collective-permute-start.6
  14.3 0.0 collective-permute-done.2.u2
  14.3 0.0 collective-permute-done.3.u1
  14.3 0.0 copy-done.2
  14.4 1.0 %early_pairs.1 = (bf16[2,512,256]{2,1,0:T(8,128)(2,1)S(1)}, f32[12,1024]{1,0:T(8,128)S(1)}) custom-call(bf16[2,3,256,256]{3,2,1,0:T(8,128)(2,1)S(1)} %get-tuple-element.19.terms, bf16[2,128,256]{2,1,0:T(8,128)(2,1)S(1)} %copy-done.2, bf16[2,128,256]{2,1,0:T(8,128)(2,1)S(1)} %collective-permute-done.v, bf16[2,128,256]{2,1,0:T(8,128)(2,1)S(1)} %collective-permute-done.1.u3, ...), custom_call_target="tpu_custom_call" | custom-call | flops 1000000000 | bytes 1000000 | tf_op jit(solution)/shard_map/early_pairs/pallas_call | solution.py:210
  15.3 1.9 %collective-permute-done.4.v3 = bf16[2,128,256]{2,1,0:T(8,128)(2,1)S(1)} collective-permute-done((bf16[2,128,256]{2,1,0:T(8,128)(2,1)S(1)}, bf16[2,128,256]{2,1,0:T(8,128)(2,1)S(1)}, u32[]{:S(2)}, u32[]{:S(2)}) %collective-permute-start.4) | collective-permute-done | bytes 131104 | tf_op jit(solution)/shard_map/ppermute | solution.py:230
  17.3 1.0 %collective-permute-done.5.v2 = bf16[2,128,256]{2,1,0:T(8,128)(2,1)S(1)} collective-permute-done((bf16[2,128,256]{2,1,0:T(8,128)(2,1)S(1)}, bf16[2,128,256]{2,1,0:T(8,128)(2,1)S(1)}, u32[]{:S(2)}, u32[]{:S(2)}) %collective-permute-start.5) | collective-permute-done | bytes 131104 | tf_op jit(solution)/shard_map/ppermute | solution.py:230
  18.3 0.0 collective-permute-done.6.v1
  18.3 1.0 %return_rows.1 = (f32[4,32]{1,0:T(4,128)S(1)}, f32[4,32]{1,0:T(4,128)S(1)}) custom-call(bf16[2,3,256,256]{3,2,1,0:T(8,128)(2,1)S(1)} %get-tuple-element.19.terms, bf16[2,512,256]{2,1,0:T(8,128)(2,1)S(1)} %get-tuple-element.24.white, bf16[1024,32]{1,0:T(8,128)(2,1)S(1)} %get-tuple-element.25.pick, f32[12,1024]{1,0:T(8,128)S(1)} %get-tuple-element.26.sums, ...), custom_call_target="tpu_custom_call" | custom-call | flops 1000000000 | bytes 1000000 | tf_op jit(solution)/shard_map/return_rows/pallas_call | solution.py:210
  19.2 1.3 %collective-permute-start.8 = (f32[4,32]{1,0:T(4,128)S(1)}, f32[4,32]{1,0:T(4,128)S(1)}, u32[]{:S(2)}, u32[]{:S(2)}) collective-permute-start(f32[4,32]{1,0:T(4,128)S(1)} %get-tuple-element.28), channel_id=1, source_target_pairs={{0,4},{1,5},{2,7},{3,6},{4,0},{5,1},{6,3},{7,2},{8,12},{9,13},{10,... | collective-permute-start | bytes 1544 | tf_op jit(solution)/shard_map/ppermute | solution.py:230
  20.6 0.9 %collective-permute-start.7 = (f32[4,32]{1,0:T(4,128)S(1)}, f32[4,32]{1,0:T(4,128)S(1)}, u32[]{:S(2)}, u32[]{:S(2)}) collective-permute-start(f32[4,32]{1,0:T(4,128)S(1)} %get-tuple-element.27), channel_id=1, source_target_pairs={{0,2},{1,3},{2,0},{3,1},{4,6},{5,7},{6,4},{7,5},{8,10},{9,11},{10,... | collective-permute-start | bytes 1544 | tf_op jit(solution)/shard_map/ppermute | solution.py:230
  21.5 0.5 %own_rows.1 = f32[4,32]{1,0:T(4,128)S(1)} custom-call(bf16[2,512,256]{2,1,0:T(8,128)(2,1)S(1)} %get-tuple-element.24.white, bf16[1024,32]{1,0:T(8,128)(2,1)S(1)} %get-tuple-element.25.pick, f32[12,1024]{1,0:T(8,128)S(1)} %get-tuple-element.26.sums, bf16[2,128,256]{2,1,0:T(8,128)(2,1)S(1)} %collective-permute-done.4.v3, ...), custom_call_target="tpu_custom_call" | custom-call | flops 1000000000 | bytes 1000000 | tf_op jit(solution)/shard_map/own_rows/pallas_call | solution.py:210
  22.0 0.9 %collective-permute-done.8 = f32[4,32]{1,0:T(4,128)S(1)} collective-permute-done((f32[4,32]{1,0:T(4,128)S(1)}, f32[4,32]{1,0:T(4,128)S(1)}, u32[]{:S(2)}, u32[]{:S(2)}) %collective-permute-start.8) | collective-permute-done | bytes 544 | tf_op jit(solution)/shard_map/ppermute | solution.py:230
  22.9 1.3 %collective-permute-done.7 = f32[4,32]{1,0:T(4,128)S(1)} collective-permute-done((f32[4,32]{1,0:T(4,128)S(1)}, f32[4,32]{1,0:T(4,128)S(1)}, u32[]{:S(2)}, u32[]{:S(2)}) %collective-permute-start.7) | collective-permute-done | bytes 544 | tf_op jit(solution)/shard_map/ppermute | solution.py:230
  24.2 2.2 %collective-permute-start.9 = (f32[2,32]{1,0:T(2,128)S(1)}, f32[2,32]{1,0:T(2,128)S(1)}, u32[]{:S(2)}, u32[]{:S(2)}) collective-permute-start(f32[2,32]{1,0:T(2,128)S(1)} %slice.7), channel_id=1, source_target_pairs={{0,8},{1,9},{2,10},{3,11},{4,12},{5,13},{6,14},{7,15},{8,0},{9,1},... | collective-permute-start | bytes 776 | tf_op jit(solution)/shard_map/ppermute | solution.py:230
  26.4 2.3 %collective-permute-done.9 = f32[2,32]{1,0:T(2,128)S(1)} collective-permute-done((f32[2,32]{1,0:T(2,128)S(1)}, f32[2,32]{1,0:T(2,128)S(1)}, u32[]{:S(2)}, u32[]{:S(2)}) %collective-permute-start.9) | collective-permute-done | bytes 288 | tf_op jit(solution)/shard_map/ppermute | solution.py:230
  28.7 0.6 %slice_add_fusion = f32[2,32]{1,0:T(2,128)} fusion(f32[2,32]{1,0:T(2,128)S(1)} %collective-permute-done.9, f32[4,32]{1,0:T(4,128)S(1)} %add_add_fusion), kind=kLoop, calls=%fused_computation.1 | loop fusion | flops 64 | bytes 768 | tf_op jit(solution)/shard_map/add | solution.py:288
  (3 shorter events, 0.0 us)
Async XLA Ops:
  0.0 10.1 %copy-start = (s32[2]{0:T(128)S(1)}, s32[2]{0:T(128)}, u32[]{:S(2)}) copy-start(s32[2]{0:T(128)} %layer_ids.1) | copy-start | bytes 28
  0.0 10.1 %copy-start.1 = (s32[32]{0:T(128)S(1)}, s32[32]{0:T(128)}, u32[]{:S(2)}) copy-start(s32[32]{0:T(128)} %param.11) | copy-start | bytes 388
  1.6 10.7 %collective-permute-start = (bf16[2,128,256]{2,1,0:T(8,128)(2,1)}, bf16[2,128,256]{2,1,0:T(8,128)(2,1)S(1)}, u32[]{:S(2)}, u32[]{:S(2)}) collective-permute-start(bf16[2,128,256]{2,1,0:T(8,128)(2,1)} %masked.2), channel_id=1, source_target_pairs={{0,8},{1,9},{2,10},{3,11},{4,12},{5,13},{6,14},{7,15},{8,0},{9,1},... | collective-permute-start | bytes 393224 | tf_op jit(solution)/shard_map/ppermute | solution.py:230
  7.2 7.0 %collective-permute-start.1 = (bf16[2,128,256]{2,1,0:T(8,128)(2,1)}, bf16[2,128,256]{2,1,0:T(8,128)(2,1)S(1)}, u32[]{:S(2)}, u32[]{:S(2)}) collective-permute-start(bf16[2,128,256]{2,1,0:T(8,128)(2,1)} %masked.3.u0), channel_id=1, source_target_pairs={{0,4},{1,5},{2,7},{3,6},{4,0},{5,1},{6,3},{7,2},{8,12},{9,13},{10,... | collective-permute-start | bytes 393224 | tf_op jit(solution)/shard_map/ppermute | solution.py:230
  8.8 5.6 %collective-permute-start.2 = (bf16[2,128,256]{2,1,0:T(8,128)(2,1)}, bf16[2,128,256]{2,1,0:T(8,128)(2,1)S(1)}, u32[]{:S(2)}, u32[]{:S(2)}) collective-permute-start(bf16[2,128,256]{2,1,0:T(8,128)(2,1)} %masked.3.u0), channel_id=1, source_target_pairs={{0,2},{1,3},{2,0},{3,1},{4,6},{5,7},{6,4},{7,5},{8,10},{9,11},{10,... | collective-permute-start | bytes 393224 | tf_op jit(solution)/shard_map/ppermute | solution.py:230
  9.4 4.9 %collective-permute-start.3 = (bf16[2,128,256]{2,1,0:T(8,128)(2,1)}, bf16[2,128,256]{2,1,0:T(8,128)(2,1)S(1)}, u32[]{:S(2)}, u32[]{:S(2)}) collective-permute-start(bf16[2,128,256]{2,1,0:T(8,128)(2,1)} %masked.3.u0), channel_id=1, source_target_pairs={{0,1},{1,0},{2,3},{3,2},{4,5},{5,4},{6,7},{7,6},{8,9},{9,8},{10,11... | collective-permute-start | bytes 393224 | tf_op jit(solution)/shard_map/ppermute | solution.py:230
  10.1 4.3 %copy-start.2 = (bf16[2,128,256]{2,1,0:T(8,128)(2,1)S(1)}, bf16[2,128,256]{2,1,0:T(8,128)(2,1)}, u32[]{:S(2)}) copy-start(bf16[2,128,256]{2,1,0:T(8,128)(2,1)} %masked.3.u0) | copy-start | bytes 393220
  12.2 5.0 %collective-permute-start.4 = (bf16[2,128,256]{2,1,0:T(8,128)(2,1)S(1)}, bf16[2,128,256]{2,1,0:T(8,128)(2,1)S(1)}, u32[]{:S(2)}, u32[]{:S(2)}) collective-permute-start(bf16[2,128,256]{2,1,0:T(8,128)(2,1)S(1)} %collective-permute-done.v), channel_id=1, source_target_pairs={{0,4},{1,5},{2,7},{3,6},{4,0},{5,1},{6,3},{7,2},{8,12},{9,13},{10,... | collective-permute-start | bytes 393224 | tf_op jit(solution)/shard_map/ppermute | solution.py:230
  13.0 5.3 %collective-permute-start.5 = (bf16[2,128,256]{2,1,0:T(8,128)(2,1)S(1)}, bf16[2,128,256]{2,1,0:T(8,128)(2,1)S(1)}, u32[]{:S(2)}, u32[]{:S(2)}) collective-permute-start(bf16[2,128,256]{2,1,0:T(8,128)(2,1)S(1)} %collective-permute-done.v), channel_id=1, source_target_pairs={{0,2},{1,3},{2,0},{3,1},{4,6},{5,7},{6,4},{7,5},{8,10},{9,11},{10,... | collective-permute-start | bytes 393224 | tf_op jit(solution)/shard_map/ppermute | solution.py:230
  14.1 4.2 %collective-permute-start.6 = (bf16[2,128,256]{2,1,0:T(8,128)(2,1)S(1)}, bf16[2,128,256]{2,1,0:T(8,128)(2,1)S(1)}, u32[]{:S(2)}, u32[]{:S(2)}) collective-permute-start(bf16[2,128,256]{2,1,0:T(8,128)(2,1)S(1)} %collective-permute-done.v), channel_id=1, source_target_pairs={{0,1},{1,0},{2,3},{3,2},{4,5},{5,4},{6,7},{7,6},{8,9},{9,8},{10,11... | collective-permute-start | bytes 393224 | tf_op jit(solution)/shard_map/ppermute | solution.py:230
  19.2 3.6 %collective-permute-start.8 = (f32[4,32]{1,0:T(4,128)S(1)}, f32[4,32]{1,0:T(4,128)S(1)}, u32[]{:S(2)}, u32[]{:S(2)}) collective-permute-start(f32[4,32]{1,0:T(4,128)S(1)} %get-tuple-element.28), channel_id=1, source_target_pairs={{0,4},{1,5},{2,7},{3,6},{4,0},{5,1},{6,3},{7,2},{8,12},{9,13},{10,... | collective-permute-start | bytes 1544 | tf_op jit(solution)/shard_map/ppermute | solution.py:230
  20.6 3.6 %collective-permute-start.7 = (f32[4,32]{1,0:T(4,128)S(1)}, f32[4,32]{1,0:T(4,128)S(1)}, u32[]{:S(2)}, u32[]{:S(2)}) collective-permute-start(f32[4,32]{1,0:T(4,128)S(1)} %get-tuple-element.27), channel_id=1, source_target_pairs={{0,2},{1,3},{2,0},{3,1},{4,6},{5,7},{6,4},{7,5},{8,10},{9,11},{10,... | collective-permute-start | bytes 1544 | tf_op jit(solution)/shard_map/ppermute | solution.py:230
  24.2 4.5 %collective-permute-start.9 = (f32[2,32]{1,0:T(2,128)S(1)}, f32[2,32]{1,0:T(2,128)S(1)}, u32[]{:S(2)}, u32[]{:S(2)}) collective-permute-start(f32[2,32]{1,0:T(2,128)S(1)} %slice.7), channel_id=1, source_target_pairs={{0,8},{1,9},{2,10},{3,11},{4,12},{5,13},{6,14},{7,15},{8,0},{9,1},... | collective-permute-start | bytes 776 | tf_op jit(solution)/shard_map/ppermute | solution.py:230

commit v7 on v6

--- a/solution.py
+++ b/solution.py
@@ -145,7 +145,7 @@
             rest = rest - term.astype(jnp.float32)
 
 
-def early_kernel(seq_len, per, terms, u0, v, u3, u2, u1, white, sums):
+def early_kernel(seq_len, per, terms, u0, v, u2, u3, u1, white, sums):
     n = u0.shape[1]
     mine, x, z = [], [], []
     for w in range(2):
@@ -168,7 +168,7 @@
             sums[row : row + per, at : at + n] = block(seq_len, left, tok[slot])
 
 
-def return_kernel(seq_len, per, terms, white, pick, sums, u3, u2, u1, v3, v2, v1, *outs):
+def return_kernel(seq_len, per, terms, white, pick, sums, u2, u3, u1, v2, v3, v1, *outs):
     v = (v1, v2, v3)
     n = u1.shape[1]
     late = [[v[i][w] for w in range(2)] for i in range(3)]
@@ -193,7 +193,7 @@
         out[...] = picked[i * r : (i + 1) * r]
 
 
-def own_kernel(seq_len, per, white, pick, sums, v3, v2, v1, out):
+def own_kernel(seq_len, per, white, pick, sums, v2, v3, v1, out):
     v = (v1, v2, v3)
     n = v[0].shape[1]
     r = 2 * per
@@ -232,7 +232,7 @@
     def opposite(d):
         return d ^ 8
 
-    ways = (z_near, lambda d: d ^ 2, lambda d: d ^ 1)
+    ways = (lambda d: d ^ 2, z_near, lambda d: d ^ 1)
     data = (activations, out_grads, lengths)
     away = masked(*data, seq_len, False)
     v = send(away, opposite)

time: 29.5 us -> 29.9 us (1.014)
  starting transfers between devices: 13.5 us -> 14.4 us
  waiting for transfers between devices: 7.92 us -> 7.43 us
    ppermute x10, starting transfers between devices: 13.5 us -> 14.4 us  [send(): return lax.ppermute(x, 'blk', [(d, to(d)) for d in range(size)])]
    ppermute x10, waiting for transfers between devices: 7.92 us -> 7.43 us  [send(): return lax.ppermute(x, 'blk', [(d, to(d)) for d in range(size)])]
  transfers between devices with their start and end apart: 10 -> 10, of which waited for: 6 -> 7; matrix products, arithmetic and copies ran while one was open for 0% -> 0% of each run, Pallas kernels for 16% -> 16%
where the time goes in v7:
time: 29.9 us; the launch traced here: 29.7 us
  starting transfers between devices  14.4 us (48%)
  waiting for transfers between devices  7.43 us (25%)
  Pallas kernels  7.26 us (24%)
  other arithmetic  0.57 us (2%)
    ppermute x10, starting transfers between devices, send(): return lax.ppermute(x, 'blk', [(d, to(d)) for d in range(size)])  14.4 us
    ppermute x10, waiting for transfers between devices, send(): return lax.ppermute(x, 'blk', [(d, to(d)) for d in range(size)])  7.43 us
    pallas_call x4, Pallas kernels, call(): pl.pallas_call(kernel, out_shape=out_shape, in_specs=specs + [vmem] * (le...  4.13 us
    pallas_call x2, Pallas kernels, masked(): pl.pallas_call(functools.partial(mask_kernel, seq_len), grid=(1,), out_sh...  3.13 us
  transfers between devices with their start and end apart: 10, of which 7 were waited for; matrix products, arithmetic and copies ran while one was open for 0% of the time, Pallas kernels for 16%

profile of v7, /device:TPU:0, one launch (start us, length us, event | category | flops | bytes accessed | tf_op | source)
XLA Modules:
  0.0 29.7 jit_solution(1008316406670676548)
XLA Ops:
  0.0 0.0 copy-start
  0.0 1.6 %masked.2 = bf16[2,128,256]{2,1,0:T(8,128)(2,1)} custom-call(s32[2]{0:T(128)} %lens.2, bf16[2,128,256]{2,1,0:T(8,128)(2,1)} %acts.2, bf16[2,128,256]{2,1,0:T(8,128)(2,1)} %grads.2), custom_call_target="tpu_custom_call" | custom-call | flops 1000000000 | bytes 1000000 | tf_op jit(solution)/shard_map/masked/pallas_call | solution.py:78
  1.6 4.0 %collective-permute-start = (bf16[2,128,256]{2,1,0:T(8,128)(2,1)}, bf16[2,128,256]{2,1,0:T(8,128)(2,1)S(1)}, u32[]{:S(2)}, u32[]{:S(2)}) collective-permute-start(bf16[2,128,256]{2,1,0:T(8,128)(2,1)} %masked.2), channel_id=1, source_target_pairs={{0,8},{1,9},{2,10},{3,11},{4,12},{5,13},{6,14},{7,15},{8,0},{9,1},... | collective-permute-start | bytes 393224 | tf_op jit(solution)/shard_map/ppermute | solution.py:230
  5.6 1.6 %masked.3.u0 = bf16[2,128,256]{2,1,0:T(8,128)(2,1)} custom-call(s32[2]{0:T(128)} %lens.2, bf16[2,128,256]{2,1,0:T(8,128)(2,1)} %acts.2, bf16[2,128,256]{2,1,0:T(8,128)(2,1)} %grads.2), custom_call_target="tpu_custom_call" | custom-call | flops 1000000000 | bytes 1000000 | tf_op jit(solution)/shard_map/masked/pallas_call | solution.py:78
  7.2 1.5 %collective-permute-start.1 = (bf16[2,128,256]{2,1,0:T(8,128)(2,1)}, bf16[2,128,256]{2,1,0:T(8,128)(2,1)S(1)}, u32[]{:S(2)}, u32[]{:S(2)}) collective-permute-start(bf16[2,128,256]{2,1,0:T(8,128)(2,1)} %masked.3.u0), channel_id=1, source_target_pairs={{0,2},{1,3},{2,0},{3,1},{4,6},{5,7},{6,4},{7,5},{8,10},{9,11},{10,... | collective-permute-start | bytes 393224 | tf_op jit(solution)/shard_map/ppermute | solution.py:230
  8.7 1.6 %collective-permute-start.2 = (bf16[2,128,256]{2,1,0:T(8,128)(2,1)}, bf16[2,128,256]{2,1,0:T(8,128)(2,1)S(1)}, u32[]{:S(2)}, u32[]{:S(2)}) collective-permute-start(bf16[2,128,256]{2,1,0:T(8,128)(2,1)} %masked.3.u0), channel_id=1, source_target_pairs={{0,4},{1,5},{2,7},{3,6},{4,0},{5,1},{6,3},{7,2},{8,12},{9,13},{10,... | collective-permute-start | bytes 393224 | tf_op jit(solution)/shard_map/ppermute | solution.py:230
  10.2 0.0 collective-permute-start.3
  10.2 0.0 copy-done
  10.2 0.0 copy-done.1
  10.3 0.0 copy-start.2
  10.3 1.7 %factor_terms.1 = (bf16[2,3,256,256]{3,2,1,0:T(8,128)(2,1)S(1)}, bf16[1024,32]{1,0:T(8,128)(2,1)S(1)}) custom-call(s32[2]{0:T(128)S(1)} %copy-done, s32[1,32]{1,0:T(1,128)S(1)} %bitcast.1, f32[16,256,256]{2,1,0:T(8,128)} %act_f.1, f32[16,256,256]{2,1,0:T(8,128)} %grad_f.1), custom_call_target="tpu_custom_call" | custom-call | flops 1000000000 | bytes 1000000 | tf_op jit(solution)/shard_map/factor_terms/pallas_call | solution.py:210
  11.9 0.3 collective-permute-done.v
  12.2 1.5 %collective-permute-start.4 = (bf16[2,128,256]{2,1,0:T(8,128)(2,1)S(1)}, bf16[2,128,256]{2,1,0:T(8,128)(2,1)S(1)}, u32[]{:S(2)}, u32[]{:S(2)}) collective-permute-start(bf16[2,128,256]{2,1,0:T(8,128)(2,1)S(1)} %collective-permute-done.v), channel_id=1, source_target_pairs={{0,2},{1,3},{2,0},{3,1},{4,6},{5,7},{6,4},{7,5},{8,10},{9,11},{10,... | collective-permute-start | bytes 393224 | tf_op jit(solution)/shard_map/ppermute | solution.py:230
  13.8 0.7 %collective-permute-start.5 = (bf16[2,128,256]{2,1,0:T(8,128)(2,1)S(1)}, bf16[2,128,256]{2,1,0:T(8,128)(2,1)S(1)}, u32[]{:S(2)}, u32[]{:S(2)}) collective-permute-start(bf16[2,128,256]{2,1,0:T(8,128)(2,1)S(1)} %collective-permute-done.v), channel_id=1, source_target_pairs={{0,4},{1,5},{2,7},{3,6},{4,0},{5,1},{6,3},{7,2},{8,12},{9,13},{10,... | collective-permute-start | bytes 393224 | tf_op jit(solution)/shard_map/ppermute | solution.py:230
  14.5 0.0 collective-permute-done.1.u2
  14.5 0.0 collective-permute-start.6
  14.5 0.4 %collective-permute-done.2.u3 = bf16[2,128,256]{2,1,0:T(8,128)(2,1)S(1)} collective-permute-done((bf16[2,128,256]{2,1,0:T(8,128)(2,1)}, bf16[2,128,256]{2,1,0:T(8,128)(2,1)S(1)}, u32[]{:S(2)}, u32[]{:S(2)}) %collective-permute-start.2) | collective-permute-done | bytes 131104 | tf_op jit(solution)/shard_map/ppermute | solution.py:230
  14.9 0.0 collective-permute-done.3.u1
  14.9 0.0 copy-done.2
  14.9 1.0 %early_pairs.1 = (bf16[2,512,256]{2,1,0:T(8,128)(2,1)S(1)}, f32[12,1024]{1,0:T(8,128)S(1)}) custom-call(bf16[2,3,256,256]{3,2,1,0:T(8,128)(2,1)S(1)} %get-tuple-element.19.terms, bf16[2,128,256]{2,1,0:T(8,128)(2,1)S(1)} %copy-done.2, bf16[2,128,256]{2,1,0:T(8,128)(2,1)S(1)} %collective-permute-done.v, bf16[2,128,256]{2,1,0:T(8,128)(2,1)S(1)} %collective-permute-done.1.u2, ...), custom_call_target="tpu_custom_call" | custom-call | flops 1000000000 | bytes 1000000 | tf_op jit(solution)/shard_map/early_pairs/pallas_call | solution.py:210
  15.9 2.0 %collective-permute-done.4.v2 = bf16[2,128,256]{2,1,0:T(8,128)(2,1)S(1)} collective-permute-done((bf16[2,128,256]{2,1,0:T(8,128)(2,1)S(1)}, bf16[2,128,256]{2,1,0:T(8,128)(2,1)S(1)}, u32[]{:S(2)}, u32[]{:S(2)}) %collective-permute-start.4) | collective-permute-done | bytes 131104 | tf_op jit(solution)/shard_map/ppermute | solution.py:230
  17.9 0.8 %collective-permute-done.5.v3 = bf16[2,128,256]{2,1,0:T(8,128)(2,1)S(1)} collective-permute-done((bf16[2,128,256]{2,1,0:T(8,128)(2,1)S(1)}, bf16[2,128,256]{2,1,0:T(8,128)(2,1)S(1)}, u32[]{:S(2)}, u32[]{:S(2)}) %collective-permute-start.5) | collective-permute-done | bytes 131104 | tf_op jit(solution)/shard_map/ppermute | solution.py:230
  18.7 0.0 collective-permute-done.6.v1
  18.8 1.0 %return_rows.1 = (f32[4,32]{1,0:T(4,128)S(1)}, f32[4,32]{1,0:T(4,128)S(1)}) custom-call(bf16[2,3,256,256]{3,2,1,0:T(8,128)(2,1)S(1)} %get-tuple-element.19.terms, bf16[2,512,256]{2,1,0:T(8,128)(2,1)S(1)} %get-tuple-element.24.white, bf16[1024,32]{1,0:T(8,128)(2,1)S(1)} %get-tuple-element.25.pick, f32[12,1024]{1,0:T(8,128)S(1)} %get-tuple-element.26.sums, ...), custom_call_target="tpu_custom_call" | custom-call | flops 1000000000 | bytes 1000000 | tf_op jit(solution)/shard_map/return_rows/pallas_call | solution.py:210
  19.7 0.9 %collective-permute-start.8 = (f32[4,32]{1,0:T(4,128)S(1)}, f32[4,32]{1,0:T(4,128)S(1)}, u32[]{:S(2)}, u32[]{:S(2)}) collective-permute-start(f32[4,32]{1,0:T(4,128)S(1)} %get-tuple-element.28), channel_id=1, source_target_pairs={{0,4},{1,5},{2,7},{3,6},{4,0},{5,1},{6,3},{7,2},{8,12},{9,13},{10,... | collective-permute-start | bytes 1544 | tf_op jit(solution)/shard_map/ppermute | solution.py:230
  20.6 0.7 %collective-permute-start.7 = (f32[4,32]{1,0:T(4,128)S(1)}, f32[4,32]{1,0:T(4,128)S(1)}, u32[]{:S(2)}, u32[]{:S(2)}) collective-permute-start(f32[4,32]{1,0:T(4,128)S(1)} %get-tuple-element.27), channel_id=1, source_target_pairs={{0,2},{1,3},{2,0},{3,1},{4,6},{5,7},{6,4},{7,5},{8,10},{9,11},{10,... | collective-permute-start | bytes 1544 | tf_op jit(solution)/shard_map/ppermute | solution.py:230
  21.4 0.5 %own_rows.1 = f32[4,32]{1,0:T(4,128)S(1)} custom-call(bf16[2,512,256]{2,1,0:T(8,128)(2,1)S(1)} %get-tuple-element.24.white, bf16[1024,32]{1,0:T(8,128)(2,1)S(1)} %get-tuple-element.25.pick, f32[12,1024]{1,0:T(8,128)S(1)} %get-tuple-element.26.sums, bf16[2,128,256]{2,1,0:T(8,128)(2,1)S(1)} %collective-permute-done.4.v2, ...), custom_call_target="tpu_custom_call" | custom-call | flops 1000000000 | bytes 1000000 | tf_op jit(solution)/shard_map/own_rows/pallas_call | solution.py:210
  21.9 1.5 %collective-permute-done.8 = f32[4,32]{1,0:T(4,128)S(1)} collective-permute-done((f32[4,32]{1,0:T(4,128)S(1)}, f32[4,32]{1,0:T(4,128)S(1)}, u32[]{:S(2)}, u32[]{:S(2)}) %collective-permute-start.8) | collective-permute-done | bytes 544 | tf_op jit(solution)/shard_map/ppermute | solution.py:230
  23.3 0.9 %collective-permute-done.7 = f32[4,32]{1,0:T(4,128)S(1)} collective-permute-done((f32[4,32]{1,0:T(4,128)S(1)}, f32[4,32]{1,0:T(4,128)S(1)}, u32[]{:S(2)}, u32[]{:S(2)}) %collective-permute-start.7) | collective-permute-done | bytes 544 | tf_op jit(solution)/shard_map/ppermute | solution.py:230
  24.2 3.3 %collective-permute-start.9 = (f32[2,32]{1,0:T(2,128)S(1)}, f32[2,32]{1,0:T(2,128)S(1)}, u32[]{:S(2)}, u32[]{:S(2)}) collective-permute-start(f32[2,32]{1,0:T(2,128)S(1)} %slice.7), channel_id=1, source_target_pairs={{0,8},{1,9},{2,10},{3,11},{4,12},{5,13},{6,14},{7,15},{8,0},{9,1},... | collective-permute-start | bytes 776 | tf_op jit(solution)/shard_map/ppermute | solution.py:230
  27.6 1.5 %collective-permute-done.9 = f32[2,32]{1,0:T(2,128)S(1)} collective-permute-done((f32[2,32]{1,0:T(2,128)S(1)}, f32[2,32]{1,0:T(2,128)S(1)}, u32[]{:S(2)}, u32[]{:S(2)}) %collective-permute-start.9) | collective-permute-done | bytes 288 | tf_op jit(solution)/shard_map/ppermute | solution.py:230
  29.1 0.6 %slice_add_fusion = f32[2,32]{1,0:T(2,128)} fusion(f32[2,32]{1,0:T(2,128)S(1)} %collective-permute-done.9, f32[4,32]{1,0:T(4,128)S(1)} %add_add_fusion), kind=kLoop, calls=%fused_computation.1 | loop fusion | flops 64 | bytes 768 | tf_op jit(solution)/shard_map/add | solution.py:288
  (3 shorter events, 0.0 us)
Async XLA Ops:
  0.0 10.2 %copy-start = (s32[2]{0:T(128)S(1)}, s32[2]{0:T(128)}, u32[]{:S(2)}) copy-start(s32[2]{0:T(128)} %layer_ids.1) | copy-start | bytes 28
  0.0 10.2 %copy-start.1 = (s32[32]{0:T(128)S(1)}, s32[32]{0:T(128)}, u32[]{:S(2)}) copy-start(s32[32]{0:T(128)} %param.11) | copy-start | bytes 388
  1.6 10.7 %collective-permute-start = (bf16[2,128,256]{2,1,0:T(8,128)(2,1)}, bf16[2,128,256]{2,1,0:T(8,128)(2,1)S(1)}, u32[]{:S(2)}, u32[]{:S(2)}) collective-permute-start(bf16[2,128,256]{2,1,0:T(8,128)(2,1)} %masked.2), channel_id=1, source_target_pairs={{0,8},{1,9},{2,10},{3,11},{4,12},{5,13},{6,14},{7,15},{8,0},{9,1},... | collective-permute-start | bytes 393224 | tf_op jit(solution)/shard_map/ppermute | solution.py:230
  7.2 7.3 %collective-permute-start.1 = (bf16[2,128,256]{2,1,0:T(8,128)(2,1)}, bf16[2,128,256]{2,1,0:T(8,128)(2,1)S(1)}, u32[]{:S(2)}, u32[]{:S(2)}) collective-permute-start(bf16[2,128,256]{2,1,0:T(8,128)(2,1)} %masked.3.u0), channel_id=1, source_target_pairs={{0,2},{1,3},{2,0},{3,1},{4,6},{5,7},{6,4},{7,5},{8,10},{9,11},{10,... | collective-permute-start | bytes 393224 | tf_op jit(solution)/shard_map/ppermute | solution.py:230
  8.7 6.3 %collective-permute-start.2 = (bf16[2,128,256]{2,1,0:T(8,128)(2,1)}, bf16[2,128,256]{2,1,0:T(8,128)(2,1)S(1)}, u32[]{:S(2)}, u32[]{:S(2)}) collective-permute-start(bf16[2,128,256]{2,1,0:T(8,128)(2,1)} %masked.3.u0), channel_id=1, source_target_pairs={{0,4},{1,5},{2,7},{3,6},{4,0},{5,1},{6,3},{7,2},{8,12},{9,13},{10,... | collective-permute-start | bytes 393224 | tf_op jit(solution)/shard_map/ppermute | solution.py:230
  10.2 4.7 %collective-permute-start.3 = (bf16[2,128,256]{2,1,0:T(8,128)(2,1)}, bf16[2,128,256]{2,1,0:T(8,128)(2,1)S(1)}, u32[]{:S(2)}, u32[]{:S(2)}) collective-permute-start(bf16[2,128,256]{2,1,0:T(8,128)(2,1)} %masked.3.u0), channel_id=1, source_target_pairs={{0,1},{1,0},{2,3},{3,2},{4,5},{5,4},{6,7},{7,6},{8,9},{9,8},{10,11... | collective-permute-start | bytes 393224 | tf_op jit(solution)/shard_map/ppermute | solution.py:230
  10.3 4.7 %copy-start.2 = (bf16[2,128,256]{2,1,0:T(8,128)(2,1)S(1)}, bf16[2,128,256]{2,1,0:T(8,128)(2,1)}, u32[]{:S(2)}) copy-start(bf16[2,128,256]{2,1,0:T(8,128)(2,1)} %masked.3.u0) | copy-start | bytes 393220
  12.2 5.7 %collective-permute-start.4 = (bf16[2,128,256]{2,1,0:T(8,128)(2,1)S(1)}, bf16[2,128,256]{2,1,0:T(8,128)(2,1)S(1)}, u32[]{:S(2)}, u32[]{:S(2)}) collective-permute-start(bf16[2,128,256]{2,1,0:T(8,128)(2,1)S(1)} %collective-permute-done.v), channel_id=1, source_target_pairs={{0,2},{1,3},{2,0},{3,1},{4,6},{5,7},{6,4},{7,5},{8,10},{9,11},{10,... | collective-permute-start | bytes 393224 | tf_op jit(solution)/shard_map/ppermute | solution.py:230
  13.8 5.0 %collective-permute-start.5 = (bf16[2,128,256]{2,1,0:T(8,128)(2,1)S(1)}, bf16[2,128,256]{2,1,0:T(8,128)(2,1)S(1)}, u32[]{:S(2)}, u32[]{:S(2)}) collective-permute-start(bf16[2,128,256]{2,1,0:T(8,128)(2,1)S(1)} %collective-permute-done.v), channel_id=1, source_target_pairs={{0,4},{1,5},{2,7},{3,6},{4,0},{5,1},{6,3},{7,2},{8,12},{9,13},{10,... | collective-permute-start | bytes 393224 | tf_op jit(solution)/shard_map/ppermute | solution.py:230
  14.5 4.2 %collective-permute-start.6 = (bf16[2,128,256]{2,1,0:T(8,128)(2,1)S(1)}, bf16[2,128,256]{2,1,0:T(8,128)(2,1)S(1)}, u32[]{:S(2)}, u32[]{:S(2)}) collective-permute-start(bf16[2,128,256]{2,1,0:T(8,128)(2,1)S(1)} %collective-permute-done.v), channel_id=1, source_target_pairs={{0,1},{1,0},{2,3},{3,2},{4,5},{5,4},{6,7},{7,6},{8,9},{9,8},{10,11... | collective-permute-start | bytes 393224 | tf_op jit(solution)/shard_map/ppermute | solution.py:230
  19.7 3.6 %collective-permute-start.8 = (f32[4,32]{1,0:T(4,128)S(1)}, f32[4,32]{1,0:T(4,128)S(1)}, u32[]{:S(2)}, u32[]{:S(2)}) collective-permute-start(f32[4,32]{1,0:T(4,128)S(1)} %get-tuple-element.28), channel_id=1, source_target_pairs={{0,4},{1,5},{2,7},{3,6},{4,0},{5,1},{6,3},{7,2},{8,12},{9,13},{10,... | collective-permute-start | bytes 1544 | tf_op jit(solution)/shard_map/ppermute | solution.py:230
  20.6 3.6 %collective-permute-start.7 = (f32[4,32]{1,0:T(4,128)S(1)}, f32[4,32]{1,0:T(4,128)S(1)}, u32[]{:S(2)}, u32[]{:S(2)}) collective-permute-start(f32[4,32]{1,0:T(4,128)S(1)} %get-tuple-element.27), channel_id=1, source_target_pairs={{0,2},{1,3},{2,0},{3,1},{4,6},{5,7},{6,4},{7,5},{8,10},{9,11},{10,... | collective-permute-start | bytes 1544 | tf_op jit(solution)/shard_map/ppermute | solution.py:230
  24.2 4.9 %collective-permute-start.9 = (f32[2,32]{1,0:T(2,128)S(1)}, f32[2,32]{1,0:T(2,128)S(1)}, u32[]{:S(2)}, u32[]{:S(2)}) collective-permute-start(f32[2,32]{1,0:T(2,128)S(1)} %slice.7), channel_id=1, source_target_pairs={{0,8},{1,9},{2,10},{3,11},{4,12},{5,13},{6,14},{7,15},{8,0},{9,1},... | collective-permute-start | bytes 776 | tf_op jit(solution)/shard_map/ppermute | solution.py:230

commit v8 on v6

--- a/solution.py
+++ b/solution.py
@@ -61,10 +61,11 @@
     row = lax.broadcasted_iota(jnp.int32, (tokens, 1), 0)
     bound = jnp.zeros_like(row)
     for s in range(tokens // seq_len):
-        bound = jnp.where(row // seq_len == s, lens[s] + s * seq_len, bound)
+        bound = jnp.where(row // seq_len == s, lens[0:1, s : s + 1] + s * seq_len, bound)
+    keep = jnp.broadcast_to(row < bound, acts.shape[1:])
     for w, src in enumerate((acts, grads)):
         x = src[0]
-        out[w] = jnp.where(row < bound, x, jnp.zeros_like(x))
+        out[w] = jnp.where(keep, x, jnp.zeros_like(x))
 
 
 def masked(activations, out_grads, lengths, seq_len, kept):
@@ -79,12 +80,12 @@
         functools.partial(mask_kernel, seq_len),
         grid=(1,),
         out_shape=jax.ShapeDtypeStruct((2, tokens, rank), activations.dtype),
-        in_specs=[pl.BlockSpec(memory_space=pltpu.SMEM), data, data],
+        in_specs=[pl.BlockSpec((1, lengths.shape[0]), lambda i: (0, 0)), data, data],
         out_specs=pl.BlockSpec((2, tokens, rank), lambda i: (0, 0, 0)),
         compiler_params=pltpu.CompilerParams(vmem_limit_bytes=59 * 1024 * 1024),
         cost_estimate=pl.CostEstimate(flops=10**9, bytes_accessed=10**6, transcendentals=0),
         name="masked",
-    )(lengths, activations, out_grads)
+    )(lengths.reshape(1, -1), activations, out_grads)
 
 
 def whiten(x, terms):

time: 29.5 us -> 29.6 us (level)
  waiting for transfers between devices: 7.92 us -> 7.52 us
    ppermute x10, waiting for transfers between devices: 7.92 us -> 7.52 us  [send(): return lax.ppermute(x, 'blk', [(d, to(d)) for d in range(size)])]
  transfers between devices with their start and end apart: 10 -> 10, of which waited for: 6 -> 7; matrix products, arithmetic and copies ran while one was open for 0% -> 0% of each run, Pallas kernels for 16% -> 17%
where the time goes in v8:
time: 29.6 us; the launch traced here: 29.4 us
  starting transfers between devices  13.7 us (46%)
  Pallas kernels  7.53 us (25%)
  waiting for transfers between devices  7.52 us (25%)
  other arithmetic  0.57 us (2%)
    ppermute x10, starting transfers between devices, send(): return lax.ppermute(x, 'blk', [(d, to(d)) for d in range(size)])  13.7 us
    ppermute x10, waiting for transfers between devices, send(): return lax.ppermute(x, 'blk', [(d, to(d)) for d in range(size)])  7.52 us
    pallas_call x4, Pallas kernels, call(): pl.pallas_call(kernel, out_shape=out_shape, in_specs=specs + [vmem] * (le...  4.13 us
    pallas_call x2, Pallas kernels, masked(): pl.pallas_call(functools.partial(mask_kernel, seq_len), grid=(1,), out_sh...  3.41 us
  transfers between devices with their start and end apart: 10, of which 7 were waited for; matrix products, arithmetic and copies ran while one was open for 0% of the time, Pallas kernels for 17%

profile of v8, /device:TPU:0, one launch (start us, length us, event | category | flops | bytes accessed | tf_op | source)
XLA Modules:
  0.0 29.4 jit_solution(15942169151937940259)
XLA Ops:
  0.0 0.0 copy-start
  0.0 0.0 copy-start.1
  0.0 1.7 %masked.2 = bf16[2,128,256]{2,1,0:T(8,128)(2,1)} custom-call(s32[1,2]{1,0:T(1,128)} %bitcast.4, bf16[2,128,256]{2,1,0:T(8,128)(2,1)} %acts.2, bf16[2,128,256]{2,1,0:T(8,128)(2,1)} %grads.2), custom_call_target="tpu_custom_call" | custom-call | flops 1000000000 | bytes 1000000 | tf_op jit(solution)/shard_map/masked/pallas_call | solution.py:79
  1.7 4.0 %collective-permute-start = (bf16[2,128,256]{2,1,0:T(8,128)(2,1)}, bf16[2,128,256]{2,1,0:T(8,128)(2,1)S(1)}, u32[]{:S(2)}, u32[]{:S(2)}) collective-permute-start(bf16[2,128,256]{2,1,0:T(8,128)(2,1)} %masked.2), channel_id=1, source_target_pairs={{0,8},{1,9},{2,10},{3,11},{4,12},{5,13},{6,14},{7,15},{8,0},{9,1},... | collective-permute-start | bytes 393224 | tf_op jit(solution)/shard_map/ppermute | solution.py:231
  5.8 1.7 %masked.3.u0 = bf16[2,128,256]{2,1,0:T(8,128)(2,1)} custom-call(s32[1,2]{1,0:T(1,128)} %bitcast.5, bf16[2,128,256]{2,1,0:T(8,128)(2,1)} %acts.2, bf16[2,128,256]{2,1,0:T(8,128)(2,1)} %grads.2), custom_call_target="tpu_custom_call" | custom-call | flops 1000000000 | bytes 1000000 | tf_op jit(solution)/shard_map/masked/pallas_call | solution.py:79
  7.5 1.6 %collective-permute-start.1 = (bf16[2,128,256]{2,1,0:T(8,128)(2,1)}, bf16[2,128,256]{2,1,0:T(8,128)(2,1)S(1)}, u32[]{:S(2)}, u32[]{:S(2)}) collective-permute-start(bf16[2,128,256]{2,1,0:T(8,128)(2,1)} %masked.3.u0), channel_id=1, source_target_pairs={{0,4},{1,5},{2,7},{3,6},{4,0},{5,1},{6,3},{7,2},{8,12},{9,13},{10,... | collective-permute-start | bytes 393224 | tf_op jit(solution)/shard_map/ppermute | solution.py:231
  9.0 0.7 %collective-permute-start.2 = (bf16[2,128,256]{2,1,0:T(8,128)(2,1)}, bf16[2,128,256]{2,1,0:T(8,128)(2,1)S(1)}, u32[]{:S(2)}, u32[]{:S(2)}) collective-permute-start(bf16[2,128,256]{2,1,0:T(8,128)(2,1)} %masked.3.u0), channel_id=1, source_target_pairs={{0,2},{1,3},{2,0},{3,1},{4,6},{5,7},{6,4},{7,5},{8,10},{9,11},{10,... | collective-permute-start | bytes 393224 | tf_op jit(solution)/shard_map/ppermute | solution.py:231
  9.7 0.7 %collective-permute-start.3 = (bf16[2,128,256]{2,1,0:T(8,128)(2,1)}, bf16[2,128,256]{2,1,0:T(8,128)(2,1)S(1)}, u32[]{:S(2)}, u32[]{:S(2)}) collective-permute-start(bf16[2,128,256]{2,1,0:T(8,128)(2,1)} %masked.3.u0), channel_id=1, source_target_pairs={{0,1},{1,0},{2,3},{3,2},{4,5},{5,4},{6,7},{7,6},{8,9},{9,8},{10,11... | collective-permute-start | bytes 393224 | tf_op jit(solution)/shard_map/ppermute | solution.py:231
  10.4 0.0 copy-done
  10.4 0.0 copy-done.1
  10.4 1.7 %factor_terms.1 = (bf16[2,3,256,256]{3,2,1,0:T(8,128)(2,1)S(1)}, bf16[1024,32]{1,0:T(8,128)(2,1)S(1)}) custom-call(s32[2]{0:T(128)S(1)} %copy-done, s32[1,32]{1,0:T(1,128)S(1)} %bitcast.3, f32[16,256,256]{2,1,0:T(8,128)} %act_f.1, f32[16,256,256]{2,1,0:T(8,128)} %grad_f.1), custom_call_target="tpu_custom_call" | custom-call | flops 1000000000 | bytes 1000000 | tf_op jit(solution)/shard_map/factor_terms/pallas_call | solution.py:211
  12.0 0.3 %collective-permute-done.v = bf16[2,128,256]{2,1,0:T(8,128)(2,1)S(1)} collective-permute-done((bf16[2,128,256]{2,1,0:T(8,128)(2,1)}, bf16[2,128,256]{2,1,0:T(8,128)(2,1)S(1)}, u32[]{:S(2)}, u32[]{:S(2)}) %collective-permute-start) | collective-permute-done | bytes 131104 | tf_op jit(solution)/shard_map/ppermute | solution.py:231
  12.4 0.8 %collective-permute-start.4 = (bf16[2,128,256]{2,1,0:T(8,128)(2,1)S(1)}, bf16[2,128,256]{2,1,0:T(8,128)(2,1)S(1)}, u32[]{:S(2)}, u32[]{:S(2)}) collective-permute-start(bf16[2,128,256]{2,1,0:T(8,128)(2,1)S(1)} %collective-permute-done.v), channel_id=1, source_target_pairs={{0,4},{1,5},{2,7},{3,6},{4,0},{5,1},{6,3},{7,2},{8,12},{9,13},{10,... | collective-permute-start | bytes 393224 | tf_op jit(solution)/shard_map/ppermute | solution.py:231
  13.1 1.1 %collective-permute-start.5 = (bf16[2,128,256]{2,1,0:T(8,128)(2,1)S(1)}, bf16[2,128,256]{2,1,0:T(8,128)(2,1)S(1)}, u32[]{:S(2)}, u32[]{:S(2)}) collective-permute-start(bf16[2,128,256]{2,1,0:T(8,128)(2,1)S(1)} %collective-permute-done.v), channel_id=1, source_target_pairs={{0,2},{1,3},{2,0},{3,1},{4,6},{5,7},{6,4},{7,5},{8,10},{9,11},{10,... | collective-permute-start | bytes 393224 | tf_op jit(solution)/shard_map/ppermute | solution.py:231
  14.3 0.0 collective-permute-done.1.u3
  14.3 0.2 collective-permute-start.6
  14.5 0.1 collective-permute-done.2.u2
  14.5 0.0 collective-permute-done.3.u1
  14.5 0.0 copy-done.2
  14.5 1.0 %early_pairs.1 = (bf16[2,512,256]{2,1,0:T(8,128)(2,1)S(1)}, f32[12,1024]{1,0:T(8,128)S(1)}) custom-call(bf16[2,3,256,256]{3,2,1,0:T(8,128)(2,1)S(1)} %get-tuple-element.19.terms, bf16[2,128,256]{2,1,0:T(8,128)(2,1)S(1)} %copy-done.2, bf16[2,128,256]{2,1,0:T(8,128)(2,1)S(1)} %collective-permute-done.v, bf16[2,128,256]{2,1,0:T(8,128)(2,1)S(1)} %collective-permute-done.1.u3, ...), custom_call_target="tpu_custom_call" | custom-call | flops 1000000000 | bytes 1000000 | tf_op jit(solution)/shard_map/early_pairs/pallas_call | solution.py:211
  15.5 2.0 %collective-permute-done.4.v3 = bf16[2,128,256]{2,1,0:T(8,128)(2,1)S(1)} collective-permute-done((bf16[2,128,256]{2,1,0:T(8,128)(2,1)S(1)}, bf16[2,128,256]{2,1,0:T(8,128)(2,1)S(1)}, u32[]{:S(2)}, u32[]{:S(2)}) %collective-permute-start.4) | collective-permute-done | bytes 131104 | tf_op jit(solution)/shard_map/ppermute | solution.py:231
  17.5 0.9 %collective-permute-done.5.v2 = bf16[2,128,256]{2,1,0:T(8,128)(2,1)S(1)} collective-permute-done((bf16[2,128,256]{2,1,0:T(8,128)(2,1)S(1)}, bf16[2,128,256]{2,1,0:T(8,128)(2,1)S(1)}, u32[]{:S(2)}, u32[]{:S(2)}) %collective-permute-start.5) | collective-permute-done | bytes 131104 | tf_op jit(solution)/shard_map/ppermute | solution.py:231
  18.4 0.0 collective-permute-done.6.v1
  18.4 1.0 %return_rows.1 = (f32[4,32]{1,0:T(4,128)S(1)}, f32[4,32]{1,0:T(4,128)S(1)}) custom-call(bf16[2,3,256,256]{3,2,1,0:T(8,128)(2,1)S(1)} %get-tuple-element.19.terms, bf16[2,512,256]{2,1,0:T(8,128)(2,1)S(1)} %get-tuple-element.24.white, bf16[1024,32]{1,0:T(8,128)(2,1)S(1)} %get-tuple-element.25.pick, f32[12,1024]{1,0:T(8,128)S(1)} %get-tuple-element.26.sums, ...), custom_call_target="tpu_custom_call" | custom-call | flops 1000000000 | bytes 1000000 | tf_op jit(solution)/shard_map/return_rows/pallas_call | solution.py:211
  19.4 1.3 %collective-permute-start.8 = (f32[4,32]{1,0:T(4,128)S(1)}, f32[4,32]{1,0:T(4,128)S(1)}, u32[]{:S(2)}, u32[]{:S(2)}) collective-permute-start(f32[4,32]{1,0:T(4,128)S(1)} %get-tuple-element.28), channel_id=1, source_target_pairs={{0,4},{1,5},{2,7},{3,6},{4,0},{5,1},{6,3},{7,2},{8,12},{9,13},{10,... | collective-permute-start | bytes 1544 | tf_op jit(solution)/shard_map/ppermute | solution.py:231
  20.7 1.2 %collective-permute-start.7 = (f32[4,32]{1,0:T(4,128)S(1)}, f32[4,32]{1,0:T(4,128)S(1)}, u32[]{:S(2)}, u32[]{:S(2)}) collective-permute-start(f32[4,32]{1,0:T(4,128)S(1)} %get-tuple-element.27), channel_id=1, source_target_pairs={{0,2},{1,3},{2,0},{3,1},{4,6},{5,7},{6,4},{7,5},{8,10},{9,11},{10,... | collective-permute-start | bytes 1544 | tf_op jit(solution)/shard_map/ppermute | solution.py:231
  21.9 0.5 %own_rows.1 = f32[4,32]{1,0:T(4,128)S(1)} custom-call(bf16[2,512,256]{2,1,0:T(8,128)(2,1)S(1)} %get-tuple-element.24.white, bf16[1024,32]{1,0:T(8,128)(2,1)S(1)} %get-tuple-element.25.pick, f32[12,1024]{1,0:T(8,128)S(1)} %get-tuple-element.26.sums, bf16[2,128,256]{2,1,0:T(8,128)(2,1)S(1)} %collective-permute-done.4.v3, ...), custom_call_target="tpu_custom_call" | custom-call | flops 1000000000 | bytes 1000000 | tf_op jit(solution)/shard_map/own_rows/pallas_call | solution.py:211
  22.4 0.6 %collective-permute-done.8 = f32[4,32]{1,0:T(4,128)S(1)} collective-permute-done((f32[4,32]{1,0:T(4,128)S(1)}, f32[4,32]{1,0:T(4,128)S(1)}, u32[]{:S(2)}, u32[]{:S(2)}) %collective-permute-start.8) | collective-permute-done | bytes 544 | tf_op jit(solution)/shard_map/ppermute | solution.py:231
  23.0 1.3 %collective-permute-done.7 = f32[4,32]{1,0:T(4,128)S(1)} collective-permute-done((f32[4,32]{1,0:T(4,128)S(1)}, f32[4,32]{1,0:T(4,128)S(1)}, u32[]{:S(2)}, u32[]{:S(2)}) %collective-permute-start.7) | collective-permute-done | bytes 544 | tf_op jit(solution)/shard_map/ppermute | solution.py:231
  24.3 2.2 %collective-permute-start.9 = (f32[2,32]{1,0:T(2,128)S(1)}, f32[2,32]{1,0:T(2,128)S(1)}, u32[]{:S(2)}, u32[]{:S(2)}) collective-permute-start(f32[2,32]{1,0:T(2,128)S(1)} %slice.7), channel_id=1, source_target_pairs={{0,8},{1,9},{2,10},{3,11},{4,12},{5,13},{6,14},{7,15},{8,0},{9,1},... | collective-permute-start | bytes 776 | tf_op jit(solution)/shard_map/ppermute | solution.py:231
  26.5 2.3 %collective-permute-done.9 = f32[2,32]{1,0:T(2,128)S(1)} collective-permute-done((f32[2,32]{1,0:T(2,128)S(1)}, f32[2,32]{1,0:T(2,128)S(1)}, u32[]{:S(2)}, u32[]{:S(2)}) %collective-permute-start.9) | collective-permute-done | bytes 288 | tf_op jit(solution)/shard_map/ppermute | solution.py:231
  28.8 0.6 %slice_add_fusion = f32[2,32]{1,0:T(2,128)} fusion(f32[2,32]{1,0:T(2,128)S(1)} %collective-permute-done.9, f32[4,32]{1,0:T(4,128)S(1)} %add_add_fusion), kind=kLoop, calls=%fused_computation.1 | loop fusion | flops 64 | bytes 768 | tf_op jit(solution)/shard_map/add | solution.py:289
  (3 shorter events, 0.0 us)
Async XLA Ops:
  0.0 10.4 %copy-start = (s32[2]{0:T(128)S(1)}, s32[2]{0:T(128)}, u32[]{:S(2)}) copy-start(s32[2]{0:T(128)} %layer_ids.1) | copy-start | bytes 28
  0.0 10.4 %copy-start.1 = (s32[32]{0:T(128)S(1)}, s32[32]{0:T(128)}, u32[]{:S(2)}) copy-start(s32[32]{0:T(128)} %param.11) | copy-start | bytes 388
  1.7 10.7 %collective-permute-start = (bf16[2,128,256]{2,1,0:T(8,128)(2,1)}, bf16[2,128,256]{2,1,0:T(8,128)(2,1)S(1)}, u32[]{:S(2)}, u32[]{:S(2)}) collective-permute-start(bf16[2,128,256]{2,1,0:T(8,128)(2,1)} %masked.2), channel_id=1, source_target_pairs={{0,8},{1,9},{2,10},{3,11},{4,12},{5,13},{6,14},{7,15},{8,0},{9,1},... | collective-permute-start | bytes 393224 | tf_op jit(solution)/shard_map/ppermute | solution.py:231
  7.5 6.8 %collective-permute-start.1 = (bf16[2,128,256]{2,1,0:T(8,128)(2,1)}, bf16[2,128,256]{2,1,0:T(8,128)(2,1)S(1)}, u32[]{:S(2)}, u32[]{:S(2)}) collective-permute-start(bf16[2,128,256]{2,1,0:T(8,128)(2,1)} %masked.3.u0), channel_id=1, source_target_pairs={{0,4},{1,5},{2,7},{3,6},{4,0},{5,1},{6,3},{7,2},{8,12},{9,13},{10,... | collective-permute-start | bytes 393224 | tf_op jit(solution)/shard_map/ppermute | solution.py:231
  9.0 5.5 %collective-permute-start.2 = (bf16[2,128,256]{2,1,0:T(8,128)(2,1)}, bf16[2,128,256]{2,1,0:T(8,128)(2,1)S(1)}, u32[]{:S(2)}, u32[]{:S(2)}) collective-permute-start(bf16[2,128,256]{2,1,0:T(8,128)(2,1)} %masked.3.u0), channel_id=1, source_target_pairs={{0,2},{1,3},{2,0},{3,1},{4,6},{5,7},{6,4},{7,5},{8,10},{9,11},{10,... | collective-permute-start | bytes 393224 | tf_op jit(solution)/shard_map/ppermute | solution.py:231
  9.7 4.9 %collective-permute-start.3 = (bf16[2,128,256]{2,1,0:T(8,128)(2,1)}, bf16[2,128,256]{2,1,0:T(8,128)(2,1)S(1)}, u32[]{:S(2)}, u32[]{:S(2)}) collective-permute-start(bf16[2,128,256]{2,1,0:T(8,128)(2,1)} %masked.3.u0), channel_id=1, source_target_pairs={{0,1},{1,0},{2,3},{3,2},{4,5},{5,4},{6,7},{7,6},{8,9},{9,8},{10,11... | collective-permute-start | bytes 393224 | tf_op jit(solution)/shard_map/ppermute | solution.py:231
  10.4 4.2 %copy-start.2 = (bf16[2,128,256]{2,1,0:T(8,128)(2,1)S(1)}, bf16[2,128,256]{2,1,0:T(8,128)(2,1)}, u32[]{:S(2)}) copy-start(bf16[2,128,256]{2,1,0:T(8,128)(2,1)} %masked.3.u0) | copy-start | bytes 393220
  12.4 5.2 %collective-permute-start.4 = (bf16[2,128,256]{2,1,0:T(8,128)(2,1)S(1)}, bf16[2,128,256]{2,1,0:T(8,128)(2,1)S(1)}, u32[]{:S(2)}, u32[]{:S(2)}) collective-permute-start(bf16[2,128,256]{2,1,0:T(8,128)(2,1)S(1)} %collective-permute-done.v), channel_id=1, source_target_pairs={{0,4},{1,5},{2,7},{3,6},{4,0},{5,1},{6,3},{7,2},{8,12},{9,13},{10,... | collective-permute-start | bytes 393224 | tf_op jit(solution)/shard_map/ppermute | solution.py:231
  13.1 5.3 %collective-permute-start.5 = (bf16[2,128,256]{2,1,0:T(8,128)(2,1)S(1)}, bf16[2,128,256]{2,1,0:T(8,128)(2,1)S(1)}, u32[]{:S(2)}, u32[]{:S(2)}) collective-permute-start(bf16[2,128,256]{2,1,0:T(8,128)(2,1)S(1)} %collective-permute-done.v), channel_id=1, source_target_pairs={{0,2},{1,3},{2,0},{3,1},{4,6},{5,7},{6,4},{7,5},{8,10},{9,11},{10,... | collective-permute-start | bytes 393224 | tf_op jit(solution)/shard_map/ppermute | solution.py:231
  14.3 4.2 %collective-permute-start.6 = (bf16[2,128,256]{2,1,0:T(8,128)(2,1)S(1)}, bf16[2,128,256]{2,1,0:T(8,128)(2,1)S(1)}, u32[]{:S(2)}, u32[]{:S(2)}) collective-permute-start(bf16[2,128,256]{2,1,0:T(8,128)(2,1)S(1)} %collective-permute-done.v), channel_id=1, source_target_pairs={{0,1},{1,0},{2,3},{3,2},{4,5},{5,4},{6,7},{7,6},{8,9},{9,8},{10,11... | collective-permute-start | bytes 393224 | tf_op jit(solution)/shard_map/ppermute | solution.py:231
  19.4 3.6 %collective-permute-start.8 = (f32[4,32]{1,0:T(4,128)S(1)}, f32[4,32]{1,0:T(4,128)S(1)}, u32[]{:S(2)}, u32[]{:S(2)}) collective-permute-start(f32[4,32]{1,0:T(4,128)S(1)} %get-tuple-element.28), channel_id=1, source_target_pairs={{0,4},{1,5},{2,7},{3,6},{4,0},{5,1},{6,3},{7,2},{8,12},{9,13},{10,... | collective-permute-start | bytes 1544 | tf_op jit(solution)/shard_map/ppermute | solution.py:231
  20.7 3.6 %collective-permute-start.7 = (f32[4,32]{1,0:T(4,128)S(1)}, f32[4,32]{1,0:T(4,128)S(1)}, u32[]{:S(2)}, u32[]{:S(2)}) collective-permute-start(f32[4,32]{1,0:T(4,128)S(1)} %get-tuple-element.27), channel_id=1, source_target_pairs={{0,2},{1,3},{2,0},{3,1},{4,6},{5,7},{6,4},{7,5},{8,10},{9,11},{10,... | collective-permute-start | bytes 1544 | tf_op jit(solution)/shard_map/ppermute | solution.py:231
  24.3 4.5 %collective-permute-start.9 = (f32[2,32]{1,0:T(2,128)S(1)}, f32[2,32]{1,0:T(2,128)S(1)}, u32[]{:S(2)}, u32[]{:S(2)}) collective-permute-start(f32[2,32]{1,0:T(2,128)S(1)} %slice.7), channel_id=1, source_target_pairs={{0,8},{1,9},{2,10},{3,11},{4,12},{5,13},{6,14},{7,15},{8,0},{9,1},... | collective-permute-start | bytes 776 | tf_op jit(solution)/shard_map/ppermute | solution.py:231

commit v9 on v6

--- a/solution.py
+++ b/solution.py
@@ -56,32 +56,38 @@
     return d ^ 4 ^ ((d >> 1) & 1)
 
 
-def mask_kernel(seq_len, lens, acts, grads, out):
+def mask_kernel(seq_len, kept, lens, acts, grads, out, held, sems):
+    half = lax.axis_index("blk") // 8
+    layer = half if kept else 1 - half
+    copies = [
+        pltpu.make_async_copy(src, dst, sems.at[i])
+        for i, (src, dst) in enumerate(
+            ((lens, held), (acts.at[layer], out.at[0]), (grads.at[layer], out.at[1]))
+        )
+    ]
+    for copy in copies:
+        copy.start()
+    for copy in copies:
+        copy.wait()
     tokens = acts.shape[1]
     row = lax.broadcasted_iota(jnp.int32, (tokens, 1), 0)
     bound = jnp.zeros_like(row)
     for s in range(tokens // seq_len):
-        bound = jnp.where(row // seq_len == s, lens[s] + s * seq_len, bound)
-    for w, src in enumerate((acts, grads)):
-        x = src[0]
-        out[w] = jnp.where(row < bound, x, jnp.zeros_like(x))
-
-
-def masked(activations, out_grads, lengths, seq_len, kept):
+        bound = jnp.where(row // seq_len == s, held[s] + s * seq_len, bound)
+    x = out[0]
+    out[0] = jnp.where(row < bound, x, jnp.zeros_like(x))
+
+
+def masked(activations, out_grads, lengths, seq_len, kept, limit):
     tokens, rank = activations.shape[1:]
-
-    def layer(i):
-        half = lax.axis_index("blk") // 8
-        return (half if kept else 1 - half, 0, 0)
-
-    data = pl.BlockSpec((1, tokens, rank), layer)
+    hbm = pl.BlockSpec(memory_space=pltpu.HBM)
     return pl.pallas_call(
-        functools.partial(mask_kernel, seq_len),
-        grid=(1,),
+        functools.partial(mask_kernel, seq_len, kept),
         out_shape=jax.ShapeDtypeStruct((2, tokens, rank), activations.dtype),
-        in_specs=[pl.BlockSpec(memory_space=pltpu.SMEM), data, data],
-        out_specs=pl.BlockSpec((2, tokens, rank), lambda i: (0, 0, 0)),
-        compiler_params=pltpu.CompilerParams(vmem_limit_bytes=59 * 1024 * 1024),
+        in_specs=[hbm, hbm, hbm],
+        out_specs=pl.BlockSpec(memory_space=pltpu.VMEM),
+        scratch_shapes=[pltpu.SMEM(lengths.shape, jnp.int32), pltpu.SemaphoreType.DMA((3,))],
+        compiler_params=pltpu.CompilerParams(vmem_limit_bytes=limit),
         cost_estimate=pl.CostEstimate(flops=10**9, bytes_accessed=10**6, transcendentals=0),
         name="masked",
     )(lengths, activations, out_grads)
@@ -234,10 +240,10 @@
 
     ways = (z_near, lambda d: d ^ 2, lambda d: d ^ 1)
     data = (activations, out_grads, lengths)
-    away = masked(*data, seq_len, False)
+    away = masked(*data, seq_len, False, 59 * 1024 * 1024)
     v = send(away, opposite)
     away, *data = lax.optimization_barrier((away, *data))
-    own = masked(*data, seq_len, True)
+    own = masked(*data, seq_len, True, 59 * 1024 * 1024)
     near = [send(own, to) for to in ways]
 
     shape = jax.ShapeDtypeStruct

time: 29.5 us -> 29.6 us (level)
  starting transfers between devices: 13.5 us -> 13.8 us
where the time goes in v9:
time: 29.6 us; the launch traced here: 29.4 us
  starting transfers between devices  13.8 us (47%)
  waiting for transfers between devices  7.69 us (26%)
  Pallas kernels  7.28 us (25%)
  other arithmetic  0.57 us (2%)
    ppermute x10, starting transfers between devices, send(): return lax.ppermute(x, 'blk', [(d, to(d)) for d in range(size)])  13.8 us
    ppermute x10, waiting for transfers between devices, send(): return lax.ppermute(x, 'blk', [(d, to(d)) for d in range(size)])  7.69 us
    pallas_call x4, Pallas kernels, call(): pl.pallas_call(kernel, out_shape=out_shape, in_specs=specs + [vmem] * (le...  4.12 us
    pallas_call x2, Pallas kernels, masked(): pl.pallas_call(functools.partial(mask_kernel, seq_len, kept), out_shape=j...  3.15 us
  transfers between devices with their start and end apart: 10, of which 6 were waited for; matrix products, arithmetic and copies ran while one was open for 0% of the time, Pallas kernels for 16%

profile of v9, /device:TPU:0, one launch (start us, length us, event | category | flops | bytes accessed | tf_op | source)
XLA Modules:
  0.0 29.4 jit_solution(292895177610472453)
XLA Ops:
  0.0 0.0 copy-start
  0.0 0.0 copy-start.1
  0.0 1.6 %masked.2 = bf16[2,128,256]{2,1,0:T(8,128)(2,1)} custom-call(s32[2]{0:T(128)} %lens.2, bf16[2,128,256]{2,1,0:T(8,128)(2,1)} %acts.2, bf16[2,128,256]{2,1,0:T(8,128)(2,1)} %grads.2), custom_call_target="tpu_custom_call" | custom-call | flops 1000000000 | bytes 1000000 | tf_op jit(solution)/shard_map/masked/pallas_call | solution.py:84
  1.6 4.1 %collective-permute-start = (bf16[2,128,256]{2,1,0:T(8,128)(2,1)}, bf16[2,128,256]{2,1,0:T(8,128)(2,1)S(1)}, u32[]{:S(2)}, u32[]{:S(2)}) collective-permute-start(bf16[2,128,256]{2,1,0:T(8,128)(2,1)} %masked.2), channel_id=1, source_target_pairs={{0,8},{1,9},{2,10},{3,11},{4,12},{5,13},{6,14},{7,15},{8,0},{9,1},... | collective-permute-start | bytes 393224 | tf_op jit(solution)/shard_map/ppermute | solution.py:236
  5.7 1.6 %masked.3.u0 = bf16[2,128,256]{2,1,0:T(8,128)(2,1)} custom-call(s32[2]{0:T(128)} %lens.2, bf16[2,128,256]{2,1,0:T(8,128)(2,1)} %acts.2, bf16[2,128,256]{2,1,0:T(8,128)(2,1)} %grads.2), custom_call_target="tpu_custom_call" | custom-call | flops 1000000000 | bytes 1000000 | tf_op jit(solution)/shard_map/masked/pallas_call | solution.py:84
  7.3 1.6 %collective-permute-start.1 = (bf16[2,128,256]{2,1,0:T(8,128)(2,1)}, bf16[2,128,256]{2,1,0:T(8,128)(2,1)S(1)}, u32[]{:S(2)}, u32[]{:S(2)}) collective-permute-start(bf16[2,128,256]{2,1,0:T(8,128)(2,1)} %masked.3.u0), channel_id=1, source_target_pairs={{0,4},{1,5},{2,7},{3,6},{4,0},{5,1},{6,3},{7,2},{8,12},{9,13},{10,... | collective-permute-start | bytes 393224 | tf_op jit(solution)/shard_map/ppermute | solution.py:236
  8.9 0.7 %collective-permute-start.2 = (bf16[2,128,256]{2,1,0:T(8,128)(2,1)}, bf16[2,128,256]{2,1,0:T(8,128)(2,1)S(1)}, u32[]{:S(2)}, u32[]{:S(2)}) collective-permute-start(bf16[2,128,256]{2,1,0:T(8,128)(2,1)} %masked.3.u0), channel_id=1, source_target_pairs={{0,2},{1,3},{2,0},{3,1},{4,6},{5,7},{6,4},{7,5},{8,10},{9,11},{10,... | collective-permute-start | bytes 393224 | tf_op jit(solution)/shard_map/ppermute | solution.py:236
  9.6 0.7 %collective-permute-start.3 = (bf16[2,128,256]{2,1,0:T(8,128)(2,1)}, bf16[2,128,256]{2,1,0:T(8,128)(2,1)S(1)}, u32[]{:S(2)}, u32[]{:S(2)}) collective-permute-start(bf16[2,128,256]{2,1,0:T(8,128)(2,1)} %masked.3.u0), channel_id=1, source_target_pairs={{0,1},{1,0},{2,3},{3,2},{4,5},{5,4},{6,7},{7,6},{8,9},{9,8},{10,11... | collective-permute-start | bytes 393224 | tf_op jit(solution)/shard_map/ppermute | solution.py:236
  10.2 0.0 copy-done
  10.2 0.0 copy-done.1
  10.3 1.7 %factor_terms.1 = (bf16[2,3,256,256]{3,2,1,0:T(8,128)(2,1)S(1)}, bf16[1024,32]{1,0:T(8,128)(2,1)S(1)}) custom-call(s32[2]{0:T(128)S(1)} %copy-done, s32[1,32]{1,0:T(1,128)S(1)} %bitcast.1, f32[16,256,256]{2,1,0:T(8,128)} %act_f.1, f32[16,256,256]{2,1,0:T(8,128)} %grad_f.1), custom_call_target="tpu_custom_call" | custom-call | flops 1000000000 | bytes 1000000 | tf_op jit(solution)/shard_map/factor_terms/pallas_call | solution.py:216
  11.9 0.4 %collective-permute-done.v = bf16[2,128,256]{2,1,0:T(8,128)(2,1)S(1)} collective-permute-done((bf16[2,128,256]{2,1,0:T(8,128)(2,1)}, bf16[2,128,256]{2,1,0:T(8,128)(2,1)S(1)}, u32[]{:S(2)}, u32[]{:S(2)}) %collective-permute-start) | collective-permute-done | bytes 131104 | tf_op jit(solution)/shard_map/ppermute | solution.py:236
  12.3 0.8 %collective-permute-start.4 = (bf16[2,128,256]{2,1,0:T(8,128)(2,1)S(1)}, bf16[2,128,256]{2,1,0:T(8,128)(2,1)S(1)}, u32[]{:S(2)}, u32[]{:S(2)}) collective-permute-start(bf16[2,128,256]{2,1,0:T(8,128)(2,1)S(1)} %collective-permute-done.v), channel_id=1, source_target_pairs={{0,4},{1,5},{2,7},{3,6},{4,0},{5,1},{6,3},{7,2},{8,12},{9,13},{10,... | collective-permute-start | bytes 393224 | tf_op jit(solution)/shard_map/ppermute | solution.py:236
  13.1 1.1 %collective-permute-start.5 = (bf16[2,128,256]{2,1,0:T(8,128)(2,1)S(1)}, bf16[2,128,256]{2,1,0:T(8,128)(2,1)S(1)}, u32[]{:S(2)}, u32[]{:S(2)}) collective-permute-start(bf16[2,128,256]{2,1,0:T(8,128)(2,1)S(1)} %collective-permute-done.v), channel_id=1, source_target_pairs={{0,2},{1,3},{2,0},{3,1},{4,6},{5,7},{6,4},{7,5},{8,10},{9,11},{10,... | collective-permute-start | bytes 393224 | tf_op jit(solution)/shard_map/ppermute | solution.py:236
  14.2 0.0 collective-permute-done.1.u3
  14.2 0.2 collective-permute-start.6
  14.4 0.0 collective-permute-done.2.u2
  14.4 0.0 collective-permute-done.3.u1
  14.4 0.0 copy-done.2
  14.4 1.0 %early_pairs.1 = (bf16[2,512,256]{2,1,0:T(8,128)(2,1)S(1)}, f32[12,1024]{1,0:T(8,128)S(1)}) custom-call(bf16[2,3,256,256]{3,2,1,0:T(8,128)(2,1)S(1)} %get-tuple-element.19.terms, bf16[2,128,256]{2,1,0:T(8,128)(2,1)S(1)} %copy-done.2, bf16[2,128,256]{2,1,0:T(8,128)(2,1)S(1)} %collective-permute-done.v, bf16[2,128,256]{2,1,0:T(8,128)(2,1)S(1)} %collective-permute-done.1.u3, ...), custom_call_target="tpu_custom_call" | custom-call | flops 1000000000 | bytes 1000000 | tf_op jit(solution)/shard_map/early_pairs/pallas_call | solution.py:216
  15.4 2.0 %collective-permute-done.4.v3 = bf16[2,128,256]{2,1,0:T(8,128)(2,1)S(1)} collective-permute-done((bf16[2,128,256]{2,1,0:T(8,128)(2,1)S(1)}, bf16[2,128,256]{2,1,0:T(8,128)(2,1)S(1)}, u32[]{:S(2)}, u32[]{:S(2)}) %collective-permute-start.4) | collective-permute-done | bytes 131104 | tf_op jit(solution)/shard_map/ppermute | solution.py:236
  17.4 0.9 %collective-permute-done.5.v2 = bf16[2,128,256]{2,1,0:T(8,128)(2,1)S(1)} collective-permute-done((bf16[2,128,256]{2,1,0:T(8,128)(2,1)S(1)}, bf16[2,128,256]{2,1,0:T(8,128)(2,1)S(1)}, u32[]{:S(2)}, u32[]{:S(2)}) %collective-permute-start.5) | collective-permute-done | bytes 131104 | tf_op jit(solution)/shard_map/ppermute | solution.py:236
  18.4 0.0 collective-permute-done.6.v1
  18.4 1.0 %return_rows.1 = (f32[4,32]{1,0:T(4,128)S(1)}, f32[4,32]{1,0:T(4,128)S(1)}) custom-call(bf16[2,3,256,256]{3,2,1,0:T(8,128)(2,1)S(1)} %get-tuple-element.19.terms, bf16[2,512,256]{2,1,0:T(8,128)(2,1)S(1)} %get-tuple-element.24.white, bf16[1024,32]{1,0:T(8,128)(2,1)S(1)} %get-tuple-element.25.pick, f32[12,1024]{1,0:T(8,128)S(1)} %get-tuple-element.26.sums, ...), custom_call_target="tpu_custom_call" | custom-call | flops 1000000000 | bytes 1000000 | tf_op jit(solution)/shard_map/return_rows/pallas_call | solution.py:216
  19.3 1.3 %collective-permute-start.8 = (f32[4,32]{1,0:T(4,128)S(1)}, f32[4,32]{1,0:T(4,128)S(1)}, u32[]{:S(2)}, u32[]{:S(2)}) collective-permute-start(f32[4,32]{1,0:T(4,128)S(1)} %get-tuple-element.28), channel_id=1, source_target_pairs={{0,4},{1,5},{2,7},{3,6},{4,0},{5,1},{6,3},{7,2},{8,12},{9,13},{10,... | collective-permute-start | bytes 1544 | tf_op jit(solution)/shard_map/ppermute | solution.py:236
  20.7 1.1 %collective-permute-start.7 = (f32[4,32]{1,0:T(4,128)S(1)}, f32[4,32]{1,0:T(4,128)S(1)}, u32[]{:S(2)}, u32[]{:S(2)}) collective-permute-start(f32[4,32]{1,0:T(4,128)S(1)} %get-tuple-element.27), channel_id=1, source_target_pairs={{0,2},{1,3},{2,0},{3,1},{4,6},{5,7},{6,4},{7,5},{8,10},{9,11},{10,... | collective-permute-start | bytes 1544 | tf_op jit(solution)/shard_map/ppermute | solution.py:236
  21.8 0.5 %own_rows.1 = f32[4,32]{1,0:T(4,128)S(1)} custom-call(bf16[2,512,256]{2,1,0:T(8,128)(2,1)S(1)} %get-tuple-element.24.white, bf16[1024,32]{1,0:T(8,128)(2,1)S(1)} %get-tuple-element.25.pick, f32[12,1024]{1,0:T(8,128)S(1)} %get-tuple-element.26.sums, bf16[2,128,256]{2,1,0:T(8,128)(2,1)S(1)} %collective-permute-done.4.v3, ...), custom_call_target="tpu_custom_call" | custom-call | flops 1000000000 | bytes 1000000 | tf_op jit(solution)/shard_map/own_rows/pallas_call | solution.py:216
  22.2 0.7 %collective-permute-done.8 = f32[4,32]{1,0:T(4,128)S(1)} collective-permute-done((f32[4,32]{1,0:T(4,128)S(1)}, f32[4,32]{1,0:T(4,128)S(1)}, u32[]{:S(2)}, u32[]{:S(2)}) %collective-permute-start.8) | collective-permute-done | bytes 544 | tf_op jit(solution)/shard_map/ppermute | solution.py:236
  23.0 1.3 %collective-permute-done.7 = f32[4,32]{1,0:T(4,128)S(1)} collective-permute-done((f32[4,32]{1,0:T(4,128)S(1)}, f32[4,32]{1,0:T(4,128)S(1)}, u32[]{:S(2)}, u32[]{:S(2)}) %collective-permute-start.7) | collective-permute-done | bytes 544 | tf_op jit(solution)/shard_map/ppermute | solution.py:236
  24.3 2.2 %collective-permute-start.9 = (f32[2,32]{1,0:T(2,128)S(1)}, f32[2,32]{1,0:T(2,128)S(1)}, u32[]{:S(2)}, u32[]{:S(2)}) collective-permute-start(f32[2,32]{1,0:T(2,128)S(1)} %slice.7), channel_id=1, source_target_pairs={{0,8},{1,9},{2,10},{3,11},{4,12},{5,13},{6,14},{7,15},{8,0},{9,1},... | collective-permute-start | bytes 776 | tf_op jit(solution)/shard_map/ppermute | solution.py:236
  26.4 2.3 %collective-permute-done.9 = f32[2,32]{1,0:T(2,128)S(1)} collective-permute-done((f32[2,32]{1,0:T(2,128)S(1)}, f32[2,32]{1,0:T(2,128)S(1)}, u32[]{:S(2)}, u32[]{:S(2)}) %collective-permute-start.9) | collective-permute-done | bytes 288 | tf_op jit(solution)/shard_map/ppermute | solution.py:236
  28.8 0.6 %slice_add_fusion = f32[2,32]{1,0:T(2,128)} fusion(f32[2,32]{1,0:T(2,128)S(1)} %collective-permute-done.9, f32[4,32]{1,0:T(4,128)S(1)} %add_add_fusion), kind=kLoop, calls=%fused_computation.1 | loop fusion | flops 64 | bytes 768 | tf_op jit(solution)/shard_map/add | solution.py:294
  (3 shorter events, 0.0 us)
Async XLA Ops:
  0.0 10.2 %copy-start = (s32[2]{0:T(128)S(1)}, s32[2]{0:T(128)}, u32[]{:S(2)}) copy-start(s32[2]{0:T(128)} %layer_ids.1) | copy-start | bytes 28
  0.0 10.2 %copy-start.1 = (s32[32]{0:T(128)S(1)}, s32[32]{0:T(128)}, u32[]{:S(2)}) copy-start(s32[32]{0:T(128)} %param.11) | copy-start | bytes 388
  1.6 10.7 %collective-permute-start = (bf16[2,128,256]{2,1,0:T(8,128)(2,1)}, bf16[2,128,256]{2,1,0:T(8,128)(2,1)S(1)}, u32[]{:S(2)}, u32[]{:S(2)}) collective-permute-start(bf16[2,128,256]{2,1,0:T(8,128)(2,1)} %masked.2), channel_id=1, source_target_pairs={{0,8},{1,9},{2,10},{3,11},{4,12},{5,13},{6,14},{7,15},{8,0},{9,1},... | collective-permute-start | bytes 393224 | tf_op jit(solution)/shard_map/ppermute | solution.py:236
  7.3 6.9 %collective-permute-start.1 = (bf16[2,128,256]{2,1,0:T(8,128)(2,1)}, bf16[2,128,256]{2,1,0:T(8,128)(2,1)S(1)}, u32[]{:S(2)}, u32[]{:S(2)}) collective-permute-start(bf16[2,128,256]{2,1,0:T(8,128)(2,1)} %masked.3.u0), channel_id=1, source_target_pairs={{0,4},{1,5},{2,7},{3,6},{4,0},{5,1},{6,3},{7,2},{8,12},{9,13},{10,... | collective-permute-start | bytes 393224 | tf_op jit(solution)/shard_map/ppermute | solution.py:236
  8.9 5.5 %collective-permute-start.2 = (bf16[2,128,256]{2,1,0:T(8,128)(2,1)}, bf16[2,128,256]{2,1,0:T(8,128)(2,1)S(1)}, u32[]{:S(2)}, u32[]{:S(2)}) collective-permute-start(bf16[2,128,256]{2,1,0:T(8,128)(2,1)} %masked.3.u0), channel_id=1, source_target_pairs={{0,2},{1,3},{2,0},{3,1},{4,6},{5,7},{6,4},{7,5},{8,10},{9,11},{10,... | collective-permute-start | bytes 393224 | tf_op jit(solution)/shard_map/ppermute | solution.py:236
  9.6 4.9 %collective-permute-start.3 = (bf16[2,128,256]{2,1,0:T(8,128)(2,1)}, bf16[2,128,256]{2,1,0:T(8,128)(2,1)S(1)}, u32[]{:S(2)}, u32[]{:S(2)}) collective-permute-start(bf16[2,128,256]{2,1,0:T(8,128)(2,1)} %masked.3.u0), channel_id=1, source_target_pairs={{0,1},{1,0},{2,3},{3,2},{4,5},{5,4},{6,7},{7,6},{8,9},{9,8},{10,11... | collective-permute-start | bytes 393224 | tf_op jit(solution)/shard_map/ppermute | solution.py:236
  10.3 4.2 %copy-start.2 = (bf16[2,128,256]{2,1,0:T(8,128)(2,1)S(1)}, bf16[2,128,256]{2,1,0:T(8,128)(2,1)}, u32[]{:S(2)}) copy-start(bf16[2,128,256]{2,1,0:T(8,128)(2,1)} %masked.3.u0) | copy-start | bytes 393220
  12.3 5.1 %collective-permute-start.4 = (bf16[2,128,256]{2,1,0:T(8,128)(2,1)S(1)}, bf16[2,128,256]{2,1,0:T(8,128)(2,1)S(1)}, u32[]{:S(2)}, u32[]{:S(2)}) collective-permute-start(bf16[2,128,256]{2,1,0:T(8,128)(2,1)S(1)} %collective-permute-done.v), channel_id=1, source_target_pairs={{0,4},{1,5},{2,7},{3,6},{4,0},{5,1},{6,3},{7,2},{8,12},{9,13},{10,... | collective-permute-start | bytes 393224 | tf_op jit(solution)/shard_map/ppermute | solution.py:236
  13.1 5.3 %collective-permute-start.5 = (bf16[2,128,256]{2,1,0:T(8,128)(2,1)S(1)}, bf16[2,128,256]{2,1,0:T(8,128)(2,1)S(1)}, u32[]{:S(2)}, u32[]{:S(2)}) collective-permute-start(bf16[2,128,256]{2,1,0:T(8,128)(2,1)S(1)} %collective-permute-done.v), channel_id=1, source_target_pairs={{0,2},{1,3},{2,0},{3,1},{4,6},{5,7},{6,4},{7,5},{8,10},{9,11},{10,... | collective-permute-start | bytes 393224 | tf_op jit(solution)/shard_map/ppermute | solution.py:236
  14.2 4.2 %collective-permute-start.6 = (bf16[2,128,256]{2,1,0:T(8,128)(2,1)S(1)}, bf16[2,128,256]{2,1,0:T(8,128)(2,1)S(1)}, u32[]{:S(2)}, u32[]{:S(2)}) collective-permute-start(bf16[2,128,256]{2,1,0:T(8,128)(2,1)S(1)} %collective-permute-done.v), channel_id=1, source_target_pairs={{0,1},{1,0},{2,3},{3,2},{4,5},{5,4},{6,7},{7,6},{8,9},{9,8},{10,11... | collective-permute-start | bytes 393224 | tf_op jit(solution)/shard_map/ppermute | solution.py:236
  19.3 3.6 %collective-permute-start.8 = (f32[4,32]{1,0:T(4,128)S(1)}, f32[4,32]{1,0:T(4,128)S(1)}, u32[]{:S(2)}, u32[]{:S(2)}) collective-permute-start(f32[4,32]{1,0:T(4,128)S(1)} %get-tuple-element.28), channel_id=1, source_target_pairs={{0,4},{1,5},{2,7},{3,6},{4,0},{5,1},{6,3},{7,2},{8,12},{9,13},{10,... | collective-permute-start | bytes 1544 | tf_op jit(solution)/shard_map/ppermute | solution.py:236
  20.7 3.6 %collective-permute-start.7 = (f32[4,32]{1,0:T(4,128)S(1)}, f32[4,32]{1,0:T(4,128)S(1)}, u32[]{:S(2)}, u32[]{:S(2)}) collective-permute-start(f32[4,32]{1,0:T(4,128)S(1)} %get-tuple-element.27), channel_id=1, source_target_pairs={{0,2},{1,3},{2,0},{3,1},{4,6},{5,7},{6,4},{7,5},{8,10},{9,11},{10,... | collective-permute-start | bytes 1544 | tf_op jit(solution)/shard_map/ppermute | solution.py:236
  24.3 4.5 %collective-permute-start.9 = (f32[2,32]{1,0:T(2,128)S(1)}, f32[2,32]{1,0:T(2,128)S(1)}, u32[]{:S(2)}, u32[]{:S(2)}) collective-permute-start(f32[2,32]{1,0:T(2,128)S(1)} %slice.7), channel_id=1, source_target_pairs={{0,8},{1,9},{2,10},{3,11},{4,12},{5,13},{6,14},{7,15},{8,0},{9,1},... | collective-permute-start | bytes 776 | tf_op jit(solution)/shard_map/ppermute | solution.py:236

commit v10 on v9

--- a/solution.py
+++ b/solution.py
@@ -56,41 +56,39 @@
     return d ^ 4 ^ ((d >> 1) & 1)
 
 
-def mask_kernel(seq_len, kept, lens, acts, grads, out, held, sems):
-    half = lax.axis_index("blk") // 8
-    layer = half if kept else 1 - half
+def copy_layer(acts, grads, layer, out, sems):
     copies = [
-        pltpu.make_async_copy(src, dst, sems.at[i])
-        for i, (src, dst) in enumerate(
-            ((lens, held), (acts.at[layer], out.at[0]), (grads.at[layer], out.at[1]))
-        )
+        pltpu.make_async_copy(src.at[layer], out.at[i], sems.at[i])
+        for i, src in enumerate((acts, grads))
     ]
     for copy in copies:
         copy.start()
     for copy in copies:
         copy.wait()
-    tokens = acts.shape[1]
+
+
+def keep_slots(lens, tokens, seq_len):
     row = lax.broadcasted_iota(jnp.int32, (tokens, 1), 0)
     bound = jnp.zeros_like(row)
     for s in range(tokens // seq_len):
-        bound = jnp.where(row // seq_len == s, held[s] + s * seq_len, bound)
+        bound = jnp.where(row // seq_len == s, lens[0:1, s : s + 1] + s * seq_len, bound)
+    return row < bound
+
+
+def away_kernel(acts, grads, out, sems):
+    copy_layer(acts, grads, 1 - lax.axis_index("blk") // 8, out, sems)
+
+
+def own_kernel(seq_len, acts, grads, lens, out, sems):
+    copy_layer(acts, grads, lax.axis_index("blk") // 8, out, sems)
     x = out[0]
-    out[0] = jnp.where(row < bound, x, jnp.zeros_like(x))
-
-
-def masked(activations, out_grads, lengths, seq_len, kept, limit):
-    tokens, rank = activations.shape[1:]
-    hbm = pl.BlockSpec(memory_space=pltpu.HBM)
-    return pl.pallas_call(
-        functools.partial(mask_kernel, seq_len, kept),
-        out_shape=jax.ShapeDtypeStruct((2, tokens, rank), activations.dtype),
-        in_specs=[hbm, hbm, hbm],
-        out_specs=pl.BlockSpec(memory_space=pltpu.VMEM),
-        scratch_shapes=[pltpu.SMEM(lengths.shape, jnp.int32), pltpu.SemaphoreType.DMA((3,))],
-        compiler_params=pltpu.CompilerParams(vmem_limit_bytes=limit),
-        cost_estimate=pl.CostEstimate(flops=10**9, bytes_accessed=10**6, transcendentals=0),
-        name="masked",
-    )(lengths, activations, out_grads)
+    out[0] = jnp.where(keep_slots(lens, x.shape[0], seq_len), x, jnp.zeros_like(x))
+
+
+def far_kernel(seq_len, lens, v, out):
+    x = v[0]
+    out[0] = jnp.where(keep_slots(lens, x.shape[0], seq_len), x, jnp.zeros_like(x))
+    out[1] = v[1]
 
 
 def whiten(x, terms):
@@ -199,7 +197,7 @@
         out[...] = picked[i * r : (i + 1) * r]
 
 
-def own_kernel(seq_len, per, white, pick, sums, v3, v2, v1, out):
+def rows_kernel(seq_len, per, white, pick, sums, v3, v2, v1, out):
     v = (v1, v2, v3)
     n = v[0].shape[1]
     r = 2 * per
@@ -211,7 +209,7 @@
     out[...] = pick_columns(sums[:r, :] + jnp.concatenate(line, axis=1), pick)
 
 
-def call(kernel, name, flops, limit, operands, specs, out_shape, scratch=()):
+def call(kernel, name, flops, limit, operands, specs, out_shape, scratch=(), **more):
     vmem = pl.BlockSpec(memory_space=pltpu.VMEM)
     return pl.pallas_call(
         kernel,
@@ -219,9 +217,10 @@
         in_specs=specs + [vmem] * (len(operands) - len(specs)),
         out_specs=jax.tree.map(lambda _: vmem, out_shape),
         scratch_shapes=scratch,
-        compiler_params=pltpu.CompilerParams(vmem_limit_bytes=limit * 1024 * 1024),
+        compiler_params=pltpu.CompilerParams(vmem_limit_bytes=int(limit * 1024 * 1024)),
         cost_estimate=pl.CostEstimate(flops=flops, bytes_accessed=10**6, transcendentals=0),
         name=name,
+        **more,
     )(*operands)
 
 
@@ -239,17 +238,28 @@
         return d ^ 8
 
     ways = (z_near, lambda d: d ^ 2, lambda d: d ^ 1)
-    data = (activations, out_grads, lengths)
-    away = masked(*data, seq_len, False, 59 * 1024 * 1024)
-    v = send(away, opposite)
-    away, *data = lax.optimization_barrier((away, *data))
-    own = masked(*data, seq_len, True, 59 * 1024 * 1024)
-    near = [send(own, to) for to in ways]
-
+    hbm = pl.BlockSpec(memory_space=pltpu.HBM)
+    vmem = pl.BlockSpec(memory_space=pltpu.VMEM)
     shape = jax.ShapeDtypeStruct
     columns = flagged.shape[0]
-    hbm = pl.BlockSpec(memory_space=pltpu.HBM)
-    vmem = pl.BlockSpec(memory_space=pltpu.VMEM)
+    unit = shape((2, tokens, rank), bf16)
+    pair_of_copies = [pltpu.SemaphoreType.DMA((2,))]
+    data = (activations, out_grads)
+    away = call(away_kernel, "away", 10**9, 53.71, data, [hbm, hbm], unit, pair_of_copies)
+    v = send(away, opposite)
+    away, lens, *data = lax.optimization_barrier((away, lengths.reshape(1, -1), *data))
+    far_lens = send(lens, opposite)
+    own = call(
+        functools.partial(own_kernel, seq_len),
+        "own",
+        10**9,
+        59,
+        (*data, lens),
+        [hbm, hbm],
+        unit,
+        pair_of_copies,
+    )
+    near = [send(own, to) for to in ways]
     terms, pick = call(
         functools.partial(setup_kernel, seq_len, per),
         "factor_terms",
@@ -261,6 +271,16 @@
         [pltpu.VMEM((2, rank, rank), f32), pltpu.SemaphoreType.DMA((2,))],
     )
     v, terms, pick = lax.optimization_barrier((v, terms, pick))
+    v = call(
+        functools.partial(far_kernel, seq_len),
+        "far",
+        10**4,
+        40,
+        (far_lens, v),
+        [],
+        unit,
+        input_output_aliases={1: 0},
+    )
     late = [send(v, to) for to in ways]
     white, sums = call(
         functools.partial(early_kernel, seq_len, per),
@@ -282,7 +302,7 @@
         (rows, rows),
     )
     mine = call(
-        functools.partial(own_kernel, seq_len, per),
+        functools.partial(rows_kernel, seq_len, per),
         "own_rows",
         10**9,
         40,

time: 29.6 us -> 30.6 us (1.034)
  waiting for transfers between devices: 7.69 us -> 9.08 us
  starting transfers between devices: 13.8 us -> 13.1 us
    pallas_call x4 -> x7, Pallas kernels: 4.12 us -> 7.55 us  [call(): pl.pallas_call(kernel, out_shape=out_shape, in_specs=specs + [vmem] * (le...]
    pallas_call x2 -> x0, Pallas kernels: 3.15 us -> none  [masked(): pl.pallas_call(functools.partial(mask_kernel, seq_len, kept), out_shape=j...]
    ppermute x10 -> x11, waiting for transfers between devices: 7.69 us -> 9.08 us  [send(): return lax.ppermute(x, 'blk', [(d, to(d)) for d in range(size)])]
    ppermute x10 -> x11, starting transfers between devices: 13.8 us -> 13.1 us  [send(): return lax.ppermute(x, 'blk', [(d, to(d)) for d in range(size)])]
  transfers between devices with their start and end apart: 10 -> 11, of which waited for: 6 -> 6; matrix products, arithmetic and copies ran while one was open for 0% -> 0% of each run, Pallas kernels for 16% -> 19%
where the time goes in v10:
time: 30.6 us; the launch traced here: 30.4 us
  starting transfers between devices  13.1 us (43%)
  waiting for transfers between devices  9.08 us (30%)
  Pallas kernels  7.55 us (25%)
  other arithmetic  0.57 us (2%)
    ppermute x11, starting transfers between devices, send(): return lax.ppermute(x, 'blk', [(d, to(d)) for d in range(size)])  13.1 us
    ppermute x11, waiting for transfers between devices, send(): return lax.ppermute(x, 'blk', [(d, to(d)) for d in range(size)])  9.08 us
    pallas_call x7, Pallas kernels, call(): pl.pallas_call(kernel, out_shape=out_shape, in_specs=specs + [vmem] * (le...  7.55 us
  transfers between devices with their start and end apart: 11, of which 6 were waited for; matrix products, arithmetic and copies ran while one was open for 0% of the time, Pallas kernels for 19%

profile of v10, /device:TPU:0, one launch (start us, length us, event | category | flops | bytes accessed | tf_op | source)
XLA Modules:
  0.0 30.4 jit_solution(17611694269956824775)
XLA Ops:
  0.0 0.9 %away.1 = bf16[2,128,256]{2,1,0:T(8,128)(2,1)S(1)} custom-call(bf16[2,128,256]{2,1,0:T(8,128)(2,1)} %acts.2, bf16[2,128,256]{2,1,0:T(8,128)(2,1)} %grads.2), custom_call_target="tpu_custom_call" | custom-call | flops 1000000000 | bytes 1000000 | tf_op jit(solution)/shard_map/away/pallas_call | solution.py:214
  0.9 4.1 %collective-permute-start = (bf16[2,128,256]{2,1,0:T(8,128)(2,1)S(1)}, bf16[2,128,256]{2,1,0:T(8,128)(2,1)S(1)}, u32[]{:S(2)}, u32[]{:S(2)}) collective-permute-start(bf16[2,128,256]{2,1,0:T(8,128)(2,1)S(1)} %away.1), channel_id=1, source_target_pairs={{0,8},{1,9},{2,10},{3,11},{4,12},{5,13},{6,14},{7,15},{8,0},{9,1},... | collective-permute-start | bytes 393224 | tf_op jit(solution)/shard_map/ppermute | solution.py:235
  5.0 2.3 %own.1.u0 = bf16[2,128,256]{2,1,0:T(8,128)(2,1)} custom-call(bf16[2,128,256]{2,1,0:T(8,128)(2,1)} %acts.2, bf16[2,128,256]{2,1,0:T(8,128)(2,1)} %grads.2, s32[1,2]{1,0:T(1,128)} %bitcast.3), custom_call_target="tpu_custom_call" | custom-call | flops 1000000000 | bytes 1000000 | tf_op jit(solution)/shard_map/own/pallas_call | solution.py:214
  7.4 1.6 %collective-permute-start.2 = (bf16[2,128,256]{2,1,0:T(8,128)(2,1)}, bf16[2,128,256]{2,1,0:T(8,128)(2,1)S(1)}, u32[]{:S(2)}, u32[]{:S(2)}) collective-permute-start(bf16[2,128,256]{2,1,0:T(8,128)(2,1)} %own.1.u0), channel_id=1, source_target_pairs={{0,4},{1,5},{2,7},{3,6},{4,0},{5,1},{6,3},{7,2},{8,12},{9,13},{10,... | collective-permute-start | bytes 393224 | tf_op jit(solution)/shard_map/ppermute | solution.py:235
  9.0 0.0 copy-done.3
  9.0 0.3 %collective-permute-start.1 = (s32[1,2]{1,0:T(1,128)S(1)}, s32[1,2]{1,0:T(1,128)S(1)}, u32[]{:S(2)}, u32[]{:S(2)}) collective-permute-start(s32[1,2]{1,0:T(1,128)S(1)} %bitcast.4), channel_id=1, source_target_pairs={{0,8},{1,9},{2,10},{3,11},{4,12},{5,13},{6,14},{7,15},{8,0},{9,1},... | collective-permute-start | bytes 32 | tf_op jit(solution)/shard_map/ppermute | solution.py:235
  9.4 0.7 %collective-permute-start.3 = (bf16[2,128,256]{2,1,0:T(8,128)(2,1)}, bf16[2,128,256]{2,1,0:T(8,128)(2,1)S(1)}, u32[]{:S(2)}, u32[]{:S(2)}) collective-permute-start(bf16[2,128,256]{2,1,0:T(8,128)(2,1)} %own.1.u0), channel_id=1, source_target_pairs={{0,2},{1,3},{2,0},{3,1},{4,6},{5,7},{6,4},{7,5},{8,10},{9,11},{10,... | collective-permute-start | bytes 393224 | tf_op jit(solution)/shard_map/ppermute | solution.py:235
  10.0 0.4 %collective-permute-start.4 = (bf16[2,128,256]{2,1,0:T(8,128)(2,1)}, bf16[2,128,256]{2,1,0:T(8,128)(2,1)S(1)}, u32[]{:S(2)}, u32[]{:S(2)}) collective-permute-start(bf16[2,128,256]{2,1,0:T(8,128)(2,1)} %own.1.u0), channel_id=1, source_target_pairs={{0,1},{1,0},{2,3},{3,2},{4,5},{5,4},{6,7},{7,6},{8,9},{9,8},{10,11... | collective-permute-start | bytes 393224 | tf_op jit(solution)/shard_map/ppermute | solution.py:235
  10.4 0.0 copy-done
  10.4 1.7 %factor_terms.1 = (bf16[2,3,256,256]{3,2,1,0:T(8,128)(2,1)S(1)}, bf16[1024,32]{1,0:T(8,128)(2,1)S(1)}) custom-call(s32[2]{0:T(128)S(1)} %copy-done, s32[1,32]{1,0:T(1,128)S(1)} %bitcast.2, f32[16,256,256]{2,1,0:T(8,128)} %act_f.1, f32[16,256,256]{2,1,0:T(8,128)} %grad_f.1), custom_call_target="tpu_custom_call" | custom-call | flops 1000000000 | bytes 1000000 | tf_op jit(solution)/shard_map/factor_terms/pallas_call | solution.py:214
  12.1 0.0 collective-permute-done.v
  12.1 1.4 %collective-permute-done.1.lens = s32[1,2]{1,0:T(1,128)S(1)} collective-permute-done((s32[1,2]{1,0:T(1,128)S(1)}, s32[1,2]{1,0:T(1,128)S(1)}, u32[]{:S(2)}, u32[]{:S(2)}) %collective-permute-start.1) | collective-permute-done | bytes 40 | tf_op jit(solution)/shard_map/ppermute | solution.py:235
  13.5 0.2 far.1.v
  13.6 0.5 %collective-permute-start.5 = (bf16[2,128,256]{2,1,0:T(8,128)(2,1)S(1)}, bf16[2,128,256]{2,1,0:T(8,128)(2,1)S(1)}, u32[]{:S(2)}, u32[]{:S(2)}) collective-permute-start(bf16[2,128,256]{2,1,0:T(8,128)(2,1)S(1)} %far.1.v), channel_id=1, source_target_pairs={{0,4},{1,5},{2,7},{3,6},{4,0},{5,1},{6,3},{7,2},{8,12},{9,13},{10,... | collective-permute-start | bytes 393224 | tf_op jit(solution)/shard_map/ppermute | solution.py:235
  14.2 0.6 %collective-permute-start.6 = (bf16[2,128,256]{2,1,0:T(8,128)(2,1)S(1)}, bf16[2,128,256]{2,1,0:T(8,128)(2,1)S(1)}, u32[]{:S(2)}, u32[]{:S(2)}) collective-permute-start(bf16[2,128,256]{2,1,0:T(8,128)(2,1)S(1)} %far.1.v), channel_id=1, source_target_pairs={{0,2},{1,3},{2,0},{3,1},{4,6},{5,7},{6,4},{7,5},{8,10},{9,11},{10,... | collective-permute-start | bytes 393224 | tf_op jit(solution)/shard_map/ppermute | solution.py:235
  14.8 0.0 collective-permute-done.2.u3
  14.8 0.5 %collective-permute-start.7 = (bf16[2,128,256]{2,1,0:T(8,128)(2,1)S(1)}, bf16[2,128,256]{2,1,0:T(8,128)(2,1)S(1)}, u32[]{:S(2)}, u32[]{:S(2)}) collective-permute-start(bf16[2,128,256]{2,1,0:T(8,128)(2,1)S(1)} %far.1.v), channel_id=1, source_target_pairs={{0,1},{1,0},{2,3},{3,2},{4,5},{5,4},{6,7},{7,6},{8,9},{9,8},{10,11... | collective-permute-start | bytes 393224 | tf_op jit(solution)/shard_map/ppermute | solution.py:235
  15.3 0.0 collective-permute-done.3.u2
  15.3 0.0 collective-permute-done.4.u1
  15.4 1.0 %early_pairs.1 = (bf16[2,512,256]{2,1,0:T(8,128)(2,1)S(1)}, f32[12,1024]{1,0:T(8,128)S(1)}) custom-call(bf16[2,3,256,256]{3,2,1,0:T(8,128)(2,1)S(1)} %get-tuple-element.19.terms, bf16[2,128,256]{2,1,0:T(8,128)(2,1)S(1)} %copy-done.2, bf16[2,128,256]{2,1,0:T(8,128)(2,1)S(1)} %far.1.v, bf16[2,128,256]{2,1,0:T(8,128)(2,1)S(1)} %collective-permute-done.2.u3, ...), custom_call_target="tpu_custom_call" | custom-call | flops 1000000000 | bytes 1000000 | tf_op jit(solution)/shard_map/early_pairs/pallas_call | solution.py:214
  16.4 2.3 %collective-permute-done.5.v3 = bf16[2,128,256]{2,1,0:T(8,128)(2,1)S(1)} collective-permute-done((bf16[2,128,256]{2,1,0:T(8,128)(2,1)S(1)}, bf16[2,128,256]{2,1,0:T(8,128)(2,1)S(1)}, u32[]{:S(2)}, u32[]{:S(2)}) %collective-permute-start.5) | collective-permute-done | bytes 131104 | tf_op jit(solution)/shard_map/ppermute | solution.py:235
  18.7 0.6 %collective-permute-done.6.v2 = bf16[2,128,256]{2,1,0:T(8,128)(2,1)S(1)} collective-permute-done((bf16[2,128,256]{2,1,0:T(8,128)(2,1)S(1)}, bf16[2,128,256]{2,1,0:T(8,128)(2,1)S(1)}, u32[]{:S(2)}, u32[]{:S(2)}) %collective-permute-start.6) | collective-permute-done | bytes 131104 | tf_op jit(solution)/shard_map/ppermute | solution.py:235
  19.3 0.0 collective-permute-done.7.v1
  19.3 1.0 %return_rows.1 = (f32[4,32]{1,0:T(4,128)S(1)}, f32[4,32]{1,0:T(4,128)S(1)}) custom-call(bf16[2,3,256,256]{3,2,1,0:T(8,128)(2,1)S(1)} %get-tuple-element.19.terms, bf16[2,512,256]{2,1,0:T(8,128)(2,1)S(1)} %get-tuple-element.24.white, bf16[1024,32]{1,0:T(8,128)(2,1)S(1)} %get-tuple-element.25.pick, f32[12,1024]{1,0:T(8,128)S(1)} %get-tuple-element.26.sums, ...), custom_call_target="tpu_custom_call" | custom-call | flops 1000000000 | bytes 1000000 | tf_op jit(solution)/shard_map/return_rows/pallas_call | solution.py:214
  20.3 1.5 %collective-permute-start.9 = (f32[4,32]{1,0:T(4,128)S(1)}, f32[4,32]{1,0:T(4,128)S(1)}, u32[]{:S(2)}, u32[]{:S(2)}) collective-permute-start(f32[4,32]{1,0:T(4,128)S(1)} %get-tuple-element.28), channel_id=1, source_target_pairs={{0,4},{1,5},{2,7},{3,6},{4,0},{5,1},{6,3},{7,2},{8,12},{9,13},{10,... | collective-permute-start | bytes 1544 | tf_op jit(solution)/shard_map/ppermute | solution.py:235
  21.7 0.6 %collective-permute-start.8 = (f32[4,32]{1,0:T(4,128)S(1)}, f32[4,32]{1,0:T(4,128)S(1)}, u32[]{:S(2)}, u32[]{:S(2)}) collective-permute-start(f32[4,32]{1,0:T(4,128)S(1)} %get-tuple-element.27), channel_id=1, source_target_pairs={{0,2},{1,3},{2,0},{3,1},{4,6},{5,7},{6,4},{7,5},{8,10},{9,11},{10,... | collective-permute-start | bytes 1544 | tf_op jit(solution)/shard_map/ppermute | solution.py:235
  22.3 0.5 %own_rows.1 = f32[4,32]{1,0:T(4,128)S(1)} custom-call(bf16[2,512,256]{2,1,0:T(8,128)(2,1)S(1)} %get-tuple-element.24.white, bf16[1024,32]{1,0:T(8,128)(2,1)S(1)} %get-tuple-element.25.pick, f32[12,1024]{1,0:T(8,128)S(1)} %get-tuple-element.26.sums, bf16[2,128,256]{2,1,0:T(8,128)(2,1)S(1)} %collective-permute-done.5.v3, ...), custom_call_target="tpu_custom_call" | custom-call | flops 1000000000 | bytes 1000000 | tf_op jit(solution)/shard_map/own_rows/pallas_call | solution.py:214
  22.8 1.1 %collective-permute-done.9 = f32[4,32]{1,0:T(4,128)S(1)} collective-permute-done((f32[4,32]{1,0:T(4,128)S(1)}, f32[4,32]{1,0:T(4,128)S(1)}, u32[]{:S(2)}, u32[]{:S(2)}) %collective-permute-start.9) | collective-permute-done | bytes 544 | tf_op jit(solution)/shard_map/ppermute | solution.py:235
  23.9 1.4 %collective-permute-done.8 = f32[4,32]{1,0:T(4,128)S(1)} collective-permute-done((f32[4,32]{1,0:T(4,128)S(1)}, f32[4,32]{1,0:T(4,128)S(1)}, u32[]{:S(2)}, u32[]{:S(2)}) %collective-permute-start.8) | collective-permute-done | bytes 544 | tf_op jit(solution)/shard_map/ppermute | solution.py:235
  25.3 2.3 %collective-permute-start.10 = (f32[2,32]{1,0:T(2,128)S(1)}, f32[2,32]{1,0:T(2,128)S(1)}, u32[]{:S(2)}, u32[]{:S(2)}) collective-permute-start(f32[2,32]{1,0:T(2,128)S(1)} %slice.7), channel_id=1, source_target_pairs={{0,8},{1,9},{2,10},{3,11},{4,12},{5,13},{6,14},{7,15},{8,0},{9,1},... | collective-permute-start | bytes 776 | tf_op jit(solution)/shard_map/ppermute | solution.py:235
  27.6 2.3 %collective-permute-done.10 = f32[2,32]{1,0:T(2,128)S(1)} collective-permute-done((f32[2,32]{1,0:T(2,128)S(1)}, f32[2,32]{1,0:T(2,128)S(1)}, u32[]{:S(2)}, u32[]{:S(2)}) %collective-permute-start.10) | collective-permute-done | bytes 288 | tf_op jit(solution)/shard_map/ppermute | solution.py:235
  29.8 0.6 %slice_add_fusion = f32[2,32]{1,0:T(2,128)} fusion(f32[2,32]{1,0:T(2,128)S(1)} %collective-permute-done.10, f32[4,32]{1,0:T(4,128)S(1)} %add_add_fusion), kind=kLoop, calls=%fused_computation.1 | loop fusion | flops 64 | bytes 768 | tf_op jit(solution)/shard_map/add | solution.py:314
  (8 shorter events, 0.0 us)
Async XLA Ops:
  0.0 9.0 %copy-start.3 = (s32[2]{0:T(128)S(1)}, s32[2]{0:T(128)}, u32[]{:S(2)}) copy-start(s32[2]{0:T(128)} %param.9) | copy-start | bytes 28
  0.0 10.4 %copy-start = (s32[2]{0:T(128)S(1)}, s32[2]{0:T(128)}, u32[]{:S(2)}) copy-start(s32[2]{0:T(128)} %layer_ids.1) | copy-start | bytes 28
  0.0 10.4 %copy-start.1 = (s32[32]{0:T(128)S(1)}, s32[32]{0:T(128)}, u32[]{:S(2)}) copy-start(s32[32]{0:T(128)} %param.11) | copy-start | bytes 388
  0.9 11.2 %collective-permute-start = (bf16[2,128,256]{2,1,0:T(8,128)(2,1)S(1)}, bf16[2,128,256]{2,1,0:T(8,128)(2,1)S(1)}, u32[]{:S(2)}, u32[]{:S(2)}) collective-permute-start(bf16[2,128,256]{2,1,0:T(8,128)(2,1)S(1)} %away.1), channel_id=1, source_target_pairs={{0,8},{1,9},{2,10},{3,11},{4,12},{5,13},{6,14},{7,15},{8,0},{9,1},... | collective-permute-start | bytes 393224 | tf_op jit(solution)/shard_map/ppermute | solution.py:235
  7.4 7.4 %collective-permute-start.2 = (bf16[2,128,256]{2,1,0:T(8,128)(2,1)}, bf16[2,128,256]{2,1,0:T(8,128)(2,1)S(1)}, u32[]{:S(2)}, u32[]{:S(2)}) collective-permute-start(bf16[2,128,256]{2,1,0:T(8,128)(2,1)} %own.1.u0), channel_id=1, source_target_pairs={{0,4},{1,5},{2,7},{3,6},{4,0},{5,1},{6,3},{7,2},{8,12},{9,13},{10,... | collective-permute-start | bytes 393224 | tf_op jit(solution)/shard_map/ppermute | solution.py:235
  9.0 4.4 %collective-permute-start.1 = (s32[1,2]{1,0:T(1,128)S(1)}, s32[1,2]{1,0:T(1,128)S(1)}, u32[]{:S(2)}, u32[]{:S(2)}) collective-permute-start(s32[1,2]{1,0:T(1,128)S(1)} %bitcast.4), channel_id=1, source_target_pairs={{0,8},{1,9},{2,10},{3,11},{4,12},{5,13},{6,14},{7,15},{8,0},{9,1},... | collective-permute-start | bytes 32 | tf_op jit(solution)/shard_map/ppermute | solution.py:235
  9.4 6.0 %collective-permute-start.3 = (bf16[2,128,256]{2,1,0:T(8,128)(2,1)}, bf16[2,128,256]{2,1,0:T(8,128)(2,1)S(1)}, u32[]{:S(2)}, u32[]{:S(2)}) collective-permute-start(bf16[2,128,256]{2,1,0:T(8,128)(2,1)} %own.1.u0), channel_id=1, source_target_pairs={{0,2},{1,3},{2,0},{3,1},{4,6},{5,7},{6,4},{7,5},{8,10},{9,11},{10,... | collective-permute-start | bytes 393224 | tf_op jit(solution)/shard_map/ppermute | solution.py:235
  10.0 5.3 %collective-permute-start.4 = (bf16[2,128,256]{2,1,0:T(8,128)(2,1)}, bf16[2,128,256]{2,1,0:T(8,128)(2,1)S(1)}, u32[]{:S(2)}, u32[]{:S(2)}) collective-permute-start(bf16[2,128,256]{2,1,0:T(8,128)(2,1)} %own.1.u0), channel_id=1, source_target_pairs={{0,1},{1,0},{2,3},{3,2},{4,5},{5,4},{6,7},{7,6},{8,9},{9,8},{10,11... | collective-permute-start | bytes 393224 | tf_op jit(solution)/shard_map/ppermute | solution.py:235
  10.4 4.9 %copy-start.2 = (bf16[2,128,256]{2,1,0:T(8,128)(2,1)S(1)}, bf16[2,128,256]{2,1,0:T(8,128)(2,1)}, u32[]{:S(2)}) copy-start(bf16[2,128,256]{2,1,0:T(8,128)(2,1)} %own.1.u0) | copy-start | bytes 393220
  13.6 5.0 %collective-permute-start.5 = (bf16[2,128,256]{2,1,0:T(8,128)(2,1)S(1)}, bf16[2,128,256]{2,1,0:T(8,128)(2,1)S(1)}, u32[]{:S(2)}, u32[]{:S(2)}) collective-permute-start(bf16[2,128,256]{2,1,0:T(8,128)(2,1)S(1)} %far.1.v), channel_id=1, source_target_pairs={{0,4},{1,5},{2,7},{3,6},{4,0},{5,1},{6,3},{7,2},{8,12},{9,13},{10,... | collective-permute-start | bytes 393224 | tf_op jit(solution)/shard_map/ppermute | solution.py:235
  14.2 5.1 %collective-permute-start.6 = (bf16[2,128,256]{2,1,0:T(8,128)(2,1)S(1)}, bf16[2,128,256]{2,1,0:T(8,128)(2,1)S(1)}, u32[]{:S(2)}, u32[]{:S(2)}) collective-permute-start(bf16[2,128,256]{2,1,0:T(8,128)(2,1)S(1)} %far.1.v), channel_id=1, source_target_pairs={{0,2},{1,3},{2,0},{3,1},{4,6},{5,7},{6,4},{7,5},{8,10},{9,11},{10,... | collective-permute-start | bytes 393224 | tf_op jit(solution)/shard_map/ppermute | solution.py:235
  14.8 4.5 %collective-permute-start.7 = (bf16[2,128,256]{2,1,0:T(8,128)(2,1)S(1)}, bf16[2,128,256]{2,1,0:T(8,128)(2,1)S(1)}, u32[]{:S(2)}, u32[]{:S(2)}) collective-permute-start(bf16[2,128,256]{2,1,0:T(8,128)(2,1)S(1)} %far.1.v), channel_id=1, source_target_pairs={{0,1},{1,0},{2,3},{3,2},{4,5},{5,4},{6,7},{7,6},{8,9},{9,8},{10,11... | collective-permute-start | bytes 393224 | tf_op jit(solution)/shard_map/ppermute | solution.py:235
  20.3 3.6 %collective-permute-start.9 = (f32[4,32]{1,0:T(4,128)S(1)}, f32[4,32]{1,0:T(4,128)S(1)}, u32[]{:S(2)}, u32[]{:S(2)}) collective-permute-start(f32[4,32]{1,0:T(4,128)S(1)} %get-tuple-element.28), channel_id=1, source_target_pairs={{0,4},{1,5},{2,7},{3,6},{4,0},{5,1},{6,3},{7,2},{8,12},{9,13},{10,... | collective-permute-start | bytes 1544 | tf_op jit(solution)/shard_map/ppermute | solution.py:235
  21.7 3.6 %collective-permute-start.8 = (f32[4,32]{1,0:T(4,128)S(1)}, f32[4,32]{1,0:T(4,128)S(1)}, u32[]{:S(2)}, u32[]{:S(2)}) collective-permute-start(f32[4,32]{1,0:T(4,128)S(1)} %get-tuple-element.27), channel_id=1, source_target_pairs={{0,2},{1,3},{2,0},{3,1},{4,6},{5,7},{6,4},{7,5},{8,10},{9,11},{10,... | collective-permute-start | bytes 1544 | tf_op jit(solution)/shard_map/ppermute | solution.py:235
  25.3 4.5 %collective-permute-start.10 = (f32[2,32]{1,0:T(2,128)S(1)}, f32[2,32]{1,0:T(2,128)S(1)}, u32[]{:S(2)}, u32[]{:S(2)}) collective-permute-start(f32[2,32]{1,0:T(2,128)S(1)} %slice.7), channel_id=1, source_target_pairs={{0,8},{1,9},{2,10},{3,11},{4,12},{5,13},{6,14},{7,15},{8,0},{9,1},... | collective-permute-start | bytes 776 | tf_op jit(solution)/shard_map/ppermute | solution.py:235

commit v11 on v10

--- a/solution.py
+++ b/solution.py
@@ -56,7 +56,8 @@
     return d ^ 4 ^ ((d >> 1) & 1)
 
 
-def copy_layer(acts, grads, layer, out, sems):
+def away_kernel(acts, grads, out, sems):
+    layer = 1 - lax.axis_index("blk") // 8
     copies = [
         pltpu.make_async_copy(src.at[layer], out.at[i], sems.at[i])
         for i, src in enumerate((acts, grads))
@@ -67,28 +68,23 @@
         copy.wait()
 
 
-def keep_slots(lens, tokens, seq_len):
-    row = lax.broadcasted_iota(jnp.int32, (tokens, 1), 0)
+def masked_acts(x, lens, seq_len):
+    row = lax.broadcasted_iota(jnp.int32, (x.shape[0], 1), 0)
     bound = jnp.zeros_like(row)
-    for s in range(tokens // seq_len):
+    for s in range(x.shape[0] // seq_len):
         bound = jnp.where(row // seq_len == s, lens[0:1, s : s + 1] + s * seq_len, bound)
-    return row < bound
-
-
-def away_kernel(acts, grads, out, sems):
-    copy_layer(acts, grads, 1 - lax.axis_index("blk") // 8, out, sems)
-
-
-def own_kernel(seq_len, acts, grads, lens, out, sems):
-    copy_layer(acts, grads, lax.axis_index("blk") // 8, out, sems)
-    x = out[0]
-    out[0] = jnp.where(keep_slots(lens, x.shape[0], seq_len), x, jnp.zeros_like(x))
-
-
-def far_kernel(seq_len, lens, v, out):
-    x = v[0]
-    out[0] = jnp.where(keep_slots(lens, x.shape[0], seq_len), x, jnp.zeros_like(x))
-    out[1] = v[1]
+    return jnp.where(row < bound, x, jnp.zeros_like(x))
+
+
+def away_mask_kernel(seq_len, lens, unit, out):
+    out[0] = masked_acts(unit[0], lens, seq_len)
+    out[1] = unit[1]
+
+
+def own_kernel(seq_len, lens, acts, grads, out):
+    half = lax.axis_index("blk") // 8
+    out[0] = masked_acts(acts[half], lens, seq_len)
+    out[1] = grads[half]
 
 
 def whiten(x, terms):
@@ -243,21 +239,24 @@
     shape = jax.ShapeDtypeStruct
     columns = flagged.shape[0]
     unit = shape((2, tokens, rank), bf16)
-    pair_of_copies = [pltpu.SemaphoreType.DMA((2,))]
     data = (activations, out_grads)
-    away = call(away_kernel, "away", 10**9, 53.71, data, [hbm, hbm], unit, pair_of_copies)
+    lens = lengths.reshape(1, -1)
+    copies = [pltpu.SemaphoreType.DMA((2,))]
+    away = call(away_kernel, "away", 3 * 10**9, 53.71, data, [hbm, hbm], unit, copies)
+    away = call(
+        functools.partial(away_mask_kernel, seq_len),
+        "away_mask",
+        10**4,
+        40,
+        (lens, away),
+        [],
+        unit,
+        input_output_aliases={1: 0},
+    )
     v = send(away, opposite)
-    away, lens, *data = lax.optimization_barrier((away, lengths.reshape(1, -1), *data))
-    far_lens = send(lens, opposite)
+    away, lens, *data = lax.optimization_barrier((away, lens, *data))
     own = call(
-        functools.partial(own_kernel, seq_len),
-        "own",
-        10**9,
-        59,
-        (*data, lens),
-        [hbm, hbm],
-        unit,
-        pair_of_copies,
+        functools.partial(own_kernel, seq_len), "own", 10**9, 40, (lens, *data), [], unit
     )
     near = [send(own, to) for to in ways]
     terms, pick = call(
@@ -271,16 +270,6 @@
         [pltpu.VMEM((2, rank, rank), f32), pltpu.SemaphoreType.DMA((2,))],
     )
     v, terms, pick = lax.optimization_barrier((v, terms, pick))
-    v = call(
-        functools.partial(far_kernel, seq_len),
-        "far",
-        10**4,
-        40,
-        (far_lens, v),
-        [],
-        unit,
-        input_output_aliases={1: 0},
-    )
     late = [send(v, to) for to in ways]
     white, sums = call(
         functools.partial(early_kernel, seq_len, per),

time: 30.6 us -> 28.9 us (0.944)
  Pallas kernels: 7.55 us -> 5.39 us
  waiting for transfers between devices: 9.08 us -> 9.44 us
    pallas_call x7, Pallas kernels: 7.55 us -> 5.39 us  [call(): pl.pallas_call(kernel, out_shape=out_shape, in_specs=specs + [vmem] * (le...]
    ppermute x11 -> x10, waiting for transfers between devices: 9.08 us -> 9.44 us  [send(): return lax.ppermute(x, 'blk', [(d, to(d)) for d in range(size)])]
    ppermute x11 -> x10, starting transfers between devices: 13.1 us -> 13.3 us  [send(): return lax.ppermute(x, 'blk', [(d, to(d)) for d in range(size)])]
  transfers between devices with their start and end apart: 11 -> 10, of which waited for: 6 -> 6; matrix products, arithmetic and copies ran while one was open for 0% -> 0% of each run, Pallas kernels for 19% -> 12%
where the time goes in v11:
time: 28.9 us; the launch traced here: 28.7 us
  starting transfers between devices  13.3 us (46%)
  waiting for transfers between devices  9.44 us (33%)
  Pallas kernels  5.39 us (19%)
  other arithmetic  0.57 us (2%)
    ppermute x10, starting transfers between devices, send(): return lax.ppermute(x, 'blk', [(d, to(d)) for d in range(size)])  13.3 us
    ppermute x10, waiting for transfers between devices, send(): return lax.ppermute(x, 'blk', [(d, to(d)) for d in range(size)])  9.44 us
    pallas_call x7, Pallas kernels, call(): pl.pallas_call(kernel, out_shape=out_shape, in_specs=specs + [vmem] * (le...  5.39 us
  transfers between devices with their start and end apart: 10, of which 6 were waited for; matrix products, arithmetic and copies ran while one was open for 0% of the time, Pallas kernels for 12%

profile of v11, /device:TPU:0, one launch (start us, length us, event | category | flops | bytes accessed | tf_op | source)
XLA Modules:
  0.0 28.7 jit_solution(4730608697658022005)
XLA Ops:
  0.0 1.0 %away.1.unit = bf16[2,128,256]{2,1,0:T(8,128)(2,1)S(1)} custom-call(bf16[2,128,256]{2,1,0:T(8,128)(2,1)} %acts.2, bf16[2,128,256]{2,1,0:T(8,128)(2,1)} %grads.2), custom_call_target="tpu_custom_call" | custom-call | flops 3000000000 | bytes 1000000 | tf_op jit(solution)/shard_map/away/pallas_call | solution.py:210
  1.0 0.0 copy-done
  1.0 0.2 away_mask.1
  1.1 4.1 %collective-permute-start = (bf16[2,128,256]{2,1,0:T(8,128)(2,1)S(1)}, bf16[2,128,256]{2,1,0:T(8,128)(2,1)S(1)}, u32[]{:S(2)}, u32[]{:S(2)}) collective-permute-start(bf16[2,128,256]{2,1,0:T(8,128)(2,1)S(1)} %away_mask.1), channel_id=1, source_target_pairs={{0,8},{1,9},{2,10},{3,11},{4,12},{5,13},{6,14},{7,15},{8,0},{9,1},... | collective-permute-start | bytes 393224 | tf_op jit(solution)/shard_map/ppermute | solution.py:231
  5.3 0.0 copy-done.3
  5.3 0.0 copy-done.4
  5.3 0.1 own.1.u0
  5.4 1.6 %collective-permute-start.1 = (bf16[2,128,256]{2,1,0:T(8,128)(2,1)S(1)}, bf16[2,128,256]{2,1,0:T(8,128)(2,1)S(1)}, u32[]{:S(2)}, u32[]{:S(2)}) collective-permute-start(bf16[2,128,256]{2,1,0:T(8,128)(2,1)S(1)} %own.1.u0), channel_id=1, source_target_pairs={{0,4},{1,5},{2,7},{3,6},{4,0},{5,1},{6,3},{7,2},{8,12},{9,13},{10,... | collective-permute-start | bytes 393224 | tf_op jit(solution)/shard_map/ppermute | solution.py:231
  7.1 0.7 %collective-permute-start.2 = (bf16[2,128,256]{2,1,0:T(8,128)(2,1)S(1)}, bf16[2,128,256]{2,1,0:T(8,128)(2,1)S(1)}, u32[]{:S(2)}, u32[]{:S(2)}) collective-permute-start(bf16[2,128,256]{2,1,0:T(8,128)(2,1)S(1)} %own.1.u0), channel_id=1, source_target_pairs={{0,2},{1,3},{2,0},{3,1},{4,6},{5,7},{6,4},{7,5},{8,10},{9,11},{10,... | collective-permute-start | bytes 393224 | tf_op jit(solution)/shard_map/ppermute | solution.py:231
  7.7 0.7 %collective-permute-start.3 = (bf16[2,128,256]{2,1,0:T(8,128)(2,1)S(1)}, bf16[2,128,256]{2,1,0:T(8,128)(2,1)S(1)}, u32[]{:S(2)}, u32[]{:S(2)}) collective-permute-start(bf16[2,128,256]{2,1,0:T(8,128)(2,1)S(1)} %own.1.u0), channel_id=1, source_target_pairs={{0,1},{1,0},{2,3},{3,2},{4,5},{5,4},{6,7},{7,6},{8,9},{9,8},{10,11... | collective-permute-start | bytes 393224 | tf_op jit(solution)/shard_map/ppermute | solution.py:231
  8.4 0.0 copy-done.2
  8.4 1.7 %factor_terms.1 = (bf16[2,3,256,256]{3,2,1,0:T(8,128)(2,1)S(1)}, bf16[1024,32]{1,0:T(8,128)(2,1)S(1)}) custom-call(s32[2]{0:T(128)S(1)} %copy-done.1, s32[1,32]{1,0:T(1,128)S(1)} %bitcast.4, f32[16,256,256]{2,1,0:T(8,128)} %act_f.1, f32[16,256,256]{2,1,0:T(8,128)} %grad_f.1), custom_call_target="tpu_custom_call" | custom-call | flops 1000000000 | bytes 1000000 | tf_op jit(solution)/shard_map/factor_terms/pallas_call | solution.py:210
  10.1 1.6 %collective-permute-done.v = bf16[2,128,256]{2,1,0:T(8,128)(2,1)S(1)} collective-permute-done((bf16[2,128,256]{2,1,0:T(8,128)(2,1)S(1)}, bf16[2,128,256]{2,1,0:T(8,128)(2,1)S(1)}, u32[]{:S(2)}, u32[]{:S(2)}) %collective-permute-start) | collective-permute-done | bytes 131104 | tf_op jit(solution)/shard_map/ppermute | solution.py:231
  11.7 0.6 %collective-permute-start.4 = (bf16[2,128,256]{2,1,0:T(8,128)(2,1)S(1)}, bf16[2,128,256]{2,1,0:T(8,128)(2,1)S(1)}, u32[]{:S(2)}, u32[]{:S(2)}) collective-permute-start(bf16[2,128,256]{2,1,0:T(8,128)(2,1)S(1)} %collective-permute-done.v), channel_id=1, source_target_pairs={{0,4},{1,5},{2,7},{3,6},{4,0},{5,1},{6,3},{7,2},{8,12},{9,13},{10,... | collective-permute-start | bytes 393224 | tf_op jit(solution)/shard_map/ppermute | solution.py:231
  12.3 1.1 %collective-permute-start.5 = (bf16[2,128,256]{2,1,0:T(8,128)(2,1)S(1)}, bf16[2,128,256]{2,1,0:T(8,128)(2,1)S(1)}, u32[]{:S(2)}, u32[]{:S(2)}) collective-permute-start(bf16[2,128,256]{2,1,0:T(8,128)(2,1)S(1)} %collective-permute-done.v), channel_id=1, source_target_pairs={{0,2},{1,3},{2,0},{3,1},{4,6},{5,7},{6,4},{7,5},{8,10},{9,11},{10,... | collective-permute-start | bytes 393224 | tf_op jit(solution)/shard_map/ppermute | solution.py:231
  13.4 0.0 collective-permute-done.1.u3
  13.4 0.2 collective-permute-start.6
  13.7 0.0 collective-permute-done.2.u2
  13.7 0.0 collective-permute-done.3.u1
  13.7 1.0 %early_pairs.1 = (bf16[2,512,256]{2,1,0:T(8,128)(2,1)S(1)}, f32[12,1024]{1,0:T(8,128)S(1)}) custom-call(bf16[2,3,256,256]{3,2,1,0:T(8,128)(2,1)S(1)} %get-tuple-element.19.terms, bf16[2,128,256]{2,1,0:T(8,128)(2,1)S(1)} %own.1.u0, bf16[2,128,256]{2,1,0:T(8,128)(2,1)S(1)} %collective-permute-done.v, bf16[2,128,256]{2,1,0:T(8,128)(2,1)S(1)} %collective-permute-done.1.u3, ...), custom_call_target="tpu_custom_call" | custom-call | flops 1000000000 | bytes 1000000 | tf_op jit(solution)/shard_map/early_pairs/pallas_call | solution.py:210
  14.7 2.0 %collective-permute-done.4.v3 = bf16[2,128,256]{2,1,0:T(8,128)(2,1)S(1)} collective-permute-done((bf16[2,128,256]{2,1,0:T(8,128)(2,1)S(1)}, bf16[2,128,256]{2,1,0:T(8,128)(2,1)S(1)}, u32[]{:S(2)}, u32[]{:S(2)}) %collective-permute-start.4) | collective-permute-done | bytes 131104 | tf_op jit(solution)/shard_map/ppermute | solution.py:231
  16.7 0.9 %collective-permute-done.5.v2 = bf16[2,128,256]{2,1,0:T(8,128)(2,1)S(1)} collective-permute-done((bf16[2,128,256]{2,1,0:T(8,128)(2,1)S(1)}, bf16[2,128,256]{2,1,0:T(8,128)(2,1)S(1)}, u32[]{:S(2)}, u32[]{:S(2)}) %collective-permute-start.5) | collective-permute-done | bytes 131104 | tf_op jit(solution)/shard_map/ppermute | solution.py:231
  17.6 0.0 collective-permute-done.6.v1
  17.6 1.0 %return_rows.1 = (f32[4,32]{1,0:T(4,128)S(1)}, f32[4,32]{1,0:T(4,128)S(1)}) custom-call(bf16[2,3,256,256]{3,2,1,0:T(8,128)(2,1)S(1)} %get-tuple-element.19.terms, bf16[2,512,256]{2,1,0:T(8,128)(2,1)S(1)} %get-tuple-element.24.white, bf16[1024,32]{1,0:T(8,128)(2,1)S(1)} %get-tuple-element.25.pick, f32[12,1024]{1,0:T(8,128)S(1)} %get-tuple-element.26.sums, ...), custom_call_target="tpu_custom_call" | custom-call | flops 1000000000 | bytes 1000000 | tf_op jit(solution)/shard_map/return_rows/pallas_call | solution.py:210
  18.6 1.5 %collective-permute-start.8 = (f32[4,32]{1,0:T(4,128)S(1)}, f32[4,32]{1,0:T(4,128)S(1)}, u32[]{:S(2)}, u32[]{:S(2)}) collective-permute-start(f32[4,32]{1,0:T(4,128)S(1)} %get-tuple-element.28), channel_id=1, source_target_pairs={{0,4},{1,5},{2,7},{3,6},{4,0},{5,1},{6,3},{7,2},{8,12},{9,13},{10,... | collective-permute-start | bytes 1544 | tf_op jit(solution)/shard_map/ppermute | solution.py:231
  20.1 0.6 %collective-permute-start.7 = (f32[4,32]{1,0:T(4,128)S(1)}, f32[4,32]{1,0:T(4,128)S(1)}, u32[]{:S(2)}, u32[]{:S(2)}) collective-permute-start(f32[4,32]{1,0:T(4,128)S(1)} %get-tuple-element.27), channel_id=1, source_target_pairs={{0,2},{1,3},{2,0},{3,1},{4,6},{5,7},{6,4},{7,5},{8,10},{9,11},{10,... | collective-permute-start | bytes 1544 | tf_op jit(solution)/shard_map/ppermute | solution.py:231
  20.6 0.5 %own_rows.1 = f32[4,32]{1,0:T(4,128)S(1)} custom-call(bf16[2,512,256]{2,1,0:T(8,128)(2,1)S(1)} %get-tuple-element.24.white, bf16[1024,32]{1,0:T(8,128)(2,1)S(1)} %get-tuple-element.25.pick, f32[12,1024]{1,0:T(8,128)S(1)} %get-tuple-element.26.sums, bf16[2,128,256]{2,1,0:T(8,128)(2,1)S(1)} %collective-permute-done.4.v3, ...), custom_call_target="tpu_custom_call" | custom-call | flops 1000000000 | bytes 1000000 | tf_op jit(solution)/shard_map/own_rows/pallas_call | solution.py:210
  21.1 1.1 %collective-permute-done.8 = f32[4,32]{1,0:T(4,128)S(1)} collective-permute-done((f32[4,32]{1,0:T(4,128)S(1)}, f32[4,32]{1,0:T(4,128)S(1)}, u32[]{:S(2)}, u32[]{:S(2)}) %collective-permute-start.8) | collective-permute-done | bytes 544 | tf_op jit(solution)/shard_map/ppermute | solution.py:231
  22.2 1.4 %collective-permute-done.7 = f32[4,32]{1,0:T(4,128)S(1)} collective-permute-done((f32[4,32]{1,0:T(4,128)S(1)}, f32[4,32]{1,0:T(4,128)S(1)}, u32[]{:S(2)}, u32[]{:S(2)}) %collective-permute-start.7) | collective-permute-done | bytes 544 | tf_op jit(solution)/shard_map/ppermute | solution.py:231
  23.7 2.1 %collective-permute-start.9 = (f32[2,32]{1,0:T(2,128)S(1)}, f32[2,32]{1,0:T(2,128)S(1)}, u32[]{:S(2)}, u32[]{:S(2)}) collective-permute-start(f32[2,32]{1,0:T(2,128)S(1)} %slice.7), channel_id=1, source_target_pairs={{0,8},{1,9},{2,10},{3,11},{4,12},{5,13},{6,14},{7,15},{8,0},{9,1},... | collective-permute-start | bytes 776 | tf_op jit(solution)/shard_map/ppermute | solution.py:231
  25.8 2.4 %collective-permute-done.9 = f32[2,32]{1,0:T(2,128)S(1)} collective-permute-done((f32[2,32]{1,0:T(2,128)S(1)}, f32[2,32]{1,0:T(2,128)S(1)}, u32[]{:S(2)}, u32[]{:S(2)}) %collective-permute-start.9) | collective-permute-done | bytes 288 | tf_op jit(solution)/shard_map/ppermute | solution.py:231
  28.2 0.6 %slice_add_fusion = f32[2,32]{1,0:T(2,128)} fusion(f32[2,32]{1,0:T(2,128)S(1)} %collective-permute-done.9, f32[4,32]{1,0:T(4,128)S(1)} %add_add_fusion), kind=kLoop, calls=%fused_computation.1 | loop fusion | flops 64 | bytes 768 | tf_op jit(solution)/shard_map/add | solution.py:303
  (8 shorter events, 0.0 us)
Async XLA Ops:
  0.0 5.3 %copy-start.3 = (bf16[2,128,256]{2,1,0:T(8,128)(2,1)S(1)}, bf16[2,128,256]{2,1,0:T(8,128)(2,1)}, u32[]{:S(2)}) copy-start(bf16[2,128,256]{2,1,0:T(8,128)(2,1)} %acts.2) | copy-start | bytes 393220
  0.0 5.3 %copy-start.4 = (bf16[2,128,256]{2,1,0:T(8,128)(2,1)S(1)}, bf16[2,128,256]{2,1,0:T(8,128)(2,1)}, u32[]{:S(2)}) copy-start(bf16[2,128,256]{2,1,0:T(8,128)(2,1)} %grads.2) | copy-start | bytes 393220
  0.0 1.0 %copy-start = (s32[2]{0:T(128)S(1)}, s32[2]{0:T(128)}, u32[]{:S(2)}) copy-start(s32[2]{0:T(128)} %param.9) | copy-start | bytes 28
  0.0 8.4 %copy-start.1 = (s32[2]{0:T(128)S(1)}, s32[2]{0:T(128)}, u32[]{:S(2)}) copy-start(s32[2]{0:T(128)} %layer_ids.1) | copy-start | bytes 28
  0.0 8.4 %copy-start.2 = (s32[32]{0:T(128)S(1)}, s32[32]{0:T(128)}, u32[]{:S(2)}) copy-start(s32[32]{0:T(128)} %param.11) | copy-start | bytes 388
  1.1 10.5 %collective-permute-start = (bf16[2,128,256]{2,1,0:T(8,128)(2,1)S(1)}, bf16[2,128,256]{2,1,0:T(8,128)(2,1)S(1)}, u32[]{:S(2)}, u32[]{:S(2)}) collective-permute-start(bf16[2,128,256]{2,1,0:T(8,128)(2,1)S(1)} %away_mask.1), channel_id=1, source_target_pairs={{0,8},{1,9},{2,10},{3,11},{4,12},{5,13},{6,14},{7,15},{8,0},{9,1},... | collective-permute-start | bytes 393224 | tf_op jit(solution)/shard_map/ppermute | solution.py:231
  5.4 8.0 %collective-permute-start.1 = (bf16[2,128,256]{2,1,0:T(8,128)(2,1)S(1)}, bf16[2,128,256]{2,1,0:T(8,128)(2,1)S(1)}, u32[]{:S(2)}, u32[]{:S(2)}) collective-permute-start(bf16[2,128,256]{2,1,0:T(8,128)(2,1)S(1)} %own.1.u0), channel_id=1, source_target_pairs={{0,4},{1,5},{2,7},{3,6},{4,0},{5,1},{6,3},{7,2},{8,12},{9,13},{10,... | collective-permute-start | bytes 393224 | tf_op jit(solution)/shard_map/ppermute | solution.py:231
  7.1 6.6 %collective-permute-start.2 = (bf16[2,128,256]{2,1,0:T(8,128)(2,1)S(1)}, bf16[2,128,256]{2,1,0:T(8,128)(2,1)S(1)}, u32[]{:S(2)}, u32[]{:S(2)}) collective-permute-start(bf16[2,128,256]{2,1,0:T(8,128)(2,1)S(1)} %own.1.u0), channel_id=1, source_target_pairs={{0,2},{1,3},{2,0},{3,1},{4,6},{5,7},{6,4},{7,5},{8,10},{9,11},{10,... | collective-permute-start | bytes 393224 | tf_op jit(solution)/shard_map/ppermute | solution.py:231
  7.7 5.9 %collective-permute-start.3 = (bf16[2,128,256]{2,1,0:T(8,128)(2,1)S(1)}, bf16[2,128,256]{2,1,0:T(8,128)(2,1)S(1)}, u32[]{:S(2)}, u32[]{:S(2)}) collective-permute-start(bf16[2,128,256]{2,1,0:T(8,128)(2,1)S(1)} %own.1.u0), channel_id=1, source_target_pairs={{0,1},{1,0},{2,3},{3,2},{4,5},{5,4},{6,7},{7,6},{8,9},{9,8},{10,11... | collective-permute-start | bytes 393224 | tf_op jit(solution)/shard_map/ppermute | solution.py:231
  11.7 5.0 %collective-permute-start.4 = (bf16[2,128,256]{2,1,0:T(8,128)(2,1)S(1)}, bf16[2,128,256]{2,1,0:T(8,128)(2,1)S(1)}, u32[]{:S(2)}, u32[]{:S(2)}) collective-permute-start(bf16[2,128,256]{2,1,0:T(8,128)(2,1)S(1)} %collective-permute-done.v), channel_id=1, source_target_pairs={{0,4},{1,5},{2,7},{3,6},{4,0},{5,1},{6,3},{7,2},{8,12},{9,13},{10,... | collective-permute-start | bytes 393224 | tf_op jit(solution)/shard_map/ppermute | solution.py:231
  12.3 5.3 %collective-permute-start.5 = (bf16[2,128,256]{2,1,0:T(8,128)(2,1)S(1)}, bf16[2,128,256]{2,1,0:T(8,128)(2,1)S(1)}, u32[]{:S(2)}, u32[]{:S(2)}) collective-permute-start(bf16[2,128,256]{2,1,0:T(8,128)(2,1)S(1)} %collective-permute-done.v), channel_id=1, source_target_pairs={{0,2},{1,3},{2,0},{3,1},{4,6},{5,7},{6,4},{7,5},{8,10},{9,11},{10,... | collective-permute-start | bytes 393224 | tf_op jit(solution)/shard_map/ppermute | solution.py:231
  13.4 4.2 %collective-permute-start.6 = (bf16[2,128,256]{2,1,0:T(8,128)(2,1)S(1)}, bf16[2,128,256]{2,1,0:T(8,128)(2,1)S(1)}, u32[]{:S(2)}, u32[]{:S(2)}) collective-permute-start(bf16[2,128,256]{2,1,0:T(8,128)(2,1)S(1)} %collective-permute-done.v), channel_id=1, source_target_pairs={{0,1},{1,0},{2,3},{3,2},{4,5},{5,4},{6,7},{7,6},{8,9},{9,8},{10,11... | collective-permute-start | bytes 393224 | tf_op jit(solution)/shard_map/ppermute | solution.py:231
  18.6 3.6 %collective-permute-start.8 = (f32[4,32]{1,0:T(4,128)S(1)}, f32[4,32]{1,0:T(4,128)S(1)}, u32[]{:S(2)}, u32[]{:S(2)}) collective-permute-start(f32[4,32]{1,0:T(4,128)S(1)} %get-tuple-element.28), channel_id=1, source_target_pairs={{0,4},{1,5},{2,7},{3,6},{4,0},{5,1},{6,3},{7,2},{8,12},{9,13},{10,... | collective-permute-start | bytes 1544 | tf_op jit(solution)/shard_map/ppermute | solution.py:231
  20.1 3.6 %collective-permute-start.7 = (f32[4,32]{1,0:T(4,128)S(1)}, f32[4,32]{1,0:T(4,128)S(1)}, u32[]{:S(2)}, u32[]{:S(2)}) collective-permute-start(f32[4,32]{1,0:T(4,128)S(1)} %get-tuple-element.27), channel_id=1, source_target_pairs={{0,2},{1,3},{2,0},{3,1},{4,6},{5,7},{6,4},{7,5},{8,10},{9,11},{10,... | collective-permute-start | bytes 1544 | tf_op jit(solution)/shard_map/ppermute | solution.py:231
  23.7 4.5 %collective-permute-start.9 = (f32[2,32]{1,0:T(2,128)S(1)}, f32[2,32]{1,0:T(2,128)S(1)}, u32[]{:S(2)}, u32[]{:S(2)}) collective-permute-start(f32[2,32]{1,0:T(2,128)S(1)} %slice.7), channel_id=1, source_target_pairs={{0,8},{1,9},{2,10},{3,11},{4,12},{5,13},{6,14},{7,15},{8,0},{9,1},... | collective-permute-start | bytes 776 | tf_op jit(solution)/shard_map/ppermute | solution.py:231

commit v12 on v11

v12 whole, which is shorter than its diff:
```python
import functools

import jax
import jax.numpy as jnp
from jax import lax
from jax.experimental import pallas as pl
from jax.experimental.pallas import tpu as pltpu
from jax.sharding import PartitionSpec as P

HIGHEST = lax.Precision.HIGHEST


def tile_scores(white_acts, white_grads, remote_acts, remote_grads, seq_len):
    gram_acts = jnp.einsum(
        "lqr,lkr->lqk", white_acts, remote_acts, preferred_element_type=jnp.float32
    )
    gram_grads = jnp.einsum(
        "lqr,lkr->lqk", white_grads, remote_grads, preferred_element_type=jnp.float32
    )
    pair = jnp.sum(gram_acts * gram_grads, axis=0)
    rows = pair.shape[0] // seq_len
    columns = pair.shape[1] // seq_len
    width = white_acts.shape[2]
    return pair.reshape(rows, seq_len, columns, seq_len).sum(axis=(1, 3)) * (
        1.0 / (width * seq_len)
    )


def gathered(activations, out_grads, lengths, layer_ids, flagged, act_factor, grad_factor):
    tok_rows = activations.shape[1]
    seq_count = lengths.shape[0]
    seq_len = tok_rows // seq_count
    slots = jnp.arange(tok_rows) % seq_len
    keep = (slots < jnp.repeat(lengths, seq_len)).astype(jnp.bfloat16)
    masked_acts = activations * keep[None, :, None]
    masked_grads = out_grads * keep[None, :, None]
    picked_act = jnp.take(act_factor, layer_ids, axis=0)
    picked_grad = jnp.take(grad_factor, layer_ids, axis=0)
    white_acts = jnp.einsum(
        "ltr,lrs->lts", masked_acts.astype(jnp.float32), picked_act, precision=HIGHEST
    ).astype(jnp.bfloat16)
    white_grads = jnp.einsum(
        "ltr,lrs->lts", masked_grads.astype(jnp.float32), picked_grad, precision=HIGHEST
    ).astype(jnp.bfloat16)
    part_scores = tile_scores(
        white_acts,
        white_grads,
        lax.all_gather(masked_acts, "blk", axis=1, tiled=True),
        lax.all_gather(masked_grads, "blk", axis=1, tiled=True),
        seq_len,
    )
    return jnp.take(part_scores, flagged, axis=1)


def z_near(d):
    return d ^ 4 ^ ((d >> 1) & 1)


def away_kernel(acts, grads, out_acts, out_grads, sems):
    layer = 1 - lax.axis_index("blk") // 8
    copies = [
        pltpu.make_async_copy(src.at[layer], out, sems.at[i])
        for i, (src, out) in enumerate(((acts, out_acts), (grads, out_grads)))
    ]
    for copy in copies:
        copy.start()
    for copy in copies:
        copy.wait()


def masked_acts(x, lens, seq_len):
    row = lax.broadcasted_iota(jnp.int32, (x.shape[0], 1), 0)
    bound = jnp.zeros_like(row)
    for s in range(x.shape[0] // seq_len):
        bound = jnp.where(row // seq_len == s, lens[0:1, s : s + 1] + s * seq_len, bound)
    return jnp.where(row < bound, x, jnp.zeros_like(x))


def away_mask_kernel(seq_len, lens, acts, out):
    out[...] = masked_acts(acts[...], lens, seq_len)


def own_kernel(seq_len, lens, acts, grads, out):
    half = lax.axis_index("blk") // 8
    out[0] = masked_acts(acts[half], lens, seq_len)
    out[1] = grads[half]


def whiten(x, terms):
    total = jnp.dot(x, terms[0], preferred_element_type=jnp.float32)
    for n in (1, 2):
        total = total + jnp.dot(x, terms[n], preferred_element_type=jnp.float32)
    return total.astype(jnp.bfloat16)


def stack(*arrays):
    return jnp.concatenate(arrays, axis=0)


def block(seq_len, left, right):
    grams = [
        lax.dot_general(a, b, (((1,), (1,)), ((), ())), preferred_element_type=jnp.float32)
        for a, b in zip(left, right)
    ]
    rows, columns = grams[0].shape
    return (grams[0] * grams[1]).reshape(rows // seq_len, seq_len, columns).sum(axis=1)


def pick_columns(sums, pick):
    rest, terms = sums, []
    for _ in range(3):
        terms.append(rest.astype(jnp.bfloat16))
        rest = rest - terms[-1].astype(jnp.float32)
    n = sums.shape[0]
    out = jnp.dot(stack(*terms), pick[...], preferred_element_type=jnp.float32)
    return out[:n] + out[n : 2 * n] + out[2 * n :]


def terms_kernel(layer_ids, act_f, grad_f, terms, factor, sems):
    layer = layer_ids[lax.axis_index("blk") // 8]
    copies = [
        pltpu.make_async_copy(src.at[layer], factor.at[i], sems.at[i])
        for i, src in enumerate((act_f, grad_f))
    ]
    for copy in copies:
        copy.start()
    for w, copy in enumerate(copies):
        copy.wait()
        rest = factor[w]
        for t in range(3):
            term = rest.astype(jnp.bfloat16)
            terms[w, t] = term
            rest = rest - term.astype(jnp.float32)


def pick_kernel(seq_len, per, rank, flagged, pick):
    d = lax.axis_index("blk")
    token = lax.broadcasted_iota(jnp.int32, pick.shape, 0)
    spot = token // (seq_len * per)
    slot = spot // 2
    owner = jnp.where(
        slot == 0, d, jnp.where(slot == 1, d ^ 1, jnp.where(slot == 2, d ^ 2, z_near(d)))
    )
    owner = owner ^ (8 * (spot % 2))
    seq = owner * per + token // seq_len % per
    pick[...] = jnp.where(seq == flagged[...], 1.0 / (rank * seq_len), 0.0).astype(pick.dtype)


def whiten(x, terms):
    total = jnp.dot(x, terms[0], preferred_element_type=jnp.float32)
    for n in (1, 2):
        total = total + jnp.dot(x, terms[n], preferred_element_type=jnp.float32)
    return total.astype(jnp.bfloat16)


def stack(*arrays):
    return jnp.concatenate(arrays, axis=0)


def gram(left, right):
    return lax.dot_general(
        left, right, (((1,), (1,)), ((), ())), preferred_element_type=jnp.float32
    )


def over_rows(pair, seq_len):
    rows, columns = pair.shape
    return pair.reshape(rows // seq_len, seq_len, columns).sum(axis=1)


def pick_columns(sums, pick):
    rest, terms = sums, []
    for _ in range(3):
        terms.append(rest.astype(jnp.bfloat16))
        rest = rest - terms[-1].astype(jnp.float32)
    n = sums.shape[0]
    out = jnp.dot(stack(*terms), pick[...], preferred_element_type=jnp.float32)
    return out[:n] + out[n : 2 * n] + out[2 * n :]


def late_blocks():
    out = [(("uv", 0), [("v", 1), ("v", 2), ("v", 3)])]
    for slot, other in ((2, 3), (3, 2)):
        out.append((("u", slot), [("v", 1), ("v", other)]))
        out.append((("v", slot), [("u", 1), ("v", 1), ("u", other), ("v", other)]))
    return out


def place(got, columns, n):
    zeros = jnp.zeros((got.shape[0], n), jnp.float32)
    at = {(kind, slot): got[:, i * n : (i + 1) * n] for i, (kind, slot) in enumerate(columns)}
    return jnp.concatenate(
        [at.get((kind, slot), zeros) for slot in range(4) for kind in "uv"], axis=1
    )


def early_kernel(seq_len, terms, u0, va0, vg0, u3, u2, u1, vg3, vg2, vg1, white, sums, *grams):
    n = va0.shape[0]
    per = n // seq_len
    tok = {("u", i): (u[0], u[1]) for i, u in enumerate((u0, u1, u2, u3))}
    tok["v", 0] = (va0[...], vg0[...])
    for i, vg in ((1, vg1), (2, vg2), (3, vg3)):
        tok["v", i] = (None, vg[...])
    rows = [("u", 0), ("v", 0), ("u", 2), ("u", 3)]
    acts = whiten(stack(*[tok[r][0] for r in rows]), terms.at[0])
    white[...] = acts
    rows = rows + [("v", 2), ("v", 3)]
    grads = whiten(stack(*[tok[r][1] for r in rows]), terms.at[1])
    part = {r: slice(i * n, (i + 1) * n) for i, r in enumerate(rows)}
    part["uv", 0] = slice(0, 2 * n)
    now = (
        (("uv", 0), [("u", 0), ("v", 0), ("u", 1), ("u", 2), ("u", 3)]),
        (("u", 2), [("u", 1), ("u", 3)]),
        (("u", 3), [("u", 1), ("u", 2)]),
    )
    lines = {}
    for row, columns in now:
        pair = gram(acts[part[row]], stack(*[tok[c][0] for c in columns])) * gram(
            grads[part[row]], stack(*[tok[c][1] for c in columns])
        )
        lines[row] = place(over_rows(pair, seq_len), columns, n)
    none = jnp.zeros((per, 8 * n), jnp.float32)
    sums[...] = stack(lines["uv", 0], lines["u", 2], none, lines["u", 3], none)
    for out, (row, columns) in zip(grams, late_blocks()):
        out[...] = gram(grads[part[row]], stack(*[tok[c][1] for c in columns]))


def partner_kernel(
    seq_len, terms, white, pick, sums, g2u, g2v, g3u, g3v, u3, u2, u1, va3, va2, va1, by_x, by_z
):
    n = va1.shape[0]
    per = n // seq_len
    tok = {("u", i): u[0] for i, u in ((1, u1), (2, u2), (3, u3))}
    tok |= {("v", i): va[...] for i, va in ((1, va1), (2, va2), (3, va3))}
    fresh = whiten(stack(tok["v", 2], tok["v", 3]), terms.at[0])
    left = {
        ("u", 2): white[2 * n : 3 * n],
        ("u", 3): white[3 * n : 4 * n],
        ("v", 2): fresh[:n],
        ("v", 3): fresh[n:],
    }
    lines = []
    for other, (row, columns) in zip((g2u, g2v, g3u, g3v), late_blocks()[1:]):
        pair = gram(left[row], stack(*[tok[c] for c in columns])) * other[...]
        lines.append(place(over_rows(pair, seq_len), columns, n))
    picked = pick_columns(sums[2 * per :, :] + stack(*lines), pick)
    by_x[...] = picked[: 2 * per]
    by_z[...] = picked[2 * per :]


def rows_kernel(seq_len, white, pick, sums, g0, va3, va2, va1, out):
    n = va1.shape[0]
    per = n // seq_len
    columns = late_blocks()[0][1]
    pair = gram(white[: 2 * n], stack(va1[...], va2[...], va3[...])) * g0[...]
    late = place(over_rows(pair, seq_len), columns, n)
    out[...] = pick_columns(sums[: 2 * per, :] + late, pick)


def call(kernel, name, flops, limit, operands, specs, out_shape, scratch=(), **more):
    vmem = pl.BlockSpec(memory_space=pltpu.VMEM)
    return pl.pallas_call(
        kernel,
        out_shape=out_shape,
        in_specs=specs + [vmem] * (len(operands) - len(specs)),
        out_specs=jax.tree.map(lambda _: vmem, out_shape),
        scratch_shapes=scratch,
        compiler_params=pltpu.CompilerParams(vmem_limit_bytes=int(limit * 1024 * 1024)),
        cost_estimate=pl.CostEstimate(flops=flops, bytes_accessed=10**6, transcendentals=0),
        name=name,
        **more,
    )(*operands)


def paired(activations, out_grads, lengths, layer_ids, flagged, act_factor, grad_factor):
    size = 16
    per = lengths.shape[0]
    tokens, rank = activations.shape[1:]
    seq_len = tokens // per
    f32, bf16 = jnp.float32, jnp.bfloat16

    def send(x, to):
        return lax.ppermute(x, "blk", [(d, to(d)) for d in range(size)])

    def opposite(d):
        return d ^ 8

    ways = (z_near, lambda d: d ^ 2, lambda d: d ^ 1)
    hbm = pl.BlockSpec(memory_space=pltpu.HBM)
    smem = pl.BlockSpec(memory_space=pltpu.SMEM)
    shape = jax.ShapeDtypeStruct
    columns = flagged.shape[0]
    half_unit = shape((tokens, rank), bf16)
    data = (activations, out_grads)
    lens = lengths.reshape(1, -1)
    away_acts, away_grads = call(
        away_kernel,
        "away",
        3 * 10**9,
        53.71,
        data,
        [hbm, hbm],
        (half_unit, half_unit),
        [pltpu.SemaphoreType.DMA((2,))],
    )
    vg = send(away_grads, opposite)
    away_acts = call(
        functools.partial(away_mask_kernel, seq_len),
        "away_mask",
        10**4,
        40,
        (lens, away_acts),
        [],
        half_unit,
        input_output_aliases={1: 0},
    )
    va = send(away_acts, opposite)
    away_acts, lens, *data = lax.optimization_barrier((away_acts, lens, *data))
    own = call(
        functools.partial(own_kernel, seq_len),
        "own",
        10**4,
        40,
        (lens, *data),
        [],
        shape((2, tokens, rank), bf16),
    )
    near = [send(own, to) for to in ways]
    own, layer_ids = lax.optimization_barrier((own, layer_ids))
    terms = call(
        terms_kernel,
        "factor_terms",
        10**4,
        51,
        (layer_ids, act_factor, grad_factor),
        [smem, hbm, hbm],
        shape((2, 3, rank, rank), bf16),
        [pltpu.VMEM((2, rank, rank), f32), pltpu.SemaphoreType.DMA((2,))],
    )
    vg, terms, flags = lax.optimization_barrier((vg, terms, flagged.reshape(1, -1)))
    pick = call(
        functools.partial(pick_kernel, seq_len, per, rank),
        "column_pick",
        15 * 10**8,
        40,
        (flags,),
        [],
        shape((8 * tokens, columns), bf16),
    )
    vg, pick, near = lax.optimization_barrier((vg, pick, near))
    late_grads = [send(vg, to) for to in ways]
    late_acts = [send(va, to) for to in ways]
    size_of = {"uv": 2, "u": 1, "v": 1}
    white, sums, *grams = call(
        functools.partial(early_kernel, seq_len),
        "early_pairs",
        10**9,
        40,
        (terms, own, va, vg, *near, *late_grads),
        [],
        [shape((4 * tokens, rank), bf16), shape((6 * per, 8 * tokens), f32)]
        + [
            shape((size_of[row[0]] * tokens, len(cols) * tokens), f32)
            for row, cols in late_blocks()
        ],
    )
    rows = shape((2 * per, columns), f32)
    by_x, by_z = call(
        functools.partial(partner_kernel, seq_len),
        "partner_rows",
        10**9,
        40,
        (terms, white, pick, sums, *grams[1:], *near, *late_acts),
        [],
        (rows, rows),
    )
    mine = call(
        functools.partial(rows_kernel, seq_len),
        "own_rows",
        10**9,
        40,
        (white, pick, sums, grams[0], *late_acts),
        [],
        rows,
    )
    half_sum = mine + send(by_x, lambda d: d ^ 2) + send(by_z, z_near)
    return half_sum[:per] + send(half_sum[per:], opposite)


def solution(mesh):
    in_specs = (
        P(None, ("grp", "blk"), None),
        P(None, ("grp", "blk"), None),
        P(("grp", "blk")),
        P("grp"),
        P("grp"),
        P(),
        P(),
    )
    out_specs = P(("grp", "blk"), None)
    shards = paired if mesh.shape["blk"] == 16 else gathered
    return jax.shard_map(shards, mesh=mesh, in_specs=in_specs, out_specs=out_specs, check_vma=False)
```

time: 28.9 us -> 32.3 us (1.12)
  starting transfers between devices: 13.3 us -> 16.1 us
    ppermute x10 -> x14, starting transfers between devices: 13.3 us -> 16.1 us  [send(): return lax.ppermute(x, 'blk', [(d, to(d)) for d in range(size)])]
    ppermute x10 -> x14, waiting for transfers between devices: 9.44 us -> 9.73 us  [send(): return lax.ppermute(x, 'blk', [(d, to(d)) for d in range(size)])]
    pallas_call x7 -> x8, Pallas kernels: 5.39 us -> 5.54 us  [call(): pl.pallas_call(kernel, out_shape=out_shape, in_specs=specs + [vmem] * (le...]
  transfers between devices with their start and end apart: 10 -> 14, of which waited for: 6 -> 8; matrix products, arithmetic and copies ran while one was open for 0% -> 0% of each run, Pallas kernels for 12% -> 12%
where the time goes in v12:
time: 32.3 us; the launch traced here: 32.1 us
  starting transfers between devices  16.1 us (50%)
  waiting for transfers between devices  9.73 us (30%)
  Pallas kernels  5.54 us (17%)
  other arithmetic  0.57 us (2%)
    ppermute x14, starting transfers between devices, send(): return lax.ppermute(x, 'blk', [(d, to(d)) for d in range(size)])  16.1 us
    ppermute x14, waiting for transfers between devices, send(): return lax.ppermute(x, 'blk', [(d, to(d)) for d in range(size)])  9.73 us
    pallas_call x8, Pallas kernels, call(): pl.pallas_call(kernel, out_shape=out_shape, in_specs=specs + [vmem] * (le...  5.54 us
  transfers between devices with their start and end apart: 14, of which 8 were waited for; matrix products, arithmetic and copies ran while one was open for 0% of the time, Pallas kernels for 12%

profile of v12, /device:TPU:0, one launch (start us, length us, event | category | flops | bytes accessed | tf_op | source)
XLA Modules:
  0.0 32.1 jit_solution(17234906488790804371)
XLA Ops:
  0.0 0.9 %away.1 = (bf16[128,256]{1,0:T(8,128)(2,1)S(1)}, bf16[128,256]{1,0:T(8,128)(2,1)S(1)}) custom-call(bf16[2,128,256]{2,1,0:T(8,128)(2,1)} %acts.2, bf16[2,128,256]{2,1,0:T(8,128)(2,1)} %grads.2), custom_call_target="tpu_custom_call" | custom-call | flops 3000000000 | bytes 1000000 | tf_op jit(solution)/shard_map/away/pallas_call | solution.py:262
  1.0 4.1 %collective-permute-start = (bf16[128,256]{1,0:T(8,128)(2,1)S(1)}, bf16[128,256]{1,0:T(8,128)(2,1)S(1)}, u32[]{:S(2)}, u32[]{:S(2)}) collective-permute-start(bf16[128,256]{1,0:T(8,128)(2,1)S(1)} %get-tuple-element.29), channel_id=1, source_target_pairs={{0,8},{1,9},{2,10},{3,11},{4,12},{5,13},{6,14},{7,15},{8,0},{9,1},... | collective-permute-start | bytes 196616 | tf_op jit(solution)/shard_map/ppermute | solution.py:283
  5.1 0.2 away_mask.1
  5.3 0.2 own.1.u0
  5.4 0.0 copy-start.4
  5.4 1.6 %collective-permute-start.2 = (bf16[2,128,256]{2,1,0:T(8,128)(2,1)S(1)}, bf16[2,128,256]{2,1,0:T(8,128)(2,1)S(1)}, u32[]{:S(2)}, u32[]{:S(2)}) collective-permute-start(bf16[2,128,256]{2,1,0:T(8,128)(2,1)S(1)} %own.1.u0), channel_id=1, source_target_pairs={{0,4},{1,5},{2,7},{3,6},{4,0},{5,1},{6,3},{7,2},{8,12},{9,13},{10,... | collective-permute-start | bytes 393224 | tf_op jit(solution)/shard_map/ppermute | solution.py:283
  7.1 0.7 %collective-permute-start.3 = (bf16[2,128,256]{2,1,0:T(8,128)(2,1)S(1)}, bf16[2,128,256]{2,1,0:T(8,128)(2,1)S(1)}, u32[]{:S(2)}, u32[]{:S(2)}) collective-permute-start(bf16[2,128,256]{2,1,0:T(8,128)(2,1)S(1)} %own.1.u0), channel_id=1, source_target_pairs={{0,2},{1,3},{2,0},{3,1},{4,6},{5,7},{6,4},{7,5},{8,10},{9,11},{10,... | collective-permute-start | bytes 393224 | tf_op jit(solution)/shard_map/ppermute | solution.py:283
  7.7 0.7 %collective-permute-start.4 = (bf16[2,128,256]{2,1,0:T(8,128)(2,1)S(1)}, bf16[2,128,256]{2,1,0:T(8,128)(2,1)S(1)}, u32[]{:S(2)}, u32[]{:S(2)}) collective-permute-start(bf16[2,128,256]{2,1,0:T(8,128)(2,1)S(1)} %own.1.u0), channel_id=1, source_target_pairs={{0,1},{1,0},{2,3},{3,2},{4,5},{5,4},{6,7},{7,6},{8,9},{9,8},{10,11... | collective-permute-start | bytes 393224 | tf_op jit(solution)/shard_map/ppermute | solution.py:283
  8.4 0.3 %collective-permute-start.1 = (bf16[128,256]{1,0:T(8,128)(2,1)S(1)}, bf16[128,256]{1,0:T(8,128)(2,1)S(1)}, u32[]{:S(2)}, u32[]{:S(2)}) collective-permute-start(bf16[128,256]{1,0:T(8,128)(2,1)S(1)} %away_mask.1), channel_id=1, source_target_pairs={{0,8},{1,9},{2,10},{3,11},{4,12},{5,13},{6,14},{7,15},{8,0},{9,1},... | collective-permute-start | bytes 196616 | tf_op jit(solution)/shard_map/ppermute | solution.py:283
  8.8 1.7 %factor_terms.1.terms = bf16[2,3,256,256]{3,2,1,0:T(8,128)(2,1)S(1)} custom-call(s32[2]{0:T(128)S(1)} %copy-done.3, f32[16,256,256]{2,1,0:T(8,128)} %act_f.1, f32[16,256,256]{2,1,0:T(8,128)} %grad_f.1), custom_call_target="tpu_custom_call" | custom-call | flops 10000 | bytes 1000000 | tf_op jit(solution)/shard_map/factor_terms/pallas_call | solution.py:262
  10.4 0.0 collective-permute-done.vg0
  10.4 0.2 column_pick.1.pick
  10.7 0.2 collective-permute-done.2.u3
  10.8 1.5 %collective-permute-done.3.u2 = bf16[2,128,256]{2,1,0:T(8,128)(2,1)S(1)} collective-permute-done((bf16[2,128,256]{2,1,0:T(8,128)(2,1)S(1)}, bf16[2,128,256]{2,1,0:T(8,128)(2,1)S(1)}, u32[]{:S(2)}, u32[]{:S(2)}) %collective-permute-start.3) | collective-permute-done | bytes 131104 | tf_op jit(solution)/shard_map/ppermute | solution.py:283
  12.4 0.5 %collective-permute-start.5 = (bf16[128,256]{1,0:T(8,128)(2,1)S(1)}, bf16[128,256]{1,0:T(8,128)(2,1)S(1)}, u32[]{:S(2)}, u32[]{:S(2)}) collective-permute-start(bf16[128,256]{1,0:T(8,128)(2,1)S(1)} %collective-permute-done.vg0), channel_id=1, source_target_pairs={{0,4},{1,5},{2,7},{3,6},{4,0},{5,1},{6,3},{7,2},{8,12},{9,13},{10,... | collective-permute-start | bytes 196616 | tf_op jit(solution)/shard_map/ppermute | solution.py:283
  12.9 1.2 %collective-permute-start.6 = (bf16[128,256]{1,0:T(8,128)(2,1)S(1)}, bf16[128,256]{1,0:T(8,128)(2,1)S(1)}, u32[]{:S(2)}, u32[]{:S(2)}) collective-permute-start(bf16[128,256]{1,0:T(8,128)(2,1)S(1)} %collective-permute-done.vg0), channel_id=1, source_target_pairs={{0,2},{1,3},{2,0},{3,1},{4,6},{5,7},{6,4},{7,5},{8,10},{9,11},{10,... | collective-permute-start | bytes 196616 | tf_op jit(solution)/shard_map/ppermute | solution.py:283
  14.1 0.3 collective-permute-start.7
  14.4 0.4 %collective-permute-done.1.va0 = bf16[128,256]{1,0:T(8,128)(2,1)S(1)} collective-permute-done((bf16[128,256]{1,0:T(8,128)(2,1)S(1)}, bf16[128,256]{1,0:T(8,128)(2,1)S(1)}, u32[]{:S(2)}, u32[]{:S(2)}) %collective-permute-start.1) | collective-permute-done | bytes 65568 | tf_op jit(solution)/shard_map/ppermute | solution.py:283
  14.8 1.6 %collective-permute-start.8 = (bf16[128,256]{1,0:T(8,128)(2,1)S(1)}, bf16[128,256]{1,0:T(8,128)(2,1)S(1)}, u32[]{:S(2)}, u32[]{:S(2)}) collective-permute-start(bf16[128,256]{1,0:T(8,128)(2,1)S(1)} %collective-permute-done.1.va0), channel_id=1, source_target_pairs={{0,4},{1,5},{2,7},{3,6},{4,0},{5,1},{6,3},{7,2},{8,12},{9,13},{10,... | collective-permute-start | bytes 196616 | tf_op jit(solution)/shard_map/ppermute | solution.py:283
  16.3 0.3 collective-permute-done.5.vg3
  16.6 1.6 %collective-permute-start.9 = (bf16[128,256]{1,0:T(8,128)(2,1)S(1)}, bf16[128,256]{1,0:T(8,128)(2,1)S(1)}, u32[]{:S(2)}, u32[]{:S(2)}) collective-permute-start(bf16[128,256]{1,0:T(8,128)(2,1)S(1)} %collective-permute-done.1.va0), channel_id=1, source_target_pairs={{0,2},{1,3},{2,0},{3,1},{4,6},{5,7},{6,4},{7,5},{8,10},{9,11},{10,... | collective-permute-start | bytes 196616 | tf_op jit(solution)/shard_map/ppermute | solution.py:283
  18.2 1.3 %early_pairs.1 = (bf16[512,256]{1,0:T(8,128)(2,1)S(1)}, f32[12,1024]{1,0:T(8,128)S(1)}, f32[256,384]{1,0:T(8,128)S(1)}, f32[128,256]{1,0:T(8,128)S(1)}, f32[128,...) custom-call(bf16[2,3,256,256]{3,2,1,0:T(8,128)(2,1)S(1)} %factor_terms.1.terms, ...), custom_call_target="tpu_custom_call" | custom-call | flops 1000000000 | bytes 1000000 | tf_op jit(solution)/shard_map/early_pairs/pallas_call | solution.py:262
  19.5 1.4 %collective-permute-done.9.va2 = bf16[128,256]{1,0:T(8,128)(2,1)S(1)} collective-permute-done((bf16[128,256]{1,0:T(8,128)(2,1)S(1)}, bf16[128,256]{1,0:T(8,128)(2,1)S(1)}, u32[]{:S(2)}, u32[]{:S(2)}) %collective-permute-start.9) | collective-permute-done | bytes 65568 | tf_op jit(solution)/shard_map/ppermute | solution.py:283
  20.9 0.7 %partner_rows.1 = (f32[4,32]{1,0:T(4,128)S(1)}, f32[4,32]{1,0:T(4,128)S(1)}) custom-call(bf16[2,3,256,256]{3,2,1,0:T(8,128)(2,1)S(1)} %factor_terms.1.terms, bf16[512,256]{1,0:T(8,128)(2,1)S(1)} %get-tuple-element.43.white, bf16[1024,32]{1,0:T(8,128)(2,1)S(1)} %column_pick.1.pick, f32[12,1024]{1,0:T(8,128)S(1)} %get-tuple-element.45.sums, ...), custom_call_target="tpu_custom_call" | custom-call | flops 1000000000 | bytes 1000000 | tf_op jit(solution)/shard_map/partner_rows/pallas_call | solution.py:262
  21.6 1.8 %collective-permute-start.11 = (f32[4,32]{1,0:T(4,128)S(1)}, f32[4,32]{1,0:T(4,128)S(1)}, u32[]{:S(2)}, u32[]{:S(2)}) collective-permute-start(f32[4,32]{1,0:T(4,128)S(1)} %get-tuple-element.51), channel_id=1, source_target_pairs={{0,2},{1,3},{2,0},{3,1},{4,6},{5,7},{6,4},{7,5},{8,10},{9,11},{10,... | collective-permute-start | bytes 1544 | tf_op jit(solution)/shard_map/ppermute | solution.py:283
  23.4 0.4 %collective-permute-start.12 = (f32[4,32]{1,0:T(4,128)S(1)}, f32[4,32]{1,0:T(4,128)S(1)}, u32[]{:S(2)}, u32[]{:S(2)}) collective-permute-start(f32[4,32]{1,0:T(4,128)S(1)} %get-tuple-element.52), channel_id=1, source_target_pairs={{0,4},{1,5},{2,7},{3,6},{4,0},{5,1},{6,3},{7,2},{8,12},{9,13},{10,... | collective-permute-start | bytes 1544 | tf_op jit(solution)/shard_map/ppermute | solution.py:283
  23.9 0.4 %own_rows.1 = f32[4,32]{1,0:T(4,128)S(1)} custom-call(bf16[512,256]{1,0:T(8,128)(2,1)S(1)} %get-tuple-element.43.white, bf16[1024,32]{1,0:T(8,128)(2,1)S(1)} %column_pick.1.pick, f32[12,1024]{1,0:T(8,128)S(1)} %get-tuple-element.45.sums, f32[256,384]{1,0:T(8,128)S(1)} %get-tuple-element.46.g0, bf16[128,256]{1,0:T(8,128)(2,1)S(1)} %collective-permute-done.8.va3, ...), custom_call_target="tpu_custom_call" | custom-call | flops 1000000000 | bytes 1000000 | tf_op jit(solution)/shard_map/own_rows/pallas_call | solution.py:262
  24.3 1.0 %collective-permute-done.11 = f32[4,32]{1,0:T(4,128)S(1)} collective-permute-done((f32[4,32]{1,0:T(4,128)S(1)}, f32[4,32]{1,0:T(4,128)S(1)}, u32[]{:S(2)}, u32[]{:S(2)}) %collective-permute-start.11) | collective-permute-done | bytes 544 | tf_op jit(solution)/shard_map/ppermute | solution.py:283
  25.3 1.8 %collective-permute-done.12 = f32[4,32]{1,0:T(4,128)S(1)} collective-permute-done((f32[4,32]{1,0:T(4,128)S(1)}, f32[4,32]{1,0:T(4,128)S(1)}, u32[]{:S(2)}, u32[]{:S(2)}) %collective-permute-start.12) | collective-permute-done | bytes 544 | tf_op jit(solution)/shard_map/ppermute | solution.py:283
  27.0 1.2 %collective-permute-start.13 = (f32[2,32]{1,0:T(2,128)S(1)}, f32[2,32]{1,0:T(2,128)S(1)}, u32[]{:S(2)}, u32[]{:S(2)}) collective-permute-start(f32[2,32]{1,0:T(2,128)S(1)} %slice.7), channel_id=1, source_target_pairs={{0,8},{1,9},{2,10},{3,11},{4,12},{5,13},{6,14},{7,15},{8,0},{9,1},... | collective-permute-start | bytes 776 | tf_op jit(solution)/shard_map/ppermute | solution.py:283
  28.3 3.3 %collective-permute-done.13 = f32[2,32]{1,0:T(2,128)S(1)} collective-permute-done((f32[2,32]{1,0:T(2,128)S(1)}, f32[2,32]{1,0:T(2,128)S(1)}, u32[]{:S(2)}, u32[]{:S(2)}) %collective-permute-start.13) | collective-permute-done | bytes 288 | tf_op jit(solution)/shard_map/ppermute | solution.py:283
  31.6 0.6 %slice_add_fusion = f32[2,32]{1,0:T(2,128)} fusion(f32[2,32]{1,0:T(2,128)S(1)} %collective-permute-done.13, f32[4,32]{1,0:T(4,128)S(1)} %add_add_fusion), kind=kLoop, calls=%fused_computation.1 | loop fusion | flops 64 | bytes 768 | tf_op jit(solution)/shard_map/add | solution.py:387
  (17 shorter events, 0.0 us)
Async XLA Ops:
  0.0 5.3 %copy-start = (bf16[2,128,256]{2,1,0:T(8,128)(2,1)S(1)}, bf16[2,128,256]{2,1,0:T(8,128)(2,1)}, u32[]{:S(2)}) copy-start(bf16[2,128,256]{2,1,0:T(8,128)(2,1)} %acts.2) | copy-start | bytes 393220
  0.0 5.3 %copy-start.1 = (bf16[2,128,256]{2,1,0:T(8,128)(2,1)S(1)}, bf16[2,128,256]{2,1,0:T(8,128)(2,1)}, u32[]{:S(2)}) copy-start(bf16[2,128,256]{2,1,0:T(8,128)(2,1)} %grads.2) | copy-start | bytes 393220
  0.0 5.1 %copy-start.2 = (s32[2]{0:T(128)S(1)}, s32[2]{0:T(128)}, u32[]{:S(2)}) copy-start(s32[2]{0:T(128)} %param.9) | copy-start | bytes 28
  0.0 8.7 %copy-start.3 = (s32[2]{0:T(128)S(1)}, s32[2]{0:T(128)}, u32[]{:S(2)}) copy-start(s32[2]{0:T(128)} %layer_ids) | copy-start | bytes 28
  1.0 9.5 %collective-permute-start = (bf16[128,256]{1,0:T(8,128)(2,1)S(1)}, bf16[128,256]{1,0:T(8,128)(2,1)S(1)}, u32[]{:S(2)}, u32[]{:S(2)}) collective-permute-start(bf16[128,256]{1,0:T(8,128)(2,1)S(1)} %get-tuple-element.29), channel_id=1, source_target_pairs={{0,8},{1,9},{2,10},{3,11},{4,12},{5,13},{6,14},{7,15},{8,0},{9,1},... | collective-permute-start | bytes 196616 | tf_op jit(solution)/shard_map/ppermute | solution.py:283
  5.4 5.0 %copy-start.4 = (s32[32]{0:T(128)S(1)}, s32[32]{0:T(128)}, u32[]{:S(2)}) copy-start(s32[32]{0:T(128)} %param.11) | copy-start | bytes 388
  5.4 5.4 %collective-permute-start.2 = (bf16[2,128,256]{2,1,0:T(8,128)(2,1)S(1)}, bf16[2,128,256]{2,1,0:T(8,128)(2,1)S(1)}, u32[]{:S(2)}, u32[]{:S(2)}) collective-permute-start(bf16[2,128,256]{2,1,0:T(8,128)(2,1)S(1)} %own.1.u0), channel_id=1, source_target_pairs={{0,4},{1,5},{2,7},{3,6},{4,0},{5,1},{6,3},{7,2},{8,12},{9,13},{10,... | collective-permute-start | bytes 393224 | tf_op jit(solution)/shard_map/ppermute | solution.py:283
  7.1 5.3 %collective-permute-start.3 = (bf16[2,128,256]{2,1,0:T(8,128)(2,1)S(1)}, bf16[2,128,256]{2,1,0:T(8,128)(2,1)S(1)}, u32[]{:S(2)}, u32[]{:S(2)}) collective-permute-start(bf16[2,128,256]{2,1,0:T(8,128)(2,1)S(1)} %own.1.u0), channel_id=1, source_target_pairs={{0,2},{1,3},{2,0},{3,1},{4,6},{5,7},{6,4},{7,5},{8,10},{9,11},{10,... | collective-permute-start | bytes 393224 | tf_op jit(solution)/shard_map/ppermute | solution.py:283
  7.7 4.6 %collective-permute-start.4 = (bf16[2,128,256]{2,1,0:T(8,128)(2,1)S(1)}, bf16[2,128,256]{2,1,0:T(8,128)(2,1)S(1)}, u32[]{:S(2)}, u32[]{:S(2)}) collective-permute-start(bf16[2,128,256]{2,1,0:T(8,128)(2,1)S(1)} %own.1.u0), channel_id=1, source_target_pairs={{0,1},{1,0},{2,3},{3,2},{4,5},{5,4},{6,7},{7,6},{8,9},{9,8},{10,11... | collective-permute-start | bytes 393224 | tf_op jit(solution)/shard_map/ppermute | solution.py:283
  8.4 6.3 %collective-permute-start.1 = (bf16[128,256]{1,0:T(8,128)(2,1)S(1)}, bf16[128,256]{1,0:T(8,128)(2,1)S(1)}, u32[]{:S(2)}, u32[]{:S(2)}) collective-permute-start(bf16[128,256]{1,0:T(8,128)(2,1)S(1)} %away_mask.1), channel_id=1, source_target_pairs={{0,8},{1,9},{2,10},{3,11},{4,12},{5,13},{6,14},{7,15},{8,0},{9,1},... | collective-permute-start | bytes 196616 | tf_op jit(solution)/shard_map/ppermute | solution.py:283
  12.4 4.3 %collective-permute-start.5 = (bf16[128,256]{1,0:T(8,128)(2,1)S(1)}, bf16[128,256]{1,0:T(8,128)(2,1)S(1)}, u32[]{:S(2)}, u32[]{:S(2)}) collective-permute-start(bf16[128,256]{1,0:T(8,128)(2,1)S(1)} %collective-permute-done.vg0), channel_id=1, source_target_pairs={{0,4},{1,5},{2,7},{3,6},{4,0},{5,1},{6,3},{7,2},{8,12},{9,13},{10,... | collective-permute-start | bytes 196616 | tf_op jit(solution)/shard_map/ppermute | solution.py:283
  12.9 5.3 %collective-permute-start.6 = (bf16[128,256]{1,0:T(8,128)(2,1)S(1)}, bf16[128,256]{1,0:T(8,128)(2,1)S(1)}, u32[]{:S(2)}, u32[]{:S(2)}) collective-permute-start(bf16[128,256]{1,0:T(8,128)(2,1)S(1)} %collective-permute-done.vg0), channel_id=1, source_target_pairs={{0,2},{1,3},{2,0},{3,1},{4,6},{5,7},{6,4},{7,5},{8,10},{9,11},{10,... | collective-permute-start | bytes 196616 | tf_op jit(solution)/shard_map/ppermute | solution.py:283
  14.1 4.1 %collective-permute-start.7 = (bf16[128,256]{1,0:T(8,128)(2,1)S(1)}, bf16[128,256]{1,0:T(8,128)(2,1)S(1)}, u32[]{:S(2)}, u32[]{:S(2)}) collective-permute-start(bf16[128,256]{1,0:T(8,128)(2,1)S(1)} %collective-permute-done.vg0), channel_id=1, source_target_pairs={{0,1},{1,0},{2,3},{3,2},{4,5},{5,4},{6,7},{7,6},{8,9},{9,8},{10,11... | collective-permute-start | bytes 196616 | tf_op jit(solution)/shard_map/ppermute | solution.py:283
  14.8 4.8 %collective-permute-start.10 = (bf16[128,256]{1,0:T(8,128)(2,1)S(1)}, bf16[128,256]{1,0:T(8,128)(2,1)S(1)}, u32[]{:S(2)}, u32[]{:S(2)}) collective-permute-start(bf16[128,256]{1,0:T(8,128)(2,1)S(1)} %collective-permute-done.1.va0), channel_id=1, source_target_pairs={{0,1},{1,0},{2,3},{3,2},{4,5},{5,4},{6,7},{7,6},{8,9},{9,8},{10,11... | collective-permute-start | bytes 196616 | tf_op jit(solution)/shard_map/ppermute | solution.py:283
  14.8 4.8 %collective-permute-start.8 = (bf16[128,256]{1,0:T(8,128)(2,1)S(1)}, bf16[128,256]{1,0:T(8,128)(2,1)S(1)}, u32[]{:S(2)}, u32[]{:S(2)}) collective-permute-start(bf16[128,256]{1,0:T(8,128)(2,1)S(1)} %collective-permute-done.1.va0), channel_id=1, source_target_pairs={{0,4},{1,5},{2,7},{3,6},{4,0},{5,1},{6,3},{7,2},{8,12},{9,13},{10,... | collective-permute-start | bytes 196616 | tf_op jit(solution)/shard_map/ppermute | solution.py:283
  16.6 4.3 %collective-permute-start.9 = (bf16[128,256]{1,0:T(8,128)(2,1)S(1)}, bf16[128,256]{1,0:T(8,128)(2,1)S(1)}, u32[]{:S(2)}, u32[]{:S(2)}) collective-permute-start(bf16[128,256]{1,0:T(8,128)(2,1)S(1)} %collective-permute-done.1.va0), channel_id=1, source_target_pairs={{0,2},{1,3},{2,0},{3,1},{4,6},{5,7},{6,4},{7,5},{8,10},{9,11},{10,... | collective-permute-start | bytes 196616 | tf_op jit(solution)/shard_map/ppermute | solution.py:283
  21.6 3.7 %collective-permute-start.11 = (f32[4,32]{1,0:T(4,128)S(1)}, f32[4,32]{1,0:T(4,128)S(1)}, u32[]{:S(2)}, u32[]{:S(2)}) collective-permute-start(f32[4,32]{1,0:T(4,128)S(1)} %get-tuple-element.51), channel_id=1, source_target_pairs={{0,2},{1,3},{2,0},{3,1},{4,6},{5,7},{6,4},{7,5},{8,10},{9,11},{10,... | collective-permute-start | bytes 1544 | tf_op jit(solution)/shard_map/ppermute | solution.py:283
  23.4 3.6 %collective-permute-start.12 = (f32[4,32]{1,0:T(4,128)S(1)}, f32[4,32]{1,0:T(4,128)S(1)}, u32[]{:S(2)}, u32[]{:S(2)}) collective-permute-start(f32[4,32]{1,0:T(4,128)S(1)} %get-tuple-element.52), channel_id=1, source_target_pairs={{0,4},{1,5},{2,7},{3,6},{4,0},{5,1},{6,3},{7,2},{8,12},{9,13},{10,... | collective-permute-start | bytes 1544 | tf_op jit(solution)/shard_map/ppermute | solution.py:283
  27.0 4.5 %collective-permute-start.13 = (f32[2,32]{1,0:T(2,128)S(1)}, f32[2,32]{1,0:T(2,128)S(1)}, u32[]{:S(2)}, u32[]{:S(2)}) collective-permute-start(f32[2,32]{1,0:T(2,128)S(1)} %slice.7), channel_id=1, source_target_pairs={{0,8},{1,9},{2,10},{3,11},{4,12},{5,13},{6,14},{7,15},{8,0},{9,1},... | collective-permute-start | bytes 776 | tf_op jit(solution)/shard_map/ppermute | solution.py:283

commit v13 on v11

--- a/solution.py
+++ b/solution.py
@@ -52,6 +52,10 @@
     return jnp.take(part_scores, flagged, axis=1)
 
 
+INNER = range(4, 12)
+OUTER = (0, 1, 2, 3, 12, 13, 14, 15)
+
+
 def z_near(d):
     return d ^ 4 ^ ((d >> 1) & 1)
 
@@ -168,8 +172,8 @@
             sums[row : row + per, at : at + n] = block(seq_len, left, tok[slot])
 
 
-def return_kernel(seq_len, per, terms, white, pick, sums, u3, u2, u1, v3, v2, v1, *outs):
-    v = (v1, v2, v3)
+def return_kernel(seq_len, per, terms, white, pick, sums, u3, u2, u1, v2_in, v3, v2_out, v1, *outs):
+    v = (v1, v2_in[...] + v2_out[...], v3)
     n = u1.shape[1]
     late = [[v[i][w] for w in range(2)] for i in range(3)]
     tok = [[u[w] for w in range(2)] for u in (u1, u2, u3)]
@@ -193,8 +197,8 @@
         out[...] = picked[i * r : (i + 1) * r]
 
 
-def rows_kernel(seq_len, per, white, pick, sums, v3, v2, v1, out):
-    v = (v1, v2, v3)
+def rows_kernel(seq_len, per, white, pick, sums, v2_in, v3, v2_out, v1, out):
+    v = (v1, v2_in[...] + v2_out[...], v3)
     n = v[0].shape[1]
     r = 2 * per
     mine = [white[w, : 2 * n] for w in range(2)]
@@ -221,14 +225,13 @@
 
 
 def paired(activations, out_grads, lengths, layer_ids, flagged, act_factor, grad_factor):
-    size = 16
     per = lengths.shape[0]
     tokens, rank = activations.shape[1:]
     seq_len = tokens // per
     f32, bf16 = jnp.float32, jnp.bfloat16
 
-    def send(x, to):
-        return lax.ppermute(x, "blk", [(d, to(d)) for d in range(size)])
+    def send(x, to, among=range(16)):
+        return lax.ppermute(x, "blk", [(d, to(d)) for d in among])
 
     def opposite(d):
         return d ^ 8
@@ -270,7 +273,8 @@
         [pltpu.VMEM((2, rank, rank), f32), pltpu.SemaphoreType.DMA((2,))],
     )
     v, terms, pick = lax.optimization_barrier((v, terms, pick))
-    late = [send(v, to) for to in ways]
+    late = [send(v, lambda d: d ^ 2, INNER)]
+    late += [send(v, z_near), send(v, lambda d: d ^ 2, OUTER), send(v, lambda d: d ^ 1)]
     white, sums = call(
         functools.partial(early_kernel, seq_len, per),
         "early_pairs",

time: 28.9 us -> 32.6 us (1.13)
  starting transfers between devices: 13.3 us -> 16.3 us
  waiting for transfers between devices: 9.44 us -> 10 us
    ppermute x10 -> x11, starting transfers between devices: 13.3 us -> 16.3 us  [send(): return lax.ppermute(x, 'blk', [(d, to(d)) for d in among])]
    ppermute x10 -> x11, waiting for transfers between devices: 9.44 us -> 10 us  [send(): return lax.ppermute(x, 'blk', [(d, to(d)) for d in among])]
  transfers between devices with their start and end apart: 10 -> 11, of which waited for: 6 -> 6; matrix products, arithmetic and copies ran while one was open for 0% -> 0% of each run, Pallas kernels for 12% -> 10%
where the time goes in v13:
time: 32.6 us; the launch traced here: 32.4 us
  starting transfers between devices  16.3 us (50%)
  waiting for transfers between devices  10 us (31%)
  Pallas kernels  5.4 us (17%)
  other arithmetic  0.57 us (2%)
    ppermute x11, starting transfers between devices, send(): return lax.ppermute(x, 'blk', [(d, to(d)) for d in among])  16.3 us
    ppermute x11, waiting for transfers between devices, send(): return lax.ppermute(x, 'blk', [(d, to(d)) for d in among])  10 us
    pallas_call x7, Pallas kernels, call(): pl.pallas_call(kernel, out_shape=out_shape, in_specs=specs + [vmem] * (le...  5.4 us
  transfers between devices with their start and end apart: 11, of which 6 were waited for; matrix products, arithmetic and copies ran while one was open for 0% of the time, Pallas kernels for 10%

profile of v13, /device:TPU:0, one launch (start us, length us, event | category | flops | bytes accessed | tf_op | source)
XLA Modules:
  0.0 32.4 jit_solution(2034616566952129629)
XLA Ops:
  0.0 1.0 %away.1.unit = bf16[2,128,256]{2,1,0:T(8,128)(2,1)S(1)} custom-call(bf16[2,128,256]{2,1,0:T(8,128)(2,1)} %acts.2, bf16[2,128,256]{2,1,0:T(8,128)(2,1)} %grads.2), custom_call_target="tpu_custom_call" | custom-call | flops 3000000000 | bytes 1000000 | tf_op jit(solution)/shard_map/away/pallas_call | solution.py:214
  1.0 0.0 copy-done
  1.0 0.2 away_mask.1
  1.1 4.1 %collective-permute-start = (bf16[2,128,256]{2,1,0:T(8,128)(2,1)S(1)}, bf16[2,128,256]{2,1,0:T(8,128)(2,1)S(1)}, u32[]{:S(2)}, u32[]{:S(2)}) collective-permute-start(bf16[2,128,256]{2,1,0:T(8,128)(2,1)S(1)} %away_mask.1), channel_id=1, source_target_pairs={{0,8},{1,9},{2,10},{3,11},{4,12},{5,13},{6,14},{7,15},{8,0},{9,1},... | collective-permute-start | bytes 393224 | tf_op jit(solution)/shard_map/ppermute | solution.py:234
  5.3 0.0 copy-done.3
  5.3 0.1 own.1.u0
  5.4 1.6 %collective-permute-start.1 = (bf16[2,128,256]{2,1,0:T(8,128)(2,1)S(1)}, bf16[2,128,256]{2,1,0:T(8,128)(2,1)S(1)}, u32[]{:S(2)}, u32[]{:S(2)}) collective-permute-start(bf16[2,128,256]{2,1,0:T(8,128)(2,1)S(1)} %own.1.u0), channel_id=1, source_target_pairs={{0,4},{1,5},{2,7},{3,6},{4,0},{5,1},{6,3},{7,2},{8,12},{9,13},{10,... | collective-permute-start | bytes 393224 | tf_op jit(solution)/shard_map/ppermute | solution.py:234
  7.1 0.7 %collective-permute-start.2 = (bf16[2,128,256]{2,1,0:T(8,128)(2,1)S(1)}, bf16[2,128,256]{2,1,0:T(8,128)(2,1)S(1)}, u32[]{:S(2)}, u32[]{:S(2)}) collective-permute-start(bf16[2,128,256]{2,1,0:T(8,128)(2,1)S(1)} %own.1.u0), channel_id=1, source_target_pairs={{0,2},{1,3},{2,0},{3,1},{4,6},{5,7},{6,4},{7,5},{8,10},{9,11},{10,... | collective-permute-start | bytes 393224 | tf_op jit(solution)/shard_map/ppermute | solution.py:234
  7.7 0.7 %collective-permute-start.3 = (bf16[2,128,256]{2,1,0:T(8,128)(2,1)S(1)}, bf16[2,128,256]{2,1,0:T(8,128)(2,1)S(1)}, u32[]{:S(2)}, u32[]{:S(2)}) collective-permute-start(bf16[2,128,256]{2,1,0:T(8,128)(2,1)S(1)} %own.1.u0), channel_id=1, source_target_pairs={{0,1},{1,0},{2,3},{3,2},{4,5},{5,4},{6,7},{7,6},{8,9},{9,8},{10,11... | collective-permute-start | bytes 393224 | tf_op jit(solution)/shard_map/ppermute | solution.py:234
  8.4 1.7 %factor_terms.1 = (bf16[2,3,256,256]{3,2,1,0:T(8,128)(2,1)S(1)}, bf16[1024,32]{1,0:T(8,128)(2,1)S(1)}) custom-call(s32[2]{0:T(128)S(1)} %copy-done.1, s32[1,32]{1,0:T(1,128)S(1)} %bitcast.4, f32[16,256,256]{2,1,0:T(8,128)} %act_f.1, f32[16,256,256]{2,1,0:T(8,128)} %grad_f.1), custom_call_target="tpu_custom_call" | custom-call | flops 1000000000 | bytes 1000000 | tf_op jit(solution)/shard_map/factor_terms/pallas_call | solution.py:214
  10.1 1.6 %collective-permute-done.v = bf16[2,128,256]{2,1,0:T(8,128)(2,1)S(1)} collective-permute-done((bf16[2,128,256]{2,1,0:T(8,128)(2,1)S(1)}, bf16[2,128,256]{2,1,0:T(8,128)(2,1)S(1)}, u32[]{:S(2)}, u32[]{:S(2)}) %collective-permute-start) | collective-permute-done | bytes 131104 | tf_op jit(solution)/shard_map/ppermute | solution.py:234
  11.7 0.7 %collective-permute-start.4 = (bf16[2,128,256]{2,1,0:T(8,128)(2,1)S(1)}, bf16[2,128,256]{2,1,0:T(8,128)(2,1)S(1)}, u32[]{:S(2)}, u32[]{:S(2)}) collective-permute-start(bf16[2,128,256]{2,1,0:T(8,128)(2,1)S(1)} %collective-permute-done.v), channel_id=1, source_target_pairs={{4,6},{5,7},{6,4},{7,5},{8,10},{9,11},{10,8},{11,9},{20,22},{21,23... | collective-permute-start | bytes 393224 | tf_op jit(solution)/shard_map/ppermute | solution.py:234
  12.4 3.4 %collective-permute-start.5 = (bf16[2,128,256]{2,1,0:T(8,128)(2,1)S(1)}, bf16[2,128,256]{2,1,0:T(8,128)(2,1)S(1)}, u32[]{:S(2)}, u32[]{:S(2)}) collective-permute-start(bf16[2,128,256]{2,1,0:T(8,128)(2,1)S(1)} %collective-permute-done.v), channel_id=1, source_target_pairs={{0,4},{1,5},{2,7},{3,6},{4,0},{5,1},{6,3},{7,2},{8,12},{9,13},{10,... | collective-permute-start | bytes 393224 | tf_op jit(solution)/shard_map/ppermute | solution.py:234
  15.8 0.0 collective-permute-done.1.u3
  15.8 1.9 %collective-permute-start.6 = (bf16[2,128,256]{2,1,0:T(8,128)(2,1)S(1)}, bf16[2,128,256]{2,1,0:T(8,128)(2,1)S(1)}, u32[]{:S(2)}, u32[]{:S(2)}) collective-permute-start(bf16[2,128,256]{2,1,0:T(8,128)(2,1)S(1)} %collective-permute-done.v), channel_id=1, source_target_pairs={{0,2},{1,3},{2,0},{3,1},{12,14},{13,15},{14,12},{15,13},{16,18},{1... | collective-permute-start | bytes 393224 | tf_op jit(solution)/shard_map/ppermute | solution.py:234
  17.7 0.0 collective-permute-done.2.u2
  17.7 0.4 %collective-permute-start.7 = (bf16[2,128,256]{2,1,0:T(8,128)(2,1)S(1)}, bf16[2,128,256]{2,1,0:T(8,128)(2,1)S(1)}, u32[]{:S(2)}, u32[]{:S(2)}) collective-permute-start(bf16[2,128,256]{2,1,0:T(8,128)(2,1)S(1)} %collective-permute-done.v), channel_id=1, source_target_pairs={{0,1},{1,0},{2,3},{3,2},{4,5},{5,4},{6,7},{7,6},{8,9},{9,8},{10,11... | collective-permute-start | bytes 393224 | tf_op jit(solution)/shard_map/ppermute | solution.py:234
  18.1 0.0 collective-permute-done.3.u1
  18.1 1.0 %early_pairs.1 = (bf16[2,512,256]{2,1,0:T(8,128)(2,1)S(1)}, f32[12,1024]{1,0:T(8,128)S(1)}) custom-call(bf16[2,3,256,256]{3,2,1,0:T(8,128)(2,1)S(1)} %get-tuple-element.19.terms, bf16[2,128,256]{2,1,0:T(8,128)(2,1)S(1)} %own.1.u0, bf16[2,128,256]{2,1,0:T(8,128)(2,1)S(1)} %collective-permute-done.v, bf16[2,128,256]{2,1,0:T(8,128)(2,1)S(1)} %collective-permute-done.1.u3, ...), custom_call_target="tpu_custom_call" | custom-call | flops 1000000000 | bytes 1000000 | tf_op jit(solution)/shard_map/early_pairs/pallas_call | solution.py:214
  19.1 0.0 collective-permute-done.4.v2_in
  19.1 0.1 collective-permute-done.5.v3
  19.2 3.5 %collective-permute-done.6.v2_out = bf16[2,128,256]{2,1,0:T(8,128)(2,1)S(1)} collective-permute-done((bf16[2,128,256]{2,1,0:T(8,128)(2,1)S(1)}, bf16[2,128,256]{2,1,0:T(8,128)(2,1)S(1)}, u32[]{:S(2)}, u32[]{:S(2)}) %collective-permute-start.6) | collective-permute-done | bytes 131104 | tf_op jit(solution)/shard_map/ppermute | solution.py:234
  22.6 0.0 collective-permute-done.7.v1
  22.6 1.0 %return_rows.1 = (f32[4,32]{1,0:T(4,128)S(1)}, f32[4,32]{1,0:T(4,128)S(1)}) custom-call(bf16[2,3,256,256]{3,2,1,0:T(8,128)(2,1)S(1)} %get-tuple-element.19.terms, bf16[2,512,256]{2,1,0:T(8,128)(2,1)S(1)} %get-tuple-element.24.white, bf16[1024,32]{1,0:T(8,128)(2,1)S(1)} %get-tuple-element.25.pick, f32[12,1024]{1,0:T(8,128)S(1)} %get-tuple-element.26.sums, ...), custom_call_target="tpu_custom_call" | custom-call | flops 1000000000 | bytes 1000000 | tf_op jit(solution)/shard_map/return_rows/pallas_call | solution.py:214
  23.6 0.0 collective-permute-start.9
  23.7 1.1 %collective-permute-start.8 = (f32[4,32]{1,0:T(4,128)S(1)}, f32[4,32]{1,0:T(4,128)S(1)}, u32[]{:S(2)}, u32[]{:S(2)}) collective-permute-start(f32[4,32]{1,0:T(4,128)S(1)} %get-tuple-element.27), channel_id=1, source_target_pairs={{0,2},{1,3},{2,0},{3,1},{4,6},{5,7},{6,4},{7,5},{8,10},{9,11},{10,... | collective-permute-start | bytes 1544 | tf_op jit(solution)/shard_map/ppermute | solution.py:234
  24.8 0.5 %own_rows.1 = f32[4,32]{1,0:T(4,128)S(1)} custom-call(bf16[2,512,256]{2,1,0:T(8,128)(2,1)S(1)} %get-tuple-element.24.white, bf16[1024,32]{1,0:T(8,128)(2,1)S(1)} %get-tuple-element.25.pick, f32[12,1024]{1,0:T(8,128)S(1)} %get-tuple-element.26.sums, bf16[2,128,256]{2,1,0:T(8,128)(2,1)S(1)} %collective-permute-done.4.v2_in, ...), custom_call_target="tpu_custom_call" | custom-call | flops 1000000000 | bytes 1000000 | tf_op jit(solution)/shard_map/own_rows/pallas_call | solution.py:214
  25.3 1.9 %collective-permute-done.9 = f32[4,32]{1,0:T(4,128)S(1)} collective-permute-done((f32[4,32]{1,0:T(4,128)S(1)}, f32[4,32]{1,0:T(4,128)S(1)}, u32[]{:S(2)}, u32[]{:S(2)}) %collective-permute-start.9) | collective-permute-done | bytes 544 | tf_op jit(solution)/shard_map/ppermute | solution.py:234
  27.2 0.1 collective-permute-done.8
  27.3 1.6 %collective-permute-start.10 = (f32[2,32]{1,0:T(2,128)S(1)}, f32[2,32]{1,0:T(2,128)S(1)}, u32[]{:S(2)}, u32[]{:S(2)}) collective-permute-start(f32[2,32]{1,0:T(2,128)S(1)} %slice.7), channel_id=1, source_target_pairs={{0,8},{1,9},{2,10},{3,11},{4,12},{5,13},{6,14},{7,15},{8,0},{9,1},... | collective-permute-start | bytes 776 | tf_op jit(solution)/shard_map/ppermute | solution.py:234
  28.9 2.9 %collective-permute-done.10 = f32[2,32]{1,0:T(2,128)S(1)} collective-permute-done((f32[2,32]{1,0:T(2,128)S(1)}, f32[2,32]{1,0:T(2,128)S(1)}, u32[]{:S(2)}, u32[]{:S(2)}) %collective-permute-start.10) | collective-permute-done | bytes 288 | tf_op jit(solution)/shard_map/ppermute | solution.py:234
  31.9 0.6 %slice_add_fusion = f32[2,32]{1,0:T(2,128)} fusion(f32[2,32]{1,0:T(2,128)S(1)} %collective-permute-done.10, f32[4,32]{1,0:T(4,128)S(1)} %add_add_fusion), kind=kLoop, calls=%fused_computation.1 | loop fusion | flops 64 | bytes 768 | tf_op jit(solution)/shard_map/add | solution.py:307
  (10 shorter events, 0.0 us)
Async XLA Ops:
  0.0 5.3 %copy-start.3 = (bf16[2,128,256]{2,1,0:T(8,128)(2,1)S(1)}, bf16[2,128,256]{2,1,0:T(8,128)(2,1)}, u32[]{:S(2)}) copy-start(bf16[2,128,256]{2,1,0:T(8,128)(2,1)} %acts.2) | copy-start | bytes 393220
  0.0 5.3 %copy-start.4 = (bf16[2,128,256]{2,1,0:T(8,128)(2,1)S(1)}, bf16[2,128,256]{2,1,0:T(8,128)(2,1)}, u32[]{:S(2)}) copy-start(bf16[2,128,256]{2,1,0:T(8,128)(2,1)} %grads.2) | copy-start | bytes 393220
  0.0 1.0 %copy-start = (s32[2]{0:T(128)S(1)}, s32[2]{0:T(128)}, u32[]{:S(2)}) copy-start(s32[2]{0:T(128)} %param.9) | copy-start | bytes 28
  0.0 8.4 %copy-start.1 = (s32[2]{0:T(128)S(1)}, s32[2]{0:T(128)}, u32[]{:S(2)}) copy-start(s32[2]{0:T(128)} %layer_ids.1) | copy-start | bytes 28
  0.0 8.4 %copy-start.2 = (s32[32]{0:T(128)S(1)}, s32[32]{0:T(128)}, u32[]{:S(2)}) copy-start(s32[32]{0:T(128)} %param.11) | copy-start | bytes 388
  1.1 10.5 %collective-permute-start = (bf16[2,128,256]{2,1,0:T(8,128)(2,1)S(1)}, bf16[2,128,256]{2,1,0:T(8,128)(2,1)S(1)}, u32[]{:S(2)}, u32[]{:S(2)}) collective-permute-start(bf16[2,128,256]{2,1,0:T(8,128)(2,1)S(1)} %away_mask.1), channel_id=1, source_target_pairs={{0,8},{1,9},{2,10},{3,11},{4,12},{5,13},{6,14},{7,15},{8,0},{9,1},... | collective-permute-start | bytes 393224 | tf_op jit(solution)/shard_map/ppermute | solution.py:234
  5.4 10.3 %collective-permute-start.1 = (bf16[2,128,256]{2,1,0:T(8,128)(2,1)S(1)}, bf16[2,128,256]{2,1,0:T(8,128)(2,1)S(1)}, u32[]{:S(2)}, u32[]{:S(2)}) collective-permute-start(bf16[2,128,256]{2,1,0:T(8,128)(2,1)S(1)} %own.1.u0), channel_id=1, source_target_pairs={{0,4},{1,5},{2,7},{3,6},{4,0},{5,1},{6,3},{7,2},{8,12},{9,13},{10,... | collective-permute-start | bytes 393224 | tf_op jit(solution)/shard_map/ppermute | solution.py:234
  7.1 10.6 %collective-permute-start.2 = (bf16[2,128,256]{2,1,0:T(8,128)(2,1)S(1)}, bf16[2,128,256]{2,1,0:T(8,128)(2,1)S(1)}, u32[]{:S(2)}, u32[]{:S(2)}) collective-permute-start(bf16[2,128,256]{2,1,0:T(8,128)(2,1)S(1)} %own.1.u0), channel_id=1, source_target_pairs={{0,2},{1,3},{2,0},{3,1},{4,6},{5,7},{6,4},{7,5},{8,10},{9,11},{10,... | collective-permute-start | bytes 393224 | tf_op jit(solution)/shard_map/ppermute | solution.py:234
  7.7 10.4 %collective-permute-start.3 = (bf16[2,128,256]{2,1,0:T(8,128)(2,1)S(1)}, bf16[2,128,256]{2,1,0:T(8,128)(2,1)S(1)}, u32[]{:S(2)}, u32[]{:S(2)}) collective-permute-start(bf16[2,128,256]{2,1,0:T(8,128)(2,1)S(1)} %own.1.u0), channel_id=1, source_target_pairs={{0,1},{1,0},{2,3},{3,2},{4,5},{5,4},{6,7},{7,6},{8,9},{9,8},{10,11... | collective-permute-start | bytes 393224 | tf_op jit(solution)/shard_map/ppermute | solution.py:234
  11.7 7.4 %collective-permute-start.4 = (bf16[2,128,256]{2,1,0:T(8,128)(2,1)S(1)}, bf16[2,128,256]{2,1,0:T(8,128)(2,1)S(1)}, u32[]{:S(2)}, u32[]{:S(2)}) collective-permute-start(bf16[2,128,256]{2,1,0:T(8,128)(2,1)S(1)} %collective-permute-done.v), channel_id=1, source_target_pairs={{4,6},{5,7},{6,4},{7,5},{8,10},{9,11},{10,8},{11,9},{20,22},{21,23... | collective-permute-start | bytes 393224 | tf_op jit(solution)/shard_map/ppermute | solution.py:234
  12.4 6.8 %collective-permute-start.5 = (bf16[2,128,256]{2,1,0:T(8,128)(2,1)S(1)}, bf16[2,128,256]{2,1,0:T(8,128)(2,1)S(1)}, u32[]{:S(2)}, u32[]{:S(2)}) collective-permute-start(bf16[2,128,256]{2,1,0:T(8,128)(2,1)S(1)} %collective-permute-done.v), channel_id=1, source_target_pairs={{0,4},{1,5},{2,7},{3,6},{4,0},{5,1},{6,3},{7,2},{8,12},{9,13},{10,... | collective-permute-start | bytes 393224 | tf_op jit(solution)/shard_map/ppermute | solution.py:234
  15.8 6.9 %collective-permute-start.6 = (bf16[2,128,256]{2,1,0:T(8,128)(2,1)S(1)}, bf16[2,128,256]{2,1,0:T(8,128)(2,1)S(1)}, u32[]{:S(2)}, u32[]{:S(2)}) collective-permute-start(bf16[2,128,256]{2,1,0:T(8,128)(2,1)S(1)} %collective-permute-done.v), channel_id=1, source_target_pairs={{0,2},{1,3},{2,0},{3,1},{12,14},{13,15},{14,12},{15,13},{16,18},{1... | collective-permute-start | bytes 393224 | tf_op jit(solution)/shard_map/ppermute | solution.py:234
  17.7 4.9 %collective-permute-start.7 = (bf16[2,128,256]{2,1,0:T(8,128)(2,1)S(1)}, bf16[2,128,256]{2,1,0:T(8,128)(2,1)S(1)}, u32[]{:S(2)}, u32[]{:S(2)}) collective-permute-start(bf16[2,128,256]{2,1,0:T(8,128)(2,1)S(1)} %collective-permute-done.v), channel_id=1, source_target_pairs={{0,1},{1,0},{2,3},{3,2},{4,5},{5,4},{6,7},{7,6},{8,9},{9,8},{10,11... | collective-permute-start | bytes 393224 | tf_op jit(solution)/shard_map/ppermute | solution.py:234
  23.6 3.6 %collective-permute-start.9 = (f32[4,32]{1,0:T(4,128)S(1)}, f32[4,32]{1,0:T(4,128)S(1)}, u32[]{:S(2)}, u32[]{:S(2)}) collective-permute-start(f32[4,32]{1,0:T(4,128)S(1)} %get-tuple-element.28), channel_id=1, source_target_pairs={{0,4},{1,5},{2,7},{3,6},{4,0},{5,1},{6,3},{7,2},{8,12},{9,13},{10,... | collective-permute-start | bytes 1544 | tf_op jit(solution)/shard_map/ppermute | solution.py:234
  23.7 3.7 %collective-permute-start.8 = (f32[4,32]{1,0:T(4,128)S(1)}, f32[4,32]{1,0:T(4,128)S(1)}, u32[]{:S(2)}, u32[]{:S(2)}) collective-permute-start(f32[4,32]{1,0:T(4,128)S(1)} %get-tuple-element.27), channel_id=1, source_target_pairs={{0,2},{1,3},{2,0},{3,1},{4,6},{5,7},{6,4},{7,5},{8,10},{9,11},{10,... | collective-permute-start | bytes 1544 | tf_op jit(solution)/shard_map/ppermute | solution.py:234
  27.3 4.5 %collective-permute-start.10 = (f32[2,32]{1,0:T(2,128)S(1)}, f32[2,32]{1,0:T(2,128)S(1)}, u32[]{:S(2)}, u32[]{:S(2)}) collective-permute-start(f32[2,32]{1,0:T(2,128)S(1)} %slice.7), channel_id=1, source_target_pairs={{0,8},{1,9},{2,10},{3,11},{4,12},{5,13},{6,14},{7,15},{8,0},{9,1},... | collective-permute-start | bytes 776 | tf_op jit(solution)/shard_map/ppermute | solution.py:234

commit v14 on v11

--- a/solution.py
+++ b/solution.py
@@ -145,64 +145,86 @@
             rest = rest - term.astype(jnp.float32)
 
 
-def early_kernel(seq_len, per, terms, u0, v, u3, u2, u1, white, sums):
+def early_kernel(seq_len, per, terms, u0, v, u3, u2, u1, white, mine, side):
     n = u0.shape[1]
-    mine, x, z = [], [], []
+    rows = []
     for w in range(2):
-        rows = whiten(stack(u0[w], v[w], u2[w], u3[w]), terms.at[w])
-        white[w] = rows
-        mine.append(rows[: 2 * n])
-        x.append(rows[2 * n : 3 * n])
-        z.append(rows[3 * n :])
+        white[w] = whiten(stack(u0[w], v[w], u2[w], u3[w], u1[w]), terms.at[w])
+        rows.append(white[w])
+    left = {
+        0: [r[: 2 * n] for r in rows],
+        2: [r[2 * n : 3 * n] for r in rows],
+        3: [r[3 * n : 4 * n] for r in rows],
+    }
     tok = [[u[w] for w in range(2)] for u in (u0, u1, u2, u3)]
-    own = [stack(u0[w], v[w]) for w in range(2)]
-    sums[...] = jnp.zeros_like(sums)
-    r = 2 * per
-    sums[0:r, 0 : 2 * n] = block(seq_len, mine, own)
+    mine[...] = jnp.zeros_like(mine)
+    mine[:, 0 : 2 * n] = block(seq_len, left[0], [stack(u0[w], v[w]) for w in range(2)])
     for slot in (1, 2, 3):
         at = 2 * n * slot
-        sums[0:r, at : at + n] = block(seq_len, mine, tok[slot])
-    for row, left, slots in ((r, x, (1, 3)), (2 * r, z, (1, 2))):
-        for slot in slots:
-            at = 2 * n * slot
-            sums[row : row + per, at : at + n] = block(seq_len, left, tok[slot])
-
-
-def return_kernel(seq_len, per, terms, white, pick, sums, u3, u2, u1, v3, v2, v1, *outs):
-    v = (v1, v2, v3)
-    n = u1.shape[1]
-    late = [[v[i][w] for w in range(2)] for i in range(3)]
-    tok = [[u[w] for w in range(2)] for u in (u1, u2, u3)]
-    both = [[stack(tok[i][w], late[i][w]) for w in range(2)] for i in range(3)]
-    fresh = [whiten(stack(late[1][w], late[2][w]), terms.at[w]) for w in range(2)]
-    zeros = jnp.zeros((per, n), jnp.float32)
-    wide = jnp.zeros((per, 2 * n), jnp.float32)
-    lines = []
-    for i, other in ((1, 2), (2, 1)):
-        early = [white[w, (i + 1) * n : (i + 2) * n] for w in range(2)]
-        got = block(seq_len, early, [stack(late[0][w], late[other][w]) for w in range(2)])
-        cols = {1: jnp.concatenate([zeros, got[:, :n]], axis=1)}
-        cols[other + 1] = jnp.concatenate([zeros, got[:, n:]], axis=1)
-        lines.append(jnp.concatenate([cols.get(slot, wide) for slot in range(4)], axis=1))
-        new = [fresh[w][(i - 1) * n : i * n] for w in range(2)]
-        cols = {1: block(seq_len, new, both[0]), other + 1: block(seq_len, new, both[other])}
-        lines.append(jnp.concatenate([cols.get(slot, wide) for slot in range(4)], axis=1))
-    r = 2 * per
-    picked = pick_columns(sums[r:, :] + stack(*lines), pick)
-    for i, out in enumerate(outs):
-        out[...] = picked[i * r : (i + 1) * r]
-
-
-def rows_kernel(seq_len, per, white, pick, sums, v3, v2, v1, out):
-    v = (v1, v2, v3)
-    n = v[0].shape[1]
-    r = 2 * per
-    mine = [white[w, : 2 * n] for w in range(2)]
-    line = [jnp.zeros((r, 2 * n), jnp.float32)]
-    for i in range(3):
-        right = [v[i][w] for w in range(2)]
-        line += [jnp.zeros((r, n), jnp.float32), block(seq_len, mine, right)]
-    out[...] = pick_columns(sums[:r, :] + jnp.concatenate(line, axis=1), pick)
+        mine[:, at : at + n] = block(seq_len, left[0], tok[slot])
+    side[...] = jnp.zeros_like(side)
+    for row, slot, other in ((0, 2, 3), (2 * per, 3, 2)):
+        for column in (1, other):
+            at = 2 * n * (column - 1)
+            side[row : row + per, at : at + n] = block(seq_len, left[slot], tok[column])
+
+
+def core_kernel(seq_len, per, terms, white, v1, mine, side, white1, mine_out, side_out):
+    n = v1.shape[1]
+    tok = [v1[w] for w in range(2)]
+    for w in range(2):
+        white1[w] = whiten(tok[w], terms.at[w])
+    mine_out[...] = mine[...]
+    mine_out[:, 3 * n : 4 * n] = block(seq_len, [white[w, : 2 * n] for w in range(2)], tok)
+    side_out[...] = side[...]
+    got = block(seq_len, [white[w, 2 * n : 4 * n] for w in range(2)], tok)
+    for i, row in enumerate((0, 2 * per)):
+        side_out[row : row + per, n : 2 * n] = got[i * per : (i + 1) * per]
+
+
+def z_kernel(seq_len, per, terms, white, u2, u1, v1, v3, side, white3, side_out):
+    n = v1.shape[1]
+    tok = [v3[w] for w in range(2)]
+    fresh = [whiten(tok[w], terms.at[w]) for w in range(2)]
+    for w in range(2):
+        white3[w] = fresh[w]
+    side_out[...] = side[...]
+    side_out[0:per, 5 * n : 6 * n] = block(
+        seq_len, [white[w, 2 * n : 3 * n] for w in range(2)], tok
+    )
+    side_out[3 * per : 4 * per, 0 : 3 * n] = block(
+        seq_len, fresh, [stack(u1[w], v1[w], u2[w]) for w in range(2)]
+    )
+
+
+def return_kernel(seq_len, per, white, white1, white3, pick, side, v2, by_x, by_z):
+    n = v2.shape[1]
+    tok = [v2[w] for w in range(2)]
+    columns = [
+        stack(white[w, 4 * n : 5 * n], white1[w], white[w, 3 * n : 4 * n], white3[w])
+        for w in range(2)
+    ]
+    by_row = block(seq_len, tok, columns)
+    by_column = block(
+        seq_len, [stack(white[w, 3 * n : 4 * n], white3[w]) for w in range(2)], tok
+    )
+    zeros = jnp.zeros((per, 2 * n), jnp.float32)
+    none = jnp.zeros((per, 6 * n), jnp.float32)
+    row = jnp.concatenate([by_row[:, : 2 * n], zeros, by_row[:, 2 * n :]], axis=1)
+    lead = jnp.zeros((2 * per, 3 * n), jnp.float32)
+    both = jnp.concatenate([lead, by_column, lead[:, : 2 * n]], axis=1)
+    picked = pick_columns(side[...] + stack(none, row, both), pick.at[2 * n :])
+    by_x[...] = picked[: 2 * per]
+    by_z[...] = picked[2 * per :]
+
+
+def rows_kernel(seq_len, per, white, pick, mine, v3, v2, out):
+    n = v2.shape[1]
+    left = [white[w, : 2 * n] for w in range(2)]
+    got = block(seq_len, left, [stack(v2[w], v3[w]) for w in range(2)])
+    zeros = jnp.zeros((2 * per, n), jnp.float32)
+    late = jnp.concatenate([zeros] * 5 + [got[:, :n], zeros, got[:, n:]], axis=1)
+    out[...] = pick_columns(mine[...] + late, pick)
 
 
 def call(kernel, name, flops, limit, operands, specs, out_shape, scratch=(), **more):
@@ -271,34 +293,40 @@
     )
     v, terms, pick = lax.optimization_barrier((v, terms, pick))
     late = [send(v, to) for to in ways]
-    white, sums = call(
-        functools.partial(early_kernel, seq_len, per),
+    whole = shape((2 * per, 8 * tokens), f32)
+    sides = shape((4 * per, 6 * tokens), f32)
+    rows = shape((2 * per, columns), f32)
+    u3, u2, u1 = near
+    v3, v2, v1 = late
+
+    def kernel(body, name, operands, out_shape, **more):
+        body = functools.partial(body, seq_len, per)
+        return call(body, name, 10**9, 40, operands, [], out_shape, **more)
+
+    white, mine, side = kernel(
+        early_kernel,
         "early_pairs",
-        10**9,
-        40,
-        (terms, own, v, *near),
-        [],
-        (shape((2, 4 * tokens, rank), bf16), shape((6 * per, 8 * tokens), f32)),
-    )
-    rows = shape((2 * per, columns), f32)
-    by_x, by_z = call(
-        functools.partial(return_kernel, seq_len, per),
-        "return_rows",
-        10**9,
-        40,
-        (terms, white, pick, sums, *near, *late),
-        [],
-        (rows, rows),
-    )
-    mine = call(
-        functools.partial(rows_kernel, seq_len, per),
-        "own_rows",
-        10**9,
-        40,
-        (white, pick, sums, *late),
-        [],
-        rows,
-    )
+        (terms, own, v, u3, u2, u1),
+        (shape((2, 5 * tokens, rank), bf16), whole, sides),
+    )
+    white1, mine, side = kernel(
+        core_kernel,
+        "core_pairs",
+        (terms, white, v1, mine, side),
+        (unit, whole, sides),
+        input_output_aliases={3: 1, 4: 2},
+    )
+    white3, side = kernel(
+        z_kernel,
+        "z_pairs",
+        (terms, white, u2, u1, v1, v3, side),
+        (unit, sides),
+        input_output_aliases={6: 1},
+    )
+    by_x, by_z = kernel(
+        return_kernel, "return_rows", (white, white1, white3, pick, side, v2), (rows, rows)
+    )
+    mine = kernel(rows_kernel, "own_rows", (white, pick, mine, v3, v2), rows)
     half_sum = mine + send(by_x, lambda d: d ^ 2) + send(by_z, z_near)
     return half_sum[:per] + send(half_sum[per:], opposite)
 

time: 28.9 us -> 29.3 us (1.014)
  waiting for transfers between devices: 9.44 us -> 6.87 us
  starting transfers between devices: 13.3 us -> 15.8 us
  Pallas kernels: 5.39 us -> 5.85 us
    ppermute x10, waiting for transfers between devices: 9.44 us -> 6.87 us  [send(): return lax.ppermute(x, 'blk', [(d, to(d)) for d in range(size)])]
    ppermute x10, starting transfers between devices: 13.3 us -> 15.8 us  [send(): return lax.ppermute(x, 'blk', [(d, to(d)) for d in range(size)])]
    pallas_call x7 -> x9, Pallas kernels: 5.39 us -> 5.85 us  [call(): pl.pallas_call(kernel, out_shape=out_shape, in_specs=specs + [vmem] * (le...]
  transfers between devices with their start and end apart: 10 -> 10, of which waited for: 6 -> 6; matrix products, arithmetic and copies ran while one was open for 0% -> 0% of each run, Pallas kernels for 12% -> 14%
where the time goes in v14:
time: 29.3 us; the launch traced here: 29.2 us
  starting transfers between devices  15.8 us (54%)
  waiting for transfers between devices  6.87 us (23%)
  Pallas kernels  5.85 us (20%)
  other arithmetic  0.57 us (2%)
    ppermute x10, starting transfers between devices, send(): return lax.ppermute(x, 'blk', [(d, to(d)) for d in range(size)])  15.8 us
    ppermute x10, waiting for transfers between devices, send(): return lax.ppermute(x, 'blk', [(d, to(d)) for d in range(size)])  6.87 us
    pallas_call x9, Pallas kernels, call(): pl.pallas_call(kernel, out_shape=out_shape, in_specs=specs + [vmem] * (le...  5.85 us
  transfers between devices with their start and end apart: 10, of which 6 were waited for; matrix products, arithmetic and copies ran while one was open for 0% of the time, Pallas kernels for 14%

profile of v14, /device:TPU:0, one launch (start us, length us, event | category | flops | bytes accessed | tf_op | source)
XLA Modules:
  0.0 29.2 jit_solution(3964283686013507692)
XLA Ops:
  0.0 1.0 %away.1.unit = bf16[2,128,256]{2,1,0:T(8,128)(2,1)S(1)} custom-call(bf16[2,128,256]{2,1,0:T(8,128)(2,1)} %acts.2, bf16[2,128,256]{2,1,0:T(8,128)(2,1)} %grads.2), custom_call_target="tpu_custom_call" | custom-call | flops 3000000000 | bytes 1000000 | tf_op jit(solution)/shard_map/away/pallas_call | solution.py:232
  1.0 0.0 copy-done
  1.0 0.2 away_mask.1
  1.1 4.1 %collective-permute-start = (bf16[2,128,256]{2,1,0:T(8,128)(2,1)S(1)}, bf16[2,128,256]{2,1,0:T(8,128)(2,1)S(1)}, u32[]{:S(2)}, u32[]{:S(2)}) collective-permute-start(bf16[2,128,256]{2,1,0:T(8,128)(2,1)S(1)} %away_mask.1), channel_id=1, source_target_pairs={{0,8},{1,9},{2,10},{3,11},{4,12},{5,13},{6,14},{7,15},{8,0},{9,1},... | collective-permute-start | bytes 393224 | tf_op jit(solution)/shard_map/ppermute | solution.py:253
  5.3 0.1 own.1.u0
  5.4 1.6 %collective-permute-start.2 = (bf16[2,128,256]{2,1,0:T(8,128)(2,1)S(1)}, bf16[2,128,256]{2,1,0:T(8,128)(2,1)S(1)}, u32[]{:S(2)}, u32[]{:S(2)}) collective-permute-start(bf16[2,128,256]{2,1,0:T(8,128)(2,1)S(1)} %own.1.u0), channel_id=1, source_target_pairs={{0,2},{1,3},{2,0},{3,1},{4,6},{5,7},{6,4},{7,5},{8,10},{9,11},{10,... | collective-permute-start | bytes 393224 | tf_op jit(solution)/shard_map/ppermute | solution.py:253
  7.0 0.0 collective-permute-start.3
  7.0 1.6 %collective-permute-start.1 = (bf16[2,128,256]{2,1,0:T(8,128)(2,1)S(1)}, bf16[2,128,256]{2,1,0:T(8,128)(2,1)S(1)}, u32[]{:S(2)}, u32[]{:S(2)}) collective-permute-start(bf16[2,128,256]{2,1,0:T(8,128)(2,1)S(1)} %own.1.u0), channel_id=1, source_target_pairs={{0,4},{1,5},{2,7},{3,6},{4,0},{5,1},{6,3},{7,2},{8,12},{9,13},{10,... | collective-permute-start | bytes 393224 | tf_op jit(solution)/shard_map/ppermute | solution.py:253
  8.6 0.0 copy-done.1
  8.6 1.7 %factor_terms.1 = (bf16[2,3,256,256]{3,2,1,0:T(8,128)(2,1)S(1)}, bf16[1024,32]{1,0:T(8,128)(2,1)S(1)}) custom-call(s32[2]{0:T(128)S(1)} %copy-done.1, s32[1,32]{1,0:T(1,128)S(1)} %bitcast.4, f32[16,256,256]{2,1,0:T(8,128)} %act_f.1, f32[16,256,256]{2,1,0:T(8,128)} %grad_f.1), custom_call_target="tpu_custom_call" | custom-call | flops 1000000000 | bytes 1000000 | tf_op jit(solution)/shard_map/factor_terms/pallas_call | solution.py:232
  10.3 1.4 %collective-permute-done.v = bf16[2,128,256]{2,1,0:T(8,128)(2,1)S(1)} collective-permute-done((bf16[2,128,256]{2,1,0:T(8,128)(2,1)S(1)}, bf16[2,128,256]{2,1,0:T(8,128)(2,1)S(1)}, u32[]{:S(2)}, u32[]{:S(2)}) %collective-permute-start) | collective-permute-done | bytes 131104 | tf_op jit(solution)/shard_map/ppermute | solution.py:253
  11.7 0.0 collective-permute-start.4
  11.7 0.7 %collective-permute-start.5 = (bf16[2,128,256]{2,1,0:T(8,128)(2,1)S(1)}, bf16[2,128,256]{2,1,0:T(8,128)(2,1)S(1)}, u32[]{:S(2)}, u32[]{:S(2)}) collective-permute-start(bf16[2,128,256]{2,1,0:T(8,128)(2,1)S(1)} %collective-permute-done.v), channel_id=1, source_target_pairs={{0,4},{1,5},{2,7},{3,6},{4,0},{5,1},{6,3},{7,2},{8,12},{9,13},{10,... | collective-permute-start | bytes 393224 | tf_op jit(solution)/shard_map/ppermute | solution.py:253
  12.4 0.0 collective-permute-done.2.u2
  12.4 1.6 %collective-permute-start.6 = (bf16[2,128,256]{2,1,0:T(8,128)(2,1)S(1)}, bf16[2,128,256]{2,1,0:T(8,128)(2,1)S(1)}, u32[]{:S(2)}, u32[]{:S(2)}) collective-permute-start(bf16[2,128,256]{2,1,0:T(8,128)(2,1)S(1)} %collective-permute-done.v), channel_id=1, source_target_pairs={{0,2},{1,3},{2,0},{3,1},{4,6},{5,7},{6,4},{7,5},{8,10},{9,11},{10,... | collective-permute-start | bytes 393224 | tf_op jit(solution)/shard_map/ppermute | solution.py:253
  14.0 0.0 collective-permute-done.3.u1
  14.0 0.4 %collective-permute-done.1.u3 = bf16[2,128,256]{2,1,0:T(8,128)(2,1)S(1)} collective-permute-done((bf16[2,128,256]{2,1,0:T(8,128)(2,1)S(1)}, bf16[2,128,256]{2,1,0:T(8,128)(2,1)S(1)}, u32[]{:S(2)}, u32[]{:S(2)}) %collective-permute-start.1) | collective-permute-done | bytes 131104 | tf_op jit(solution)/shard_map/ppermute | solution.py:253
  14.4 1.1 %early_pairs.1 = (bf16[2,640,256]{2,1,0:T(8,128)(2,1)S(1)}, f32[4,1024]{1,0:T(4,128)S(1)}, f32[8,768]{1,0:T(8,128)S(1)}) custom-call(bf16[2,3,256,256]{3,2,1,0:T(8,128)(2,1)S(1)} %get-tuple-element.25.terms, bf16[2,128,256]{2,1,0:T(8,128)(2,1)S(1)} %own.1.u0, bf16[2,128,256]{2,1,0:T(8,128)(2,1)S(1)} %collective-permute-done.v, ...), custom_call_target="tpu_custom_call" | custom-call | flops 1000000000 | bytes 1000000 | tf_op jit(solution)/shard_map/early_pairs/pallas_call | solution.py:232
  15.5 0.0 collective-permute-done.4.v1
  15.5 0.4 %core_pairs.1 = (bf16[2,128,256]{2,1,0:T(8,128)(2,1)S(1)}, f32[4,1024]{1,0:T(4,128)S(1)}, f32[8,768]{1,0:T(8,128)S(1)}) custom-call(bf16[2,3,256,256]{3,2,1,0:T(8,128)(2,1)S(1)} %get-tuple-element.25.terms, bf16[2,640,256]{2,1,0:T(8,128)(2,1)S(1)} %get-tuple-element.30.white, ...), custom_call_target="tpu_custom_call", output_to_operand_aliasing={{1}: (3, {}), {2}: (4, {})} | custom-call | flops 1000000000 | bytes 1000000 | tf_op jit(solution)/shard_map/core_pairs/pallas_call | solution.py:232
  15.9 1.7 %collective-permute-done.5.v3 = bf16[2,128,256]{2,1,0:T(8,128)(2,1)S(1)} collective-permute-done((bf16[2,128,256]{2,1,0:T(8,128)(2,1)S(1)}, bf16[2,128,256]{2,1,0:T(8,128)(2,1)S(1)}, u32[]{:S(2)}, u32[]{:S(2)}) %collective-permute-start.5) | collective-permute-done | bytes 131104 | tf_op jit(solution)/shard_map/ppermute | solution.py:253
  17.6 0.5 %z_pairs.1 = (bf16[2,128,256]{2,1,0:T(8,128)(2,1)S(1)}, f32[8,768]{1,0:T(8,128)S(1)}) custom-call(bf16[2,3,256,256]{3,2,1,0:T(8,128)(2,1)S(1)} %get-tuple-element.25.terms, bf16[2,640,256]{2,1,0:T(8,128)(2,1)S(1)} %get-tuple-element.30.white, bf16[2,128,256]{2,1,0:T(8,128)(2,1)S(1)} %collective-permute-done.2.u2, ...), custom_call_target="tpu_custom_call", output_to_operand_aliasing={{1}: (6, {})} | custom-call | flops 1000000000 | bytes 1000000 | tf_op jit(solution)/shard_map/z_pairs/pallas_call | solution.py:232
  18.1 0.0 collective-permute-done.6.v2
  18.1 0.5 %return_rows.1 = (f32[4,32]{1,0:T(4,128)S(1)}, f32[4,32]{1,0:T(4,128)S(1)}) custom-call(bf16[2,640,256]{2,1,0:T(8,128)(2,1)S(1)} %get-tuple-element.30.white, bf16[2,128,256]{2,1,0:T(8,128)(2,1)S(1)} %get-tuple-element.35.white1, bf16[2,128,256]{2,1,0:T(8,128)(2,1)S(1)} %get-tuple-element.37.white3, bf16[1024,32]{1,0:T(8,128)(2,1)S(1)} %get-tuple-element.31.pick, ...), custom_call_target="tpu_custom_call" | custom-call | flops 1000000000 | bytes 1000000 | tf_op jit(solution)/shard_map/return_rows/pallas_call | solution.py:232
  18.6 1.3 %collective-permute-start.7 = (f32[4,32]{1,0:T(4,128)S(1)}, f32[4,32]{1,0:T(4,128)S(1)}, u32[]{:S(2)}, u32[]{:S(2)}) collective-permute-start(f32[4,32]{1,0:T(4,128)S(1)} %get-tuple-element.39), channel_id=1, source_target_pairs={{0,2},{1,3},{2,0},{3,1},{4,6},{5,7},{6,4},{7,5},{8,10},{9,11},{10,... | collective-permute-start | bytes 1544 | tf_op jit(solution)/shard_map/ppermute | solution.py:253
  20.0 1.4 %collective-permute-start.8 = (f32[4,32]{1,0:T(4,128)S(1)}, f32[4,32]{1,0:T(4,128)S(1)}, u32[]{:S(2)}, u32[]{:S(2)}) collective-permute-start(f32[4,32]{1,0:T(4,128)S(1)} %get-tuple-element.40), channel_id=1, source_target_pairs={{0,4},{1,5},{2,7},{3,6},{4,0},{5,1},{6,3},{7,2},{8,12},{9,13},{10,... | collective-permute-start | bytes 1544 | tf_op jit(solution)/shard_map/ppermute | solution.py:253
  21.4 0.4 %own_rows.1 = f32[4,32]{1,0:T(4,128)S(1)} custom-call(bf16[2,640,256]{2,1,0:T(8,128)(2,1)S(1)} %get-tuple-element.30.white, bf16[1024,32]{1,0:T(8,128)(2,1)S(1)} %get-tuple-element.31.pick, f32[4,1024]{1,0:T(4,128)S(1)} %get-tuple-element.34.mine, bf16[2,128,256]{2,1,0:T(8,128)(2,1)S(1)} %collective-permute-done.5.v3, ...), custom_call_target="tpu_custom_call" | custom-call | flops 1000000000 | bytes 1000000 | tf_op jit(solution)/shard_map/own_rows/pallas_call | solution.py:232
  21.8 0.5 %collective-permute-done.7 = f32[4,32]{1,0:T(4,128)S(1)} collective-permute-done((f32[4,32]{1,0:T(4,128)S(1)}, f32[4,32]{1,0:T(4,128)S(1)}, u32[]{:S(2)}, u32[]{:S(2)}) %collective-permute-start.7) | collective-permute-done | bytes 544 | tf_op jit(solution)/shard_map/ppermute | solution.py:253
  22.3 1.3 %collective-permute-done.8 = f32[4,32]{1,0:T(4,128)S(1)} collective-permute-done((f32[4,32]{1,0:T(4,128)S(1)}, f32[4,32]{1,0:T(4,128)S(1)}, u32[]{:S(2)}, u32[]{:S(2)}) %collective-permute-start.8) | collective-permute-done | bytes 544 | tf_op jit(solution)/shard_map/ppermute | solution.py:253
  23.6 3.5 %collective-permute-start.9 = (f32[2,32]{1,0:T(2,128)S(1)}, f32[2,32]{1,0:T(2,128)S(1)}, u32[]{:S(2)}, u32[]{:S(2)}) collective-permute-start(f32[2,32]{1,0:T(2,128)S(1)} %slice.7), channel_id=1, source_target_pairs={{0,8},{1,9},{2,10},{3,11},{4,12},{5,13},{6,14},{7,15},{8,0},{9,1},... | collective-permute-start | bytes 776 | tf_op jit(solution)/shard_map/ppermute | solution.py:253
  27.1 1.5 %collective-permute-done.9 = f32[2,32]{1,0:T(2,128)S(1)} collective-permute-done((f32[2,32]{1,0:T(2,128)S(1)}, f32[2,32]{1,0:T(2,128)S(1)}, u32[]{:S(2)}, u32[]{:S(2)}) %collective-permute-start.9) | collective-permute-done | bytes 288 | tf_op jit(solution)/shard_map/ppermute | solution.py:253
  28.6 0.6 %slice_add_fusion = f32[2,32]{1,0:T(2,128)} fusion(f32[2,32]{1,0:T(2,128)S(1)} %collective-permute-done.9, f32[4,32]{1,0:T(4,128)S(1)} %add_add_fusion), kind=kLoop, calls=%fused_computation.1 | loop fusion | flops 64 | bytes 768 | tf_op jit(solution)/shard_map/add | solution.py:331
  (10 shorter events, 0.0 us)
Async XLA Ops:
  0.0 5.3 %copy-start.3 = (bf16[2,128,256]{2,1,0:T(8,128)(2,1)S(1)}, bf16[2,128,256]{2,1,0:T(8,128)(2,1)}, u32[]{:S(2)}) copy-start(bf16[2,128,256]{2,1,0:T(8,128)(2,1)} %acts.2) | copy-start | bytes 393220
  0.0 5.3 %copy-start.4 = (bf16[2,128,256]{2,1,0:T(8,128)(2,1)S(1)}, bf16[2,128,256]{2,1,0:T(8,128)(2,1)}, u32[]{:S(2)}) copy-start(bf16[2,128,256]{2,1,0:T(8,128)(2,1)} %grads.2) | copy-start | bytes 393220
  0.0 1.0 %copy-start = (s32[2]{0:T(128)S(1)}, s32[2]{0:T(128)}, u32[]{:S(2)}) copy-start(s32[2]{0:T(128)} %param.9) | copy-start | bytes 28
  0.0 8.6 %copy-start.2 = (s32[32]{0:T(128)S(1)}, s32[32]{0:T(128)}, u32[]{:S(2)}) copy-start(s32[32]{0:T(128)} %param.11) | copy-start | bytes 388
  0.0 8.6 %copy-start.1 = (s32[2]{0:T(128)S(1)}, s32[2]{0:T(128)}, u32[]{:S(2)}) copy-start(s32[2]{0:T(128)} %layer_ids.1) | copy-start | bytes 28
  1.1 10.5 %collective-permute-start = (bf16[2,128,256]{2,1,0:T(8,128)(2,1)S(1)}, bf16[2,128,256]{2,1,0:T(8,128)(2,1)S(1)}, u32[]{:S(2)}, u32[]{:S(2)}) collective-permute-start(bf16[2,128,256]{2,1,0:T(8,128)(2,1)S(1)} %away_mask.1), channel_id=1, source_target_pairs={{0,8},{1,9},{2,10},{3,11},{4,12},{5,13},{6,14},{7,15},{8,0},{9,1},... | collective-permute-start | bytes 393224 | tf_op jit(solution)/shard_map/ppermute | solution.py:253
  5.4 6.9 %collective-permute-start.2 = (bf16[2,128,256]{2,1,0:T(8,128)(2,1)S(1)}, bf16[2,128,256]{2,1,0:T(8,128)(2,1)S(1)}, u32[]{:S(2)}, u32[]{:S(2)}) collective-permute-start(bf16[2,128,256]{2,1,0:T(8,128)(2,1)S(1)} %own.1.u0), channel_id=1, source_target_pairs={{0,2},{1,3},{2,0},{3,1},{4,6},{5,7},{6,4},{7,5},{8,10},{9,11},{10,... | collective-permute-start | bytes 393224 | tf_op jit(solution)/shard_map/ppermute | solution.py:253
  7.0 7.0 %collective-permute-start.3 = (bf16[2,128,256]{2,1,0:T(8,128)(2,1)S(1)}, bf16[2,128,256]{2,1,0:T(8,128)(2,1)S(1)}, u32[]{:S(2)}, u32[]{:S(2)}) collective-permute-start(bf16[2,128,256]{2,1,0:T(8,128)(2,1)S(1)} %own.1.u0), channel_id=1, source_target_pairs={{0,1},{1,0},{2,3},{3,2},{4,5},{5,4},{6,7},{7,6},{8,9},{9,8},{10,11... | collective-permute-start | bytes 393224 | tf_op jit(solution)/shard_map/ppermute | solution.py:253
  7.0 7.4 %collective-permute-start.1 = (bf16[2,128,256]{2,1,0:T(8,128)(2,1)S(1)}, bf16[2,128,256]{2,1,0:T(8,128)(2,1)S(1)}, u32[]{:S(2)}, u32[]{:S(2)}) collective-permute-start(bf16[2,128,256]{2,1,0:T(8,128)(2,1)S(1)} %own.1.u0), channel_id=1, source_target_pairs={{0,4},{1,5},{2,7},{3,6},{4,0},{5,1},{6,3},{7,2},{8,12},{9,13},{10,... | collective-permute-start | bytes 393224 | tf_op jit(solution)/shard_map/ppermute | solution.py:253
  11.7 3.8 %collective-permute-start.4 = (bf16[2,128,256]{2,1,0:T(8,128)(2,1)S(1)}, bf16[2,128,256]{2,1,0:T(8,128)(2,1)S(1)}, u32[]{:S(2)}, u32[]{:S(2)}) collective-permute-start(bf16[2,128,256]{2,1,0:T(8,128)(2,1)S(1)} %collective-permute-done.v), channel_id=1, source_target_pairs={{0,1},{1,0},{2,3},{3,2},{4,5},{5,4},{6,7},{7,6},{8,9},{9,8},{10,11... | collective-permute-start | bytes 393224 | tf_op jit(solution)/shard_map/ppermute | solution.py:253
  11.7 5.9 %collective-permute-start.5 = (bf16[2,128,256]{2,1,0:T(8,128)(2,1)S(1)}, bf16[2,128,256]{2,1,0:T(8,128)(2,1)S(1)}, u32[]{:S(2)}, u32[]{:S(2)}) collective-permute-start(bf16[2,128,256]{2,1,0:T(8,128)(2,1)S(1)} %collective-permute-done.v), channel_id=1, source_target_pairs={{0,4},{1,5},{2,7},{3,6},{4,0},{5,1},{6,3},{7,2},{8,12},{9,13},{10,... | collective-permute-start | bytes 393224 | tf_op jit(solution)/shard_map/ppermute | solution.py:253
  12.4 5.7 %collective-permute-start.6 = (bf16[2,128,256]{2,1,0:T(8,128)(2,1)S(1)}, bf16[2,128,256]{2,1,0:T(8,128)(2,1)S(1)}, u32[]{:S(2)}, u32[]{:S(2)}) collective-permute-start(bf16[2,128,256]{2,1,0:T(8,128)(2,1)S(1)} %collective-permute-done.v), channel_id=1, source_target_pairs={{0,2},{1,3},{2,0},{3,1},{4,6},{5,7},{6,4},{7,5},{8,10},{9,11},{10,... | collective-permute-start | bytes 393224 | tf_op jit(solution)/shard_map/ppermute | solution.py:253
  18.6 3.7 %collective-permute-start.7 = (f32[4,32]{1,0:T(4,128)S(1)}, f32[4,32]{1,0:T(4,128)S(1)}, u32[]{:S(2)}, u32[]{:S(2)}) collective-permute-start(f32[4,32]{1,0:T(4,128)S(1)} %get-tuple-element.39), channel_id=1, source_target_pairs={{0,2},{1,3},{2,0},{3,1},{4,6},{5,7},{6,4},{7,5},{8,10},{9,11},{10,... | collective-permute-start | bytes 1544 | tf_op jit(solution)/shard_map/ppermute | solution.py:253
  20.0 3.6 %collective-permute-start.8 = (f32[4,32]{1,0:T(4,128)S(1)}, f32[4,32]{1,0:T(4,128)S(1)}, u32[]{:S(2)}, u32[]{:S(2)}) collective-permute-start(f32[4,32]{1,0:T(4,128)S(1)} %get-tuple-element.40), channel_id=1, source_target_pairs={{0,4},{1,5},{2,7},{3,6},{4,0},{5,1},{6,3},{7,2},{8,12},{9,13},{10,... | collective-permute-start | bytes 1544 | tf_op jit(solution)/shard_map/ppermute | solution.py:253
  23.6 5.0 %collective-permute-start.9 = (f32[2,32]{1,0:T(2,128)S(1)}, f32[2,32]{1,0:T(2,128)S(1)}, u32[]{:S(2)}, u32[]{:S(2)}) collective-permute-start(f32[2,32]{1,0:T(2,128)S(1)} %slice.7), channel_id=1, source_target_pairs={{0,8},{1,9},{2,10},{3,11},{4,12},{5,13},{6,14},{7,15},{8,0},{9,1},... | collective-permute-start | bytes 776 | tf_op jit(solution)/shard_map/ppermute | solution.py:253

commit v15 on v14

--- a/solution.py
+++ b/solution.py
@@ -169,21 +169,8 @@
             side[row : row + per, at : at + n] = block(seq_len, left[slot], tok[column])
 
 
-def core_kernel(seq_len, per, terms, white, v1, mine, side, white1, mine_out, side_out):
-    n = v1.shape[1]
-    tok = [v1[w] for w in range(2)]
-    for w in range(2):
-        white1[w] = whiten(tok[w], terms.at[w])
-    mine_out[...] = mine[...]
-    mine_out[:, 3 * n : 4 * n] = block(seq_len, [white[w, : 2 * n] for w in range(2)], tok)
-    side_out[...] = side[...]
-    got = block(seq_len, [white[w, 2 * n : 4 * n] for w in range(2)], tok)
-    for i, row in enumerate((0, 2 * per)):
-        side_out[row : row + per, n : 2 * n] = got[i * per : (i + 1) * per]
-
-
-def z_kernel(seq_len, per, terms, white, u2, u1, v1, v3, side, white3, side_out):
-    n = v1.shape[1]
+def z_kernel(seq_len, per, terms, white, u2, u1, v3, side, white3, side_out):
+    n = v3.shape[1]
     tok = [v3[w] for w in range(2)]
     fresh = [whiten(tok[w], terms.at[w]) for w in range(2)]
     for w in range(2):
@@ -192,39 +179,47 @@
     side_out[0:per, 5 * n : 6 * n] = block(
         seq_len, [white[w, 2 * n : 3 * n] for w in range(2)], tok
     )
-    side_out[3 * per : 4 * per, 0 : 3 * n] = block(
-        seq_len, fresh, [stack(u1[w], v1[w], u2[w]) for w in range(2)]
-    )
-
-
-def return_kernel(seq_len, per, white, white1, white3, pick, side, v2, by_x, by_z):
+    got = block(seq_len, fresh, [stack(u1[w], u2[w]) for w in range(2)])
+    side_out[3 * per : 4 * per, 0:n] = got[:, :n]
+    side_out[3 * per : 4 * per, 2 * n : 3 * n] = got[:, n:]
+
+
+def return_kernel(seq_len, per, terms, white, white3, pick, side, v2, v1, by_z, by_x):
     n = v2.shape[1]
-    tok = [v2[w] for w in range(2)]
+    x = [v2[w] for w in range(2)]
+    core = [v1[w] for w in range(2)]
     columns = [
-        stack(white[w, 4 * n : 5 * n], white1[w], white[w, 3 * n : 4 * n], white3[w])
-        for w in range(2)
+        stack(white[w, 4 * n : 5 * n], white[w, 3 * n : 4 * n], white3[w]) for w in range(2)
     ]
-    by_row = block(seq_len, tok, columns)
-    by_column = block(
-        seq_len, [stack(white[w, 3 * n : 4 * n], white3[w]) for w in range(2)], tok
-    )
-    zeros = jnp.zeros((per, 2 * n), jnp.float32)
-    none = jnp.zeros((per, 6 * n), jnp.float32)
-    row = jnp.concatenate([by_row[:, : 2 * n], zeros, by_row[:, 2 * n :]], axis=1)
-    lead = jnp.zeros((2 * per, 3 * n), jnp.float32)
-    both = jnp.concatenate([lead, by_column, lead[:, : 2 * n]], axis=1)
-    picked = pick_columns(side[...] + stack(none, row, both), pick.at[2 * n :])
+    near = block(seq_len, x, columns)
+    far = block(seq_len, x, [whiten(core[w], terms.at[w]) for w in range(2)])
+    at_core = block(seq_len, [stack(white[w, 2 * n : 4 * n], white3[w]) for w in range(2)], core)
+    at_x = block(seq_len, [stack(white[w, 3 * n : 4 * n], white3[w]) for w in range(2)], x)
+    zeros = jnp.zeros((per, n), jnp.float32)
+
+    def line(*blocks):
+        return jnp.concatenate([zeros if x is None else x for x in blocks], axis=1)
+
+    late = stack(
+        line(None, at_core[:per], None, None, None, None),
+        line(near[:, :n], far, None, None, near[:, n : 2 * n], near[:, 2 * n :]),
+        line(None, at_core[per : 2 * per], None, at_x[:per], None, None),
+        line(None, at_core[2 * per :], None, at_x[per:], None, None),
+    )
+    picked = pick_columns(side[...] + late, pick.at[2 * n :])
     by_x[...] = picked[: 2 * per]
     by_z[...] = picked[2 * per :]
 
 
-def rows_kernel(seq_len, per, white, pick, mine, v3, v2, out):
+def rows_kernel(seq_len, per, white, pick, mine, v3, v2, v1, out):
     n = v2.shape[1]
     left = [white[w, : 2 * n] for w in range(2)]
-    got = block(seq_len, left, [stack(v2[w], v3[w]) for w in range(2)])
+    got = block(seq_len, left, [stack(v1[w], v2[w], v3[w]) for w in range(2)])
     zeros = jnp.zeros((2 * per, n), jnp.float32)
-    late = jnp.concatenate([zeros] * 5 + [got[:, :n], zeros, got[:, n:]], axis=1)
-    out[...] = pick_columns(mine[...] + late, pick)
+    late = [zeros, zeros]
+    for i in range(3):
+        late += [zeros, got[:, i * n : (i + 1) * n]]
+    out[...] = pick_columns(mine[...] + jnp.concatenate(late, axis=1), pick)
 
 
 def call(kernel, name, flops, limit, operands, specs, out_shape, scratch=(), **more):
@@ -309,24 +304,17 @@
         (terms, own, v, u3, u2, u1),
         (shape((2, 5 * tokens, rank), bf16), whole, sides),
     )
-    white1, mine, side = kernel(
-        core_kernel,
-        "core_pairs",
-        (terms, white, v1, mine, side),
-        (unit, whole, sides),
-        input_output_aliases={3: 1, 4: 2},
-    )
     white3, side = kernel(
         z_kernel,
         "z_pairs",
-        (terms, white, u2, u1, v1, v3, side),
+        (terms, white, u2, u1, v3, side),
         (unit, sides),
-        input_output_aliases={6: 1},
-    )
-    by_x, by_z = kernel(
-        return_kernel, "return_rows", (white, white1, white3, pick, side, v2), (rows, rows)
-    )
-    mine = kernel(rows_kernel, "own_rows", (white, pick, mine, v3, v2), rows)
+        input_output_aliases={5: 1},
+    )
+    by_z, by_x = kernel(
+        return_kernel, "return_rows", (terms, white, white3, pick, side, v2, v1), (rows, rows)
+    )
+    mine = kernel(rows_kernel, "own_rows", (white, pick, mine, v3, v2, v1), rows)
     half_sum = mine + send(by_x, lambda d: d ^ 2) + send(by_z, z_near)
     return half_sum[:per] + send(half_sum[per:], opposite)
 

time: 29.3 us -> 28.8 us (0.983)
  starting transfers between devices: 15.8 us -> 13.9 us
  waiting for transfers between devices: 6.87 us -> 8.37 us
    ppermute x10, starting transfers between devices: 15.8 us -> 13.9 us  [send(): return lax.ppermute(x, 'blk', [(d, to(d)) for d in range(size)])]
    ppermute x10, waiting for transfers between devices: 6.87 us -> 8.37 us  [send(): return lax.ppermute(x, 'blk', [(d, to(d)) for d in range(size)])]
    pallas_call x9 -> x8, Pallas kernels: 5.85 us -> 5.73 us  [call(): pl.pallas_call(kernel, out_shape=out_shape, in_specs=specs + [vmem] * (le...]
  transfers between devices with their start and end apart: 10 -> 10, of which waited for: 6 -> 6; matrix products, arithmetic and copies ran while one was open for 0% -> 0% of each run, Pallas kernels for 14% -> 13%
where the time goes in v15:
time: 28.8 us; the launch traced here: 28.6 us
  starting transfers between devices  13.9 us (48%)
  waiting for transfers between devices  8.37 us (29%)
  Pallas kernels  5.73 us (20%)
  other arithmetic  0.57 us (2%)
    ppermute x10, starting transfers between devices, send(): return lax.ppermute(x, 'blk', [(d, to(d)) for d in range(size)])  13.9 us
    ppermute x10, waiting for transfers between devices, send(): return lax.ppermute(x, 'blk', [(d, to(d)) for d in range(size)])  8.37 us
    pallas_call x8, Pallas kernels, call(): pl.pallas_call(kernel, out_shape=out_shape, in_specs=specs + [vmem] * (le...  5.73 us
  transfers between devices with their start and end apart: 10, of which 6 were waited for; matrix products, arithmetic and copies ran while one was open for 0% of the time, Pallas kernels for 13%

profile of v15, /device:TPU:0, one launch (start us, length us, event | category | flops | bytes accessed | tf_op | source)
XLA Modules:
  0.0 28.6 jit_solution(8440245986897682094)
XLA Ops:
  0.0 1.0 %away.1.unit = bf16[2,128,256]{2,1,0:T(8,128)(2,1)S(1)} custom-call(bf16[2,128,256]{2,1,0:T(8,128)(2,1)} %acts.2, bf16[2,128,256]{2,1,0:T(8,128)(2,1)} %grads.2), custom_call_target="tpu_custom_call" | custom-call | flops 3000000000 | bytes 1000000 | tf_op jit(solution)/shard_map/away/pallas_call | solution.py:227
  1.0 0.0 copy-done
  1.0 0.2 away_mask.1
  1.1 4.1 %collective-permute-start = (bf16[2,128,256]{2,1,0:T(8,128)(2,1)S(1)}, bf16[2,128,256]{2,1,0:T(8,128)(2,1)S(1)}, u32[]{:S(2)}, u32[]{:S(2)}) collective-permute-start(bf16[2,128,256]{2,1,0:T(8,128)(2,1)S(1)} %away_mask.1), channel_id=1, source_target_pairs={{0,8},{1,9},{2,10},{3,11},{4,12},{5,13},{6,14},{7,15},{8,0},{9,1},... | collective-permute-start | bytes 393224 | tf_op jit(solution)/shard_map/ppermute | solution.py:248
  5.3 0.0 copy-done.3
  5.3 0.0 copy-done.4
  5.3 0.1 own.1.u0
  5.4 1.6 %collective-permute-start.1 = (bf16[2,128,256]{2,1,0:T(8,128)(2,1)S(1)}, bf16[2,128,256]{2,1,0:T(8,128)(2,1)S(1)}, u32[]{:S(2)}, u32[]{:S(2)}) collective-permute-start(bf16[2,128,256]{2,1,0:T(8,128)(2,1)S(1)} %own.1.u0), channel_id=1, source_target_pairs={{0,4},{1,5},{2,7},{3,6},{4,0},{5,1},{6,3},{7,2},{8,12},{9,13},{10,... | collective-permute-start | bytes 393224 | tf_op jit(solution)/shard_map/ppermute | solution.py:248
  7.1 0.7 %collective-permute-start.2 = (bf16[2,128,256]{2,1,0:T(8,128)(2,1)S(1)}, bf16[2,128,256]{2,1,0:T(8,128)(2,1)S(1)}, u32[]{:S(2)}, u32[]{:S(2)}) collective-permute-start(bf16[2,128,256]{2,1,0:T(8,128)(2,1)S(1)} %own.1.u0), channel_id=1, source_target_pairs={{0,2},{1,3},{2,0},{3,1},{4,6},{5,7},{6,4},{7,5},{8,10},{9,11},{10,... | collective-permute-start | bytes 393224 | tf_op jit(solution)/shard_map/ppermute | solution.py:248
  7.7 0.7 %collective-permute-start.3 = (bf16[2,128,256]{2,1,0:T(8,128)(2,1)S(1)}, bf16[2,128,256]{2,1,0:T(8,128)(2,1)S(1)}, u32[]{:S(2)}, u32[]{:S(2)}) collective-permute-start(bf16[2,128,256]{2,1,0:T(8,128)(2,1)S(1)} %own.1.u0), channel_id=1, source_target_pairs={{0,1},{1,0},{2,3},{3,2},{4,5},{5,4},{6,7},{7,6},{8,9},{9,8},{10,11... | collective-permute-start | bytes 393224 | tf_op jit(solution)/shard_map/ppermute | solution.py:248
  8.4 1.7 %factor_terms.1 = (bf16[2,3,256,256]{3,2,1,0:T(8,128)(2,1)S(1)}, bf16[1024,32]{1,0:T(8,128)(2,1)S(1)}) custom-call(s32[2]{0:T(128)S(1)} %copy-done.1, s32[1,32]{1,0:T(1,128)S(1)} %bitcast.4, f32[16,256,256]{2,1,0:T(8,128)} %act_f.1, f32[16,256,256]{2,1,0:T(8,128)} %grad_f.1), custom_call_target="tpu_custom_call" | custom-call | flops 1000000000 | bytes 1000000 | tf_op jit(solution)/shard_map/factor_terms/pallas_call | solution.py:227
  10.1 1.6 %collective-permute-done.v = bf16[2,128,256]{2,1,0:T(8,128)(2,1)S(1)} collective-permute-done((bf16[2,128,256]{2,1,0:T(8,128)(2,1)S(1)}, bf16[2,128,256]{2,1,0:T(8,128)(2,1)S(1)}, u32[]{:S(2)}, u32[]{:S(2)}) %collective-permute-start) | collective-permute-done | bytes 131104 | tf_op jit(solution)/shard_map/ppermute | solution.py:248
  11.7 0.6 %collective-permute-start.4 = (bf16[2,128,256]{2,1,0:T(8,128)(2,1)S(1)}, bf16[2,128,256]{2,1,0:T(8,128)(2,1)S(1)}, u32[]{:S(2)}, u32[]{:S(2)}) collective-permute-start(bf16[2,128,256]{2,1,0:T(8,128)(2,1)S(1)} %collective-permute-done.v), channel_id=1, source_target_pairs={{0,4},{1,5},{2,7},{3,6},{4,0},{5,1},{6,3},{7,2},{8,12},{9,13},{10,... | collective-permute-start | bytes 393224 | tf_op jit(solution)/shard_map/ppermute | solution.py:248
  12.3 1.1 %collective-permute-start.5 = (bf16[2,128,256]{2,1,0:T(8,128)(2,1)S(1)}, bf16[2,128,256]{2,1,0:T(8,128)(2,1)S(1)}, u32[]{:S(2)}, u32[]{:S(2)}) collective-permute-start(bf16[2,128,256]{2,1,0:T(8,128)(2,1)S(1)} %collective-permute-done.v), channel_id=1, source_target_pairs={{0,2},{1,3},{2,0},{3,1},{4,6},{5,7},{6,4},{7,5},{8,10},{9,11},{10,... | collective-permute-start | bytes 393224 | tf_op jit(solution)/shard_map/ppermute | solution.py:248
  13.4 0.0 collective-permute-done.1.u3
  13.4 0.2 collective-permute-start.6
  13.7 0.0 collective-permute-done.2.u2
  13.7 0.0 collective-permute-done.3.u1
  13.7 1.1 %early_pairs.1 = (bf16[2,640,256]{2,1,0:T(8,128)(2,1)S(1)}, f32[4,1024]{1,0:T(4,128)S(1)}, f32[8,768]{1,0:T(8,128)S(1)}) custom-call(bf16[2,3,256,256]{3,2,1,0:T(8,128)(2,1)S(1)} %get-tuple-element.22.terms, bf16[2,128,256]{2,1,0:T(8,128)(2,1)S(1)} %own.1.u0, bf16[2,128,256]{2,1,0:T(8,128)(2,1)S(1)} %collective-permute-done.v, ...), custom_call_target="tpu_custom_call" | custom-call | flops 1000000000 | bytes 1000000 | tf_op jit(solution)/shard_map/early_pairs/pallas_call | solution.py:227
  14.8 1.9 %collective-permute-done.4.v3 = bf16[2,128,256]{2,1,0:T(8,128)(2,1)S(1)} collective-permute-done((bf16[2,128,256]{2,1,0:T(8,128)(2,1)S(1)}, bf16[2,128,256]{2,1,0:T(8,128)(2,1)S(1)}, u32[]{:S(2)}, u32[]{:S(2)}) %collective-permute-start.4) | collective-permute-done | bytes 131104 | tf_op jit(solution)/shard_map/ppermute | solution.py:248
  16.7 0.4 %z_pairs.1 = (bf16[2,128,256]{2,1,0:T(8,128)(2,1)S(1)}, f32[8,768]{1,0:T(8,128)S(1)}) custom-call(bf16[2,3,256,256]{3,2,1,0:T(8,128)(2,1)S(1)} %get-tuple-element.22.terms, bf16[2,640,256]{2,1,0:T(8,128)(2,1)S(1)} %get-tuple-element.27.white, bf16[2,128,256]{2,1,0:T(8,128)(2,1)S(1)} %collective-permute-done.2.u2, ...), custom_call_target="tpu_custom_call", output_to_operand_aliasing={{1}: (5, {})} | custom-call | flops 1000000000 | bytes 1000000 | tf_op jit(solution)/shard_map/z_pairs/pallas_call | solution.py:227
  17.1 0.5 %collective-permute-done.5.v2 = bf16[2,128,256]{2,1,0:T(8,128)(2,1)S(1)} collective-permute-done((bf16[2,128,256]{2,1,0:T(8,128)(2,1)S(1)}, bf16[2,128,256]{2,1,0:T(8,128)(2,1)S(1)}, u32[]{:S(2)}, u32[]{:S(2)}) %collective-permute-start.5) | collective-permute-done | bytes 131104 | tf_op jit(solution)/shard_map/ppermute | solution.py:248
  17.6 0.0 collective-permute-done.6.v1
  17.6 0.8 %return_rows.1 = (f32[4,32]{1,0:T(4,128)S(1)}, f32[4,32]{1,0:T(4,128)S(1)}) custom-call(bf16[2,3,256,256]{3,2,1,0:T(8,128)(2,1)S(1)} %get-tuple-element.22.terms, bf16[2,640,256]{2,1,0:T(8,128)(2,1)S(1)} %get-tuple-element.27.white, bf16[2,128,256]{2,1,0:T(8,128)(2,1)S(1)} %get-tuple-element.31.white3, bf16[1024,32]{1,0:T(8,128)(2,1)S(1)} %get-tuple-element.28.pick, ...), custom_call_target="tpu_custom_call" | custom-call | flops 1000000000 | bytes 1000000 | tf_op jit(solution)/shard_map/return_rows/pallas_call | solution.py:227
  18.4 1.5 %collective-permute-start.8 = (f32[4,32]{1,0:T(4,128)S(1)}, f32[4,32]{1,0:T(4,128)S(1)}, u32[]{:S(2)}, u32[]{:S(2)}) collective-permute-start(f32[4,32]{1,0:T(4,128)S(1)} %get-tuple-element.34), channel_id=1, source_target_pairs={{0,4},{1,5},{2,7},{3,6},{4,0},{5,1},{6,3},{7,2},{8,12},{9,13},{10,... | collective-permute-start | bytes 1544 | tf_op jit(solution)/shard_map/ppermute | solution.py:248
  20.0 0.7 %collective-permute-start.7 = (f32[4,32]{1,0:T(4,128)S(1)}, f32[4,32]{1,0:T(4,128)S(1)}, u32[]{:S(2)}, u32[]{:S(2)}) collective-permute-start(f32[4,32]{1,0:T(4,128)S(1)} %get-tuple-element.33), channel_id=1, source_target_pairs={{0,2},{1,3},{2,0},{3,1},{4,6},{5,7},{6,4},{7,5},{8,10},{9,11},{10,... | collective-permute-start | bytes 1544 | tf_op jit(solution)/shard_map/ppermute | solution.py:248
  20.7 0.5 %own_rows.1 = f32[4,32]{1,0:T(4,128)S(1)} custom-call(bf16[2,640,256]{2,1,0:T(8,128)(2,1)S(1)} %get-tuple-element.27.white, bf16[1024,32]{1,0:T(8,128)(2,1)S(1)} %get-tuple-element.28.pick, f32[4,1024]{1,0:T(4,128)S(1)} %get-tuple-element.29.mine, bf16[2,128,256]{2,1,0:T(8,128)(2,1)S(1)} %collective-permute-done.4.v3, ...), custom_call_target="tpu_custom_call" | custom-call | flops 1000000000 | bytes 1000000 | tf_op jit(solution)/shard_map/own_rows/pallas_call | solution.py:227
  21.2 0.9 %collective-permute-done.8 = f32[4,32]{1,0:T(4,128)S(1)} collective-permute-done((f32[4,32]{1,0:T(4,128)S(1)}, f32[4,32]{1,0:T(4,128)S(1)}, u32[]{:S(2)}, u32[]{:S(2)}) %collective-permute-start.8) | collective-permute-done | bytes 544 | tf_op jit(solution)/shard_map/ppermute | solution.py:248
  22.1 1.4 %collective-permute-done.7 = f32[4,32]{1,0:T(4,128)S(1)} collective-permute-done((f32[4,32]{1,0:T(4,128)S(1)}, f32[4,32]{1,0:T(4,128)S(1)}, u32[]{:S(2)}, u32[]{:S(2)}) %collective-permute-start.7) | collective-permute-done | bytes 544 | tf_op jit(solution)/shard_map/ppermute | solution.py:248
  23.6 2.6 %collective-permute-start.9 = (f32[2,32]{1,0:T(2,128)S(1)}, f32[2,32]{1,0:T(2,128)S(1)}, u32[]{:S(2)}, u32[]{:S(2)}) collective-permute-start(f32[2,32]{1,0:T(2,128)S(1)} %slice.7), channel_id=1, source_target_pairs={{0,8},{1,9},{2,10},{3,11},{4,12},{5,13},{6,14},{7,15},{8,0},{9,1},... | collective-permute-start | bytes 776 | tf_op jit(solution)/shard_map/ppermute | solution.py:248
  26.1 2.0 %collective-permute-done.9 = f32[2,32]{1,0:T(2,128)S(1)} collective-permute-done((f32[2,32]{1,0:T(2,128)S(1)}, f32[2,32]{1,0:T(2,128)S(1)}, u32[]{:S(2)}, u32[]{:S(2)}) %collective-permute-start.9) | collective-permute-done | bytes 288 | tf_op jit(solution)/shard_map/ppermute | solution.py:248
  28.1 0.6 %slice_add_fusion = f32[2,32]{1,0:T(2,128)} fusion(f32[2,32]{1,0:T(2,128)S(1)} %collective-permute-done.9, f32[4,32]{1,0:T(4,128)S(1)} %add_add_fusion), kind=kLoop, calls=%fused_computation.1 | loop fusion | flops 64 | bytes 768 | tf_op jit(solution)/shard_map/add | solution.py:319
  (9 shorter events, 0.0 us)
Async XLA Ops:
  0.0 5.3 %copy-start.3 = (bf16[2,128,256]{2,1,0:T(8,128)(2,1)S(1)}, bf16[2,128,256]{2,1,0:T(8,128)(2,1)}, u32[]{:S(2)}) copy-start(bf16[2,128,256]{2,1,0:T(8,128)(2,1)} %acts.2) | copy-start | bytes 393220
  0.0 5.3 %copy-start.4 = (bf16[2,128,256]{2,1,0:T(8,128)(2,1)S(1)}, bf16[2,128,256]{2,1,0:T(8,128)(2,1)}, u32[]{:S(2)}) copy-start(bf16[2,128,256]{2,1,0:T(8,128)(2,1)} %grads.2) | copy-start | bytes 393220
  0.0 1.0 %copy-start = (s32[2]{0:T(128)S(1)}, s32[2]{0:T(128)}, u32[]{:S(2)}) copy-start(s32[2]{0:T(128)} %param.9) | copy-start | bytes 28
  0.0 8.4 %copy-start.1 = (s32[2]{0:T(128)S(1)}, s32[2]{0:T(128)}, u32[]{:S(2)}) copy-start(s32[2]{0:T(128)} %layer_ids.1) | copy-start | bytes 28
  0.0 8.4 %copy-start.2 = (s32[32]{0:T(128)S(1)}, s32[32]{0:T(128)}, u32[]{:S(2)}) copy-start(s32[32]{0:T(128)} %param.11) | copy-start | bytes 388
  1.1 10.5 %collective-permute-start = (bf16[2,128,256]{2,1,0:T(8,128)(2,1)S(1)}, bf16[2,128,256]{2,1,0:T(8,128)(2,1)S(1)}, u32[]{:S(2)}, u32[]{:S(2)}) collective-permute-start(bf16[2,128,256]{2,1,0:T(8,128)(2,1)S(1)} %away_mask.1), channel_id=1, source_target_pairs={{0,8},{1,9},{2,10},{3,11},{4,12},{5,13},{6,14},{7,15},{8,0},{9,1},... | collective-permute-start | bytes 393224 | tf_op jit(solution)/shard_map/ppermute | solution.py:248
  5.4 8.0 %collective-permute-start.1 = (bf16[2,128,256]{2,1,0:T(8,128)(2,1)S(1)}, bf16[2,128,256]{2,1,0:T(8,128)(2,1)S(1)}, u32[]{:S(2)}, u32[]{:S(2)}) collective-permute-start(bf16[2,128,256]{2,1,0:T(8,128)(2,1)S(1)} %own.1.u0), channel_id=1, source_target_pairs={{0,4},{1,5},{2,7},{3,6},{4,0},{5,1},{6,3},{7,2},{8,12},{9,13},{10,... | collective-permute-start | bytes 393224 | tf_op jit(solution)/shard_map/ppermute | solution.py:248
  7.1 6.6 %collective-permute-start.2 = (bf16[2,128,256]{2,1,0:T(8,128)(2,1)S(1)}, bf16[2,128,256]{2,1,0:T(8,128)(2,1)S(1)}, u32[]{:S(2)}, u32[]{:S(2)}) collective-permute-start(bf16[2,128,256]{2,1,0:T(8,128)(2,1)S(1)} %own.1.u0), channel_id=1, source_target_pairs={{0,2},{1,3},{2,0},{3,1},{4,6},{5,7},{6,4},{7,5},{8,10},{9,11},{10,... | collective-permute-start | bytes 393224 | tf_op jit(solution)/shard_map/ppermute | solution.py:248
  7.7 5.9 %collective-permute-start.3 = (bf16[2,128,256]{2,1,0:T(8,128)(2,1)S(1)}, bf16[2,128,256]{2,1,0:T(8,128)(2,1)S(1)}, u32[]{:S(2)}, u32[]{:S(2)}) collective-permute-start(bf16[2,128,256]{2,1,0:T(8,128)(2,1)S(1)} %own.1.u0), channel_id=1, source_target_pairs={{0,1},{1,0},{2,3},{3,2},{4,5},{5,4},{6,7},{7,6},{8,9},{9,8},{10,11... | collective-permute-start | bytes 393224 | tf_op jit(solution)/shard_map/ppermute | solution.py:248
  11.7 5.0 %collective-permute-start.4 = (bf16[2,128,256]{2,1,0:T(8,128)(2,1)S(1)}, bf16[2,128,256]{2,1,0:T(8,128)(2,1)S(1)}, u32[]{:S(2)}, u32[]{:S(2)}) collective-permute-start(bf16[2,128,256]{2,1,0:T(8,128)(2,1)S(1)} %collective-permute-done.v), channel_id=1, source_target_pairs={{0,4},{1,5},{2,7},{3,6},{4,0},{5,1},{6,3},{7,2},{8,12},{9,13},{10,... | collective-permute-start | bytes 393224 | tf_op jit(solution)/shard_map/ppermute | solution.py:248
  12.3 5.3 %collective-permute-start.5 = (bf16[2,128,256]{2,1,0:T(8,128)(2,1)S(1)}, bf16[2,128,256]{2,1,0:T(8,128)(2,1)S(1)}, u32[]{:S(2)}, u32[]{:S(2)}) collective-permute-start(bf16[2,128,256]{2,1,0:T(8,128)(2,1)S(1)} %collective-permute-done.v), channel_id=1, source_target_pairs={{0,2},{1,3},{2,0},{3,1},{4,6},{5,7},{6,4},{7,5},{8,10},{9,11},{10,... | collective-permute-start | bytes 393224 | tf_op jit(solution)/shard_map/ppermute | solution.py:248
  13.4 4.2 %collective-permute-start.6 = (bf16[2,128,256]{2,1,0:T(8,128)(2,1)S(1)}, bf16[2,128,256]{2,1,0:T(8,128)(2,1)S(1)}, u32[]{:S(2)}, u32[]{:S(2)}) collective-permute-start(bf16[2,128,256]{2,1,0:T(8,128)(2,1)S(1)} %collective-permute-done.v), channel_id=1, source_target_pairs={{0,1},{1,0},{2,3},{3,2},{4,5},{5,4},{6,7},{7,6},{8,9},{9,8},{10,11... | collective-permute-start | bytes 393224 | tf_op jit(solution)/shard_map/ppermute | solution.py:248
  18.4 3.6 %collective-permute-start.8 = (f32[4,32]{1,0:T(4,128)S(1)}, f32[4,32]{1,0:T(4,128)S(1)}, u32[]{:S(2)}, u32[]{:S(2)}) collective-permute-start(f32[4,32]{1,0:T(4,128)S(1)} %get-tuple-element.34), channel_id=1, source_target_pairs={{0,4},{1,5},{2,7},{3,6},{4,0},{5,1},{6,3},{7,2},{8,12},{9,13},{10,... | collective-permute-start | bytes 1544 | tf_op jit(solution)/shard_map/ppermute | solution.py:248
  20.0 3.6 %collective-permute-start.7 = (f32[4,32]{1,0:T(4,128)S(1)}, f32[4,32]{1,0:T(4,128)S(1)}, u32[]{:S(2)}, u32[]{:S(2)}) collective-permute-start(f32[4,32]{1,0:T(4,128)S(1)} %get-tuple-element.33), channel_id=1, source_target_pairs={{0,2},{1,3},{2,0},{3,1},{4,6},{5,7},{6,4},{7,5},{8,10},{9,11},{10,... | collective-permute-start | bytes 1544 | tf_op jit(solution)/shard_map/ppermute | solution.py:248
  23.6 4.5 %collective-permute-start.9 = (f32[2,32]{1,0:T(2,128)S(1)}, f32[2,32]{1,0:T(2,128)S(1)}, u32[]{:S(2)}, u32[]{:S(2)}) collective-permute-start(f32[2,32]{1,0:T(2,128)S(1)} %slice.7), channel_id=1, source_target_pairs={{0,8},{1,9},{2,10},{3,11},{4,12},{5,13},{6,14},{7,15},{8,0},{9,1},... | collective-permute-start | bytes 776 | tf_op jit(solution)/shard_map/ppermute | solution.py:248

commit v16 on v15

--- a/solution.py
+++ b/solution.py
@@ -287,12 +287,12 @@
         [pltpu.VMEM((2, rank, rank), f32), pltpu.SemaphoreType.DMA((2,))],
     )
     v, terms, pick = lax.optimization_barrier((v, terms, pick))
-    late = [send(v, to) for to in ways]
+    late = [send(v, to) for to in ways[:2]]
     whole = shape((2 * per, 8 * tokens), f32)
     sides = shape((4 * per, 6 * tokens), f32)
     rows = shape((2 * per, columns), f32)
     u3, u2, u1 = near
-    v3, v2, v1 = late
+    v3, v2 = late
 
     def kernel(body, name, operands, out_shape, **more):
         body = functools.partial(body, seq_len, per)
@@ -304,6 +304,8 @@
         (terms, own, v, u3, u2, u1),
         (shape((2, 5 * tokens, rank), bf16), whole, sides),
     )
+    v, white = lax.optimization_barrier((v, white))
+    v1 = send(v, ways[2])
     white3, side = kernel(
         z_kernel,
         "z_pairs",

time: 28.8 us -> 28.8 us (level)
  no operation moved by 1% of the time
where the time goes in v16:
time: 28.8 us; the launch traced here: 28.6 us
  starting transfers between devices  13.9 us (48%)
  waiting for transfers between devices  8.31 us (29%)
  Pallas kernels  5.72 us (20%)
  other arithmetic  0.57 us (2%)
    ppermute x10, starting transfers between devices, send(): return lax.ppermute(x, 'blk', [(d, to(d)) for d in range(size)])  13.9 us
    ppermute x10, waiting for transfers between devices, send(): return lax.ppermute(x, 'blk', [(d, to(d)) for d in range(size)])  8.31 us
    pallas_call x8, Pallas kernels, call(): pl.pallas_call(kernel, out_shape=out_shape, in_specs=specs + [vmem] * (le...  5.72 us
  transfers between devices with their start and end apart: 10, of which 6 were waited for; matrix products, arithmetic and copies ran while one was open for 0% of the time, Pallas kernels for 13%

profile of v16, /device:TPU:0, one launch (start us, length us, event | category | flops | bytes accessed | tf_op | source)
XLA Modules:
  0.0 28.6 jit_solution(12855655889757140720)
XLA Ops:
  0.0 1.0 %away.1.unit = bf16[2,128,256]{2,1,0:T(8,128)(2,1)S(1)} custom-call(bf16[2,128,256]{2,1,0:T(8,128)(2,1)} %acts.2, bf16[2,128,256]{2,1,0:T(8,128)(2,1)} %grads.2), custom_call_target="tpu_custom_call" | custom-call | flops 3000000000 | bytes 1000000 | tf_op jit(solution)/shard_map/away/pallas_call | solution.py:227
  1.0 0.0 copy-done
  1.0 0.2 away_mask.1
  1.1 4.1 %collective-permute-start = (bf16[2,128,256]{2,1,0:T(8,128)(2,1)S(1)}, bf16[2,128,256]{2,1,0:T(8,128)(2,1)S(1)}, u32[]{:S(2)}, u32[]{:S(2)}) collective-permute-start(bf16[2,128,256]{2,1,0:T(8,128)(2,1)S(1)} %away_mask.1), channel_id=1, source_target_pairs={{0,8},{1,9},{2,10},{3,11},{4,12},{5,13},{6,14},{7,15},{8,0},{9,1},... | collective-permute-start | bytes 393224 | tf_op jit(solution)/shard_map/ppermute | solution.py:248
  5.3 0.0 copy-done.3
  5.3 0.1 own.1.u0
  5.4 1.6 %collective-permute-start.1 = (bf16[2,128,256]{2,1,0:T(8,128)(2,1)S(1)}, bf16[2,128,256]{2,1,0:T(8,128)(2,1)S(1)}, u32[]{:S(2)}, u32[]{:S(2)}) collective-permute-start(bf16[2,128,256]{2,1,0:T(8,128)(2,1)S(1)} %own.1.u0), channel_id=1, source_target_pairs={{0,4},{1,5},{2,7},{3,6},{4,0},{5,1},{6,3},{7,2},{8,12},{9,13},{10,... | collective-permute-start | bytes 393224 | tf_op jit(solution)/shard_map/ppermute | solution.py:248
  7.1 0.7 %collective-permute-start.2 = (bf16[2,128,256]{2,1,0:T(8,128)(2,1)S(1)}, bf16[2,128,256]{2,1,0:T(8,128)(2,1)S(1)}, u32[]{:S(2)}, u32[]{:S(2)}) collective-permute-start(bf16[2,128,256]{2,1,0:T(8,128)(2,1)S(1)} %own.1.u0), channel_id=1, source_target_pairs={{0,2},{1,3},{2,0},{3,1},{4,6},{5,7},{6,4},{7,5},{8,10},{9,11},{10,... | collective-permute-start | bytes 393224 | tf_op jit(solution)/shard_map/ppermute | solution.py:248
  7.7 0.7 %collective-permute-start.3 = (bf16[2,128,256]{2,1,0:T(8,128)(2,1)S(1)}, bf16[2,128,256]{2,1,0:T(8,128)(2,1)S(1)}, u32[]{:S(2)}, u32[]{:S(2)}) collective-permute-start(bf16[2,128,256]{2,1,0:T(8,128)(2,1)S(1)} %own.1.u0), channel_id=1, source_target_pairs={{0,1},{1,0},{2,3},{3,2},{4,5},{5,4},{6,7},{7,6},{8,9},{9,8},{10,11... | collective-permute-start | bytes 393224 | tf_op jit(solution)/shard_map/ppermute | solution.py:248
  8.4 0.0 copy-done.2
  8.4 1.7 %factor_terms.1 = (bf16[2,3,256,256]{3,2,1,0:T(8,128)(2,1)S(1)}, bf16[1024,32]{1,0:T(8,128)(2,1)S(1)}) custom-call(s32[2]{0:T(128)S(1)} %copy-done.1, s32[1,32]{1,0:T(1,128)S(1)} %bitcast.4, f32[16,256,256]{2,1,0:T(8,128)} %act_f.1, f32[16,256,256]{2,1,0:T(8,128)} %grad_f.1), custom_call_target="tpu_custom_call" | custom-call | flops 1000000000 | bytes 1000000 | tf_op jit(solution)/shard_map/factor_terms/pallas_call | solution.py:227
  10.1 1.6 %collective-permute-done.v = bf16[2,128,256]{2,1,0:T(8,128)(2,1)S(1)} collective-permute-done((bf16[2,128,256]{2,1,0:T(8,128)(2,1)S(1)}, bf16[2,128,256]{2,1,0:T(8,128)(2,1)S(1)}, u32[]{:S(2)}, u32[]{:S(2)}) %collective-permute-start) | collective-permute-done | bytes 131104 | tf_op jit(solution)/shard_map/ppermute | solution.py:248
  11.7 0.6 %collective-permute-start.4 = (bf16[2,128,256]{2,1,0:T(8,128)(2,1)S(1)}, bf16[2,128,256]{2,1,0:T(8,128)(2,1)S(1)}, u32[]{:S(2)}, u32[]{:S(2)}) collective-permute-start(bf16[2,128,256]{2,1,0:T(8,128)(2,1)S(1)} %collective-permute-done.v), channel_id=1, source_target_pairs={{0,4},{1,5},{2,7},{3,6},{4,0},{5,1},{6,3},{7,2},{8,12},{9,13},{10,... | collective-permute-start | bytes 393224 | tf_op jit(solution)/shard_map/ppermute | solution.py:248
  12.3 1.1 %collective-permute-start.5 = (bf16[2,128,256]{2,1,0:T(8,128)(2,1)S(1)}, bf16[2,128,256]{2,1,0:T(8,128)(2,1)S(1)}, u32[]{:S(2)}, u32[]{:S(2)}) collective-permute-start(bf16[2,128,256]{2,1,0:T(8,128)(2,1)S(1)} %collective-permute-done.v), channel_id=1, source_target_pairs={{0,2},{1,3},{2,0},{3,1},{4,6},{5,7},{6,4},{7,5},{8,10},{9,11},{10,... | collective-permute-start | bytes 393224 | tf_op jit(solution)/shard_map/ppermute | solution.py:248
  13.4 0.0 collective-permute-done.1.u3
  13.4 0.0 collective-permute-done.2.u2
  13.5 0.0 collective-permute-done.3.u1
  13.5 1.1 %early_pairs.1 = (bf16[2,640,256]{2,1,0:T(8,128)(2,1)S(1)}, f32[4,1024]{1,0:T(4,128)S(1)}, f32[8,768]{1,0:T(8,128)S(1)}) custom-call(bf16[2,3,256,256]{3,2,1,0:T(8,128)(2,1)S(1)} %get-tuple-element.25.terms, bf16[2,128,256]{2,1,0:T(8,128)(2,1)S(1)} %own.1.u0, bf16[2,128,256]{2,1,0:T(8,128)(2,1)S(1)} %collective-permute-done.v, ...), custom_call_target="tpu_custom_call" | custom-call | flops 1000000000 | bytes 1000000 | tf_op jit(solution)/shard_map/early_pairs/pallas_call | solution.py:227
  14.5 0.3 collective-permute-start.6
  14.8 1.8 %collective-permute-done.4.v3 = bf16[2,128,256]{2,1,0:T(8,128)(2,1)S(1)} collective-permute-done((bf16[2,128,256]{2,1,0:T(8,128)(2,1)S(1)}, bf16[2,128,256]{2,1,0:T(8,128)(2,1)S(1)}, u32[]{:S(2)}, u32[]{:S(2)}) %collective-permute-start.4) | collective-permute-done | bytes 131104 | tf_op jit(solution)/shard_map/ppermute | solution.py:248
  16.7 0.4 %z_pairs.1 = (bf16[2,128,256]{2,1,0:T(8,128)(2,1)S(1)}, f32[8,768]{1,0:T(8,128)S(1)}) custom-call(bf16[2,3,256,256]{3,2,1,0:T(8,128)(2,1)S(1)} %get-tuple-element.25.terms, bf16[2,640,256]{2,1,0:T(8,128)(2,1)S(1)} %get-tuple-element.30.white, bf16[2,128,256]{2,1,0:T(8,128)(2,1)S(1)} %collective-permute-done.2.u2, ...), custom_call_target="tpu_custom_call", output_to_operand_aliasing={{1}: (5, {})} | custom-call | flops 1000000000 | bytes 1000000 | tf_op jit(solution)/shard_map/z_pairs/pallas_call | solution.py:227
  17.1 0.5 %collective-permute-done.5.v2 = bf16[2,128,256]{2,1,0:T(8,128)(2,1)S(1)} collective-permute-done((bf16[2,128,256]{2,1,0:T(8,128)(2,1)S(1)}, bf16[2,128,256]{2,1,0:T(8,128)(2,1)S(1)}, u32[]{:S(2)}, u32[]{:S(2)}) %collective-permute-start.5) | collective-permute-done | bytes 131104 | tf_op jit(solution)/shard_map/ppermute | solution.py:248
  17.6 0.0 collective-permute-done.6.v1
  17.6 0.8 %return_rows.1 = (f32[4,32]{1,0:T(4,128)S(1)}, f32[4,32]{1,0:T(4,128)S(1)}) custom-call(bf16[2,3,256,256]{3,2,1,0:T(8,128)(2,1)S(1)} %get-tuple-element.25.terms, bf16[2,640,256]{2,1,0:T(8,128)(2,1)S(1)} %get-tuple-element.30.white, bf16[2,128,256]{2,1,0:T(8,128)(2,1)S(1)} %get-tuple-element.35.white3, bf16[1024,32]{1,0:T(8,128)(2,1)S(1)} %get-tuple-element.31.pick, ...), custom_call_target="tpu_custom_call" | custom-call | flops 1000000000 | bytes 1000000 | tf_op jit(solution)/shard_map/return_rows/pallas_call | solution.py:227
  18.4 1.5 %collective-permute-start.8 = (f32[4,32]{1,0:T(4,128)S(1)}, f32[4,32]{1,0:T(4,128)S(1)}, u32[]{:S(2)}, u32[]{:S(2)}) collective-permute-start(f32[4,32]{1,0:T(4,128)S(1)} %get-tuple-element.38), channel_id=1, source_target_pairs={{0,4},{1,5},{2,7},{3,6},{4,0},{5,1},{6,3},{7,2},{8,12},{9,13},{10,... | collective-permute-start | bytes 1544 | tf_op jit(solution)/shard_map/ppermute | solution.py:248
  20.0 0.7 %collective-permute-start.7 = (f32[4,32]{1,0:T(4,128)S(1)}, f32[4,32]{1,0:T(4,128)S(1)}, u32[]{:S(2)}, u32[]{:S(2)}) collective-permute-start(f32[4,32]{1,0:T(4,128)S(1)} %get-tuple-element.37), channel_id=1, source_target_pairs={{0,2},{1,3},{2,0},{3,1},{4,6},{5,7},{6,4},{7,5},{8,10},{9,11},{10,... | collective-permute-start | bytes 1544 | tf_op jit(solution)/shard_map/ppermute | solution.py:248
  20.7 0.5 %own_rows.1 = f32[4,32]{1,0:T(4,128)S(1)} custom-call(bf16[2,640,256]{2,1,0:T(8,128)(2,1)S(1)} %get-tuple-element.30.white, bf16[1024,32]{1,0:T(8,128)(2,1)S(1)} %get-tuple-element.31.pick, f32[4,1024]{1,0:T(4,128)S(1)} %get-tuple-element.32.mine, bf16[2,128,256]{2,1,0:T(8,128)(2,1)S(1)} %collective-permute-done.4.v3, ...), custom_call_target="tpu_custom_call" | custom-call | flops 1000000000 | bytes 1000000 | tf_op jit(solution)/shard_map/own_rows/pallas_call | solution.py:227
  21.1 0.9 %collective-permute-done.8 = f32[4,32]{1,0:T(4,128)S(1)} collective-permute-done((f32[4,32]{1,0:T(4,128)S(1)}, f32[4,32]{1,0:T(4,128)S(1)}, u32[]{:S(2)}, u32[]{:S(2)}) %collective-permute-start.8) | collective-permute-done | bytes 544 | tf_op jit(solution)/shard_map/ppermute | solution.py:248
  22.1 1.4 %collective-permute-done.7 = f32[4,32]{1,0:T(4,128)S(1)} collective-permute-done((f32[4,32]{1,0:T(4,128)S(1)}, f32[4,32]{1,0:T(4,128)S(1)}, u32[]{:S(2)}, u32[]{:S(2)}) %collective-permute-start.7) | collective-permute-done | bytes 544 | tf_op jit(solution)/shard_map/ppermute | solution.py:248
  23.5 2.6 %collective-permute-start.9 = (f32[2,32]{1,0:T(2,128)S(1)}, f32[2,32]{1,0:T(2,128)S(1)}, u32[]{:S(2)}, u32[]{:S(2)}) collective-permute-start(f32[2,32]{1,0:T(2,128)S(1)} %slice.7), channel_id=1, source_target_pairs={{0,8},{1,9},{2,10},{3,11},{4,12},{5,13},{6,14},{7,15},{8,0},{9,1},... | collective-permute-start | bytes 776 | tf_op jit(solution)/shard_map/ppermute | solution.py:248
  26.1 2.0 %collective-permute-done.9 = f32[2,32]{1,0:T(2,128)S(1)} collective-permute-done((f32[2,32]{1,0:T(2,128)S(1)}, f32[2,32]{1,0:T(2,128)S(1)}, u32[]{:S(2)}, u32[]{:S(2)}) %collective-permute-start.9) | collective-permute-done | bytes 288 | tf_op jit(solution)/shard_map/ppermute | solution.py:248
  28.1 0.6 %slice_add_fusion = f32[2,32]{1,0:T(2,128)} fusion(f32[2,32]{1,0:T(2,128)S(1)} %collective-permute-done.9, f32[4,32]{1,0:T(4,128)S(1)} %add_add_fusion), kind=kLoop, calls=%fused_computation.1 | loop fusion | flops 64 | bytes 768 | tf_op jit(solution)/shard_map/add | solution.py:321
  (9 shorter events, 0.0 us)
Async XLA Ops:
  0.0 5.3 %copy-start.3 = (bf16[2,128,256]{2,1,0:T(8,128)(2,1)S(1)}, bf16[2,128,256]{2,1,0:T(8,128)(2,1)}, u32[]{:S(2)}) copy-start(bf16[2,128,256]{2,1,0:T(8,128)(2,1)} %acts.2) | copy-start | bytes 393220
  0.0 5.3 %copy-start.4 = (bf16[2,128,256]{2,1,0:T(8,128)(2,1)S(1)}, bf16[2,128,256]{2,1,0:T(8,128)(2,1)}, u32[]{:S(2)}) copy-start(bf16[2,128,256]{2,1,0:T(8,128)(2,1)} %grads.2) | copy-start | bytes 393220
  0.0 1.0 %copy-start = (s32[2]{0:T(128)S(1)}, s32[2]{0:T(128)}, u32[]{:S(2)}) copy-start(s32[2]{0:T(128)} %param.9) | copy-start | bytes 28
  0.0 8.4 %copy-start.1 = (s32[2]{0:T(128)S(1)}, s32[2]{0:T(128)}, u32[]{:S(2)}) copy-start(s32[2]{0:T(128)} %layer_ids.1) | copy-start | bytes 28
  0.0 8.4 %copy-start.2 = (s32[32]{0:T(128)S(1)}, s32[32]{0:T(128)}, u32[]{:S(2)}) copy-start(s32[32]{0:T(128)} %param.11) | copy-start | bytes 388
  1.1 10.5 %collective-permute-start = (bf16[2,128,256]{2,1,0:T(8,128)(2,1)S(1)}, bf16[2,128,256]{2,1,0:T(8,128)(2,1)S(1)}, u32[]{:S(2)}, u32[]{:S(2)}) collective-permute-start(bf16[2,128,256]{2,1,0:T(8,128)(2,1)S(1)} %away_mask.1), channel_id=1, source_target_pairs={{0,8},{1,9},{2,10},{3,11},{4,12},{5,13},{6,14},{7,15},{8,0},{9,1},... | collective-permute-start | bytes 393224 | tf_op jit(solution)/shard_map/ppermute | solution.py:248
  5.4 8.0 %collective-permute-start.1 = (bf16[2,128,256]{2,1,0:T(8,128)(2,1)S(1)}, bf16[2,128,256]{2,1,0:T(8,128)(2,1)S(1)}, u32[]{:S(2)}, u32[]{:S(2)}) collective-permute-start(bf16[2,128,256]{2,1,0:T(8,128)(2,1)S(1)} %own.1.u0), channel_id=1, source_target_pairs={{0,4},{1,5},{2,7},{3,6},{4,0},{5,1},{6,3},{7,2},{8,12},{9,13},{10,... | collective-permute-start | bytes 393224 | tf_op jit(solution)/shard_map/ppermute | solution.py:248
  7.1 6.4 %collective-permute-start.2 = (bf16[2,128,256]{2,1,0:T(8,128)(2,1)S(1)}, bf16[2,128,256]{2,1,0:T(8,128)(2,1)S(1)}, u32[]{:S(2)}, u32[]{:S(2)}) collective-permute-start(bf16[2,128,256]{2,1,0:T(8,128)(2,1)S(1)} %own.1.u0), channel_id=1, source_target_pairs={{0,2},{1,3},{2,0},{3,1},{4,6},{5,7},{6,4},{7,5},{8,10},{9,11},{10,... | collective-permute-start | bytes 393224 | tf_op jit(solution)/shard_map/ppermute | solution.py:248
  7.7 5.7 %collective-permute-start.3 = (bf16[2,128,256]{2,1,0:T(8,128)(2,1)S(1)}, bf16[2,128,256]{2,1,0:T(8,128)(2,1)S(1)}, u32[]{:S(2)}, u32[]{:S(2)}) collective-permute-start(bf16[2,128,256]{2,1,0:T(8,128)(2,1)S(1)} %own.1.u0), channel_id=1, source_target_pairs={{0,1},{1,0},{2,3},{3,2},{4,5},{5,4},{6,7},{7,6},{8,9},{9,8},{10,11... | collective-permute-start | bytes 393224 | tf_op jit(solution)/shard_map/ppermute | solution.py:248
  11.7 5.0 %collective-permute-start.4 = (bf16[2,128,256]{2,1,0:T(8,128)(2,1)S(1)}, bf16[2,128,256]{2,1,0:T(8,128)(2,1)S(1)}, u32[]{:S(2)}, u32[]{:S(2)}) collective-permute-start(bf16[2,128,256]{2,1,0:T(8,128)(2,1)S(1)} %collective-permute-done.v), channel_id=1, source_target_pairs={{0,4},{1,5},{2,7},{3,6},{4,0},{5,1},{6,3},{7,2},{8,12},{9,13},{10,... | collective-permute-start | bytes 393224 | tf_op jit(solution)/shard_map/ppermute | solution.py:248
  12.3 5.3 %collective-permute-start.5 = (bf16[2,128,256]{2,1,0:T(8,128)(2,1)S(1)}, bf16[2,128,256]{2,1,0:T(8,128)(2,1)S(1)}, u32[]{:S(2)}, u32[]{:S(2)}) collective-permute-start(bf16[2,128,256]{2,1,0:T(8,128)(2,1)S(1)} %collective-permute-done.v), channel_id=1, source_target_pairs={{0,2},{1,3},{2,0},{3,1},{4,6},{5,7},{6,4},{7,5},{8,10},{9,11},{10,... | collective-permute-start | bytes 393224 | tf_op jit(solution)/shard_map/ppermute | solution.py:248
  14.5 3.1 %collective-permute-start.6 = (bf16[2,128,256]{2,1,0:T(8,128)(2,1)S(1)}, bf16[2,128,256]{2,1,0:T(8,128)(2,1)S(1)}, u32[]{:S(2)}, u32[]{:S(2)}) collective-permute-start(bf16[2,128,256]{2,1,0:T(8,128)(2,1)S(1)} %collective-permute-done.v), channel_id=1, source_target_pairs={{0,1},{1,0},{2,3},{3,2},{4,5},{5,4},{6,7},{7,6},{8,9},{9,8},{10,11... | collective-permute-start | bytes 393224 | tf_op jit(solution)/shard_map/ppermute | solution.py:248
  18.4 3.6 %collective-permute-start.8 = (f32[4,32]{1,0:T(4,128)S(1)}, f32[4,32]{1,0:T(4,128)S(1)}, u32[]{:S(2)}, u32[]{:S(2)}) collective-permute-start(f32[4,32]{1,0:T(4,128)S(1)} %get-tuple-element.38), channel_id=1, source_target_pairs={{0,4},{1,5},{2,7},{3,6},{4,0},{5,1},{6,3},{7,2},{8,12},{9,13},{10,... | collective-permute-start | bytes 1544 | tf_op jit(solution)/shard_map/ppermute | solution.py:248
  20.0 3.6 %collective-permute-start.7 = (f32[4,32]{1,0:T(4,128)S(1)}, f32[4,32]{1,0:T(4,128)S(1)}, u32[]{:S(2)}, u32[]{:S(2)}) collective-permute-start(f32[4,32]{1,0:T(4,128)S(1)} %get-tuple-element.37), channel_id=1, source_target_pairs={{0,2},{1,3},{2,0},{3,1},{4,6},{5,7},{6,4},{7,5},{8,10},{9,11},{10,... | collective-permute-start | bytes 1544 | tf_op jit(solution)/shard_map/ppermute | solution.py:248
  23.5 4.5 %collective-permute-start.9 = (f32[2,32]{1,0:T(2,128)S(1)}, f32[2,32]{1,0:T(2,128)S(1)}, u32[]{:S(2)}, u32[]{:S(2)}) collective-permute-start(f32[2,32]{1,0:T(2,128)S(1)} %slice.7), channel_id=1, source_target_pairs={{0,8},{1,9},{2,10},{3,11},{4,12},{5,13},{6,14},{7,15},{8,0},{9,1},... | collective-permute-start | bytes 776 | tf_op jit(solution)/shard_map/ppermute | solution.py:248

commit v17 on v14

--- a/solution.py
+++ b/solution.py
@@ -169,21 +169,8 @@
             side[row : row + per, at : at + n] = block(seq_len, left[slot], tok[column])
 
 
-def core_kernel(seq_len, per, terms, white, v1, mine, side, white1, mine_out, side_out):
-    n = v1.shape[1]
-    tok = [v1[w] for w in range(2)]
-    for w in range(2):
-        white1[w] = whiten(tok[w], terms.at[w])
-    mine_out[...] = mine[...]
-    mine_out[:, 3 * n : 4 * n] = block(seq_len, [white[w, : 2 * n] for w in range(2)], tok)
-    side_out[...] = side[...]
-    got = block(seq_len, [white[w, 2 * n : 4 * n] for w in range(2)], tok)
-    for i, row in enumerate((0, 2 * per)):
-        side_out[row : row + per, n : 2 * n] = got[i * per : (i + 1) * per]
-
-
-def z_kernel(seq_len, per, terms, white, u2, u1, v1, v3, side, white3, side_out):
-    n = v1.shape[1]
+def z_kernel(seq_len, per, terms, white, u2, u1, v3, side, white3, side_out):
+    n = v3.shape[1]
     tok = [v3[w] for w in range(2)]
     fresh = [whiten(tok[w], terms.at[w]) for w in range(2)]
     for w in range(2):
@@ -192,12 +179,28 @@
     side_out[0:per, 5 * n : 6 * n] = block(
         seq_len, [white[w, 2 * n : 3 * n] for w in range(2)], tok
     )
-    side_out[3 * per : 4 * per, 0 : 3 * n] = block(
-        seq_len, fresh, [stack(u1[w], v1[w], u2[w]) for w in range(2)]
-    )
-
-
-def return_kernel(seq_len, per, white, white1, white3, pick, side, v2, by_x, by_z):
+    got = block(seq_len, fresh, [stack(u1[w], u2[w]) for w in range(2)])
+    side_out[3 * per : 4 * per, 0:n] = got[:, :n]
+    side_out[3 * per : 4 * per, 2 * n : 3 * n] = got[:, n:]
+
+
+def core_kernel(
+    seq_len, per, terms, white, white3, acts, grads, mine, side, white1, mine_out, side_out
+):
+    n = acts.shape[0]
+    tok = [acts[...], grads[...]]
+    for w in range(2):
+        white1[w] = whiten(tok[w], terms.at[w])
+    mine_out[...] = mine[...]
+    mine_out[:, 3 * n : 4 * n] = block(seq_len, [white[w, : 2 * n] for w in range(2)], tok)
+    side_out[...] = side[...]
+    left = [stack(white[w, 2 * n : 4 * n], white3[w]) for w in range(2)]
+    got = block(seq_len, left, tok)
+    for i, row in enumerate((0, 2 * per, 3 * per)):
+        side_out[row : row + per, n : 2 * n] = got[i * per : (i + 1) * per]
+
+
+def return_kernel(seq_len, per, white, white1, white3, pick, side, v2, by_z, by_x):
     n = v2.shape[1]
     tok = [v2[w] for w in range(2)]
     columns = [
@@ -292,16 +295,16 @@
         [pltpu.VMEM((2, rank, rank), f32), pltpu.SemaphoreType.DMA((2,))],
     )
     v, terms, pick = lax.optimization_barrier((v, terms, pick))
-    late = [send(v, to) for to in ways]
+    late = [send(v, to) for to in ways[:2]]
     whole = shape((2 * per, 8 * tokens), f32)
     sides = shape((4 * per, 6 * tokens), f32)
     rows = shape((2 * per, columns), f32)
     u3, u2, u1 = near
-    v3, v2, v1 = late
-
-    def kernel(body, name, operands, out_shape, **more):
+    v3, v2 = late
+
+    def kernel(body, name, operands, out_shape, flops=10**9, **more):
         body = functools.partial(body, seq_len, per)
-        return call(body, name, 10**9, 40, operands, [], out_shape, **more)
+        return call(body, name, flops, 40, operands, [], out_shape, **more)
 
     white, mine, side = kernel(
         early_kernel,
@@ -309,25 +312,29 @@
         (terms, own, v, u3, u2, u1),
         (shape((2, 5 * tokens, rank), bf16), whole, sides),
     )
+    v, white = lax.optimization_barrier((v, white))
+    v1 = [send(v[w], ways[2]) for w in range(2)]
+    white3, side = kernel(
+        z_kernel,
+        "z_pairs",
+        (terms, white, u2, u1, v3, side),
+        (unit, sides),
+        flops=10**4,
+        input_output_aliases={5: 1},
+    )
     white1, mine, side = kernel(
         core_kernel,
         "core_pairs",
-        (terms, white, v1, mine, side),
+        (terms, white, white3, *v1, mine, side),
         (unit, whole, sides),
-        input_output_aliases={3: 1, 4: 2},
-    )
-    white3, side = kernel(
-        z_kernel,
-        "z_pairs",
-        (terms, white, u2, u1, v1, v3, side),
-        (unit, sides),
-        input_output_aliases={6: 1},
-    )
-    by_x, by_z = kernel(
+        flops=10**4,
+        input_output_aliases={5: 1, 6: 2},
+    )
+    by_z, by_x = kernel(
         return_kernel, "return_rows", (white, white1, white3, pick, side, v2), (rows, rows)
     )
     mine = kernel(rows_kernel, "own_rows", (white, pick, mine, v3, v2), rows)
-    half_sum = mine + send(by_x, lambda d: d ^ 2) + send(by_z, z_near)
+    half_sum = mine + send(by_z, z_near) + send(by_x, lambda d: d ^ 2)
     return half_sum[:per] + send(half_sum[per:], opposite)
 
 

time: 29.3 us -> 28.6 us (0.976)
  starting transfers between devices: 15.8 us -> 14.9 us
    ppermute x10 -> x11, starting transfers between devices: 15.8 us -> 14.9 us  [send(): return lax.ppermute(x, 'blk', [(d, to(d)) for d in range(size)])]
    ppermute x10 -> x11, waiting for transfers between devices: 6.87 us -> 6.96 us  [send(): return lax.ppermute(x, 'blk', [(d, to(d)) for d in range(size)])]
  transfers between devices with their start and end apart: 10 -> 11, of which waited for: 6 -> 6; matrix products, arithmetic and copies ran while one was open for 0% -> 0% of each run, Pallas kernels for 14% -> 15%
where the time goes in v17:
time: 28.6 us; the launch traced here: 28.4 us
  starting transfers between devices  14.9 us (52%)
  waiting for transfers between devices  6.96 us (24%)
  Pallas kernels  5.82 us (20%)
  other arithmetic  0.57 us (2%)
    ppermute x11, starting transfers between devices, send(): return lax.ppermute(x, 'blk', [(d, to(d)) for d in range(size)])  14.9 us
    ppermute x11, waiting for transfers between devices, send(): return lax.ppermute(x, 'blk', [(d, to(d)) for d in range(size)])  6.96 us
    pallas_call x9, Pallas kernels, call(): pl.pallas_call(kernel, out_shape=out_shape, in_specs=specs + [vmem] * (le...  5.82 us
  transfers between devices with their start and end apart: 11, of which 6 were waited for; matrix products, arithmetic and copies ran while one was open for 0% of the time, Pallas kernels for 15%

profile of v17, /device:TPU:0, one launch (start us, length us, event | category | flops | bytes accessed | tf_op | source)
XLA Modules:
  0.0 28.4 jit_solution(6641120011264139334)
XLA Ops:
  0.0 1.0 %away.1.unit = bf16[2,128,256]{2,1,0:T(8,128)(2,1)S(1)} custom-call(bf16[2,128,256]{2,1,0:T(8,128)(2,1)} %acts.2, bf16[2,128,256]{2,1,0:T(8,128)(2,1)} %grads.2), custom_call_target="tpu_custom_call" | custom-call | flops 3000000000 | bytes 1000000 | tf_op jit(solution)/shard_map/away/pallas_call | solution.py:235
  1.0 0.2 away_mask.1
  1.1 4.1 %collective-permute-start = (bf16[2,128,256]{2,1,0:T(8,128)(2,1)S(1)}, bf16[2,128,256]{2,1,0:T(8,128)(2,1)S(1)}, u32[]{:S(2)}, u32[]{:S(2)}) collective-permute-start(bf16[2,128,256]{2,1,0:T(8,128)(2,1)S(1)} %away_mask.1), channel_id=1, source_target_pairs={{0,8},{1,9},{2,10},{3,11},{4,12},{5,13},{6,14},{7,15},{8,0},{9,1},... | collective-permute-start | bytes 393224 | tf_op jit(solution)/shard_map/ppermute | solution.py:256
  5.3 0.1 own.1.u0
  5.4 1.6 %collective-permute-start.2 = (bf16[2,128,256]{2,1,0:T(8,128)(2,1)S(1)}, bf16[2,128,256]{2,1,0:T(8,128)(2,1)S(1)}, u32[]{:S(2)}, u32[]{:S(2)}) collective-permute-start(bf16[2,128,256]{2,1,0:T(8,128)(2,1)S(1)} %own.1.u0), channel_id=1, source_target_pairs={{0,2},{1,3},{2,0},{3,1},{4,6},{5,7},{6,4},{7,5},{8,10},{9,11},{10,... | collective-permute-start | bytes 393224 | tf_op jit(solution)/shard_map/ppermute | solution.py:256
  7.0 0.0 collective-permute-start.3
  7.0 1.6 %collective-permute-start.1 = (bf16[2,128,256]{2,1,0:T(8,128)(2,1)S(1)}, bf16[2,128,256]{2,1,0:T(8,128)(2,1)S(1)}, u32[]{:S(2)}, u32[]{:S(2)}) collective-permute-start(bf16[2,128,256]{2,1,0:T(8,128)(2,1)S(1)} %own.1.u0), channel_id=1, source_target_pairs={{0,4},{1,5},{2,7},{3,6},{4,0},{5,1},{6,3},{7,2},{8,12},{9,13},{10,... | collective-permute-start | bytes 393224 | tf_op jit(solution)/shard_map/ppermute | solution.py:256
  8.6 1.7 %factor_terms.1 = (bf16[2,3,256,256]{3,2,1,0:T(8,128)(2,1)S(1)}, bf16[1024,32]{1,0:T(8,128)(2,1)S(1)}) custom-call(s32[2]{0:T(128)S(1)} %copy-done.1, s32[1,32]{1,0:T(1,128)S(1)} %bitcast.8, f32[16,256,256]{2,1,0:T(8,128)} %act_f.1, f32[16,256,256]{2,1,0:T(8,128)} %grad_f.1), custom_call_target="tpu_custom_call" | custom-call | flops 1000000000 | bytes 1000000 | tf_op jit(solution)/shard_map/factor_terms/pallas_call | solution.py:235
  10.3 1.4 %collective-permute-done.v = bf16[2,128,256]{2,1,0:T(8,128)(2,1)S(1)} collective-permute-done((bf16[2,128,256]{2,1,0:T(8,128)(2,1)S(1)}, bf16[2,128,256]{2,1,0:T(8,128)(2,1)S(1)}, u32[]{:S(2)}, u32[]{:S(2)}) %collective-permute-start) | collective-permute-done | bytes 131104 | tf_op jit(solution)/shard_map/ppermute | solution.py:256
  11.7 0.7 %collective-permute-start.4 = (bf16[2,128,256]{2,1,0:T(8,128)(2,1)S(1)}, bf16[2,128,256]{2,1,0:T(8,128)(2,1)S(1)}, u32[]{:S(2)}, u32[]{:S(2)}) collective-permute-start(bf16[2,128,256]{2,1,0:T(8,128)(2,1)S(1)} %collective-permute-done.v), channel_id=1, source_target_pairs={{0,4},{1,5},{2,7},{3,6},{4,0},{5,1},{6,3},{7,2},{8,12},{9,13},{10,... | collective-permute-start | bytes 393224 | tf_op jit(solution)/shard_map/ppermute | solution.py:256
  12.4 1.1 %collective-permute-start.7 = (bf16[2,128,256]{2,1,0:T(8,128)(2,1)S(1)}, bf16[2,128,256]{2,1,0:T(8,128)(2,1)S(1)}, u32[]{:S(2)}, u32[]{:S(2)}) collective-permute-start(bf16[2,128,256]{2,1,0:T(8,128)(2,1)S(1)} %collective-permute-done.v), channel_id=1, source_target_pairs={{0,2},{1,3},{2,0},{3,1},{4,6},{5,7},{6,4},{7,5},{8,10},{9,11},{10,... | collective-permute-start | bytes 393224 | tf_op jit(solution)/shard_map/ppermute | solution.py:256
  13.5 0.0 collective-permute-done.2.u2
  13.5 0.0 collective-permute-done.3.u1
  13.5 1.0 %collective-permute-done.1.u3 = bf16[2,128,256]{2,1,0:T(8,128)(2,1)S(1)} collective-permute-done((bf16[2,128,256]{2,1,0:T(8,128)(2,1)S(1)}, bf16[2,128,256]{2,1,0:T(8,128)(2,1)S(1)}, u32[]{:S(2)}, u32[]{:S(2)}) %collective-permute-start.1) | collective-permute-done | bytes 131104 | tf_op jit(solution)/shard_map/ppermute | solution.py:256
  14.4 1.1 %early_pairs.1 = (bf16[2,640,256]{2,1,0:T(8,128)(2,1)S(1)}, f32[4,1024]{1,0:T(4,128)S(1)}, f32[8,768]{1,0:T(8,128)S(1)}) custom-call(bf16[2,3,256,256]{3,2,1,0:T(8,128)(2,1)S(1)} %get-tuple-element.28.terms, bf16[2,128,256]{2,1,0:T(8,128)(2,1)S(1)} %own.1.u0, bf16[2,128,256]{2,1,0:T(8,128)(2,1)S(1)} %collective-permute-done.v, ...), custom_call_target="tpu_custom_call" | custom-call | flops 1000000000 | bytes 1000000 | tf_op jit(solution)/shard_map/early_pairs/pallas_call | solution.py:235
  15.6 0.1 collective-permute-start.5
  15.7 0.5 %collective-permute-start.6 = (bf16[128,256]{1,0:T(8,128)(2,1)S(1)}, bf16[128,256]{1,0:T(8,128)(2,1)S(1)}, u32[]{:S(2)}, u32[]{:S(2)}) collective-permute-start(bf16[128,256]{1,0:T(8,128)(2,1)S(1)} %get-tuple-element.45), channel_id=1, source_target_pairs={{0,1},{1,0},{2,3},{3,2},{4,5},{5,4},{6,7},{7,6},{8,9},{9,8},{10,11... | collective-permute-start | bytes 196616 | tf_op jit(solution)/shard_map/ppermute | solution.py:256
  16.1 1.1 %collective-permute-done.4.v3 = bf16[2,128,256]{2,1,0:T(8,128)(2,1)S(1)} collective-permute-done((bf16[2,128,256]{2,1,0:T(8,128)(2,1)S(1)}, bf16[2,128,256]{2,1,0:T(8,128)(2,1)S(1)}, u32[]{:S(2)}, u32[]{:S(2)}) %collective-permute-start.4) | collective-permute-done | bytes 131104 | tf_op jit(solution)/shard_map/ppermute | solution.py:256
  17.2 0.4 %z_pairs.1 = (bf16[2,128,256]{2,1,0:T(8,128)(2,1)S(1)}, f32[8,768]{1,0:T(8,128)S(1)}) custom-call(bf16[2,3,256,256]{3,2,1,0:T(8,128)(2,1)S(1)} %get-tuple-element.28.terms, bf16[2,640,256]{2,1,0:T(8,128)(2,1)S(1)} %get-tuple-element.33.white, bf16[2,128,256]{2,1,0:T(8,128)(2,1)S(1)} %collective-permute-done.2.u2, ...), custom_call_target="tpu_custom_call", output_to_operand_aliasing={{1}: (5, {})} | custom-call | flops 10000 | bytes 1000000 | tf_op jit(solution)/shard_map/z_pairs/pallas_call | solution.py:235
  17.6 0.0 collective-permute-done.5.acts
  17.6 0.0 collective-permute-done.6.grads
  17.7 0.5 %core_pairs.1 = (bf16[2,128,256]{2,1,0:T(8,128)(2,1)S(1)}, f32[4,1024]{1,0:T(4,128)S(1)}, f32[8,768]{1,0:T(8,128)S(1)}) custom-call(bf16[2,3,256,256]{3,2,1,0:T(8,128)(2,1)S(1)} %get-tuple-element.28.terms, bf16[2,640,256]{2,1,0:T(8,128)(2,1)S(1)} %get-tuple-element.33.white, ...), custom_call_target="tpu_custom_call", output_to_operand_aliasing={{1}: (5, {}), {2}: (6, {})} | custom-call | flops 10000 | bytes 1000000 | tf_op jit(solution)/shard_map/core_pairs/pallas_call | solution.py:235
  18.1 0.0 collective-permute-done.7.v2
  18.1 0.5 %return_rows.1 = (f32[4,32]{1,0:T(4,128)S(1)}, f32[4,32]{1,0:T(4,128)S(1)}) custom-call(bf16[2,640,256]{2,1,0:T(8,128)(2,1)S(1)} %get-tuple-element.33.white, bf16[2,128,256]{2,1,0:T(8,128)(2,1)S(1)} %get-tuple-element.41.white1, bf16[2,128,256]{2,1,0:T(8,128)(2,1)S(1)} %get-tuple-element.36.white3, bf16[1024,32]{1,0:T(8,128)(2,1)S(1)} %get-tuple-element.34.pick, ...), custom_call_target="tpu_custom_call" | custom-call | flops 1000000000 | bytes 1000000 | tf_op jit(solution)/shard_map/return_rows/pallas_call | solution.py:235
  18.6 1.0 %collective-permute-start.8 = (f32[4,32]{1,0:T(4,128)S(1)}, f32[4,32]{1,0:T(4,128)S(1)}, u32[]{:S(2)}, u32[]{:S(2)}) collective-permute-start(f32[4,32]{1,0:T(4,128)S(1)} %get-tuple-element.43), channel_id=1, source_target_pairs={{0,4},{1,5},{2,7},{3,6},{4,0},{5,1},{6,3},{7,2},{8,12},{9,13},{10,... | collective-permute-start | bytes 1544 | tf_op jit(solution)/shard_map/ppermute | solution.py:256
  19.6 1.2 %collective-permute-start.9 = (f32[4,32]{1,0:T(4,128)S(1)}, f32[4,32]{1,0:T(4,128)S(1)}, u32[]{:S(2)}, u32[]{:S(2)}) collective-permute-start(f32[4,32]{1,0:T(4,128)S(1)} %get-tuple-element.44), channel_id=1, source_target_pairs={{0,2},{1,3},{2,0},{3,1},{4,6},{5,7},{6,4},{7,5},{8,10},{9,11},{10,... | collective-permute-start | bytes 1544 | tf_op jit(solution)/shard_map/ppermute | solution.py:256
  20.9 0.4 %own_rows.1 = f32[4,32]{1,0:T(4,128)S(1)} custom-call(bf16[2,640,256]{2,1,0:T(8,128)(2,1)S(1)} %get-tuple-element.33.white, bf16[1024,32]{1,0:T(8,128)(2,1)S(1)} %get-tuple-element.34.pick, f32[4,1024]{1,0:T(4,128)S(1)} %get-tuple-element.40.mine, bf16[2,128,256]{2,1,0:T(8,128)(2,1)S(1)} %collective-permute-done.4.v3, ...), custom_call_target="tpu_custom_call" | custom-call | flops 1000000000 | bytes 1000000 | tf_op jit(solution)/shard_map/own_rows/pallas_call | solution.py:235
  21.3 1.0 %collective-permute-done.8 = f32[4,32]{1,0:T(4,128)S(1)} collective-permute-done((f32[4,32]{1,0:T(4,128)S(1)}, f32[4,32]{1,0:T(4,128)S(1)}, u32[]{:S(2)}, u32[]{:S(2)}) %collective-permute-start.8) | collective-permute-done | bytes 544 | tf_op jit(solution)/shard_map/ppermute | solution.py:256
  22.3 0.9 %collective-permute-done.9 = f32[4,32]{1,0:T(4,128)S(1)} collective-permute-done((f32[4,32]{1,0:T(4,128)S(1)}, f32[4,32]{1,0:T(4,128)S(1)}, u32[]{:S(2)}, u32[]{:S(2)}) %collective-permute-start.9) | collective-permute-done | bytes 544 | tf_op jit(solution)/shard_map/ppermute | solution.py:256
  23.2 3.1 %collective-permute-start.10 = (f32[2,32]{1,0:T(2,128)S(1)}, f32[2,32]{1,0:T(2,128)S(1)}, u32[]{:S(2)}, u32[]{:S(2)}) collective-permute-start(f32[2,32]{1,0:T(2,128)S(1)} %slice.15), channel_id=1, source_target_pairs={{0,8},{1,9},{2,10},{3,11},{4,12},{5,13},{6,14},{7,15},{8,0},{9,1},... | collective-permute-start | bytes 776 | tf_op jit(solution)/shard_map/ppermute | solution.py:256
  26.3 1.5 %collective-permute-done.10 = f32[2,32]{1,0:T(2,128)S(1)} collective-permute-done((f32[2,32]{1,0:T(2,128)S(1)}, f32[2,32]{1,0:T(2,128)S(1)}, u32[]{:S(2)}, u32[]{:S(2)}) %collective-permute-start.10) | collective-permute-done | bytes 288 | tf_op jit(solution)/shard_map/ppermute | solution.py:256
  27.9 0.6 %slice_add_fusion = f32[2,32]{1,0:T(2,128)} fusion(f32[2,32]{1,0:T(2,128)S(1)} %collective-permute-done.10, f32[4,32]{1,0:T(4,128)S(1)} %add_add_fusion), kind=kLoop, calls=%fused_computation.3 | loop fusion | flops 64 | bytes 768 | tf_op jit(solution)/shard_map/add | solution.py:338
  (13 shorter events, 0.0 us)
Async XLA Ops:
  0.0 5.3 %copy-start.3 = (bf16[2,128,256]{2,1,0:T(8,128)(2,1)S(1)}, bf16[2,128,256]{2,1,0:T(8,128)(2,1)}, u32[]{:S(2)}) copy-start(bf16[2,128,256]{2,1,0:T(8,128)(2,1)} %acts.2) | copy-start | bytes 393220
  0.0 5.3 %copy-start.4 = (bf16[2,128,256]{2,1,0:T(8,128)(2,1)S(1)}, bf16[2,128,256]{2,1,0:T(8,128)(2,1)}, u32[]{:S(2)}) copy-start(bf16[2,128,256]{2,1,0:T(8,128)(2,1)} %grads.2) | copy-start | bytes 393220
  0.0 1.0 %copy-start = (s32[2]{0:T(128)S(1)}, s32[2]{0:T(128)}, u32[]{:S(2)}) copy-start(s32[2]{0:T(128)} %param.9) | copy-start | bytes 28
  0.0 8.6 %copy-start.2 = (s32[32]{0:T(128)S(1)}, s32[32]{0:T(128)}, u32[]{:S(2)}) copy-start(s32[32]{0:T(128)} %param.11) | copy-start | bytes 388
  0.0 8.6 %copy-start.1 = (s32[2]{0:T(128)S(1)}, s32[2]{0:T(128)}, u32[]{:S(2)}) copy-start(s32[2]{0:T(128)} %layer_ids.1) | copy-start | bytes 28
  1.1 10.5 %collective-permute-start = (bf16[2,128,256]{2,1,0:T(8,128)(2,1)S(1)}, bf16[2,128,256]{2,1,0:T(8,128)(2,1)S(1)}, u32[]{:S(2)}, u32[]{:S(2)}) collective-permute-start(bf16[2,128,256]{2,1,0:T(8,128)(2,1)S(1)} %away_mask.1), channel_id=1, source_target_pairs={{0,8},{1,9},{2,10},{3,11},{4,12},{5,13},{6,14},{7,15},{8,0},{9,1},... | collective-permute-start | bytes 393224 | tf_op jit(solution)/shard_map/ppermute | solution.py:256
  5.4 8.0 %collective-permute-start.2 = (bf16[2,128,256]{2,1,0:T(8,128)(2,1)S(1)}, bf16[2,128,256]{2,1,0:T(8,128)(2,1)S(1)}, u32[]{:S(2)}, u32[]{:S(2)}) collective-permute-start(bf16[2,128,256]{2,1,0:T(8,128)(2,1)S(1)} %own.1.u0), channel_id=1, source_target_pairs={{0,2},{1,3},{2,0},{3,1},{4,6},{5,7},{6,4},{7,5},{8,10},{9,11},{10,... | collective-permute-start | bytes 393224 | tf_op jit(solution)/shard_map/ppermute | solution.py:256
  7.0 6.5 %collective-permute-start.3 = (bf16[2,128,256]{2,1,0:T(8,128)(2,1)S(1)}, bf16[2,128,256]{2,1,0:T(8,128)(2,1)S(1)}, u32[]{:S(2)}, u32[]{:S(2)}) collective-permute-start(bf16[2,128,256]{2,1,0:T(8,128)(2,1)S(1)} %own.1.u0), channel_id=1, source_target_pairs={{0,1},{1,0},{2,3},{3,2},{4,5},{5,4},{6,7},{7,6},{8,9},{9,8},{10,11... | collective-permute-start | bytes 393224 | tf_op jit(solution)/shard_map/ppermute | solution.py:256
  7.0 7.4 %collective-permute-start.1 = (bf16[2,128,256]{2,1,0:T(8,128)(2,1)S(1)}, bf16[2,128,256]{2,1,0:T(8,128)(2,1)S(1)}, u32[]{:S(2)}, u32[]{:S(2)}) collective-permute-start(bf16[2,128,256]{2,1,0:T(8,128)(2,1)S(1)} %own.1.u0), channel_id=1, source_target_pairs={{0,4},{1,5},{2,7},{3,6},{4,0},{5,1},{6,3},{7,2},{8,12},{9,13},{10,... | collective-permute-start | bytes 393224 | tf_op jit(solution)/shard_map/ppermute | solution.py:256
  11.7 5.5 %collective-permute-start.4 = (bf16[2,128,256]{2,1,0:T(8,128)(2,1)S(1)}, bf16[2,128,256]{2,1,0:T(8,128)(2,1)S(1)}, u32[]{:S(2)}, u32[]{:S(2)}) collective-permute-start(bf16[2,128,256]{2,1,0:T(8,128)(2,1)S(1)} %collective-permute-done.v), channel_id=1, source_target_pairs={{0,4},{1,5},{2,7},{3,6},{4,0},{5,1},{6,3},{7,2},{8,12},{9,13},{10,... | collective-permute-start | bytes 393224 | tf_op jit(solution)/shard_map/ppermute | solution.py:256
  12.4 5.8 %collective-permute-start.7 = (bf16[2,128,256]{2,1,0:T(8,128)(2,1)S(1)}, bf16[2,128,256]{2,1,0:T(8,128)(2,1)S(1)}, u32[]{:S(2)}, u32[]{:S(2)}) collective-permute-start(bf16[2,128,256]{2,1,0:T(8,128)(2,1)S(1)} %collective-permute-done.v), channel_id=1, source_target_pairs={{0,2},{1,3},{2,0},{3,1},{4,6},{5,7},{6,4},{7,5},{8,10},{9,11},{10,... | collective-permute-start | bytes 393224 | tf_op jit(solution)/shard_map/ppermute | solution.py:256
  15.6 2.1 %collective-permute-start.5 = (bf16[128,256]{1,0:T(8,128)(2,1)S(1)}, bf16[128,256]{1,0:T(8,128)(2,1)S(1)}, u32[]{:S(2)}, u32[]{:S(2)}) collective-permute-start(bf16[128,256]{1,0:T(8,128)(2,1)S(1)} %get-tuple-element.46), channel_id=1, source_target_pairs={{0,1},{1,0},{2,3},{3,2},{4,5},{5,4},{6,7},{7,6},{8,9},{9,8},{10,11... | collective-permute-start | bytes 196616 | tf_op jit(solution)/shard_map/ppermute | solution.py:256
  15.7 2.0 %collective-permute-start.6 = (bf16[128,256]{1,0:T(8,128)(2,1)S(1)}, bf16[128,256]{1,0:T(8,128)(2,1)S(1)}, u32[]{:S(2)}, u32[]{:S(2)}) collective-permute-start(bf16[128,256]{1,0:T(8,128)(2,1)S(1)} %get-tuple-element.45), channel_id=1, source_target_pairs={{0,1},{1,0},{2,3},{3,2},{4,5},{5,4},{6,7},{7,6},{8,9},{9,8},{10,11... | collective-permute-start | bytes 196616 | tf_op jit(solution)/shard_map/ppermute | solution.py:256
  18.6 3.6 %collective-permute-start.8 = (f32[4,32]{1,0:T(4,128)S(1)}, f32[4,32]{1,0:T(4,128)S(1)}, u32[]{:S(2)}, u32[]{:S(2)}) collective-permute-start(f32[4,32]{1,0:T(4,128)S(1)} %get-tuple-element.43), channel_id=1, source_target_pairs={{0,4},{1,5},{2,7},{3,6},{4,0},{5,1},{6,3},{7,2},{8,12},{9,13},{10,... | collective-permute-start | bytes 1544 | tf_op jit(solution)/shard_map/ppermute | solution.py:256
  19.6 3.6 %collective-permute-start.9 = (f32[4,32]{1,0:T(4,128)S(1)}, f32[4,32]{1,0:T(4,128)S(1)}, u32[]{:S(2)}, u32[]{:S(2)}) collective-permute-start(f32[4,32]{1,0:T(4,128)S(1)} %get-tuple-element.44), channel_id=1, source_target_pairs={{0,2},{1,3},{2,0},{3,1},{4,6},{5,7},{6,4},{7,5},{8,10},{9,11},{10,... | collective-permute-start | bytes 1544 | tf_op jit(solution)/shard_map/ppermute | solution.py:256
  23.2 4.6 %collective-permute-start.10 = (f32[2,32]{1,0:T(2,128)S(1)}, f32[2,32]{1,0:T(2,128)S(1)}, u32[]{:S(2)}, u32[]{:S(2)}) collective-permute-start(f32[2,32]{1,0:T(2,128)S(1)} %slice.15), channel_id=1, source_target_pairs={{0,8},{1,9},{2,10},{3,11},{4,12},{5,13},{6,14},{7,15},{8,0},{9,1},... | collective-permute-start | bytes 776 | tf_op jit(solution)/shard_map/ppermute | solution.py:256

commit v18 on v17

--- a/solution.py
+++ b/solution.py
@@ -149,7 +149,7 @@
     n = u0.shape[1]
     rows = []
     for w in range(2):
-        white[w] = whiten(stack(u0[w], v[w], u2[w], u3[w], u1[w]), terms.at[w])
+        white[w] = whiten(stack(u0[w], v[w], u2[w], u3[w]), terms.at[w])
         rows.append(white[w])
     left = {
         0: [r[: 2 * n] for r in rows],
@@ -184,13 +184,9 @@
     side_out[3 * per : 4 * per, 2 * n : 3 * n] = got[:, n:]
 
 
-def core_kernel(
-    seq_len, per, terms, white, white3, acts, grads, mine, side, white1, mine_out, side_out
-):
+def core_kernel(seq_len, per, white, white3, acts, grads, mine, side, mine_out, side_out):
     n = acts.shape[0]
     tok = [acts[...], grads[...]]
-    for w in range(2):
-        white1[w] = whiten(tok[w], terms.at[w])
     mine_out[...] = mine[...]
     mine_out[:, 3 * n : 4 * n] = block(seq_len, [white[w, : 2 * n] for w in range(2)], tok)
     side_out[...] = side[...]
@@ -200,14 +196,17 @@
         side_out[row : row + per, n : 2 * n] = got[i * per : (i + 1) * per]
 
 
-def return_kernel(seq_len, per, white, white1, white3, pick, side, v2, by_z, by_x):
+def return_kernel(
+    seq_len, per, terms, white, white3, pick, side, u3, u1, v3, acts, grads, v2, by_z, by_x
+):
     n = v2.shape[1]
     tok = [v2[w] for w in range(2)]
-    columns = [
-        stack(white[w, 4 * n : 5 * n], white1[w], white[w, 3 * n : 4 * n], white3[w])
-        for w in range(2)
-    ]
-    by_row = block(seq_len, tok, columns)
+    core = (acts[...], grads[...])
+    by_row = block(
+        seq_len,
+        [whiten(tok[w], terms.at[w]) for w in range(2)],
+        [stack(u1[w], core[w], u3[w], v3[w]) for w in range(2)],
+    )
     by_column = block(
         seq_len, [stack(white[w, 3 * n : 4 * n], white3[w]) for w in range(2)], tok
     )
@@ -310,7 +309,7 @@
         early_kernel,
         "early_pairs",
         (terms, own, v, u3, u2, u1),
-        (shape((2, 5 * tokens, rank), bf16), whole, sides),
+        (shape((2, 4 * tokens, rank), bf16), whole, sides),
     )
     v, white = lax.optimization_barrier((v, white))
     v1 = [send(v[w], ways[2]) for w in range(2)]
@@ -322,19 +321,22 @@
         flops=10**4,
         input_output_aliases={5: 1},
     )
-    white1, mine, side = kernel(
+    mine, side = kernel(
         core_kernel,
         "core_pairs",
-        (terms, white, white3, *v1, mine, side),
-        (unit, whole, sides),
+        (white, white3, *v1, mine, side),
+        (whole, sides),
         flops=10**4,
-        input_output_aliases={5: 1, 6: 2},
+        input_output_aliases={4: 0, 5: 1},
     )
     by_z, by_x = kernel(
-        return_kernel, "return_rows", (white, white1, white3, pick, side, v2), (rows, rows)
+        return_kernel,
+        "return_rows",
+        (terms, white, white3, pick, side, u3, u1, v3, *v1, v2),
+        (rows, rows),
     )
     mine = kernel(rows_kernel, "own_rows", (white, pick, mine, v3, v2), rows)
-    half_sum = mine + send(by_z, z_near) + send(by_x, lambda d: d ^ 2)
+    half_sum = mine + send(by_x, lambda d: d ^ 2) + send(by_z, z_near)
     return half_sum[:per] + send(half_sum[per:], opposite)
 
 

time: 28.6 us -> 28.6 us (level)
  transfers between devices with their start and end apart: 11 -> 11, of which waited for: 6 -> 6; matrix products, arithmetic and copies ran while one was open for 0% -> 0% of each run, Pallas kernels for 15% -> 14%
where the time goes in v18:
time: 28.6 us; the launch traced here: 28.5 us
  starting transfers between devices  14.9 us (52%)
  waiting for transfers between devices  7.06 us (25%)
  Pallas kernels  5.78 us (20%)
  other arithmetic  0.57 us (2%)
    ppermute x11, starting transfers between devices, send(): return lax.ppermute(x, 'blk', [(d, to(d)) for d in range(size)])  14.9 us
    ppermute x11, waiting for transfers between devices, send(): return lax.ppermute(x, 'blk', [(d, to(d)) for d in range(size)])  7.06 us
    pallas_call x9, Pallas kernels, call(): pl.pallas_call(kernel, out_shape=out_shape, in_specs=specs + [vmem] * (le...  5.78 us
  transfers between devices with their start and end apart: 11, of which 6 were waited for; matrix products, arithmetic and copies ran while one was open for 0% of the time, Pallas kernels for 14%

profile of v18, /device:TPU:0, one launch (start us, length us, event | category | flops | bytes accessed | tf_op | source)
XLA Modules:
  0.0 28.5 jit_solution(6086109168957751512)
XLA Ops:
  0.0 1.0 %away.1.unit = bf16[2,128,256]{2,1,0:T(8,128)(2,1)S(1)} custom-call(bf16[2,128,256]{2,1,0:T(8,128)(2,1)} %acts.2, bf16[2,128,256]{2,1,0:T(8,128)(2,1)} %grads.2), custom_call_target="tpu_custom_call" | custom-call | flops 3000000000 | bytes 1000000 | tf_op jit(solution)/shard_map/away/pallas_call | solution.py:234
  1.0 0.2 away_mask.1
  1.1 4.1 %collective-permute-start = (bf16[2,128,256]{2,1,0:T(8,128)(2,1)S(1)}, bf16[2,128,256]{2,1,0:T(8,128)(2,1)S(1)}, u32[]{:S(2)}, u32[]{:S(2)}) collective-permute-start(bf16[2,128,256]{2,1,0:T(8,128)(2,1)S(1)} %away_mask.1), channel_id=1, source_target_pairs={{0,8},{1,9},{2,10},{3,11},{4,12},{5,13},{6,14},{7,15},{8,0},{9,1},... | collective-permute-start | bytes 393224 | tf_op jit(solution)/shard_map/ppermute | solution.py:255
  5.3 0.1 own.1.u0
  5.4 1.6 %collective-permute-start.1 = (bf16[2,128,256]{2,1,0:T(8,128)(2,1)S(1)}, bf16[2,128,256]{2,1,0:T(8,128)(2,1)S(1)}, u32[]{:S(2)}, u32[]{:S(2)}) collective-permute-start(bf16[2,128,256]{2,1,0:T(8,128)(2,1)S(1)} %own.1.u0), channel_id=1, source_target_pairs={{0,4},{1,5},{2,7},{3,6},{4,0},{5,1},{6,3},{7,2},{8,12},{9,13},{10,... | collective-permute-start | bytes 393224 | tf_op jit(solution)/shard_map/ppermute | solution.py:255
  7.1 0.7 %collective-permute-start.2 = (bf16[2,128,256]{2,1,0:T(8,128)(2,1)S(1)}, bf16[2,128,256]{2,1,0:T(8,128)(2,1)S(1)}, u32[]{:S(2)}, u32[]{:S(2)}) collective-permute-start(bf16[2,128,256]{2,1,0:T(8,128)(2,1)S(1)} %own.1.u0), channel_id=1, source_target_pairs={{0,2},{1,3},{2,0},{3,1},{4,6},{5,7},{6,4},{7,5},{8,10},{9,11},{10,... | collective-permute-start | bytes 393224 | tf_op jit(solution)/shard_map/ppermute | solution.py:255
  7.7 0.7 %collective-permute-start.3 = (bf16[2,128,256]{2,1,0:T(8,128)(2,1)S(1)}, bf16[2,128,256]{2,1,0:T(8,128)(2,1)S(1)}, u32[]{:S(2)}, u32[]{:S(2)}) collective-permute-start(bf16[2,128,256]{2,1,0:T(8,128)(2,1)S(1)} %own.1.u0), channel_id=1, source_target_pairs={{0,1},{1,0},{2,3},{3,2},{4,5},{5,4},{6,7},{7,6},{8,9},{9,8},{10,11... | collective-permute-start | bytes 393224 | tf_op jit(solution)/shard_map/ppermute | solution.py:255
  8.4 1.7 %factor_terms.1 = (bf16[2,3,256,256]{3,2,1,0:T(8,128)(2,1)S(1)}, bf16[1024,32]{1,0:T(8,128)(2,1)S(1)}) custom-call(s32[2]{0:T(128)S(1)} %copy-done.1, s32[1,32]{1,0:T(1,128)S(1)} %bitcast.8, f32[16,256,256]{2,1,0:T(8,128)} %act_f.1, f32[16,256,256]{2,1,0:T(8,128)} %grad_f.1), custom_call_target="tpu_custom_call" | custom-call | flops 1000000000 | bytes 1000000 | tf_op jit(solution)/shard_map/factor_terms/pallas_call | solution.py:234
  10.1 1.6 %collective-permute-done.v = bf16[2,128,256]{2,1,0:T(8,128)(2,1)S(1)} collective-permute-done((bf16[2,128,256]{2,1,0:T(8,128)(2,1)S(1)}, bf16[2,128,256]{2,1,0:T(8,128)(2,1)S(1)}, u32[]{:S(2)}, u32[]{:S(2)}) %collective-permute-start) | collective-permute-done | bytes 131104 | tf_op jit(solution)/shard_map/ppermute | solution.py:255
  11.7 0.6 %collective-permute-start.4 = (bf16[2,128,256]{2,1,0:T(8,128)(2,1)S(1)}, bf16[2,128,256]{2,1,0:T(8,128)(2,1)S(1)}, u32[]{:S(2)}, u32[]{:S(2)}) collective-permute-start(bf16[2,128,256]{2,1,0:T(8,128)(2,1)S(1)} %collective-permute-done.v), channel_id=1, source_target_pairs={{0,4},{1,5},{2,7},{3,6},{4,0},{5,1},{6,3},{7,2},{8,12},{9,13},{10,... | collective-permute-start | bytes 393224 | tf_op jit(solution)/shard_map/ppermute | solution.py:255
  12.3 1.1 %collective-permute-start.7 = (bf16[2,128,256]{2,1,0:T(8,128)(2,1)S(1)}, bf16[2,128,256]{2,1,0:T(8,128)(2,1)S(1)}, u32[]{:S(2)}, u32[]{:S(2)}) collective-permute-start(bf16[2,128,256]{2,1,0:T(8,128)(2,1)S(1)} %collective-permute-done.v), channel_id=1, source_target_pairs={{0,2},{1,3},{2,0},{3,1},{4,6},{5,7},{6,4},{7,5},{8,10},{9,11},{10,... | collective-permute-start | bytes 393224 | tf_op jit(solution)/shard_map/ppermute | solution.py:255
  13.4 0.0 collective-permute-done.1.u3
  13.4 0.0 collective-permute-done.2.u2
  13.5 0.0 collective-permute-done.3.u1
  13.5 1.0 %early_pairs.1 = (bf16[2,512,256]{2,1,0:T(8,128)(2,1)S(1)}, f32[4,1024]{1,0:T(4,128)S(1)}, f32[8,768]{1,0:T(8,128)S(1)}) custom-call(bf16[2,3,256,256]{3,2,1,0:T(8,128)(2,1)S(1)} %get-tuple-element.27.terms, bf16[2,128,256]{2,1,0:T(8,128)(2,1)S(1)} %own.1.u0, bf16[2,128,256]{2,1,0:T(8,128)(2,1)S(1)} %collective-permute-done.v, ...), custom_call_target="tpu_custom_call" | custom-call | flops 1000000000 | bytes 1000000 | tf_op jit(solution)/shard_map/early_pairs/pallas_call | solution.py:234
  14.5 0.3 collective-permute-start.5
  14.8 0.3 %collective-permute-start.6 = (bf16[128,256]{1,0:T(8,128)(2,1)S(1)}, bf16[128,256]{1,0:T(8,128)(2,1)S(1)}, u32[]{:S(2)}, u32[]{:S(2)}) collective-permute-start(bf16[128,256]{1,0:T(8,128)(2,1)S(1)} %get-tuple-element.43), channel_id=1, source_target_pairs={{0,1},{1,0},{2,3},{3,2},{4,5},{5,4},{6,7},{7,6},{8,9},{9,8},{10,11... | collective-permute-start | bytes 196616 | tf_op jit(solution)/shard_map/ppermute | solution.py:255
  15.0 1.6 %collective-permute-done.4.v3 = bf16[2,128,256]{2,1,0:T(8,128)(2,1)S(1)} collective-permute-done((bf16[2,128,256]{2,1,0:T(8,128)(2,1)S(1)}, bf16[2,128,256]{2,1,0:T(8,128)(2,1)S(1)}, u32[]{:S(2)}, u32[]{:S(2)}) %collective-permute-start.4) | collective-permute-done | bytes 131104 | tf_op jit(solution)/shard_map/ppermute | solution.py:255
  16.7 0.4 %z_pairs.1 = (bf16[2,128,256]{2,1,0:T(8,128)(2,1)S(1)}, f32[8,768]{1,0:T(8,128)S(1)}) custom-call(bf16[2,3,256,256]{3,2,1,0:T(8,128)(2,1)S(1)} %get-tuple-element.27.terms, bf16[2,512,256]{2,1,0:T(8,128)(2,1)S(1)} %get-tuple-element.32.white, bf16[2,128,256]{2,1,0:T(8,128)(2,1)S(1)} %collective-permute-done.2.u2, ...), custom_call_target="tpu_custom_call", output_to_operand_aliasing={{1}: (5, {})} | custom-call | flops 10000 | bytes 1000000 | tf_op jit(solution)/shard_map/z_pairs/pallas_call | solution.py:234
  17.1 0.0 collective-permute-done.5.acts
  17.1 0.0 collective-permute-done.6.grads
  17.1 0.3 %core_pairs.1 = (f32[4,1024]{1,0:T(4,128)S(1)}, f32[8,768]{1,0:T(8,128)S(1)}) custom-call(bf16[2,512,256]{2,1,0:T(8,128)(2,1)S(1)} %get-tuple-element.32.white, bf16[2,128,256]{2,1,0:T(8,128)(2,1)S(1)} %get-tuple-element.35.white3, bf16[128,256]{1,0:T(8,128)(2,1)S(1)} %collective-permute-done.5.acts, ...), custom_call_target="tpu_custom_call", output_to_operand_aliasing={{0}: (4, {}), {1}: (5, {})} | custom-call | flops 10000 | bytes 1000000 | tf_op jit(solution)/shard_map/core_pairs/pallas_call | solution.py:234
  17.4 0.1 collective-permute-done.7.v2
  17.6 0.7 %return_rows.1 = (f32[4,32]{1,0:T(4,128)S(1)}, f32[4,32]{1,0:T(4,128)S(1)}) custom-call(bf16[2,3,256,256]{3,2,1,0:T(8,128)(2,1)S(1)} %get-tuple-element.27.terms, bf16[2,512,256]{2,1,0:T(8,128)(2,1)S(1)} %get-tuple-element.32.white, bf16[2,128,256]{2,1,0:T(8,128)(2,1)S(1)} %get-tuple-element.35.white3, bf16[1024,32]{1,0:T(8,128)(2,1)S(1)} %get-tuple-element.33.pick, ...), custom_call_target="tpu_custom_call" | custom-call | flops 1000000000 | bytes 1000000 | tf_op jit(solution)/shard_map/return_rows/pallas_call | solution.py:234
  18.3 1.5 %collective-permute-start.9 = (f32[4,32]{1,0:T(4,128)S(1)}, f32[4,32]{1,0:T(4,128)S(1)}, u32[]{:S(2)}, u32[]{:S(2)}) collective-permute-start(f32[4,32]{1,0:T(4,128)S(1)} %get-tuple-element.42), channel_id=1, source_target_pairs={{0,4},{1,5},{2,7},{3,6},{4,0},{5,1},{6,3},{7,2},{8,12},{9,13},{10,... | collective-permute-start | bytes 1544 | tf_op jit(solution)/shard_map/ppermute | solution.py:255
  19.8 1.1 %collective-permute-start.8 = (f32[4,32]{1,0:T(4,128)S(1)}, f32[4,32]{1,0:T(4,128)S(1)}, u32[]{:S(2)}, u32[]{:S(2)}) collective-permute-start(f32[4,32]{1,0:T(4,128)S(1)} %get-tuple-element.41), channel_id=1, source_target_pairs={{0,2},{1,3},{2,0},{3,1},{4,6},{5,7},{6,4},{7,5},{8,10},{9,11},{10,... | collective-permute-start | bytes 1544 | tf_op jit(solution)/shard_map/ppermute | solution.py:255
  20.9 0.4 %own_rows.1 = f32[4,32]{1,0:T(4,128)S(1)} custom-call(bf16[2,512,256]{2,1,0:T(8,128)(2,1)S(1)} %get-tuple-element.32.white, bf16[1024,32]{1,0:T(8,128)(2,1)S(1)} %get-tuple-element.33.pick, f32[4,1024]{1,0:T(4,128)S(1)} %get-tuple-element.39.mine, bf16[2,128,256]{2,1,0:T(8,128)(2,1)S(1)} %collective-permute-done.4.v3, ...), custom_call_target="tpu_custom_call" | custom-call | flops 1000000000 | bytes 1000000 | tf_op jit(solution)/shard_map/own_rows/pallas_call | solution.py:234
  21.3 0.6 %collective-permute-done.9 = f32[4,32]{1,0:T(4,128)S(1)} collective-permute-done((f32[4,32]{1,0:T(4,128)S(1)}, f32[4,32]{1,0:T(4,128)S(1)}, u32[]{:S(2)}, u32[]{:S(2)}) %collective-permute-start.9) | collective-permute-done | bytes 544 | tf_op jit(solution)/shard_map/ppermute | solution.py:255
  22.0 1.4 %collective-permute-done.8 = f32[4,32]{1,0:T(4,128)S(1)} collective-permute-done((f32[4,32]{1,0:T(4,128)S(1)}, f32[4,32]{1,0:T(4,128)S(1)}, u32[]{:S(2)}, u32[]{:S(2)}) %collective-permute-start.8) | collective-permute-done | bytes 544 | tf_op jit(solution)/shard_map/ppermute | solution.py:255
  23.4 2.9 %collective-permute-start.10 = (f32[2,32]{1,0:T(2,128)S(1)}, f32[2,32]{1,0:T(2,128)S(1)}, u32[]{:S(2)}, u32[]{:S(2)}) collective-permute-start(f32[2,32]{1,0:T(2,128)S(1)} %slice.15), channel_id=1, source_target_pairs={{0,8},{1,9},{2,10},{3,11},{4,12},{5,13},{6,14},{7,15},{8,0},{9,1},... | collective-permute-start | bytes 776 | tf_op jit(solution)/shard_map/ppermute | solution.py:255
  26.3 1.6 %collective-permute-done.10 = f32[2,32]{1,0:T(2,128)S(1)} collective-permute-done((f32[2,32]{1,0:T(2,128)S(1)}, f32[2,32]{1,0:T(2,128)S(1)}, u32[]{:S(2)}, u32[]{:S(2)}) %collective-permute-start.10) | collective-permute-done | bytes 288 | tf_op jit(solution)/shard_map/ppermute | solution.py:255
  27.9 0.6 %slice_add_fusion = f32[2,32]{1,0:T(2,128)} fusion(f32[2,32]{1,0:T(2,128)S(1)} %collective-permute-done.10, f32[4,32]{1,0:T(4,128)S(1)} %add_add_fusion), kind=kLoop, calls=%fused_computation.3 | loop fusion | flops 64 | bytes 768 | tf_op jit(solution)/shard_map/add | solution.py:340
  (13 shorter events, 0.0 us)
Async XLA Ops:
  0.0 5.3 %copy-start.3 = (bf16[2,128,256]{2,1,0:T(8,128)(2,1)S(1)}, bf16[2,128,256]{2,1,0:T(8,128)(2,1)}, u32[]{:S(2)}) copy-start(bf16[2,128,256]{2,1,0:T(8,128)(2,1)} %acts.2) | copy-start | bytes 393220
  0.0 5.3 %copy-start.4 = (bf16[2,128,256]{2,1,0:T(8,128)(2,1)S(1)}, bf16[2,128,256]{2,1,0:T(8,128)(2,1)}, u32[]{:S(2)}) copy-start(bf16[2,128,256]{2,1,0:T(8,128)(2,1)} %grads.2) | copy-start | bytes 393220
  0.0 1.0 %copy-start = (s32[2]{0:T(128)S(1)}, s32[2]{0:T(128)}, u32[]{:S(2)}) copy-start(s32[2]{0:T(128)} %param.9) | copy-start | bytes 28
  0.0 8.4 %copy-start.1 = (s32[2]{0:T(128)S(1)}, s32[2]{0:T(128)}, u32[]{:S(2)}) copy-start(s32[2]{0:T(128)} %layer_ids.1) | copy-start | bytes 28
  0.0 8.4 %copy-start.2 = (s32[32]{0:T(128)S(1)}, s32[32]{0:T(128)}, u32[]{:S(2)}) copy-start(s32[32]{0:T(128)} %param.11) | copy-start | bytes 388
  1.1 10.5 %collective-permute-start = (bf16[2,128,256]{2,1,0:T(8,128)(2,1)S(1)}, bf16[2,128,256]{2,1,0:T(8,128)(2,1)S(1)}, u32[]{:S(2)}, u32[]{:S(2)}) collective-permute-start(bf16[2,128,256]{2,1,0:T(8,128)(2,1)S(1)} %away_mask.1), channel_id=1, source_target_pairs={{0,8},{1,9},{2,10},{3,11},{4,12},{5,13},{6,14},{7,15},{8,0},{9,1},... | collective-permute-start | bytes 393224 | tf_op jit(solution)/shard_map/ppermute | solution.py:255
  5.4 8.0 %collective-permute-start.1 = (bf16[2,128,256]{2,1,0:T(8,128)(2,1)S(1)}, bf16[2,128,256]{2,1,0:T(8,128)(2,1)S(1)}, u32[]{:S(2)}, u32[]{:S(2)}) collective-permute-start(bf16[2,128,256]{2,1,0:T(8,128)(2,1)S(1)} %own.1.u0), channel_id=1, source_target_pairs={{0,4},{1,5},{2,7},{3,6},{4,0},{5,1},{6,3},{7,2},{8,12},{9,13},{10,... | collective-permute-start | bytes 393224 | tf_op jit(solution)/shard_map/ppermute | solution.py:255
  7.1 6.4 %collective-permute-start.2 = (bf16[2,128,256]{2,1,0:T(8,128)(2,1)S(1)}, bf16[2,128,256]{2,1,0:T(8,128)(2,1)S(1)}, u32[]{:S(2)}, u32[]{:S(2)}) collective-permute-start(bf16[2,128,256]{2,1,0:T(8,128)(2,1)S(1)} %own.1.u0), channel_id=1, source_target_pairs={{0,2},{1,3},{2,0},{3,1},{4,6},{5,7},{6,4},{7,5},{8,10},{9,11},{10,... | collective-permute-start | bytes 393224 | tf_op jit(solution)/shard_map/ppermute | solution.py:255
  7.7 5.7 %collective-permute-start.3 = (bf16[2,128,256]{2,1,0:T(8,128)(2,1)S(1)}, bf16[2,128,256]{2,1,0:T(8,128)(2,1)S(1)}, u32[]{:S(2)}, u32[]{:S(2)}) collective-permute-start(bf16[2,128,256]{2,1,0:T(8,128)(2,1)S(1)} %own.1.u0), channel_id=1, source_target_pairs={{0,1},{1,0},{2,3},{3,2},{4,5},{5,4},{6,7},{7,6},{8,9},{9,8},{10,11... | collective-permute-start | bytes 393224 | tf_op jit(solution)/shard_map/ppermute | solution.py:255
  11.7 5.0 %collective-permute-start.4 = (bf16[2,128,256]{2,1,0:T(8,128)(2,1)S(1)}, bf16[2,128,256]{2,1,0:T(8,128)(2,1)S(1)}, u32[]{:S(2)}, u32[]{:S(2)}) collective-permute-start(bf16[2,128,256]{2,1,0:T(8,128)(2,1)S(1)} %collective-permute-done.v), channel_id=1, source_target_pairs={{0,4},{1,5},{2,7},{3,6},{4,0},{5,1},{6,3},{7,2},{8,12},{9,13},{10,... | collective-permute-start | bytes 393224 | tf_op jit(solution)/shard_map/ppermute | solution.py:255
  12.3 5.3 %collective-permute-start.7 = (bf16[2,128,256]{2,1,0:T(8,128)(2,1)S(1)}, bf16[2,128,256]{2,1,0:T(8,128)(2,1)S(1)}, u32[]{:S(2)}, u32[]{:S(2)}) collective-permute-start(bf16[2,128,256]{2,1,0:T(8,128)(2,1)S(1)} %collective-permute-done.v), channel_id=1, source_target_pairs={{0,2},{1,3},{2,0},{3,1},{4,6},{5,7},{6,4},{7,5},{8,10},{9,11},{10,... | collective-permute-start | bytes 393224 | tf_op jit(solution)/shard_map/ppermute | solution.py:255
  14.5 2.6 %collective-permute-start.5 = (bf16[128,256]{1,0:T(8,128)(2,1)S(1)}, bf16[128,256]{1,0:T(8,128)(2,1)S(1)}, u32[]{:S(2)}, u32[]{:S(2)}) collective-permute-start(bf16[128,256]{1,0:T(8,128)(2,1)S(1)} %get-tuple-element.44), channel_id=1, source_target_pairs={{0,1},{1,0},{2,3},{3,2},{4,5},{5,4},{6,7},{7,6},{8,9},{9,8},{10,11... | collective-permute-start | bytes 196616 | tf_op jit(solution)/shard_map/ppermute | solution.py:255
  14.8 2.3 %collective-permute-start.6 = (bf16[128,256]{1,0:T(8,128)(2,1)S(1)}, bf16[128,256]{1,0:T(8,128)(2,1)S(1)}, u32[]{:S(2)}, u32[]{:S(2)}) collective-permute-start(bf16[128,256]{1,0:T(8,128)(2,1)S(1)} %get-tuple-element.43), channel_id=1, source_target_pairs={{0,1},{1,0},{2,3},{3,2},{4,5},{5,4},{6,7},{7,6},{8,9},{9,8},{10,11... | collective-permute-start | bytes 196616 | tf_op jit(solution)/shard_map/ppermute | solution.py:255
  18.3 3.6 %collective-permute-start.9 = (f32[4,32]{1,0:T(4,128)S(1)}, f32[4,32]{1,0:T(4,128)S(1)}, u32[]{:S(2)}, u32[]{:S(2)}) collective-permute-start(f32[4,32]{1,0:T(4,128)S(1)} %get-tuple-element.42), channel_id=1, source_target_pairs={{0,4},{1,5},{2,7},{3,6},{4,0},{5,1},{6,3},{7,2},{8,12},{9,13},{10,... | collective-permute-start | bytes 1544 | tf_op jit(solution)/shard_map/ppermute | solution.py:255
  19.8 3.6 %collective-permute-start.8 = (f32[4,32]{1,0:T(4,128)S(1)}, f32[4,32]{1,0:T(4,128)S(1)}, u32[]{:S(2)}, u32[]{:S(2)}) collective-permute-start(f32[4,32]{1,0:T(4,128)S(1)} %get-tuple-element.41), channel_id=1, source_target_pairs={{0,2},{1,3},{2,0},{3,1},{4,6},{5,7},{6,4},{7,5},{8,10},{9,11},{10,... | collective-permute-start | bytes 1544 | tf_op jit(solution)/shard_map/ppermute | solution.py:255
  23.4 4.5 %collective-permute-start.10 = (f32[2,32]{1,0:T(2,128)S(1)}, f32[2,32]{1,0:T(2,128)S(1)}, u32[]{:S(2)}, u32[]{:S(2)}) collective-permute-start(f32[2,32]{1,0:T(2,128)S(1)} %slice.15), channel_id=1, source_target_pairs={{0,8},{1,9},{2,10},{3,11},{4,12},{5,13},{6,14},{7,15},{8,0},{9,1},... | collective-permute-start | bytes 776 | tf_op jit(solution)/shard_map/ppermute | solution.py:255

commit v19 on v18

--- a/solution.py
+++ b/solution.py
@@ -56,6 +56,10 @@
     return d ^ 4 ^ ((d >> 1) & 1)
 
 
+def is_inner(d):
+    return (d >= 4) & (d < 12)
+
+
 def away_kernel(acts, grads, out, sems):
     layer = 1 - lax.axis_index("blk") // 8
     copies = [
@@ -169,7 +173,7 @@
             side[row : row + per, at : at + n] = block(seq_len, left[slot], tok[column])
 
 
-def z_kernel(seq_len, per, terms, white, u2, u1, v3, side, white3, side_out):
+def z_kernel(seq_len, per, terms, white, u2, u1, first, v3, side, white3, side_out):
     n = v3.shape[1]
     tok = [v3[w] for w in range(2)]
     fresh = [whiten(tok[w], terms.at[w]) for w in range(2)]
@@ -196,11 +200,16 @@
         side_out[row : row + per, n : 2 * n] = got[i * per : (i + 1) * per]
 
 
+def x_unit(first, last):
+    inner = is_inner(lax.axis_index("blk"))
+    return [jnp.where(inner, first[w], last[w]) for w in range(2)]
+
+
 def return_kernel(
-    seq_len, per, terms, white, white3, pick, side, u3, u1, v3, acts, grads, v2, by_z, by_x
+    seq_len, per, terms, white, white3, pick, side, u3, u1, v3, acts, grads, first, last, by_z, by_x
 ):
-    n = v2.shape[1]
-    tok = [v2[w] for w in range(2)]
+    n = first.shape[1]
+    tok = x_unit(first, last)
     core = (acts[...], grads[...])
     by_row = block(
         seq_len,
@@ -220,8 +229,9 @@
     by_z[...] = picked[2 * per :]
 
 
-def rows_kernel(seq_len, per, white, pick, mine, v3, v2, out):
-    n = v2.shape[1]
+def rows_kernel(seq_len, per, white, pick, mine, v3, first, last, out):
+    n = v3.shape[1]
+    v2 = x_unit(first, last)
     left = [white[w, : 2 * n] for w in range(2)]
     got = block(seq_len, left, [stack(v2[w], v3[w]) for w in range(2)])
     zeros = jnp.zeros((2 * per, n), jnp.float32)
@@ -294,12 +304,13 @@
         [pltpu.VMEM((2, rank, rank), f32), pltpu.SemaphoreType.DMA((2,))],
     )
     v, terms, pick = lax.optimization_barrier((v, terms, pick))
-    late = [send(v, to) for to in ways[:2]]
+    first = send(v, lambda d: d ^ 2 if is_inner(d) else d)
+    v3 = send(v, z_near)
+    last = send(v, lambda d: d if is_inner(d) else d ^ 2)
     whole = shape((2 * per, 8 * tokens), f32)
     sides = shape((4 * per, 6 * tokens), f32)
     rows = shape((2 * per, columns), f32)
     u3, u2, u1 = near
-    v3, v2 = late
 
     def kernel(body, name, operands, out_shape, flops=10**9, **more):
         body = functools.partial(body, seq_len, per)
@@ -316,10 +327,10 @@
     white3, side = kernel(
         z_kernel,
         "z_pairs",
-        (terms, white, u2, u1, v3, side),
+        (terms, white, u2, u1, first, v3, side),
         (unit, sides),
         flops=10**4,
-        input_output_aliases={5: 1},
+        input_output_aliases={6: 1},
     )
     mine, side = kernel(
         core_kernel,
@@ -332,10 +343,10 @@
     by_z, by_x = kernel(
         return_kernel,
         "return_rows",
-        (terms, white, white3, pick, side, u3, u1, v3, *v1, v2),
+        (terms, white, white3, pick, side, u3, u1, v3, *v1, first, last),
         (rows, rows),
     )
-    mine = kernel(rows_kernel, "own_rows", (white, pick, mine, v3, v2), rows)
+    mine = kernel(rows_kernel, "own_rows", (white, pick, mine, v3, first, last), rows)
     half_sum = mine + send(by_x, lambda d: d ^ 2) + send(by_z, z_near)
     return half_sum[:per] + send(half_sum[per:], opposite)
 

time: 28.6 us -> 32.4 us (1.13)
  waiting for transfers between devices: 7.06 us -> 9.19 us
  starting transfers between devices: 14.9 us -> 16.5 us
    ppermute x11 -> x12, waiting for transfers between devices: 7.06 us -> 9.19 us  [send(): return lax.ppermute(x, 'blk', [(d, to(d)) for d in range(size)])]
    ppermute x11 -> x12, starting transfers between devices: 14.9 us -> 16.5 us  [send(): return lax.ppermute(x, 'blk', [(d, to(d)) for d in range(size)])]
  transfers between devices with their start and end apart: 11 -> 12, of which waited for: 6 -> 7; matrix products, arithmetic and copies ran while one was open for 0% -> 0% of each run, Pallas kernels for 14% -> 12%
where the time goes in v19:
time: 32.4 us; the launch traced here: 32.2 us
  starting transfers between devices  16.5 us (51%)
  waiting for transfers between devices  9.19 us (28%)
  Pallas kernels  5.79 us (18%)
  other arithmetic  0.57 us (2%)
    ppermute x12, starting transfers between devices, send(): return lax.ppermute(x, 'blk', [(d, to(d)) for d in range(size)])  16.5 us
    ppermute x12, waiting for transfers between devices, send(): return lax.ppermute(x, 'blk', [(d, to(d)) for d in range(size)])  9.19 us
    pallas_call x9, Pallas kernels, call(): pl.pallas_call(kernel, out_shape=out_shape, in_specs=specs + [vmem] * (le...  5.79 us
  transfers between devices with their start and end apart: 12, of which 7 were waited for; matrix products, arithmetic and copies ran while one was open for 0% of the time, Pallas kernels for 12%

profile of v19, /device:TPU:0, one launch (start us, length us, event | category | flops | bytes accessed | tf_op | source)
XLA Modules:
  0.0 32.2 jit_solution(17885326451026060970)
XLA Ops:
  0.0 1.0 %away.1.unit = bf16[2,128,256]{2,1,0:T(8,128)(2,1)S(1)} custom-call(bf16[2,128,256]{2,1,0:T(8,128)(2,1)} %acts.2, bf16[2,128,256]{2,1,0:T(8,128)(2,1)} %grads.2), custom_call_target="tpu_custom_call" | custom-call | flops 3000000000 | bytes 1000000 | tf_op jit(solution)/shard_map/away/pallas_call | solution.py:244
  1.0 0.2 away_mask.1
  1.1 4.1 %collective-permute-start = (bf16[2,128,256]{2,1,0:T(8,128)(2,1)S(1)}, bf16[2,128,256]{2,1,0:T(8,128)(2,1)S(1)}, u32[]{:S(2)}, u32[]{:S(2)}) collective-permute-start(bf16[2,128,256]{2,1,0:T(8,128)(2,1)S(1)} %away_mask.1), channel_id=1, source_target_pairs={{0,8},{1,9},{2,10},{3,11},{4,12},{5,13},{6,14},{7,15},{8,0},{9,1},... | collective-permute-start | bytes 393224 | tf_op jit(solution)/shard_map/ppermute | solution.py:265
  5.3 0.1 own.1.u0
  5.4 1.6 %collective-permute-start.1 = (bf16[2,128,256]{2,1,0:T(8,128)(2,1)S(1)}, bf16[2,128,256]{2,1,0:T(8,128)(2,1)S(1)}, u32[]{:S(2)}, u32[]{:S(2)}) collective-permute-start(bf16[2,128,256]{2,1,0:T(8,128)(2,1)S(1)} %own.1.u0), channel_id=1, source_target_pairs={{0,4},{1,5},{2,7},{3,6},{4,0},{5,1},{6,3},{7,2},{8,12},{9,13},{10,... | collective-permute-start | bytes 393224 | tf_op jit(solution)/shard_map/ppermute | solution.py:265
  7.1 0.7 %collective-permute-start.2 = (bf16[2,128,256]{2,1,0:T(8,128)(2,1)S(1)}, bf16[2,128,256]{2,1,0:T(8,128)(2,1)S(1)}, u32[]{:S(2)}, u32[]{:S(2)}) collective-permute-start(bf16[2,128,256]{2,1,0:T(8,128)(2,1)S(1)} %own.1.u0), channel_id=1, source_target_pairs={{0,2},{1,3},{2,0},{3,1},{4,6},{5,7},{6,4},{7,5},{8,10},{9,11},{10,... | collective-permute-start | bytes 393224 | tf_op jit(solution)/shard_map/ppermute | solution.py:265
  7.7 0.7 %collective-permute-start.3 = (bf16[2,128,256]{2,1,0:T(8,128)(2,1)S(1)}, bf16[2,128,256]{2,1,0:T(8,128)(2,1)S(1)}, u32[]{:S(2)}, u32[]{:S(2)}) collective-permute-start(bf16[2,128,256]{2,1,0:T(8,128)(2,1)S(1)} %own.1.u0), channel_id=1, source_target_pairs={{0,1},{1,0},{2,3},{3,2},{4,5},{5,4},{6,7},{7,6},{8,9},{9,8},{10,11... | collective-permute-start | bytes 393224 | tf_op jit(solution)/shard_map/ppermute | solution.py:265
  8.4 1.7 %factor_terms.1 = (bf16[2,3,256,256]{3,2,1,0:T(8,128)(2,1)S(1)}, bf16[1024,32]{1,0:T(8,128)(2,1)S(1)}) custom-call(s32[2]{0:T(128)S(1)} %copy-done.1, s32[1,32]{1,0:T(1,128)S(1)} %bitcast.8, f32[16,256,256]{2,1,0:T(8,128)} %act_f.1, f32[16,256,256]{2,1,0:T(8,128)} %grad_f.1), custom_call_target="tpu_custom_call" | custom-call | flops 1000000000 | bytes 1000000 | tf_op jit(solution)/shard_map/factor_terms/pallas_call | solution.py:244
  10.1 1.6 %collective-permute-done.v = bf16[2,128,256]{2,1,0:T(8,128)(2,1)S(1)} collective-permute-done((bf16[2,128,256]{2,1,0:T(8,128)(2,1)S(1)}, bf16[2,128,256]{2,1,0:T(8,128)(2,1)S(1)}, u32[]{:S(2)}, u32[]{:S(2)}) %collective-permute-start) | collective-permute-done | bytes 131104 | tf_op jit(solution)/shard_map/ppermute | solution.py:265
  11.7 0.7 %collective-permute-start.4 = (bf16[2,128,256]{2,1,0:T(8,128)(2,1)S(1)}, bf16[2,128,256]{2,1,0:T(8,128)(2,1)S(1)}, u32[]{:S(2)}, u32[]{:S(2)}) collective-permute-start(bf16[2,128,256]{2,1,0:T(8,128)(2,1)S(1)} %collective-permute-done.v), channel_id=1, source_target_pairs={{0,0},{1,1},{2,2},{3,3},{4,6},{5,7},{6,4},{7,5},{8,10},{9,11},{10,... | collective-permute-start | bytes 393224 | tf_op jit(solution)/shard_map/ppermute | solution.py:265
  12.4 3.4 %collective-permute-start.5 = (bf16[2,128,256]{2,1,0:T(8,128)(2,1)S(1)}, bf16[2,128,256]{2,1,0:T(8,128)(2,1)S(1)}, u32[]{:S(2)}, u32[]{:S(2)}) collective-permute-start(bf16[2,128,256]{2,1,0:T(8,128)(2,1)S(1)} %collective-permute-done.v), channel_id=1, source_target_pairs={{0,4},{1,5},{2,7},{3,6},{4,0},{5,1},{6,3},{7,2},{8,12},{9,13},{10,... | collective-permute-start | bytes 393224 | tf_op jit(solution)/shard_map/ppermute | solution.py:265
  15.8 1.9 %collective-permute-start.8 = (bf16[2,128,256]{2,1,0:T(8,128)(2,1)S(1)}, bf16[2,128,256]{2,1,0:T(8,128)(2,1)S(1)}, u32[]{:S(2)}, u32[]{:S(2)}) collective-permute-start(bf16[2,128,256]{2,1,0:T(8,128)(2,1)S(1)} %collective-permute-done.v), channel_id=1, source_target_pairs={{0,2},{1,3},{2,0},{3,1},{4,4},{5,5},{6,6},{7,7},{8,8},{9,9},{10,10... | collective-permute-start | bytes 393224 | tf_op jit(solution)/shard_map/ppermute | solution.py:265
  17.7 0.0 collective-permute-done.2.u2
  17.7 1.0 %early_pairs.1 = (bf16[2,512,256]{2,1,0:T(8,128)(2,1)S(1)}, f32[4,1024]{1,0:T(4,128)S(1)}, f32[8,768]{1,0:T(8,128)S(1)}) custom-call(bf16[2,3,256,256]{3,2,1,0:T(8,128)(2,1)S(1)} %get-tuple-element.27.terms, bf16[2,128,256]{2,1,0:T(8,128)(2,1)S(1)} %own.1.u0, bf16[2,128,256]{2,1,0:T(8,128)(2,1)S(1)} %collective-permute-done.v, ...), custom_call_target="tpu_custom_call" | custom-call | flops 1000000000 | bytes 1000000 | tf_op jit(solution)/shard_map/early_pairs/pallas_call | solution.py:244
  18.7 0.4 %collective-permute-start.6 = (bf16[128,256]{1,0:T(8,128)(2,1)S(1)}, bf16[128,256]{1,0:T(8,128)(2,1)S(1)}, u32[]{:S(2)}, u32[]{:S(2)}) collective-permute-start(bf16[128,256]{1,0:T(8,128)(2,1)S(1)} %get-tuple-element.44), channel_id=1, source_target_pairs={{0,1},{1,0},{2,3},{3,2},{4,5},{5,4},{6,7},{7,6},{8,9},{9,8},{10,11... | collective-permute-start | bytes 196616 | tf_op jit(solution)/shard_map/ppermute | solution.py:265
  19.2 0.2 collective-permute-start.7
  19.3 0.0 collective-permute-done.4.first
  19.3 0.0 collective-permute-done.5.v3
  19.3 0.4 %z_pairs.1 = (bf16[2,128,256]{2,1,0:T(8,128)(2,1)S(1)}, f32[8,768]{1,0:T(8,128)S(1)}) custom-call(bf16[2,3,256,256]{3,2,1,0:T(8,128)(2,1)S(1)} %get-tuple-element.27.terms, bf16[2,512,256]{2,1,0:T(8,128)(2,1)S(1)} %get-tuple-element.32.white, bf16[2,128,256]{2,1,0:T(8,128)(2,1)S(1)} %collective-permute-done.2.u2, ...), custom_call_target="tpu_custom_call", output_to_operand_aliasing={{1}: (6, {})} | custom-call | flops 10000 | bytes 1000000 | tf_op jit(solution)/shard_map/z_pairs/pallas_call | solution.py:244
  19.7 0.3 %collective-permute-done.6.acts = bf16[128,256]{1,0:T(8,128)(2,1)S(1)} collective-permute-done((bf16[128,256]{1,0:T(8,128)(2,1)S(1)}, bf16[128,256]{1,0:T(8,128)(2,1)S(1)}, u32[]{:S(2)}, u32[]{:S(2)}) %collective-permute-start.6) | collective-permute-done | bytes 65568 | tf_op jit(solution)/shard_map/ppermute | solution.py:265
  20.1 0.3 %collective-permute-done.7.grads = bf16[128,256]{1,0:T(8,128)(2,1)S(1)} collective-permute-done((bf16[128,256]{1,0:T(8,128)(2,1)S(1)}, bf16[128,256]{1,0:T(8,128)(2,1)S(1)}, u32[]{:S(2)}, u32[]{:S(2)}) %collective-permute-start.7) | collective-permute-done | bytes 65568 | tf_op jit(solution)/shard_map/ppermute | solution.py:265
  20.4 0.3 %core_pairs.1 = (f32[4,1024]{1,0:T(4,128)S(1)}, f32[8,768]{1,0:T(8,128)S(1)}) custom-call(bf16[2,512,256]{2,1,0:T(8,128)(2,1)S(1)} %get-tuple-element.32.white, bf16[2,128,256]{2,1,0:T(8,128)(2,1)S(1)} %get-tuple-element.35.white3, bf16[128,256]{1,0:T(8,128)(2,1)S(1)} %collective-permute-done.6.acts, ...), custom_call_target="tpu_custom_call", output_to_operand_aliasing={{0}: (4, {}), {1}: (5, {})} | custom-call | flops 10000 | bytes 1000000 | tf_op jit(solution)/shard_map/core_pairs/pallas_call | solution.py:244
  20.8 1.9 %collective-permute-done.8.last = bf16[2,128,256]{2,1,0:T(8,128)(2,1)S(1)} collective-permute-done((bf16[2,128,256]{2,1,0:T(8,128)(2,1)S(1)}, bf16[2,128,256]{2,1,0:T(8,128)(2,1)S(1)}, u32[]{:S(2)}, u32[]{:S(2)}) %collective-permute-start.8) | collective-permute-done | bytes 131104 | tf_op jit(solution)/shard_map/ppermute | solution.py:265
  22.6 0.7 %return_rows.1 = (f32[4,32]{1,0:T(4,128)S(1)}, f32[4,32]{1,0:T(4,128)S(1)}) custom-call(bf16[2,3,256,256]{3,2,1,0:T(8,128)(2,1)S(1)} %get-tuple-element.27.terms, bf16[2,512,256]{2,1,0:T(8,128)(2,1)S(1)} %get-tuple-element.32.white, bf16[2,128,256]{2,1,0:T(8,128)(2,1)S(1)} %get-tuple-element.35.white3, bf16[1024,32]{1,0:T(8,128)(2,1)S(1)} %get-tuple-element.33.pick, ...), custom_call_target="tpu_custom_call" | custom-call | flops 1000000000 | bytes 1000000 | tf_op jit(solution)/shard_map/return_rows/pallas_call | solution.py:244
  23.4 0.1 collective-permute-start.10
  23.4 1.1 %collective-permute-start.9 = (f32[4,32]{1,0:T(4,128)S(1)}, f32[4,32]{1,0:T(4,128)S(1)}, u32[]{:S(2)}, u32[]{:S(2)}) collective-permute-start(f32[4,32]{1,0:T(4,128)S(1)} %get-tuple-element.41), channel_id=1, source_target_pairs={{0,2},{1,3},{2,0},{3,1},{4,6},{5,7},{6,4},{7,5},{8,10},{9,11},{10,... | collective-permute-start | bytes 1544 | tf_op jit(solution)/shard_map/ppermute | solution.py:265
  24.6 0.4 %own_rows.1 = f32[4,32]{1,0:T(4,128)S(1)} custom-call(bf16[2,512,256]{2,1,0:T(8,128)(2,1)S(1)} %get-tuple-element.32.white, bf16[1024,32]{1,0:T(8,128)(2,1)S(1)} %get-tuple-element.33.pick, f32[4,1024]{1,0:T(4,128)S(1)} %get-tuple-element.39.mine, bf16[2,128,256]{2,1,0:T(8,128)(2,1)S(1)} %collective-permute-done.5.v3, ...), custom_call_target="tpu_custom_call" | custom-call | flops 1000000000 | bytes 1000000 | tf_op jit(solution)/shard_map/own_rows/pallas_call | solution.py:244
  25.0 2.0 %collective-permute-done.10 = f32[4,32]{1,0:T(4,128)S(1)} collective-permute-done((f32[4,32]{1,0:T(4,128)S(1)}, f32[4,32]{1,0:T(4,128)S(1)}, u32[]{:S(2)}, u32[]{:S(2)}) %collective-permute-start.10) | collective-permute-done | bytes 544 | tf_op jit(solution)/shard_map/ppermute | solution.py:265
  27.0 0.1 collective-permute-done.9
  27.1 1.6 %collective-permute-start.11 = (f32[2,32]{1,0:T(2,128)S(1)}, f32[2,32]{1,0:T(2,128)S(1)}, u32[]{:S(2)}, u32[]{:S(2)}) collective-permute-start(f32[2,32]{1,0:T(2,128)S(1)} %slice.15), channel_id=1, source_target_pairs={{0,8},{1,9},{2,10},{3,11},{4,12},{5,13},{6,14},{7,15},{8,0},{9,1},... | collective-permute-start | bytes 776 | tf_op jit(solution)/shard_map/ppermute | solution.py:265
  28.7 2.9 %collective-permute-done.11 = f32[2,32]{1,0:T(2,128)S(1)} collective-permute-done((f32[2,32]{1,0:T(2,128)S(1)}, f32[2,32]{1,0:T(2,128)S(1)}, u32[]{:S(2)}, u32[]{:S(2)}) %collective-permute-start.11) | collective-permute-done | bytes 288 | tf_op jit(solution)/shard_map/ppermute | solution.py:265
  31.6 0.6 %slice_add_fusion = f32[2,32]{1,0:T(2,128)} fusion(f32[2,32]{1,0:T(2,128)S(1)} %collective-permute-done.11, f32[4,32]{1,0:T(4,128)S(1)} %add_add_fusion), kind=kLoop, calls=%fused_computation.3 | loop fusion | flops 64 | bytes 768 | tf_op jit(solution)/shard_map/add | solution.py:351
  (15 shorter events, 0.0 us)
Async XLA Ops:
  0.0 5.3 %copy-start.3 = (bf16[2,128,256]{2,1,0:T(8,128)(2,1)S(1)}, bf16[2,128,256]{2,1,0:T(8,128)(2,1)}, u32[]{:S(2)}) copy-start(bf16[2,128,256]{2,1,0:T(8,128)(2,1)} %acts.2) | copy-start | bytes 393220
  0.0 5.3 %copy-start.4 = (bf16[2,128,256]{2,1,0:T(8,128)(2,1)S(1)}, bf16[2,128,256]{2,1,0:T(8,128)(2,1)}, u32[]{:S(2)}) copy-start(bf16[2,128,256]{2,1,0:T(8,128)(2,1)} %grads.2) | copy-start | bytes 393220
  0.0 1.0 %copy-start = (s32[2]{0:T(128)S(1)}, s32[2]{0:T(128)}, u32[]{:S(2)}) copy-start(s32[2]{0:T(128)} %param.9) | copy-start | bytes 28
  0.0 8.4 %copy-start.1 = (s32[2]{0:T(128)S(1)}, s32[2]{0:T(128)}, u32[]{:S(2)}) copy-start(s32[2]{0:T(128)} %layer_ids.1) | copy-start | bytes 28
  0.0 8.4 %copy-start.2 = (s32[32]{0:T(128)S(1)}, s32[32]{0:T(128)}, u32[]{:S(2)}) copy-start(s32[32]{0:T(128)} %param.11) | copy-start | bytes 388
  1.1 10.5 %collective-permute-start = (bf16[2,128,256]{2,1,0:T(8,128)(2,1)S(1)}, bf16[2,128,256]{2,1,0:T(8,128)(2,1)S(1)}, u32[]{:S(2)}, u32[]{:S(2)}) collective-permute-start(bf16[2,128,256]{2,1,0:T(8,128)(2,1)S(1)} %away_mask.1), channel_id=1, source_target_pairs={{0,8},{1,9},{2,10},{3,11},{4,12},{5,13},{6,14},{7,15},{8,0},{9,1},... | collective-permute-start | bytes 393224 | tf_op jit(solution)/shard_map/ppermute | solution.py:265
  5.4 10.3 %collective-permute-start.1 = (bf16[2,128,256]{2,1,0:T(8,128)(2,1)S(1)}, bf16[2,128,256]{2,1,0:T(8,128)(2,1)S(1)}, u32[]{:S(2)}, u32[]{:S(2)}) collective-permute-start(bf16[2,128,256]{2,1,0:T(8,128)(2,1)S(1)} %own.1.u0), channel_id=1, source_target_pairs={{0,4},{1,5},{2,7},{3,6},{4,0},{5,1},{6,3},{7,2},{8,12},{9,13},{10,... | collective-permute-start | bytes 393224 | tf_op jit(solution)/shard_map/ppermute | solution.py:265
  7.1 10.6 %collective-permute-start.2 = (bf16[2,128,256]{2,1,0:T(8,128)(2,1)S(1)}, bf16[2,128,256]{2,1,0:T(8,128)(2,1)S(1)}, u32[]{:S(2)}, u32[]{:S(2)}) collective-permute-start(bf16[2,128,256]{2,1,0:T(8,128)(2,1)S(1)} %own.1.u0), channel_id=1, source_target_pairs={{0,2},{1,3},{2,0},{3,1},{4,6},{5,7},{6,4},{7,5},{8,10},{9,11},{10,... | collective-permute-start | bytes 393224 | tf_op jit(solution)/shard_map/ppermute | solution.py:265
  7.7 10.0 %collective-permute-start.3 = (bf16[2,128,256]{2,1,0:T(8,128)(2,1)S(1)}, bf16[2,128,256]{2,1,0:T(8,128)(2,1)S(1)}, u32[]{:S(2)}, u32[]{:S(2)}) collective-permute-start(bf16[2,128,256]{2,1,0:T(8,128)(2,1)S(1)} %own.1.u0), channel_id=1, source_target_pairs={{0,1},{1,0},{2,3},{3,2},{4,5},{5,4},{6,7},{7,6},{8,9},{9,8},{10,11... | collective-permute-start | bytes 393224 | tf_op jit(solution)/shard_map/ppermute | solution.py:265
  11.7 7.6 %collective-permute-start.4 = (bf16[2,128,256]{2,1,0:T(8,128)(2,1)S(1)}, bf16[2,128,256]{2,1,0:T(8,128)(2,1)S(1)}, u32[]{:S(2)}, u32[]{:S(2)}) collective-permute-start(bf16[2,128,256]{2,1,0:T(8,128)(2,1)S(1)} %collective-permute-done.v), channel_id=1, source_target_pairs={{0,0},{1,1},{2,2},{3,3},{4,6},{5,7},{6,4},{7,5},{8,10},{9,11},{10,... | collective-permute-start | bytes 393224 | tf_op jit(solution)/shard_map/ppermute | solution.py:265
  12.4 7.0 %collective-permute-start.5 = (bf16[2,128,256]{2,1,0:T(8,128)(2,1)S(1)}, bf16[2,128,256]{2,1,0:T(8,128)(2,1)S(1)}, u32[]{:S(2)}, u32[]{:S(2)}) collective-permute-start(bf16[2,128,256]{2,1,0:T(8,128)(2,1)S(1)} %collective-permute-done.v), channel_id=1, source_target_pairs={{0,4},{1,5},{2,7},{3,6},{4,0},{5,1},{6,3},{7,2},{8,12},{9,13},{10,... | collective-permute-start | bytes 393224 | tf_op jit(solution)/shard_map/ppermute | solution.py:265
  15.8 6.9 %collective-permute-start.8 = (bf16[2,128,256]{2,1,0:T(8,128)(2,1)S(1)}, bf16[2,128,256]{2,1,0:T(8,128)(2,1)S(1)}, u32[]{:S(2)}, u32[]{:S(2)}) collective-permute-start(bf16[2,128,256]{2,1,0:T(8,128)(2,1)S(1)} %collective-permute-done.v), channel_id=1, source_target_pairs={{0,2},{1,3},{2,0},{3,1},{4,4},{5,5},{6,6},{7,7},{8,8},{9,9},{10,10... | collective-permute-start | bytes 393224 | tf_op jit(solution)/shard_map/ppermute | solution.py:265
  18.7 1.3 %collective-permute-start.6 = (bf16[128,256]{1,0:T(8,128)(2,1)S(1)}, bf16[128,256]{1,0:T(8,128)(2,1)S(1)}, u32[]{:S(2)}, u32[]{:S(2)}) collective-permute-start(bf16[128,256]{1,0:T(8,128)(2,1)S(1)} %get-tuple-element.44), channel_id=1, source_target_pairs={{0,1},{1,0},{2,3},{3,2},{4,5},{5,4},{6,7},{7,6},{8,9},{9,8},{10,11... | collective-permute-start | bytes 196616 | tf_op jit(solution)/shard_map/ppermute | solution.py:265
  19.2 1.3 %collective-permute-start.7 = (bf16[128,256]{1,0:T(8,128)(2,1)S(1)}, bf16[128,256]{1,0:T(8,128)(2,1)S(1)}, u32[]{:S(2)}, u32[]{:S(2)}) collective-permute-start(bf16[128,256]{1,0:T(8,128)(2,1)S(1)} %get-tuple-element.43), channel_id=1, source_target_pairs={{0,1},{1,0},{2,3},{3,2},{4,5},{5,4},{6,7},{7,6},{8,9},{9,8},{10,11... | collective-permute-start | bytes 196616 | tf_op jit(solution)/shard_map/ppermute | solution.py:265
  23.4 3.6 %collective-permute-start.10 = (f32[4,32]{1,0:T(4,128)S(1)}, f32[4,32]{1,0:T(4,128)S(1)}, u32[]{:S(2)}, u32[]{:S(2)}) collective-permute-start(f32[4,32]{1,0:T(4,128)S(1)} %get-tuple-element.42), channel_id=1, source_target_pairs={{0,4},{1,5},{2,7},{3,6},{4,0},{5,1},{6,3},{7,2},{8,12},{9,13},{10,... | collective-permute-start | bytes 1544 | tf_op jit(solution)/shard_map/ppermute | solution.py:265
  23.4 3.7 %collective-permute-start.9 = (f32[4,32]{1,0:T(4,128)S(1)}, f32[4,32]{1,0:T(4,128)S(1)}, u32[]{:S(2)}, u32[]{:S(2)}) collective-permute-start(f32[4,32]{1,0:T(4,128)S(1)} %get-tuple-element.41), channel_id=1, source_target_pairs={{0,2},{1,3},{2,0},{3,1},{4,6},{5,7},{6,4},{7,5},{8,10},{9,11},{10,... | collective-permute-start | bytes 1544 | tf_op jit(solution)/shard_map/ppermute | solution.py:265
  27.1 4.5 %collective-permute-start.11 = (f32[2,32]{1,0:T(2,128)S(1)}, f32[2,32]{1,0:T(2,128)S(1)}, u32[]{:S(2)}, u32[]{:S(2)}) collective-permute-start(f32[2,32]{1,0:T(2,128)S(1)} %slice.15), channel_id=1, source_target_pairs={{0,8},{1,9},{2,10},{3,11},{4,12},{5,13},{6,14},{7,15},{8,0},{9,1},... | collective-permute-start | bytes 776 | tf_op jit(solution)/shard_map/ppermute | solution.py:265

commit v20 on v18

--- a/solution.py
+++ b/solution.py
@@ -278,21 +278,22 @@
         input_output_aliases={1: 0},
     )
     v = send(away, opposite)
-    away, lens, *data = lax.optimization_barrier((away, lens, *data))
-    own = call(
-        functools.partial(own_kernel, seq_len), "own", 10**9, 40, (lens, *data), [], unit
-    )
-    near = [send(own, to) for to in ways]
+    away, ids = lax.optimization_barrier((away, layer_ids))
     terms, pick = call(
         functools.partial(setup_kernel, seq_len, per),
         "factor_terms",
         10**9,
         51,
-        (layer_ids, flagged.reshape(1, -1), act_factor, grad_factor),
+        (ids, flagged.reshape(1, -1), act_factor, grad_factor),
         [pl.BlockSpec(memory_space=pltpu.SMEM), vmem, hbm, hbm],
         (shape((2, 3, rank, rank), bf16), shape((8 * tokens, columns), bf16)),
         [pltpu.VMEM((2, rank, rank), f32), pltpu.SemaphoreType.DMA((2,))],
     )
+    away, terms, lens, *data = lax.optimization_barrier((away, terms, lens, *data))
+    own = call(
+        functools.partial(own_kernel, seq_len), "own", 10**9, 40, (lens, *data), [], unit
+    )
+    near = [send(own, to) for to in ways]
     v, terms, pick = lax.optimization_barrier((v, terms, pick))
     late = [send(v, to) for to in ways[:2]]
     whole = shape((2 * per, 8 * tokens), f32)

time: 28.6 us -> 28.6 us (level)
  transfers between devices with their start and end apart: 11 -> 11, of which waited for: 6 -> 8; matrix products, arithmetic and copies ran while one was open for 0% -> 0% of each run, Pallas kernels for 14% -> 14%
where the time goes in v20:
time: 28.6 us; the launch traced here: 28.4 us
  starting transfers between devices  15 us (52%)
  waiting for transfers between devices  6.94 us (24%)
  Pallas kernels  5.76 us (20%)
  other arithmetic  0.57 us (2%)
    ppermute x11, starting transfers between devices, send(): return lax.ppermute(x, 'blk', [(d, to(d)) for d in range(size)])  15 us
    ppermute x11, waiting for transfers between devices, send(): return lax.ppermute(x, 'blk', [(d, to(d)) for d in range(size)])  6.94 us
    pallas_call x9, Pallas kernels, call(): pl.pallas_call(kernel, out_shape=out_shape, in_specs=specs + [vmem] * (le...  5.76 us
  transfers between devices with their start and end apart: 11, of which 8 were waited for; matrix products, arithmetic and copies ran while one was open for 0% of the time, Pallas kernels for 14%

profile of v20, /device:TPU:0, one launch (start us, length us, event | category | flops | bytes accessed | tf_op | source)
XLA Modules:
  0.0 28.4 jit_solution(9316279988620546832)
XLA Ops:
  0.0 0.9 %away.1.unit = bf16[2,128,256]{2,1,0:T(8,128)(2,1)S(1)} custom-call(bf16[2,128,256]{2,1,0:T(8,128)(2,1)} %acts.2, bf16[2,128,256]{2,1,0:T(8,128)(2,1)} %grads.2), custom_call_target="tpu_custom_call" | custom-call | flops 3000000000 | bytes 1000000 | tf_op jit(solution)/shard_map/away/pallas_call | solution.py:234
  1.0 0.2 away_mask.1
  1.1 4.1 %collective-permute-start = (bf16[2,128,256]{2,1,0:T(8,128)(2,1)S(1)}, bf16[2,128,256]{2,1,0:T(8,128)(2,1)S(1)}, u32[]{:S(2)}, u32[]{:S(2)}) collective-permute-start(bf16[2,128,256]{2,1,0:T(8,128)(2,1)S(1)} %away_mask.1), channel_id=1, source_target_pairs={{0,8},{1,9},{2,10},{3,11},{4,12},{5,13},{6,14},{7,15},{8,0},{9,1},... | collective-permute-start | bytes 393224 | tf_op jit(solution)/shard_map/ppermute | solution.py:255
  5.2 1.7 %factor_terms.1 = (bf16[2,3,256,256]{3,2,1,0:T(8,128)(2,1)S(1)}, bf16[1024,32]{1,0:T(8,128)(2,1)S(1)}) custom-call(s32[2]{0:T(128)S(1)} %copy-done, s32[1,32]{1,0:T(1,128)S(1)} %bitcast.6, f32[16,256,256]{2,1,0:T(8,128)} %act_f.1, f32[16,256,256]{2,1,0:T(8,128)} %grad_f.1), custom_call_target="tpu_custom_call" | custom-call | flops 1000000000 | bytes 1000000 | tf_op jit(solution)/shard_map/factor_terms/pallas_call | solution.py:234
  6.9 0.2 own.1.u0
  7.1 1.6 %collective-permute-start.1 = (bf16[2,128,256]{2,1,0:T(8,128)(2,1)S(1)}, bf16[2,128,256]{2,1,0:T(8,128)(2,1)S(1)}, u32[]{:S(2)}, u32[]{:S(2)}) collective-permute-start(bf16[2,128,256]{2,1,0:T(8,128)(2,1)S(1)} %own.1.u0), channel_id=1, source_target_pairs={{0,4},{1,5},{2,7},{3,6},{4,0},{5,1},{6,3},{7,2},{8,12},{9,13},{10,... | collective-permute-start | bytes 393224 | tf_op jit(solution)/shard_map/ppermute | solution.py:255
  8.7 0.7 %collective-permute-start.2 = (bf16[2,128,256]{2,1,0:T(8,128)(2,1)S(1)}, bf16[2,128,256]{2,1,0:T(8,128)(2,1)S(1)}, u32[]{:S(2)}, u32[]{:S(2)}) collective-permute-start(bf16[2,128,256]{2,1,0:T(8,128)(2,1)S(1)} %own.1.u0), channel_id=1, source_target_pairs={{0,2},{1,3},{2,0},{3,1},{4,6},{5,7},{6,4},{7,5},{8,10},{9,11},{10,... | collective-permute-start | bytes 393224 | tf_op jit(solution)/shard_map/ppermute | solution.py:255
  9.4 0.7 %collective-permute-start.3 = (bf16[2,128,256]{2,1,0:T(8,128)(2,1)S(1)}, bf16[2,128,256]{2,1,0:T(8,128)(2,1)S(1)}, u32[]{:S(2)}, u32[]{:S(2)}) collective-permute-start(bf16[2,128,256]{2,1,0:T(8,128)(2,1)S(1)} %own.1.u0), channel_id=1, source_target_pairs={{0,1},{1,0},{2,3},{3,2},{4,5},{5,4},{6,7},{7,6},{8,9},{9,8},{10,11... | collective-permute-start | bytes 393224 | tf_op jit(solution)/shard_map/ppermute | solution.py:255
  10.1 1.6 %collective-permute-done.v = bf16[2,128,256]{2,1,0:T(8,128)(2,1)S(1)} collective-permute-done((bf16[2,128,256]{2,1,0:T(8,128)(2,1)S(1)}, bf16[2,128,256]{2,1,0:T(8,128)(2,1)S(1)}, u32[]{:S(2)}, u32[]{:S(2)}) %collective-permute-start) | collective-permute-done | bytes 131104 | tf_op jit(solution)/shard_map/ppermute | solution.py:255
  11.6 0.7 %collective-permute-start.4 = (bf16[2,128,256]{2,1,0:T(8,128)(2,1)S(1)}, bf16[2,128,256]{2,1,0:T(8,128)(2,1)S(1)}, u32[]{:S(2)}, u32[]{:S(2)}) collective-permute-start(bf16[2,128,256]{2,1,0:T(8,128)(2,1)S(1)} %collective-permute-done.v), channel_id=1, source_target_pairs={{0,4},{1,5},{2,7},{3,6},{4,0},{5,1},{6,3},{7,2},{8,12},{9,13},{10,... | collective-permute-start | bytes 393224 | tf_op jit(solution)/shard_map/ppermute | solution.py:255
  12.3 1.1 %collective-permute-start.7 = (bf16[2,128,256]{2,1,0:T(8,128)(2,1)S(1)}, bf16[2,128,256]{2,1,0:T(8,128)(2,1)S(1)}, u32[]{:S(2)}, u32[]{:S(2)}) collective-permute-start(bf16[2,128,256]{2,1,0:T(8,128)(2,1)S(1)} %collective-permute-done.v), channel_id=1, source_target_pairs={{0,2},{1,3},{2,0},{3,1},{4,6},{5,7},{6,4},{7,5},{8,10},{9,11},{10,... | collective-permute-start | bytes 393224 | tf_op jit(solution)/shard_map/ppermute | solution.py:255
  13.4 0.5 %collective-permute-done.1.u3 = bf16[2,128,256]{2,1,0:T(8,128)(2,1)S(1)} collective-permute-done((bf16[2,128,256]{2,1,0:T(8,128)(2,1)S(1)}, bf16[2,128,256]{2,1,0:T(8,128)(2,1)S(1)}, u32[]{:S(2)}, u32[]{:S(2)}) %collective-permute-start.1) | collective-permute-done | bytes 131104 | tf_op jit(solution)/shard_map/ppermute | solution.py:255
  13.9 0.1 collective-permute-done.2.u2
  14.0 0.0 collective-permute-done.3.u1
  14.0 1.0 %early_pairs.1 = (bf16[2,512,256]{2,1,0:T(8,128)(2,1)S(1)}, f32[4,1024]{1,0:T(4,128)S(1)}, f32[8,768]{1,0:T(8,128)S(1)}) custom-call(bf16[2,3,256,256]{3,2,1,0:T(8,128)(2,1)S(1)} %get-tuple-element.31.terms, bf16[2,128,256]{2,1,0:T(8,128)(2,1)S(1)} %own.1.u0, bf16[2,128,256]{2,1,0:T(8,128)(2,1)S(1)} %collective-permute-done.v, ...), custom_call_target="tpu_custom_call" | custom-call | flops 1000000000 | bytes 1000000 | tf_op jit(solution)/shard_map/early_pairs/pallas_call | solution.py:234
  15.0 0.1 collective-permute-start.5
  15.1 0.5 %collective-permute-start.6 = (bf16[128,256]{1,0:T(8,128)(2,1)S(1)}, bf16[128,256]{1,0:T(8,128)(2,1)S(1)}, u32[]{:S(2)}, u32[]{:S(2)}) collective-permute-start(bf16[128,256]{1,0:T(8,128)(2,1)S(1)} %get-tuple-element.47), channel_id=1, source_target_pairs={{0,1},{1,0},{2,3},{3,2},{4,5},{5,4},{6,7},{7,6},{8,9},{9,8},{10,11... | collective-permute-start | bytes 196616 | tf_op jit(solution)/shard_map/ppermute | solution.py:255
  15.6 1.0 %collective-permute-done.4.v3 = bf16[2,128,256]{2,1,0:T(8,128)(2,1)S(1)} collective-permute-done((bf16[2,128,256]{2,1,0:T(8,128)(2,1)S(1)}, bf16[2,128,256]{2,1,0:T(8,128)(2,1)S(1)}, u32[]{:S(2)}, u32[]{:S(2)}) %collective-permute-start.4) | collective-permute-done | bytes 131104 | tf_op jit(solution)/shard_map/ppermute | solution.py:255
  16.6 0.4 %z_pairs.1 = (bf16[2,128,256]{2,1,0:T(8,128)(2,1)S(1)}, f32[8,768]{1,0:T(8,128)S(1)}) custom-call(bf16[2,3,256,256]{3,2,1,0:T(8,128)(2,1)S(1)} %get-tuple-element.31.terms, bf16[2,512,256]{2,1,0:T(8,128)(2,1)S(1)} %get-tuple-element.36.white, bf16[2,128,256]{2,1,0:T(8,128)(2,1)S(1)} %collective-permute-done.2.u2, ...), custom_call_target="tpu_custom_call", output_to_operand_aliasing={{1}: (5, {})} | custom-call | flops 10000 | bytes 1000000 | tf_op jit(solution)/shard_map/z_pairs/pallas_call | solution.py:234
  17.0 0.0 collective-permute-done.5.acts
  17.0 0.0 collective-permute-done.6.grads
  17.0 0.3 %core_pairs.1 = (f32[4,1024]{1,0:T(4,128)S(1)}, f32[8,768]{1,0:T(8,128)S(1)}) custom-call(bf16[2,512,256]{2,1,0:T(8,128)(2,1)S(1)} %get-tuple-element.36.white, bf16[2,128,256]{2,1,0:T(8,128)(2,1)S(1)} %get-tuple-element.39.white3, bf16[128,256]{1,0:T(8,128)(2,1)S(1)} %collective-permute-done.5.acts, ...), custom_call_target="tpu_custom_call", output_to_operand_aliasing={{0}: (4, {}), {1}: (5, {})} | custom-call | flops 10000 | bytes 1000000 | tf_op jit(solution)/shard_map/core_pairs/pallas_call | solution.py:234
  17.4 0.2 collective-permute-done.7.v2
  17.6 0.7 %return_rows.1 = (f32[4,32]{1,0:T(4,128)S(1)}, f32[4,32]{1,0:T(4,128)S(1)}) custom-call(bf16[2,3,256,256]{3,2,1,0:T(8,128)(2,1)S(1)} %get-tuple-element.31.terms, bf16[2,512,256]{2,1,0:T(8,128)(2,1)S(1)} %get-tuple-element.36.white, bf16[2,128,256]{2,1,0:T(8,128)(2,1)S(1)} %get-tuple-element.39.white3, bf16[1024,32]{1,0:T(8,128)(2,1)S(1)} %get-tuple-element.37.pick, ...), custom_call_target="tpu_custom_call" | custom-call | flops 1000000000 | bytes 1000000 | tf_op jit(solution)/shard_map/return_rows/pallas_call | solution.py:234
  18.3 1.5 %collective-permute-start.9 = (f32[4,32]{1,0:T(4,128)S(1)}, f32[4,32]{1,0:T(4,128)S(1)}, u32[]{:S(2)}, u32[]{:S(2)}) collective-permute-start(f32[4,32]{1,0:T(4,128)S(1)} %get-tuple-element.46), channel_id=1, source_target_pairs={{0,4},{1,5},{2,7},{3,6},{4,0},{5,1},{6,3},{7,2},{8,12},{9,13},{10,... | collective-permute-start | bytes 1544 | tf_op jit(solution)/shard_map/ppermute | solution.py:255
  19.7 1.1 %collective-permute-start.8 = (f32[4,32]{1,0:T(4,128)S(1)}, f32[4,32]{1,0:T(4,128)S(1)}, u32[]{:S(2)}, u32[]{:S(2)}) collective-permute-start(f32[4,32]{1,0:T(4,128)S(1)} %get-tuple-element.45), channel_id=1, source_target_pairs={{0,2},{1,3},{2,0},{3,1},{4,6},{5,7},{6,4},{7,5},{8,10},{9,11},{10,... | collective-permute-start | bytes 1544 | tf_op jit(solution)/shard_map/ppermute | solution.py:255
  20.9 0.4 %own_rows.1 = f32[4,32]{1,0:T(4,128)S(1)} custom-call(bf16[2,512,256]{2,1,0:T(8,128)(2,1)S(1)} %get-tuple-element.36.white, bf16[1024,32]{1,0:T(8,128)(2,1)S(1)} %get-tuple-element.37.pick, f32[4,1024]{1,0:T(4,128)S(1)} %get-tuple-element.43.mine, bf16[2,128,256]{2,1,0:T(8,128)(2,1)S(1)} %collective-permute-done.4.v3, ...), custom_call_target="tpu_custom_call" | custom-call | flops 1000000000 | bytes 1000000 | tf_op jit(solution)/shard_map/own_rows/pallas_call | solution.py:234
  21.3 0.6 %collective-permute-done.9 = f32[4,32]{1,0:T(4,128)S(1)} collective-permute-done((f32[4,32]{1,0:T(4,128)S(1)}, f32[4,32]{1,0:T(4,128)S(1)}, u32[]{:S(2)}, u32[]{:S(2)}) %collective-permute-start.9) | collective-permute-done | bytes 544 | tf_op jit(solution)/shard_map/ppermute | solution.py:255
  21.9 1.4 %collective-permute-done.8 = f32[4,32]{1,0:T(4,128)S(1)} collective-permute-done((f32[4,32]{1,0:T(4,128)S(1)}, f32[4,32]{1,0:T(4,128)S(1)}, u32[]{:S(2)}, u32[]{:S(2)}) %collective-permute-start.8) | collective-permute-done | bytes 544 | tf_op jit(solution)/shard_map/ppermute | solution.py:255
  23.3 3.0 %collective-permute-start.10 = (f32[2,32]{1,0:T(2,128)S(1)}, f32[2,32]{1,0:T(2,128)S(1)}, u32[]{:S(2)}, u32[]{:S(2)}) collective-permute-start(f32[2,32]{1,0:T(2,128)S(1)} %slice.15), channel_id=1, source_target_pairs={{0,8},{1,9},{2,10},{3,11},{4,12},{5,13},{6,14},{7,15},{8,0},{9,1},... | collective-permute-start | bytes 776 | tf_op jit(solution)/shard_map/ppermute | solution.py:255
  26.3 1.5 %collective-permute-done.10 = f32[2,32]{1,0:T(2,128)S(1)} collective-permute-done((f32[2,32]{1,0:T(2,128)S(1)}, f32[2,32]{1,0:T(2,128)S(1)}, u32[]{:S(2)}, u32[]{:S(2)}) %collective-permute-start.10) | collective-permute-done | bytes 288 | tf_op jit(solution)/shard_map/ppermute | solution.py:255
  27.9 0.6 %slice_add_fusion = f32[2,32]{1,0:T(2,128)} fusion(f32[2,32]{1,0:T(2,128)S(1)} %collective-permute-done.10, f32[4,32]{1,0:T(4,128)S(1)} %add_add_fusion), kind=kLoop, calls=%fused_computation.3 | loop fusion | flops 64 | bytes 768 | tf_op jit(solution)/shard_map/add | solution.py:341
  (13 shorter events, 0.0 us)
Async XLA Ops:
  0.0 0.9 %copy-start.2 = (s32[2]{0:T(128)S(1)}, s32[2]{0:T(128)}, u32[]{:S(2)}) copy-start(s32[2]{0:T(128)} %param.9) | copy-start | bytes 28
  0.0 5.2 %copy-start = (s32[2]{0:T(128)S(1)}, s32[2]{0:T(128)}, u32[]{:S(2)}) copy-start(s32[2]{0:T(128)} %layer_ids) | copy-start | bytes 28
  0.0 5.2 %copy-start.1 = (s32[32]{0:T(128)S(1)}, s32[32]{0:T(128)}, u32[]{:S(2)}) copy-start(s32[32]{0:T(128)} %param.11) | copy-start | bytes 388
  1.1 10.5 %collective-permute-start = (bf16[2,128,256]{2,1,0:T(8,128)(2,1)S(1)}, bf16[2,128,256]{2,1,0:T(8,128)(2,1)S(1)}, u32[]{:S(2)}, u32[]{:S(2)}) collective-permute-start(bf16[2,128,256]{2,1,0:T(8,128)(2,1)S(1)} %away_mask.1), channel_id=1, source_target_pairs={{0,8},{1,9},{2,10},{3,11},{4,12},{5,13},{6,14},{7,15},{8,0},{9,1},... | collective-permute-start | bytes 393224 | tf_op jit(solution)/shard_map/ppermute | solution.py:255
  5.2 1.7 %copy-start.3 = (bf16[2,128,256]{2,1,0:T(8,128)(2,1)S(1)}, bf16[2,128,256]{2,1,0:T(8,128)(2,1)}, u32[]{:S(2)}) copy-start(bf16[2,128,256]{2,1,0:T(8,128)(2,1)} %acts.2) | copy-start | bytes 393220
  5.2 1.7 %copy-start.4 = (bf16[2,128,256]{2,1,0:T(8,128)(2,1)S(1)}, bf16[2,128,256]{2,1,0:T(8,128)(2,1)}, u32[]{:S(2)}) copy-start(bf16[2,128,256]{2,1,0:T(8,128)(2,1)} %grads.2) | copy-start | bytes 393220
  7.1 6.8 %collective-permute-start.1 = (bf16[2,128,256]{2,1,0:T(8,128)(2,1)S(1)}, bf16[2,128,256]{2,1,0:T(8,128)(2,1)S(1)}, u32[]{:S(2)}, u32[]{:S(2)}) collective-permute-start(bf16[2,128,256]{2,1,0:T(8,128)(2,1)S(1)} %own.1.u0), channel_id=1, source_target_pairs={{0,4},{1,5},{2,7},{3,6},{4,0},{5,1},{6,3},{7,2},{8,12},{9,13},{10,... | collective-permute-start | bytes 393224 | tf_op jit(solution)/shard_map/ppermute | solution.py:255
  8.7 5.3 %collective-permute-start.2 = (bf16[2,128,256]{2,1,0:T(8,128)(2,1)S(1)}, bf16[2,128,256]{2,1,0:T(8,128)(2,1)S(1)}, u32[]{:S(2)}, u32[]{:S(2)}) collective-permute-start(bf16[2,128,256]{2,1,0:T(8,128)(2,1)S(1)} %own.1.u0), channel_id=1, source_target_pairs={{0,2},{1,3},{2,0},{3,1},{4,6},{5,7},{6,4},{7,5},{8,10},{9,11},{10,... | collective-permute-start | bytes 393224 | tf_op jit(solution)/shard_map/ppermute | solution.py:255
  9.4 4.6 %collective-permute-start.3 = (bf16[2,128,256]{2,1,0:T(8,128)(2,1)S(1)}, bf16[2,128,256]{2,1,0:T(8,128)(2,1)S(1)}, u32[]{:S(2)}, u32[]{:S(2)}) collective-permute-start(bf16[2,128,256]{2,1,0:T(8,128)(2,1)S(1)} %own.1.u0), channel_id=1, source_target_pairs={{0,1},{1,0},{2,3},{3,2},{4,5},{5,4},{6,7},{7,6},{8,9},{9,8},{10,11... | collective-permute-start | bytes 393224 | tf_op jit(solution)/shard_map/ppermute | solution.py:255
  11.6 5.0 %collective-permute-start.4 = (bf16[2,128,256]{2,1,0:T(8,128)(2,1)S(1)}, bf16[2,128,256]{2,1,0:T(8,128)(2,1)S(1)}, u32[]{:S(2)}, u32[]{:S(2)}) collective-permute-start(bf16[2,128,256]{2,1,0:T(8,128)(2,1)S(1)} %collective-permute-done.v), channel_id=1, source_target_pairs={{0,4},{1,5},{2,7},{3,6},{4,0},{5,1},{6,3},{7,2},{8,12},{9,13},{10,... | collective-permute-start | bytes 393224 | tf_op jit(solution)/shard_map/ppermute | solution.py:255
  12.3 5.3 %collective-permute-start.7 = (bf16[2,128,256]{2,1,0:T(8,128)(2,1)S(1)}, bf16[2,128,256]{2,1,0:T(8,128)(2,1)S(1)}, u32[]{:S(2)}, u32[]{:S(2)}) collective-permute-start(bf16[2,128,256]{2,1,0:T(8,128)(2,1)S(1)} %collective-permute-done.v), channel_id=1, source_target_pairs={{0,2},{1,3},{2,0},{3,1},{4,6},{5,7},{6,4},{7,5},{8,10},{9,11},{10,... | collective-permute-start | bytes 393224 | tf_op jit(solution)/shard_map/ppermute | solution.py:255
  15.0 2.0 %collective-permute-start.5 = (bf16[128,256]{1,0:T(8,128)(2,1)S(1)}, bf16[128,256]{1,0:T(8,128)(2,1)S(1)}, u32[]{:S(2)}, u32[]{:S(2)}) collective-permute-start(bf16[128,256]{1,0:T(8,128)(2,1)S(1)} %get-tuple-element.48), channel_id=1, source_target_pairs={{0,1},{1,0},{2,3},{3,2},{4,5},{5,4},{6,7},{7,6},{8,9},{9,8},{10,11... | collective-permute-start | bytes 196616 | tf_op jit(solution)/shard_map/ppermute | solution.py:255
  15.1 1.9 %collective-permute-start.6 = (bf16[128,256]{1,0:T(8,128)(2,1)S(1)}, bf16[128,256]{1,0:T(8,128)(2,1)S(1)}, u32[]{:S(2)}, u32[]{:S(2)}) collective-permute-start(bf16[128,256]{1,0:T(8,128)(2,1)S(1)} %get-tuple-element.47), channel_id=1, source_target_pairs={{0,1},{1,0},{2,3},{3,2},{4,5},{5,4},{6,7},{7,6},{8,9},{9,8},{10,11... | collective-permute-start | bytes 196616 | tf_op jit(solution)/shard_map/ppermute | solution.py:255
  18.3 3.6 %collective-permute-start.9 = (f32[4,32]{1,0:T(4,128)S(1)}, f32[4,32]{1,0:T(4,128)S(1)}, u32[]{:S(2)}, u32[]{:S(2)}) collective-permute-start(f32[4,32]{1,0:T(4,128)S(1)} %get-tuple-element.46), channel_id=1, source_target_pairs={{0,4},{1,5},{2,7},{3,6},{4,0},{5,1},{6,3},{7,2},{8,12},{9,13},{10,... | collective-permute-start | bytes 1544 | tf_op jit(solution)/shard_map/ppermute | solution.py:255
  19.7 3.6 %collective-permute-start.8 = (f32[4,32]{1,0:T(4,128)S(1)}, f32[4,32]{1,0:T(4,128)S(1)}, u32[]{:S(2)}, u32[]{:S(2)}) collective-permute-start(f32[4,32]{1,0:T(4,128)S(1)} %get-tuple-element.45), channel_id=1, source_target_pairs={{0,2},{1,3},{2,0},{3,1},{4,6},{5,7},{6,4},{7,5},{8,10},{9,11},{10,... | collective-permute-start | bytes 1544 | tf_op jit(solution)/shard_map/ppermute | solution.py:255
  23.3 4.5 %collective-permute-start.10 = (f32[2,32]{1,0:T(2,128)S(1)}, f32[2,32]{1,0:T(2,128)S(1)}, u32[]{:S(2)}, u32[]{:S(2)}) collective-permute-start(f32[2,32]{1,0:T(2,128)S(1)} %slice.15), channel_id=1, source_target_pairs={{0,8},{1,9},{2,10},{3,11},{4,12},{5,13},{6,14},{7,15},{8,0},{9,1},... | collective-permute-start | bytes 776 | tf_op jit(solution)/shard_map/ppermute | solution.py:255

commit v21 on v18

--- a/solution.py
+++ b/solution.py
@@ -169,9 +169,23 @@
             side[row : row + per, at : at + n] = block(seq_len, left[slot], tok[column])
 
 
-def z_kernel(seq_len, per, terms, white, u2, u1, v3, side, white3, side_out):
+def core_kernel(seq_len, per, white, acts, grads, mine, side, mine_out, side_out):
+    n = acts.shape[0]
+    tok = [acts[...], grads[...]]
+    mine_out[...] = mine[...]
+    mine_out[:, 3 * n : 4 * n] = block(seq_len, [white[w, : 2 * n] for w in range(2)], tok)
+    side_out[...] = side[...]
+    got = block(seq_len, [white[w, 2 * n : 4 * n] for w in range(2)], tok)
+    for i, row in enumerate((0, 2 * per)):
+        side_out[row : row + per, n : 2 * n] = got[i * per : (i + 1) * per]
+
+
+def z_kernel(
+    seq_len, per, terms, white, u2, u1, acts, grads, v3, side, white3, side_out
+):
     n = v3.shape[1]
     tok = [v3[w] for w in range(2)]
+    core = (acts[...], grads[...])
     fresh = [whiten(tok[w], terms.at[w]) for w in range(2)]
     for w in range(2):
         white3[w] = fresh[w]
@@ -179,21 +193,9 @@
     side_out[0:per, 5 * n : 6 * n] = block(
         seq_len, [white[w, 2 * n : 3 * n] for w in range(2)], tok
     )
-    got = block(seq_len, fresh, [stack(u1[w], u2[w]) for w in range(2)])
-    side_out[3 * per : 4 * per, 0:n] = got[:, :n]
-    side_out[3 * per : 4 * per, 2 * n : 3 * n] = got[:, n:]
-
-
-def core_kernel(seq_len, per, white, white3, acts, grads, mine, side, mine_out, side_out):
-    n = acts.shape[0]
-    tok = [acts[...], grads[...]]
-    mine_out[...] = mine[...]
-    mine_out[:, 3 * n : 4 * n] = block(seq_len, [white[w, : 2 * n] for w in range(2)], tok)
-    side_out[...] = side[...]
-    left = [stack(white[w, 2 * n : 4 * n], white3[w]) for w in range(2)]
-    got = block(seq_len, left, tok)
-    for i, row in enumerate((0, 2 * per, 3 * per)):
-        side_out[row : row + per, n : 2 * n] = got[i * per : (i + 1) * per]
+    side_out[3 * per : 4 * per, 0 : 3 * n] = block(
+        seq_len, fresh, [stack(u1[w], core[w], u2[w]) for w in range(2)]
+    )
 
 
 def return_kernel(
@@ -294,12 +296,13 @@
         [pltpu.VMEM((2, rank, rank), f32), pltpu.SemaphoreType.DMA((2,))],
     )
     v, terms, pick = lax.optimization_barrier((v, terms, pick))
-    late = [send(v, to) for to in ways[:2]]
+    v3 = send(v, ways[0])
+    v, near[2], near[1], near[0] = lax.optimization_barrier((v, near[2], near[1], near[0]))
+    v2 = send(v, ways[1])
     whole = shape((2 * per, 8 * tokens), f32)
     sides = shape((4 * per, 6 * tokens), f32)
     rows = shape((2 * per, columns), f32)
     u3, u2, u1 = near
-    v3, v2 = late
 
     def kernel(body, name, operands, out_shape, flops=10**9, **more):
         body = functools.partial(body, seq_len, per)
@@ -313,21 +316,21 @@
     )
     v, white = lax.optimization_barrier((v, white))
     v1 = [send(v[w], ways[2]) for w in range(2)]
+    mine, side = kernel(
+        core_kernel,
+        "core_pairs",
+        (white, *v1, mine, side),
+        (whole, sides),
+        flops=10**4,
+        input_output_aliases={3: 0, 4: 1},
+    )
     white3, side = kernel(
         z_kernel,
         "z_pairs",
-        (terms, white, u2, u1, v3, side),
+        (terms, white, u2, u1, *v1, v3, side),
         (unit, sides),
         flops=10**4,
-        input_output_aliases={5: 1},
-    )
-    mine, side = kernel(
-        core_kernel,
-        "core_pairs",
-        (white, white3, *v1, mine, side),
-        (whole, sides),
-        flops=10**4,
-        input_output_aliases={4: 0, 5: 1},
+        input_output_aliases={7: 1},
     )
     by_z, by_x = kernel(
         return_kernel,
@@ -336,7 +339,7 @@
         (rows, rows),
     )
     mine = kernel(rows_kernel, "own_rows", (white, pick, mine, v3, v2), rows)
-    half_sum = mine + send(by_x, lambda d: d ^ 2) + send(by_z, z_near)
+    half_sum = mine + send(by_z, z_near) + send(by_x, lambda d: d ^ 2)
     return half_sum[:per] + send(half_sum[per:], opposite)
 
 

time: 28.6 us -> 28.7 us (level)
  starting transfers between devices: 14.9 us -> 15.3 us
  waiting for transfers between devices: 7.06 us -> 6.77 us
    ppermute x11, starting transfers between devices: 14.9 us -> 15.3 us  [send(): return lax.ppermute(x, 'blk', [(d, to(d)) for d in range(size)])]
    ppermute x11, waiting for transfers between devices: 7.06 us -> 6.77 us  [send(): return lax.ppermute(x, 'blk', [(d, to(d)) for d in range(size)])]
  transfers between devices with their start and end apart: 11 -> 11, of which waited for: 6 -> 7; matrix products, arithmetic and copies ran while one was open for 0% -> 0% of each run, Pallas kernels for 14% -> 14%
where the time goes in v21:
time: 28.7 us; the launch traced here: 28.6 us
  starting transfers between devices  15.3 us (53%)
  waiting for transfers between devices  6.77 us (24%)
  Pallas kernels  5.81 us (20%)
  other arithmetic  0.57 us (2%)
    ppermute x11, starting transfers between devices, send(): return lax.ppermute(x, 'blk', [(d, to(d)) for d in range(size)])  15.3 us
    ppermute x11, waiting for transfers between devices, send(): return lax.ppermute(x, 'blk', [(d, to(d)) for d in range(size)])  6.77 us
    pallas_call x9, Pallas kernels, call(): pl.pallas_call(kernel, out_shape=out_shape, in_specs=specs + [vmem] * (le...  5.81 us
  transfers between devices with their start and end apart: 11, of which 7 were waited for; matrix products, arithmetic and copies ran while one was open for 0% of the time, Pallas kernels for 14%

profile of v21, /device:TPU:0, one launch (start us, length us, event | category | flops | bytes accessed | tf_op | source)
XLA Modules:
  0.0 28.6 jit_solution(8321468228885323592)
XLA Ops:
  0.0 1.0 %away.1.unit = bf16[2,128,256]{2,1,0:T(8,128)(2,1)S(1)} custom-call(bf16[2,128,256]{2,1,0:T(8,128)(2,1)} %acts.2, bf16[2,128,256]{2,1,0:T(8,128)(2,1)} %grads.2), custom_call_target="tpu_custom_call" | custom-call | flops 3000000000 | bytes 1000000 | tf_op jit(solution)/shard_map/away/pallas_call | solution.py:236
  1.0 0.2 away_mask.1
  1.1 4.1 %collective-permute-start = (bf16[2,128,256]{2,1,0:T(8,128)(2,1)S(1)}, bf16[2,128,256]{2,1,0:T(8,128)(2,1)S(1)}, u32[]{:S(2)}, u32[]{:S(2)}) collective-permute-start(bf16[2,128,256]{2,1,0:T(8,128)(2,1)S(1)} %away_mask.1), channel_id=1, source_target_pairs={{0,8},{1,9},{2,10},{3,11},{4,12},{5,13},{6,14},{7,15},{8,0},{9,1},... | collective-permute-start | bytes 393224 | tf_op jit(solution)/shard_map/ppermute | solution.py:257
  5.3 0.1 own.1.u0
  5.4 1.6 %collective-permute-start.3 = (bf16[2,128,256]{2,1,0:T(8,128)(2,1)S(1)}, bf16[2,128,256]{2,1,0:T(8,128)(2,1)S(1)}, u32[]{:S(2)}, u32[]{:S(2)}) collective-permute-start(bf16[2,128,256]{2,1,0:T(8,128)(2,1)S(1)} %own.1.u0), channel_id=1, source_target_pairs={{0,4},{1,5},{2,7},{3,6},{4,0},{5,1},{6,3},{7,2},{8,12},{9,13},{10,... | collective-permute-start | bytes 393224 | tf_op jit(solution)/shard_map/ppermute | solution.py:257
  7.1 0.7 %collective-permute-start.2 = (bf16[2,128,256]{2,1,0:T(8,128)(2,1)S(1)}, bf16[2,128,256]{2,1,0:T(8,128)(2,1)S(1)}, u32[]{:S(2)}, u32[]{:S(2)}) collective-permute-start(bf16[2,128,256]{2,1,0:T(8,128)(2,1)S(1)} %own.1.u0), channel_id=1, source_target_pairs={{0,2},{1,3},{2,0},{3,1},{4,6},{5,7},{6,4},{7,5},{8,10},{9,11},{10,... | collective-permute-start | bytes 393224 | tf_op jit(solution)/shard_map/ppermute | solution.py:257
  7.7 0.7 %collective-permute-start.1 = (bf16[2,128,256]{2,1,0:T(8,128)(2,1)S(1)}, bf16[2,128,256]{2,1,0:T(8,128)(2,1)S(1)}, u32[]{:S(2)}, u32[]{:S(2)}) collective-permute-start(bf16[2,128,256]{2,1,0:T(8,128)(2,1)S(1)} %own.1.u0), channel_id=1, source_target_pairs={{0,1},{1,0},{2,3},{3,2},{4,5},{5,4},{6,7},{7,6},{8,9},{9,8},{10,11... | collective-permute-start | bytes 393224 | tf_op jit(solution)/shard_map/ppermute | solution.py:257
  8.4 1.7 %factor_terms.1 = (bf16[2,3,256,256]{3,2,1,0:T(8,128)(2,1)S(1)}, bf16[1024,32]{1,0:T(8,128)(2,1)S(1)}) custom-call(s32[2]{0:T(128)S(1)} %copy-done.1, s32[1,32]{1,0:T(1,128)S(1)} %bitcast.8, f32[16,256,256]{2,1,0:T(8,128)} %act_f.1, f32[16,256,256]{2,1,0:T(8,128)} %grad_f.1), custom_call_target="tpu_custom_call" | custom-call | flops 1000000000 | bytes 1000000 | tf_op jit(solution)/shard_map/factor_terms/pallas_call | solution.py:236
  10.1 1.6 %collective-permute-done.v = bf16[2,128,256]{2,1,0:T(8,128)(2,1)S(1)} collective-permute-done((bf16[2,128,256]{2,1,0:T(8,128)(2,1)S(1)}, bf16[2,128,256]{2,1,0:T(8,128)(2,1)S(1)}, u32[]{:S(2)}, u32[]{:S(2)}) %collective-permute-start) | collective-permute-done | bytes 131104 | tf_op jit(solution)/shard_map/ppermute | solution.py:257
  11.7 0.6 %collective-permute-start.6 = (bf16[2,128,256]{2,1,0:T(8,128)(2,1)S(1)}, bf16[2,128,256]{2,1,0:T(8,128)(2,1)S(1)}, u32[]{:S(2)}, u32[]{:S(2)}) collective-permute-start(bf16[2,128,256]{2,1,0:T(8,128)(2,1)S(1)} %collective-permute-done.v), channel_id=1, source_target_pairs={{0,4},{1,5},{2,7},{3,6},{4,0},{5,1},{6,3},{7,2},{8,12},{9,13},{10,... | collective-permute-start | bytes 393224 | tf_op jit(solution)/shard_map/ppermute | solution.py:257
  12.3 0.0 collective-permute-done.3.u3
  12.3 0.0 collective-permute-done.2.u2
  12.4 0.0 collective-permute-done.1.u1
  12.4 2.0 %collective-permute-start.7 = (bf16[2,128,256]{2,1,0:T(8,128)(2,1)S(1)}, bf16[2,128,256]{2,1,0:T(8,128)(2,1)S(1)}, u32[]{:S(2)}, u32[]{:S(2)}) collective-permute-start(bf16[2,128,256]{2,1,0:T(8,128)(2,1)S(1)} %collective-permute-done.v), channel_id=1, source_target_pairs={{0,2},{1,3},{2,0},{3,1},{4,6},{5,7},{6,4},{7,5},{8,10},{9,11},{10,... | collective-permute-start | bytes 393224 | tf_op jit(solution)/shard_map/ppermute | solution.py:257
  14.4 1.0 %early_pairs.1 = (bf16[2,512,256]{2,1,0:T(8,128)(2,1)S(1)}, f32[4,1024]{1,0:T(4,128)S(1)}, f32[8,768]{1,0:T(8,128)S(1)}) custom-call(bf16[2,3,256,256]{3,2,1,0:T(8,128)(2,1)S(1)} %get-tuple-element.35.terms, bf16[2,128,256]{2,1,0:T(8,128)(2,1)S(1)} %own.1.u0, bf16[2,128,256]{2,1,0:T(8,128)(2,1)S(1)} %collective-permute-done.v, ...), custom_call_target="tpu_custom_call" | custom-call | flops 1000000000 | bytes 1000000 | tf_op jit(solution)/shard_map/early_pairs/pallas_call | solution.py:236
  15.4 0.1 collective-permute-start.5
  15.5 0.5 %collective-permute-start.4 = (bf16[128,256]{1,0:T(8,128)(2,1)S(1)}, bf16[128,256]{1,0:T(8,128)(2,1)S(1)}, u32[]{:S(2)}, u32[]{:S(2)}) collective-permute-start(bf16[128,256]{1,0:T(8,128)(2,1)S(1)} %get-tuple-element.52), channel_id=1, source_target_pairs={{0,1},{1,0},{2,3},{3,2},{4,5},{5,4},{6,7},{7,6},{8,9},{9,8},{10,11... | collective-permute-start | bytes 196616 | tf_op jit(solution)/shard_map/ppermute | solution.py:257
  16.0 0.7 %collective-permute-done.5.grads = bf16[128,256]{1,0:T(8,128)(2,1)S(1)} collective-permute-done((bf16[128,256]{1,0:T(8,128)(2,1)S(1)}, bf16[128,256]{1,0:T(8,128)(2,1)S(1)}, u32[]{:S(2)}, u32[]{:S(2)}) %collective-permute-start.5) | collective-permute-done | bytes 65568 | tf_op jit(solution)/shard_map/ppermute | solution.py:257
  16.7 0.2 collective-permute-done.4.acts
  16.9 0.3 %core_pairs.1 = (f32[4,1024]{1,0:T(4,128)S(1)}, f32[8,768]{1,0:T(8,128)S(1)}) custom-call(bf16[2,512,256]{2,1,0:T(8,128)(2,1)S(1)} %get-tuple-element.40.white, bf16[128,256]{1,0:T(8,128)(2,1)S(1)} %collective-permute-done.4.acts, bf16[128,256]{1,0:T(8,128)(2,1)S(1)} %collective-permute-done.5.grads, ...), custom_call_target="tpu_custom_call", output_to_operand_aliasing={{0}: (3, {}), {1}: (4, {})} | custom-call | flops 10000 | bytes 1000000 | tf_op jit(solution)/shard_map/core_pairs/pallas_call | solution.py:236
  17.2 0.0 collective-permute-done.6.v3
  17.2 0.5 %z_pairs.1 = (bf16[2,128,256]{2,1,0:T(8,128)(2,1)S(1)}, f32[8,768]{1,0:T(8,128)S(1)}) custom-call(bf16[2,3,256,256]{3,2,1,0:T(8,128)(2,1)S(1)} %get-tuple-element.35.terms, bf16[2,512,256]{2,1,0:T(8,128)(2,1)S(1)} %get-tuple-element.40.white, bf16[2,128,256]{2,1,0:T(8,128)(2,1)S(1)} %collective-permute-done.2.u2, ...), custom_call_target="tpu_custom_call", output_to_operand_aliasing={{1}: (7, {})} | custom-call | flops 10000 | bytes 1000000 | tf_op jit(solution)/shard_map/z_pairs/pallas_call | solution.py:236
  17.7 0.5 %collective-permute-done.7.v2 = bf16[2,128,256]{2,1,0:T(8,128)(2,1)S(1)} collective-permute-done((bf16[2,128,256]{2,1,0:T(8,128)(2,1)S(1)}, bf16[2,128,256]{2,1,0:T(8,128)(2,1)S(1)}, u32[]{:S(2)}, u32[]{:S(2)}) %collective-permute-start.7) | collective-permute-done | bytes 131104 | tf_op jit(solution)/shard_map/ppermute | solution.py:257
  18.1 0.7 %return_rows.1 = (f32[4,32]{1,0:T(4,128)S(1)}, f32[4,32]{1,0:T(4,128)S(1)}) custom-call(bf16[2,3,256,256]{3,2,1,0:T(8,128)(2,1)S(1)} %get-tuple-element.35.terms, bf16[2,512,256]{2,1,0:T(8,128)(2,1)S(1)} %get-tuple-element.40.white, bf16[2,128,256]{2,1,0:T(8,128)(2,1)S(1)} %get-tuple-element.47.white3, bf16[1024,32]{1,0:T(8,128)(2,1)S(1)} %get-tuple-element.41.pick, ...), custom_call_target="tpu_custom_call" | custom-call | flops 1000000000 | bytes 1000000 | tf_op jit(solution)/shard_map/return_rows/pallas_call | solution.py:236
  18.8 1.0 %collective-permute-start.8 = (f32[4,32]{1,0:T(4,128)S(1)}, f32[4,32]{1,0:T(4,128)S(1)}, u32[]{:S(2)}, u32[]{:S(2)}) collective-permute-start(f32[4,32]{1,0:T(4,128)S(1)} %get-tuple-element.49), channel_id=1, source_target_pairs={{0,4},{1,5},{2,7},{3,6},{4,0},{5,1},{6,3},{7,2},{8,12},{9,13},{10,... | collective-permute-start | bytes 1544 | tf_op jit(solution)/shard_map/ppermute | solution.py:257
  19.9 1.4 %collective-permute-start.9 = (f32[4,32]{1,0:T(4,128)S(1)}, f32[4,32]{1,0:T(4,128)S(1)}, u32[]{:S(2)}, u32[]{:S(2)}) collective-permute-start(f32[4,32]{1,0:T(4,128)S(1)} %get-tuple-element.50), channel_id=1, source_target_pairs={{0,2},{1,3},{2,0},{3,1},{4,6},{5,7},{6,4},{7,5},{8,10},{9,11},{10,... | collective-permute-start | bytes 1544 | tf_op jit(solution)/shard_map/ppermute | solution.py:257
  21.3 0.4 %own_rows.1 = f32[4,32]{1,0:T(4,128)S(1)} custom-call(bf16[2,512,256]{2,1,0:T(8,128)(2,1)S(1)} %get-tuple-element.40.white, bf16[1024,32]{1,0:T(8,128)(2,1)S(1)} %get-tuple-element.41.pick, f32[4,1024]{1,0:T(4,128)S(1)} %get-tuple-element.45.mine, bf16[2,128,256]{2,1,0:T(8,128)(2,1)S(1)} %collective-permute-done.6.v3, ...), custom_call_target="tpu_custom_call" | custom-call | flops 1000000000 | bytes 1000000 | tf_op jit(solution)/shard_map/own_rows/pallas_call | solution.py:236
  21.7 0.8 %collective-permute-done.8 = f32[4,32]{1,0:T(4,128)S(1)} collective-permute-done((f32[4,32]{1,0:T(4,128)S(1)}, f32[4,32]{1,0:T(4,128)S(1)}, u32[]{:S(2)}, u32[]{:S(2)}) %collective-permute-start.8) | collective-permute-done | bytes 544 | tf_op jit(solution)/shard_map/ppermute | solution.py:257
  22.5 1.0 %collective-permute-done.9 = f32[4,32]{1,0:T(4,128)S(1)} collective-permute-done((f32[4,32]{1,0:T(4,128)S(1)}, f32[4,32]{1,0:T(4,128)S(1)}, u32[]{:S(2)}, u32[]{:S(2)}) %collective-permute-start.9) | collective-permute-done | bytes 544 | tf_op jit(solution)/shard_map/ppermute | solution.py:257
  23.5 2.5 %collective-permute-start.10 = (f32[2,32]{1,0:T(2,128)S(1)}, f32[2,32]{1,0:T(2,128)S(1)}, u32[]{:S(2)}, u32[]{:S(2)}) collective-permute-start(f32[2,32]{1,0:T(2,128)S(1)} %slice.15), channel_id=1, source_target_pairs={{0,8},{1,9},{2,10},{3,11},{4,12},{5,13},{6,14},{7,15},{8,0},{9,1},... | collective-permute-start | bytes 776 | tf_op jit(solution)/shard_map/ppermute | solution.py:257
  26.0 2.0 %collective-permute-done.10 = f32[2,32]{1,0:T(2,128)S(1)} collective-permute-done((f32[2,32]{1,0:T(2,128)S(1)}, f32[2,32]{1,0:T(2,128)S(1)}, u32[]{:S(2)}, u32[]{:S(2)}) %collective-permute-start.10) | collective-permute-done | bytes 288 | tf_op jit(solution)/shard_map/ppermute | solution.py:257
  28.0 0.6 %slice_add_fusion = f32[2,32]{1,0:T(2,128)} fusion(f32[2,32]{1,0:T(2,128)S(1)} %collective-permute-done.10, f32[4,32]{1,0:T(4,128)S(1)} %add_add_fusion), kind=kLoop, calls=%fused_computation.3 | loop fusion | flops 64 | bytes 768 | tf_op jit(solution)/shard_map/add | solution.py:343
  (13 shorter events, 0.0 us)
Async XLA Ops:
  0.0 5.3 %copy-start.4 = (bf16[2,128,256]{2,1,0:T(8,128)(2,1)S(1)}, bf16[2,128,256]{2,1,0:T(8,128)(2,1)}, u32[]{:S(2)}) copy-start(bf16[2,128,256]{2,1,0:T(8,128)(2,1)} %grads.2) | copy-start | bytes 393220
  0.0 5.3 %copy-start.3 = (bf16[2,128,256]{2,1,0:T(8,128)(2,1)S(1)}, bf16[2,128,256]{2,1,0:T(8,128)(2,1)}, u32[]{:S(2)}) copy-start(bf16[2,128,256]{2,1,0:T(8,128)(2,1)} %acts.2) | copy-start | bytes 393220
  0.0 1.0 %copy-start = (s32[2]{0:T(128)S(1)}, s32[2]{0:T(128)}, u32[]{:S(2)}) copy-start(s32[2]{0:T(128)} %param.9) | copy-start | bytes 28
  0.0 8.4 %copy-start.2 = (s32[32]{0:T(128)S(1)}, s32[32]{0:T(128)}, u32[]{:S(2)}) copy-start(s32[32]{0:T(128)} %param.11) | copy-start | bytes 388
  0.0 8.4 %copy-start.1 = (s32[2]{0:T(128)S(1)}, s32[2]{0:T(128)}, u32[]{:S(2)}) copy-start(s32[2]{0:T(128)} %layer_ids.1) | copy-start | bytes 28
  1.1 10.5 %collective-permute-start = (bf16[2,128,256]{2,1,0:T(8,128)(2,1)S(1)}, bf16[2,128,256]{2,1,0:T(8,128)(2,1)S(1)}, u32[]{:S(2)}, u32[]{:S(2)}) collective-permute-start(bf16[2,128,256]{2,1,0:T(8,128)(2,1)S(1)} %away_mask.1), channel_id=1, source_target_pairs={{0,8},{1,9},{2,10},{3,11},{4,12},{5,13},{6,14},{7,15},{8,0},{9,1},... | collective-permute-start | bytes 393224 | tf_op jit(solution)/shard_map/ppermute | solution.py:257
  5.4 6.9 %collective-permute-start.3 = (bf16[2,128,256]{2,1,0:T(8,128)(2,1)S(1)}, bf16[2,128,256]{2,1,0:T(8,128)(2,1)S(1)}, u32[]{:S(2)}, u32[]{:S(2)}) collective-permute-start(bf16[2,128,256]{2,1,0:T(8,128)(2,1)S(1)} %own.1.u0), channel_id=1, source_target_pairs={{0,4},{1,5},{2,7},{3,6},{4,0},{5,1},{6,3},{7,2},{8,12},{9,13},{10,... | collective-permute-start | bytes 393224 | tf_op jit(solution)/shard_map/ppermute | solution.py:257
  7.1 5.3 %collective-permute-start.2 = (bf16[2,128,256]{2,1,0:T(8,128)(2,1)S(1)}, bf16[2,128,256]{2,1,0:T(8,128)(2,1)S(1)}, u32[]{:S(2)}, u32[]{:S(2)}) collective-permute-start(bf16[2,128,256]{2,1,0:T(8,128)(2,1)S(1)} %own.1.u0), channel_id=1, source_target_pairs={{0,2},{1,3},{2,0},{3,1},{4,6},{5,7},{6,4},{7,5},{8,10},{9,11},{10,... | collective-permute-start | bytes 393224 | tf_op jit(solution)/shard_map/ppermute | solution.py:257
  7.7 4.6 %collective-permute-start.1 = (bf16[2,128,256]{2,1,0:T(8,128)(2,1)S(1)}, bf16[2,128,256]{2,1,0:T(8,128)(2,1)S(1)}, u32[]{:S(2)}, u32[]{:S(2)}) collective-permute-start(bf16[2,128,256]{2,1,0:T(8,128)(2,1)S(1)} %own.1.u0), channel_id=1, source_target_pairs={{0,1},{1,0},{2,3},{3,2},{4,5},{5,4},{6,7},{7,6},{8,9},{9,8},{10,11... | collective-permute-start | bytes 393224 | tf_op jit(solution)/shard_map/ppermute | solution.py:257
  11.7 5.5 %collective-permute-start.6 = (bf16[2,128,256]{2,1,0:T(8,128)(2,1)S(1)}, bf16[2,128,256]{2,1,0:T(8,128)(2,1)S(1)}, u32[]{:S(2)}, u32[]{:S(2)}) collective-permute-start(bf16[2,128,256]{2,1,0:T(8,128)(2,1)S(1)} %collective-permute-done.v), channel_id=1, source_target_pairs={{0,4},{1,5},{2,7},{3,6},{4,0},{5,1},{6,3},{7,2},{8,12},{9,13},{10,... | collective-permute-start | bytes 393224 | tf_op jit(solution)/shard_map/ppermute | solution.py:257
  12.4 5.8 %collective-permute-start.7 = (bf16[2,128,256]{2,1,0:T(8,128)(2,1)S(1)}, bf16[2,128,256]{2,1,0:T(8,128)(2,1)S(1)}, u32[]{:S(2)}, u32[]{:S(2)}) collective-permute-start(bf16[2,128,256]{2,1,0:T(8,128)(2,1)S(1)} %collective-permute-done.v), channel_id=1, source_target_pairs={{0,2},{1,3},{2,0},{3,1},{4,6},{5,7},{6,4},{7,5},{8,10},{9,11},{10,... | collective-permute-start | bytes 393224 | tf_op jit(solution)/shard_map/ppermute | solution.py:257
  15.4 1.3 %collective-permute-start.5 = (bf16[128,256]{1,0:T(8,128)(2,1)S(1)}, bf16[128,256]{1,0:T(8,128)(2,1)S(1)}, u32[]{:S(2)}, u32[]{:S(2)}) collective-permute-start(bf16[128,256]{1,0:T(8,128)(2,1)S(1)} %get-tuple-element.51), channel_id=1, source_target_pairs={{0,1},{1,0},{2,3},{3,2},{4,5},{5,4},{6,7},{7,6},{8,9},{9,8},{10,11... | collective-permute-start | bytes 196616 | tf_op jit(solution)/shard_map/ppermute | solution.py:257
  15.5 1.4 %collective-permute-start.4 = (bf16[128,256]{1,0:T(8,128)(2,1)S(1)}, bf16[128,256]{1,0:T(8,128)(2,1)S(1)}, u32[]{:S(2)}, u32[]{:S(2)}) collective-permute-start(bf16[128,256]{1,0:T(8,128)(2,1)S(1)} %get-tuple-element.52), channel_id=1, source_target_pairs={{0,1},{1,0},{2,3},{3,2},{4,5},{5,4},{6,7},{7,6},{8,9},{9,8},{10,11... | collective-permute-start | bytes 196616 | tf_op jit(solution)/shard_map/ppermute | solution.py:257
  18.8 3.6 %collective-permute-start.8 = (f32[4,32]{1,0:T(4,128)S(1)}, f32[4,32]{1,0:T(4,128)S(1)}, u32[]{:S(2)}, u32[]{:S(2)}) collective-permute-start(f32[4,32]{1,0:T(4,128)S(1)} %get-tuple-element.49), channel_id=1, source_target_pairs={{0,4},{1,5},{2,7},{3,6},{4,0},{5,1},{6,3},{7,2},{8,12},{9,13},{10,... | collective-permute-start | bytes 1544 | tf_op jit(solution)/shard_map/ppermute | solution.py:257
  19.9 3.6 %collective-permute-start.9 = (f32[4,32]{1,0:T(4,128)S(1)}, f32[4,32]{1,0:T(4,128)S(1)}, u32[]{:S(2)}, u32[]{:S(2)}) collective-permute-start(f32[4,32]{1,0:T(4,128)S(1)} %get-tuple-element.50), channel_id=1, source_target_pairs={{0,2},{1,3},{2,0},{3,1},{4,6},{5,7},{6,4},{7,5},{8,10},{9,11},{10,... | collective-permute-start | bytes 1544 | tf_op jit(solution)/shard_map/ppermute | solution.py:257
  23.5 4.5 %collective-permute-start.10 = (f32[2,32]{1,0:T(2,128)S(1)}, f32[2,32]{1,0:T(2,128)S(1)}, u32[]{:S(2)}, u32[]{:S(2)}) collective-permute-start(f32[2,32]{1,0:T(2,128)S(1)} %slice.15), channel_id=1, source_target_pairs={{0,8},{1,9},{2,10},{3,11},{4,12},{5,13},{6,14},{7,15},{8,0},{9,1},... | collective-permute-start | bytes 776 | tf_op jit(solution)/shard_map/ppermute | solution.py:257

commit v22 on v21

--- a/solution.py
+++ b/solution.py
@@ -145,7 +145,7 @@
             rest = rest - term.astype(jnp.float32)
 
 
-def early_kernel(seq_len, per, terms, u0, v, u3, u2, u1, white, mine, side):
+def early_kernel(seq_len, per, terms, u0, v, u1, u2, u3, white, mine, side):
     n = u0.shape[1]
     rows = []
     for w in range(2):
@@ -297,7 +297,7 @@
     )
     v, terms, pick = lax.optimization_barrier((v, terms, pick))
     v3 = send(v, ways[0])
-    v, near[2], near[1], near[0] = lax.optimization_barrier((v, near[2], near[1], near[0]))
+    v, near[0] = lax.optimization_barrier((v, near[0]))
     v2 = send(v, ways[1])
     whole = shape((2 * per, 8 * tokens), f32)
     sides = shape((4 * per, 6 * tokens), f32)
@@ -311,7 +311,7 @@
     white, mine, side = kernel(
         early_kernel,
         "early_pairs",
-        (terms, own, v, u3, u2, u1),
+        (terms, own, v, u1, u2, u3),
         (shape((2, 4 * tokens, rank), bf16), whole, sides),
     )
     v, white = lax.optimization_barrier((v, white))

time: 28.7 us -> 28.6 us (level)
  no operation moved by 1% of the time
where the time goes in v22:
time: 28.6 us; the launch traced here: 28.5 us
  starting transfers between devices  15.4 us (54%)
  waiting for transfers between devices  6.56 us (23%)
  Pallas kernels  5.82 us (20%)
  other arithmetic  0.57 us (2%)
    ppermute x11, starting transfers between devices, send(): return lax.ppermute(x, 'blk', [(d, to(d)) for d in range(size)])  15.4 us
    ppermute x11, waiting for transfers between devices, send(): return lax.ppermute(x, 'blk', [(d, to(d)) for d in range(size)])  6.56 us
    pallas_call x9, Pallas kernels, call(): pl.pallas_call(kernel, out_shape=out_shape, in_specs=specs + [vmem] * (le...  5.82 us
  transfers between devices with their start and end apart: 11, of which 7 were waited for; matrix products, arithmetic and copies ran while one was open for 0% of the time, Pallas kernels for 14%

profile of v22, /device:TPU:0, one launch (start us, length us, event | category | flops | bytes accessed | tf_op | source)
XLA Modules:
  0.0 28.5 jit_solution(9379314845916769682)
XLA Ops:
  0.0 1.0 %away.1.unit = bf16[2,128,256]{2,1,0:T(8,128)(2,1)S(1)} custom-call(bf16[2,128,256]{2,1,0:T(8,128)(2,1)} %acts.2, bf16[2,128,256]{2,1,0:T(8,128)(2,1)} %grads.2), custom_call_target="tpu_custom_call" | custom-call | flops 3000000000 | bytes 1000000 | tf_op jit(solution)/shard_map/away/pallas_call | solution.py:236
  1.0 0.2 away_mask.1
  1.1 4.1 %collective-permute-start = (bf16[2,128,256]{2,1,0:T(8,128)(2,1)S(1)}, bf16[2,128,256]{2,1,0:T(8,128)(2,1)S(1)}, u32[]{:S(2)}, u32[]{:S(2)}) collective-permute-start(bf16[2,128,256]{2,1,0:T(8,128)(2,1)S(1)} %away_mask.1), channel_id=1, source_target_pairs={{0,8},{1,9},{2,10},{3,11},{4,12},{5,13},{6,14},{7,15},{8,0},{9,1},... | collective-permute-start | bytes 393224 | tf_op jit(solution)/shard_map/ppermute | solution.py:257
  5.3 0.1 own.1.u0
  5.4 1.6 %collective-permute-start.1 = (bf16[2,128,256]{2,1,0:T(8,128)(2,1)S(1)}, bf16[2,128,256]{2,1,0:T(8,128)(2,1)S(1)}, u32[]{:S(2)}, u32[]{:S(2)}) collective-permute-start(bf16[2,128,256]{2,1,0:T(8,128)(2,1)S(1)} %own.1.u0), channel_id=1, source_target_pairs={{0,4},{1,5},{2,7},{3,6},{4,0},{5,1},{6,3},{7,2},{8,12},{9,13},{10,... | collective-permute-start | bytes 393224 | tf_op jit(solution)/shard_map/ppermute | solution.py:257
  7.1 0.7 %collective-permute-start.3 = (bf16[2,128,256]{2,1,0:T(8,128)(2,1)S(1)}, bf16[2,128,256]{2,1,0:T(8,128)(2,1)S(1)}, u32[]{:S(2)}, u32[]{:S(2)}) collective-permute-start(bf16[2,128,256]{2,1,0:T(8,128)(2,1)S(1)} %own.1.u0), channel_id=1, source_target_pairs={{0,2},{1,3},{2,0},{3,1},{4,6},{5,7},{6,4},{7,5},{8,10},{9,11},{10,... | collective-permute-start | bytes 393224 | tf_op jit(solution)/shard_map/ppermute | solution.py:257
  7.7 0.7 %collective-permute-start.2 = (bf16[2,128,256]{2,1,0:T(8,128)(2,1)S(1)}, bf16[2,128,256]{2,1,0:T(8,128)(2,1)S(1)}, u32[]{:S(2)}, u32[]{:S(2)}) collective-permute-start(bf16[2,128,256]{2,1,0:T(8,128)(2,1)S(1)} %own.1.u0), channel_id=1, source_target_pairs={{0,1},{1,0},{2,3},{3,2},{4,5},{5,4},{6,7},{7,6},{8,9},{9,8},{10,11... | collective-permute-start | bytes 393224 | tf_op jit(solution)/shard_map/ppermute | solution.py:257
  8.4 1.7 %factor_terms.1 = (bf16[2,3,256,256]{3,2,1,0:T(8,128)(2,1)S(1)}, bf16[1024,32]{1,0:T(8,128)(2,1)S(1)}) custom-call(s32[2]{0:T(128)S(1)} %copy-done.1, s32[1,32]{1,0:T(1,128)S(1)} %bitcast.8, f32[16,256,256]{2,1,0:T(8,128)} %act_f.1, f32[16,256,256]{2,1,0:T(8,128)} %grad_f.1), custom_call_target="tpu_custom_call" | custom-call | flops 1000000000 | bytes 1000000 | tf_op jit(solution)/shard_map/factor_terms/pallas_call | solution.py:236
  10.1 1.6 %collective-permute-done.v = bf16[2,128,256]{2,1,0:T(8,128)(2,1)S(1)} collective-permute-done((bf16[2,128,256]{2,1,0:T(8,128)(2,1)S(1)}, bf16[2,128,256]{2,1,0:T(8,128)(2,1)S(1)}, u32[]{:S(2)}, u32[]{:S(2)}) %collective-permute-start) | collective-permute-done | bytes 131104 | tf_op jit(solution)/shard_map/ppermute | solution.py:257
  11.7 0.6 %collective-permute-start.6 = (bf16[2,128,256]{2,1,0:T(8,128)(2,1)S(1)}, bf16[2,128,256]{2,1,0:T(8,128)(2,1)S(1)}, u32[]{:S(2)}, u32[]{:S(2)}) collective-permute-start(bf16[2,128,256]{2,1,0:T(8,128)(2,1)S(1)} %collective-permute-done.v), channel_id=1, source_target_pairs={{0,4},{1,5},{2,7},{3,6},{4,0},{5,1},{6,3},{7,2},{8,12},{9,13},{10,... | collective-permute-start | bytes 393224 | tf_op jit(solution)/shard_map/ppermute | solution.py:257
  12.3 0.0 collective-permute-done.1.u3
  12.3 2.0 %collective-permute-start.7 = (bf16[2,128,256]{2,1,0:T(8,128)(2,1)S(1)}, bf16[2,128,256]{2,1,0:T(8,128)(2,1)S(1)}, u32[]{:S(2)}, u32[]{:S(2)}) collective-permute-start(bf16[2,128,256]{2,1,0:T(8,128)(2,1)S(1)} %collective-permute-done.v), channel_id=1, source_target_pairs={{0,2},{1,3},{2,0},{3,1},{4,6},{5,7},{6,4},{7,5},{8,10},{9,11},{10,... | collective-permute-start | bytes 393224 | tf_op jit(solution)/shard_map/ppermute | solution.py:257
  14.4 0.0 collective-permute-done.3.u2
  14.4 0.0 collective-permute-done.2.u1
  14.4 1.0 %early_pairs.1 = (bf16[2,512,256]{2,1,0:T(8,128)(2,1)S(1)}, f32[4,1024]{1,0:T(4,128)S(1)}, f32[8,768]{1,0:T(8,128)S(1)}) custom-call(bf16[2,3,256,256]{3,2,1,0:T(8,128)(2,1)S(1)} %get-tuple-element.33.terms, bf16[2,128,256]{2,1,0:T(8,128)(2,1)S(1)} %own.1.u0, bf16[2,128,256]{2,1,0:T(8,128)(2,1)S(1)} %collective-permute-done.v, ...), custom_call_target="tpu_custom_call" | custom-call | flops 1000000000 | bytes 1000000 | tf_op jit(solution)/shard_map/early_pairs/pallas_call | solution.py:236
  15.4 0.1 collective-permute-start.5
  15.5 0.5 %collective-permute-start.4 = (bf16[128,256]{1,0:T(8,128)(2,1)S(1)}, bf16[128,256]{1,0:T(8,128)(2,1)S(1)}, u32[]{:S(2)}, u32[]{:S(2)}) collective-permute-start(bf16[128,256]{1,0:T(8,128)(2,1)S(1)} %get-tuple-element.48), channel_id=1, source_target_pairs={{0,1},{1,0},{2,3},{3,2},{4,5},{5,4},{6,7},{7,6},{8,9},{9,8},{10,11... | collective-permute-start | bytes 196616 | tf_op jit(solution)/shard_map/ppermute | solution.py:257
  16.0 0.7 %collective-permute-done.5.grads = bf16[128,256]{1,0:T(8,128)(2,1)S(1)} collective-permute-done((bf16[128,256]{1,0:T(8,128)(2,1)S(1)}, bf16[128,256]{1,0:T(8,128)(2,1)S(1)}, u32[]{:S(2)}, u32[]{:S(2)}) %collective-permute-start.5) | collective-permute-done | bytes 65568 | tf_op jit(solution)/shard_map/ppermute | solution.py:257
  16.7 0.2 collective-permute-done.4.acts
  16.9 0.3 %core_pairs.1 = (f32[4,1024]{1,0:T(4,128)S(1)}, f32[8,768]{1,0:T(8,128)S(1)}) custom-call(bf16[2,512,256]{2,1,0:T(8,128)(2,1)S(1)} %get-tuple-element.36.white, bf16[128,256]{1,0:T(8,128)(2,1)S(1)} %collective-permute-done.4.acts, bf16[128,256]{1,0:T(8,128)(2,1)S(1)} %collective-permute-done.5.grads, ...), custom_call_target="tpu_custom_call", output_to_operand_aliasing={{0}: (3, {}), {1}: (4, {})} | custom-call | flops 10000 | bytes 1000000 | tf_op jit(solution)/shard_map/core_pairs/pallas_call | solution.py:236
  17.2 0.0 collective-permute-done.6.v3
  17.2 0.5 %z_pairs.1 = (bf16[2,128,256]{2,1,0:T(8,128)(2,1)S(1)}, f32[8,768]{1,0:T(8,128)S(1)}) custom-call(bf16[2,3,256,256]{3,2,1,0:T(8,128)(2,1)S(1)} %get-tuple-element.33.terms, bf16[2,512,256]{2,1,0:T(8,128)(2,1)S(1)} %get-tuple-element.36.white, bf16[2,128,256]{2,1,0:T(8,128)(2,1)S(1)} %collective-permute-done.3.u2, ...), custom_call_target="tpu_custom_call", output_to_operand_aliasing={{1}: (7, {})} | custom-call | flops 10000 | bytes 1000000 | tf_op jit(solution)/shard_map/z_pairs/pallas_call | solution.py:236
  17.7 0.5 %collective-permute-done.7.v2 = bf16[2,128,256]{2,1,0:T(8,128)(2,1)S(1)} collective-permute-done((bf16[2,128,256]{2,1,0:T(8,128)(2,1)S(1)}, bf16[2,128,256]{2,1,0:T(8,128)(2,1)S(1)}, u32[]{:S(2)}, u32[]{:S(2)}) %collective-permute-start.7) | collective-permute-done | bytes 131104 | tf_op jit(solution)/shard_map/ppermute | solution.py:257
  18.1 0.7 %return_rows.1 = (f32[4,32]{1,0:T(4,128)S(1)}, f32[4,32]{1,0:T(4,128)S(1)}) custom-call(bf16[2,3,256,256]{3,2,1,0:T(8,128)(2,1)S(1)} %get-tuple-element.33.terms, bf16[2,512,256]{2,1,0:T(8,128)(2,1)S(1)} %get-tuple-element.36.white, bf16[2,128,256]{2,1,0:T(8,128)(2,1)S(1)} %get-tuple-element.43.white3, bf16[1024,32]{1,0:T(8,128)(2,1)S(1)} %get-tuple-element.37.pick, ...), custom_call_target="tpu_custom_call" | custom-call | flops 1000000000 | bytes 1000000 | tf_op jit(solution)/shard_map/return_rows/pallas_call | solution.py:236
  18.8 1.0 %collective-permute-start.8 = (f32[4,32]{1,0:T(4,128)S(1)}, f32[4,32]{1,0:T(4,128)S(1)}, u32[]{:S(2)}, u32[]{:S(2)}) collective-permute-start(f32[4,32]{1,0:T(4,128)S(1)} %get-tuple-element.45), channel_id=1, source_target_pairs={{0,4},{1,5},{2,7},{3,6},{4,0},{5,1},{6,3},{7,2},{8,12},{9,13},{10,... | collective-permute-start | bytes 1544 | tf_op jit(solution)/shard_map/ppermute | solution.py:257
  19.8 1.5 %collective-permute-start.9 = (f32[4,32]{1,0:T(4,128)S(1)}, f32[4,32]{1,0:T(4,128)S(1)}, u32[]{:S(2)}, u32[]{:S(2)}) collective-permute-start(f32[4,32]{1,0:T(4,128)S(1)} %get-tuple-element.46), channel_id=1, source_target_pairs={{0,2},{1,3},{2,0},{3,1},{4,6},{5,7},{6,4},{7,5},{8,10},{9,11},{10,... | collective-permute-start | bytes 1544 | tf_op jit(solution)/shard_map/ppermute | solution.py:257
  21.3 0.4 %own_rows.1 = f32[4,32]{1,0:T(4,128)S(1)} custom-call(bf16[2,512,256]{2,1,0:T(8,128)(2,1)S(1)} %get-tuple-element.36.white, bf16[1024,32]{1,0:T(8,128)(2,1)S(1)} %get-tuple-element.37.pick, f32[4,1024]{1,0:T(4,128)S(1)} %get-tuple-element.41.mine, bf16[2,128,256]{2,1,0:T(8,128)(2,1)S(1)} %collective-permute-done.6.v3, ...), custom_call_target="tpu_custom_call" | custom-call | flops 1000000000 | bytes 1000000 | tf_op jit(solution)/shard_map/own_rows/pallas_call | solution.py:236
  21.7 0.8 %collective-permute-done.8 = f32[4,32]{1,0:T(4,128)S(1)} collective-permute-done((f32[4,32]{1,0:T(4,128)S(1)}, f32[4,32]{1,0:T(4,128)S(1)}, u32[]{:S(2)}, u32[]{:S(2)}) %collective-permute-start.8) | collective-permute-done | bytes 544 | tf_op jit(solution)/shard_map/ppermute | solution.py:257
  22.5 0.9 %collective-permute-done.9 = f32[4,32]{1,0:T(4,128)S(1)} collective-permute-done((f32[4,32]{1,0:T(4,128)S(1)}, f32[4,32]{1,0:T(4,128)S(1)}, u32[]{:S(2)}, u32[]{:S(2)}) %collective-permute-start.9) | collective-permute-done | bytes 544 | tf_op jit(solution)/shard_map/ppermute | solution.py:257
  23.4 2.6 %collective-permute-start.10 = (f32[2,32]{1,0:T(2,128)S(1)}, f32[2,32]{1,0:T(2,128)S(1)}, u32[]{:S(2)}, u32[]{:S(2)}) collective-permute-start(f32[2,32]{1,0:T(2,128)S(1)} %slice.15), channel_id=1, source_target_pairs={{0,8},{1,9},{2,10},{3,11},{4,12},{5,13},{6,14},{7,15},{8,0},{9,1},... | collective-permute-start | bytes 776 | tf_op jit(solution)/shard_map/ppermute | solution.py:257
  26.0 1.9 %collective-permute-done.10 = f32[2,32]{1,0:T(2,128)S(1)} collective-permute-done((f32[2,32]{1,0:T(2,128)S(1)}, f32[2,32]{1,0:T(2,128)S(1)}, u32[]{:S(2)}, u32[]{:S(2)}) %collective-permute-start.10) | collective-permute-done | bytes 288 | tf_op jit(solution)/shard_map/ppermute | solution.py:257
  27.9 0.6 %slice_add_fusion = f32[2,32]{1,0:T(2,128)} fusion(f32[2,32]{1,0:T(2,128)S(1)} %collective-permute-done.10, f32[4,32]{1,0:T(4,128)S(1)} %add_add_fusion), kind=kLoop, calls=%fused_computation.3 | loop fusion | flops 64 | bytes 768 | tf_op jit(solution)/shard_map/add | solution.py:343
  (13 shorter events, 0.0 us)
Async XLA Ops:
  0.0 5.3 %copy-start.4 = (bf16[2,128,256]{2,1,0:T(8,128)(2,1)S(1)}, bf16[2,128,256]{2,1,0:T(8,128)(2,1)}, u32[]{:S(2)}) copy-start(bf16[2,128,256]{2,1,0:T(8,128)(2,1)} %grads.2) | copy-start | bytes 393220
  0.0 5.3 %copy-start.3 = (bf16[2,128,256]{2,1,0:T(8,128)(2,1)S(1)}, bf16[2,128,256]{2,1,0:T(8,128)(2,1)}, u32[]{:S(2)}) copy-start(bf16[2,128,256]{2,1,0:T(8,128)(2,1)} %acts.2) | copy-start | bytes 393220
  0.0 1.0 %copy-start = (s32[2]{0:T(128)S(1)}, s32[2]{0:T(128)}, u32[]{:S(2)}) copy-start(s32[2]{0:T(128)} %param.9) | copy-start | bytes 28
  0.0 8.4 %copy-start.2 = (s32[32]{0:T(128)S(1)}, s32[32]{0:T(128)}, u32[]{:S(2)}) copy-start(s32[32]{0:T(128)} %param.11) | copy-start | bytes 388
  0.0 8.4 %copy-start.1 = (s32[2]{0:T(128)S(1)}, s32[2]{0:T(128)}, u32[]{:S(2)}) copy-start(s32[2]{0:T(128)} %layer_ids.1) | copy-start | bytes 28
  1.1 10.5 %collective-permute-start = (bf16[2,128,256]{2,1,0:T(8,128)(2,1)S(1)}, bf16[2,128,256]{2,1,0:T(8,128)(2,1)S(1)}, u32[]{:S(2)}, u32[]{:S(2)}) collective-permute-start(bf16[2,128,256]{2,1,0:T(8,128)(2,1)S(1)} %away_mask.1), channel_id=1, source_target_pairs={{0,8},{1,9},{2,10},{3,11},{4,12},{5,13},{6,14},{7,15},{8,0},{9,1},... | collective-permute-start | bytes 393224 | tf_op jit(solution)/shard_map/ppermute | solution.py:257
  5.4 6.9 %collective-permute-start.1 = (bf16[2,128,256]{2,1,0:T(8,128)(2,1)S(1)}, bf16[2,128,256]{2,1,0:T(8,128)(2,1)S(1)}, u32[]{:S(2)}, u32[]{:S(2)}) collective-permute-start(bf16[2,128,256]{2,1,0:T(8,128)(2,1)S(1)} %own.1.u0), channel_id=1, source_target_pairs={{0,4},{1,5},{2,7},{3,6},{4,0},{5,1},{6,3},{7,2},{8,12},{9,13},{10,... | collective-permute-start | bytes 393224 | tf_op jit(solution)/shard_map/ppermute | solution.py:257
  7.1 7.3 %collective-permute-start.3 = (bf16[2,128,256]{2,1,0:T(8,128)(2,1)S(1)}, bf16[2,128,256]{2,1,0:T(8,128)(2,1)S(1)}, u32[]{:S(2)}, u32[]{:S(2)}) collective-permute-start(bf16[2,128,256]{2,1,0:T(8,128)(2,1)S(1)} %own.1.u0), channel_id=1, source_target_pairs={{0,2},{1,3},{2,0},{3,1},{4,6},{5,7},{6,4},{7,5},{8,10},{9,11},{10,... | collective-permute-start | bytes 393224 | tf_op jit(solution)/shard_map/ppermute | solution.py:257
  7.7 6.6 %collective-permute-start.2 = (bf16[2,128,256]{2,1,0:T(8,128)(2,1)S(1)}, bf16[2,128,256]{2,1,0:T(8,128)(2,1)S(1)}, u32[]{:S(2)}, u32[]{:S(2)}) collective-permute-start(bf16[2,128,256]{2,1,0:T(8,128)(2,1)S(1)} %own.1.u0), channel_id=1, source_target_pairs={{0,1},{1,0},{2,3},{3,2},{4,5},{5,4},{6,7},{7,6},{8,9},{9,8},{10,11... | collective-permute-start | bytes 393224 | tf_op jit(solution)/shard_map/ppermute | solution.py:257
  11.7 5.5 %collective-permute-start.6 = (bf16[2,128,256]{2,1,0:T(8,128)(2,1)S(1)}, bf16[2,128,256]{2,1,0:T(8,128)(2,1)S(1)}, u32[]{:S(2)}, u32[]{:S(2)}) collective-permute-start(bf16[2,128,256]{2,1,0:T(8,128)(2,1)S(1)} %collective-permute-done.v), channel_id=1, source_target_pairs={{0,4},{1,5},{2,7},{3,6},{4,0},{5,1},{6,3},{7,2},{8,12},{9,13},{10,... | collective-permute-start | bytes 393224 | tf_op jit(solution)/shard_map/ppermute | solution.py:257
  12.3 5.8 %collective-permute-start.7 = (bf16[2,128,256]{2,1,0:T(8,128)(2,1)S(1)}, bf16[2,128,256]{2,1,0:T(8,128)(2,1)S(1)}, u32[]{:S(2)}, u32[]{:S(2)}) collective-permute-start(bf16[2,128,256]{2,1,0:T(8,128)(2,1)S(1)} %collective-permute-done.v), channel_id=1, source_target_pairs={{0,2},{1,3},{2,0},{3,1},{4,6},{5,7},{6,4},{7,5},{8,10},{9,11},{10,... | collective-permute-start | bytes 393224 | tf_op jit(solution)/shard_map/ppermute | solution.py:257
  15.4 1.3 %collective-permute-start.5 = (bf16[128,256]{1,0:T(8,128)(2,1)S(1)}, bf16[128,256]{1,0:T(8,128)(2,1)S(1)}, u32[]{:S(2)}, u32[]{:S(2)}) collective-permute-start(bf16[128,256]{1,0:T(8,128)(2,1)S(1)} %get-tuple-element.47), channel_id=1, source_target_pairs={{0,1},{1,0},{2,3},{3,2},{4,5},{5,4},{6,7},{7,6},{8,9},{9,8},{10,11... | collective-permute-start | bytes 196616 | tf_op jit(solution)/shard_map/ppermute | solution.py:257
  15.5 1.4 %collective-permute-start.4 = (bf16[128,256]{1,0:T(8,128)(2,1)S(1)}, bf16[128,256]{1,0:T(8,128)(2,1)S(1)}, u32[]{:S(2)}, u32[]{:S(2)}) collective-permute-start(bf16[128,256]{1,0:T(8,128)(2,1)S(1)} %get-tuple-element.48), channel_id=1, source_target_pairs={{0,1},{1,0},{2,3},{3,2},{4,5},{5,4},{6,7},{7,6},{8,9},{9,8},{10,11... | collective-permute-start | bytes 196616 | tf_op jit(solution)/shard_map/ppermute | solution.py:257
  18.8 3.6 %collective-permute-start.8 = (f32[4,32]{1,0:T(4,128)S(1)}, f32[4,32]{1,0:T(4,128)S(1)}, u32[]{:S(2)}, u32[]{:S(2)}) collective-permute-start(f32[4,32]{1,0:T(4,128)S(1)} %get-tuple-element.45), channel_id=1, source_target_pairs={{0,4},{1,5},{2,7},{3,6},{4,0},{5,1},{6,3},{7,2},{8,12},{9,13},{10,... | collective-permute-start | bytes 1544 | tf_op jit(solution)/shard_map/ppermute | solution.py:257
  19.8 3.6 %collective-permute-start.9 = (f32[4,32]{1,0:T(4,128)S(1)}, f32[4,32]{1,0:T(4,128)S(1)}, u32[]{:S(2)}, u32[]{:S(2)}) collective-permute-start(f32[4,32]{1,0:T(4,128)S(1)} %get-tuple-element.46), channel_id=1, source_target_pairs={{0,2},{1,3},{2,0},{3,1},{4,6},{5,7},{6,4},{7,5},{8,10},{9,11},{10,... | collective-permute-start | bytes 1544 | tf_op jit(solution)/shard_map/ppermute | solution.py:257
  23.4 4.5 %collective-permute-start.10 = (f32[2,32]{1,0:T(2,128)S(1)}, f32[2,32]{1,0:T(2,128)S(1)}, u32[]{:S(2)}, u32[]{:S(2)}) collective-permute-start(f32[2,32]{1,0:T(2,128)S(1)} %slice.15), channel_id=1, source_target_pairs={{0,8},{1,9},{2,10},{3,11},{4,12},{5,13},{6,14},{7,15},{8,0},{9,1},... | collective-permute-start | bytes 776 | tf_op jit(solution)/shard_map/ppermute | solution.py:257

commit v23 on v22

--- a/solution.py
+++ b/solution.py
@@ -297,7 +297,7 @@
     )
     v, terms, pick = lax.optimization_barrier((v, terms, pick))
     v3 = send(v, ways[0])
-    v, near[0] = lax.optimization_barrier((v, near[0]))
+    v, near[2] = lax.optimization_barrier((v, near[2]))
     v2 = send(v, ways[1])
     whole = shape((2 * per, 8 * tokens), f32)
     sides = shape((4 * per, 6 * tokens), f32)

time: 28.6 us -> 28.6 us (level)
  starting transfers between devices: 15.4 us -> 14.7 us
  waiting for transfers between devices: 6.56 us -> 7.26 us
    ppermute x11, waiting for transfers between devices: 6.56 us -> 7.26 us  [send(): return lax.ppermute(x, 'blk', [(d, to(d)) for d in range(size)])]
    ppermute x11, starting transfers between devices: 15.4 us -> 14.7 us  [send(): return lax.ppermute(x, 'blk', [(d, to(d)) for d in range(size)])]
  transfers between devices with their start and end apart: 11 -> 11, of which waited for: 7 -> 8; matrix products, arithmetic and copies ran while one was open for 0% -> 0% of each run, Pallas kernels for 14% -> 14%
where the time goes in v23:
time: 28.6 us; the launch traced here: 28.5 us
  starting transfers between devices  14.7 us (51%)
  waiting for transfers between devices  7.26 us (25%)
  Pallas kernels  5.81 us (20%)
  other arithmetic  0.57 us (2%)
    ppermute x11, starting transfers between devices, send(): return lax.ppermute(x, 'blk', [(d, to(d)) for d in range(size)])  14.7 us
    ppermute x11, waiting for transfers between devices, send(): return lax.ppermute(x, 'blk', [(d, to(d)) for d in range(size)])  7.26 us
    pallas_call x9, Pallas kernels, call(): pl.pallas_call(kernel, out_shape=out_shape, in_specs=specs + [vmem] * (le...  5.81 us
  transfers between devices with their start and end apart: 11, of which 8 were waited for; matrix products, arithmetic and copies ran while one was open for 0% of the time, Pallas kernels for 14%

profile of v23, /device:TPU:0, one launch (start us, length us, event | category | flops | bytes accessed | tf_op | source)
XLA Modules:
  0.0 28.5 jit_solution(11406588605809392271)
XLA Ops:
  0.0 1.0 %away.1.unit = bf16[2,128,256]{2,1,0:T(8,128)(2,1)S(1)} custom-call(bf16[2,128,256]{2,1,0:T(8,128)(2,1)} %acts.2, bf16[2,128,256]{2,1,0:T(8,128)(2,1)} %grads.2), custom_call_target="tpu_custom_call" | custom-call | flops 3000000000 | bytes 1000000 | tf_op jit(solution)/shard_map/away/pallas_call | solution.py:236
  1.0 0.2 away_mask.1
  1.1 4.1 %collective-permute-start = (bf16[2,128,256]{2,1,0:T(8,128)(2,1)S(1)}, bf16[2,128,256]{2,1,0:T(8,128)(2,1)S(1)}, u32[]{:S(2)}, u32[]{:S(2)}) collective-permute-start(bf16[2,128,256]{2,1,0:T(8,128)(2,1)S(1)} %away_mask.1), channel_id=1, source_target_pairs={{0,8},{1,9},{2,10},{3,11},{4,12},{5,13},{6,14},{7,15},{8,0},{9,1},... | collective-permute-start | bytes 393224 | tf_op jit(solution)/shard_map/ppermute | solution.py:257
  5.3 0.1 own.1.u0
  5.4 0.1 collective-permute-start.1
  5.5 1.6 %collective-permute-start.3 = (bf16[2,128,256]{2,1,0:T(8,128)(2,1)S(1)}, bf16[2,128,256]{2,1,0:T(8,128)(2,1)S(1)}, u32[]{:S(2)}, u32[]{:S(2)}) collective-permute-start(bf16[2,128,256]{2,1,0:T(8,128)(2,1)S(1)} %own.1.u0), channel_id=1, source_target_pairs={{0,4},{1,5},{2,7},{3,6},{4,0},{5,1},{6,3},{7,2},{8,12},{9,13},{10,... | collective-permute-start | bytes 393224 | tf_op jit(solution)/shard_map/ppermute | solution.py:257
  7.2 1.5 %collective-permute-start.2 = (bf16[2,128,256]{2,1,0:T(8,128)(2,1)S(1)}, bf16[2,128,256]{2,1,0:T(8,128)(2,1)S(1)}, u32[]{:S(2)}, u32[]{:S(2)}) collective-permute-start(bf16[2,128,256]{2,1,0:T(8,128)(2,1)S(1)} %own.1.u0), channel_id=1, source_target_pairs={{0,2},{1,3},{2,0},{3,1},{4,6},{5,7},{6,4},{7,5},{8,10},{9,11},{10,... | collective-permute-start | bytes 393224 | tf_op jit(solution)/shard_map/ppermute | solution.py:257
  8.7 1.7 %factor_terms.1 = (bf16[2,3,256,256]{3,2,1,0:T(8,128)(2,1)S(1)}, bf16[1024,32]{1,0:T(8,128)(2,1)S(1)}) custom-call(s32[2]{0:T(128)S(1)} %copy-done.1, s32[1,32]{1,0:T(1,128)S(1)} %bitcast.8, f32[16,256,256]{2,1,0:T(8,128)} %act_f.1, f32[16,256,256]{2,1,0:T(8,128)} %grad_f.1), custom_call_target="tpu_custom_call" | custom-call | flops 1000000000 | bytes 1000000 | tf_op jit(solution)/shard_map/factor_terms/pallas_call | solution.py:236
  10.4 1.3 %collective-permute-done.v = bf16[2,128,256]{2,1,0:T(8,128)(2,1)S(1)} collective-permute-done((bf16[2,128,256]{2,1,0:T(8,128)(2,1)S(1)}, bf16[2,128,256]{2,1,0:T(8,128)(2,1)S(1)}, u32[]{:S(2)}, u32[]{:S(2)}) %collective-permute-start) | collective-permute-done | bytes 131104 | tf_op jit(solution)/shard_map/ppermute | solution.py:257
  11.7 0.7 %collective-permute-start.6 = (bf16[2,128,256]{2,1,0:T(8,128)(2,1)S(1)}, bf16[2,128,256]{2,1,0:T(8,128)(2,1)S(1)}, u32[]{:S(2)}, u32[]{:S(2)}) collective-permute-start(bf16[2,128,256]{2,1,0:T(8,128)(2,1)S(1)} %collective-permute-done.v), channel_id=1, source_target_pairs={{0,4},{1,5},{2,7},{3,6},{4,0},{5,1},{6,3},{7,2},{8,12},{9,13},{10,... | collective-permute-start | bytes 393224 | tf_op jit(solution)/shard_map/ppermute | solution.py:257
  12.4 0.0 collective-permute-done.1.u1
  12.4 1.1 %collective-permute-start.7 = (bf16[2,128,256]{2,1,0:T(8,128)(2,1)S(1)}, bf16[2,128,256]{2,1,0:T(8,128)(2,1)S(1)}, u32[]{:S(2)}, u32[]{:S(2)}) collective-permute-start(bf16[2,128,256]{2,1,0:T(8,128)(2,1)S(1)} %collective-permute-done.v), channel_id=1, source_target_pairs={{0,2},{1,3},{2,0},{3,1},{4,6},{5,7},{6,4},{7,5},{8,10},{9,11},{10,... | collective-permute-start | bytes 393224 | tf_op jit(solution)/shard_map/ppermute | solution.py:257
  13.5 0.0 collective-permute-done.3.u3
  13.5 0.0 collective-permute-done.2.u2
  13.5 1.0 %early_pairs.1 = (bf16[2,512,256]{2,1,0:T(8,128)(2,1)S(1)}, f32[4,1024]{1,0:T(4,128)S(1)}, f32[8,768]{1,0:T(8,128)S(1)}) custom-call(bf16[2,3,256,256]{3,2,1,0:T(8,128)(2,1)S(1)} %get-tuple-element.33.terms, bf16[2,128,256]{2,1,0:T(8,128)(2,1)S(1)} %own.1.u0, bf16[2,128,256]{2,1,0:T(8,128)(2,1)S(1)} %collective-permute-done.v, ...), custom_call_target="tpu_custom_call" | custom-call | flops 1000000000 | bytes 1000000 | tf_op jit(solution)/shard_map/early_pairs/pallas_call | solution.py:236
  14.5 0.3 collective-permute-start.5
  14.8 0.3 %collective-permute-start.4 = (bf16[128,256]{1,0:T(8,128)(2,1)S(1)}, bf16[128,256]{1,0:T(8,128)(2,1)S(1)}, u32[]{:S(2)}, u32[]{:S(2)}) collective-permute-start(bf16[128,256]{1,0:T(8,128)(2,1)S(1)} %get-tuple-element.48), channel_id=1, source_target_pairs={{0,1},{1,0},{2,3},{3,2},{4,5},{5,4},{6,7},{7,6},{8,9},{9,8},{10,11... | collective-permute-start | bytes 196616 | tf_op jit(solution)/shard_map/ppermute | solution.py:257
  15.1 0.7 %collective-permute-done.5.grads = bf16[128,256]{1,0:T(8,128)(2,1)S(1)} collective-permute-done((bf16[128,256]{1,0:T(8,128)(2,1)S(1)}, bf16[128,256]{1,0:T(8,128)(2,1)S(1)}, u32[]{:S(2)}, u32[]{:S(2)}) %collective-permute-start.5) | collective-permute-done | bytes 65568 | tf_op jit(solution)/shard_map/ppermute | solution.py:257
  15.8 0.2 collective-permute-done.4.acts
  16.0 0.3 %core_pairs.1 = (f32[4,1024]{1,0:T(4,128)S(1)}, f32[8,768]{1,0:T(8,128)S(1)}) custom-call(bf16[2,512,256]{2,1,0:T(8,128)(2,1)S(1)} %get-tuple-element.36.white, bf16[128,256]{1,0:T(8,128)(2,1)S(1)} %collective-permute-done.4.acts, bf16[128,256]{1,0:T(8,128)(2,1)S(1)} %collective-permute-done.5.grads, ...), custom_call_target="tpu_custom_call", output_to_operand_aliasing={{0}: (3, {}), {1}: (4, {})} | custom-call | flops 10000 | bytes 1000000 | tf_op jit(solution)/shard_map/core_pairs/pallas_call | solution.py:236
  16.3 0.3 %collective-permute-done.6.v3 = bf16[2,128,256]{2,1,0:T(8,128)(2,1)S(1)} collective-permute-done((bf16[2,128,256]{2,1,0:T(8,128)(2,1)S(1)}, bf16[2,128,256]{2,1,0:T(8,128)(2,1)S(1)}, u32[]{:S(2)}, u32[]{:S(2)}) %collective-permute-start.6) | collective-permute-done | bytes 131104 | tf_op jit(solution)/shard_map/ppermute | solution.py:257
  16.7 0.5 %z_pairs.1 = (bf16[2,128,256]{2,1,0:T(8,128)(2,1)S(1)}, f32[8,768]{1,0:T(8,128)S(1)}) custom-call(bf16[2,3,256,256]{3,2,1,0:T(8,128)(2,1)S(1)} %get-tuple-element.33.terms, bf16[2,512,256]{2,1,0:T(8,128)(2,1)S(1)} %get-tuple-element.36.white, bf16[2,128,256]{2,1,0:T(8,128)(2,1)S(1)} %collective-permute-done.2.u2, ...), custom_call_target="tpu_custom_call", output_to_operand_aliasing={{1}: (7, {})} | custom-call | flops 10000 | bytes 1000000 | tf_op jit(solution)/shard_map/z_pairs/pallas_call | solution.py:236
  17.2 0.5 %collective-permute-done.7.v2 = bf16[2,128,256]{2,1,0:T(8,128)(2,1)S(1)} collective-permute-done((bf16[2,128,256]{2,1,0:T(8,128)(2,1)S(1)}, bf16[2,128,256]{2,1,0:T(8,128)(2,1)S(1)}, u32[]{:S(2)}, u32[]{:S(2)}) %collective-permute-start.7) | collective-permute-done | bytes 131104 | tf_op jit(solution)/shard_map/ppermute | solution.py:257
  17.6 0.7 %return_rows.1 = (f32[4,32]{1,0:T(4,128)S(1)}, f32[4,32]{1,0:T(4,128)S(1)}) custom-call(bf16[2,3,256,256]{3,2,1,0:T(8,128)(2,1)S(1)} %get-tuple-element.33.terms, bf16[2,512,256]{2,1,0:T(8,128)(2,1)S(1)} %get-tuple-element.36.white, bf16[2,128,256]{2,1,0:T(8,128)(2,1)S(1)} %get-tuple-element.43.white3, bf16[1024,32]{1,0:T(8,128)(2,1)S(1)} %get-tuple-element.37.pick, ...), custom_call_target="tpu_custom_call" | custom-call | flops 1000000000 | bytes 1000000 | tf_op jit(solution)/shard_map/return_rows/pallas_call | solution.py:236
  18.3 1.5 %collective-permute-start.8 = (f32[4,32]{1,0:T(4,128)S(1)}, f32[4,32]{1,0:T(4,128)S(1)}, u32[]{:S(2)}, u32[]{:S(2)}) collective-permute-start(f32[4,32]{1,0:T(4,128)S(1)} %get-tuple-element.45), channel_id=1, source_target_pairs={{0,4},{1,5},{2,7},{3,6},{4,0},{5,1},{6,3},{7,2},{8,12},{9,13},{10,... | collective-permute-start | bytes 1544 | tf_op jit(solution)/shard_map/ppermute | solution.py:257
  19.8 0.8 %collective-permute-start.9 = (f32[4,32]{1,0:T(4,128)S(1)}, f32[4,32]{1,0:T(4,128)S(1)}, u32[]{:S(2)}, u32[]{:S(2)}) collective-permute-start(f32[4,32]{1,0:T(4,128)S(1)} %get-tuple-element.46), channel_id=1, source_target_pairs={{0,2},{1,3},{2,0},{3,1},{4,6},{5,7},{6,4},{7,5},{8,10},{9,11},{10,... | collective-permute-start | bytes 1544 | tf_op jit(solution)/shard_map/ppermute | solution.py:257
  20.6 0.4 %own_rows.1 = f32[4,32]{1,0:T(4,128)S(1)} custom-call(bf16[2,512,256]{2,1,0:T(8,128)(2,1)S(1)} %get-tuple-element.36.white, bf16[1024,32]{1,0:T(8,128)(2,1)S(1)} %get-tuple-element.37.pick, f32[4,1024]{1,0:T(4,128)S(1)} %get-tuple-element.41.mine, bf16[2,128,256]{2,1,0:T(8,128)(2,1)S(1)} %collective-permute-done.6.v3, ...), custom_call_target="tpu_custom_call" | custom-call | flops 1000000000 | bytes 1000000 | tf_op jit(solution)/shard_map/own_rows/pallas_call | solution.py:236
  21.0 0.9 %collective-permute-done.8 = f32[4,32]{1,0:T(4,128)S(1)} collective-permute-done((f32[4,32]{1,0:T(4,128)S(1)}, f32[4,32]{1,0:T(4,128)S(1)}, u32[]{:S(2)}, u32[]{:S(2)}) %collective-permute-start.8) | collective-permute-done | bytes 544 | tf_op jit(solution)/shard_map/ppermute | solution.py:257
  22.0 1.4 %collective-permute-done.9 = f32[4,32]{1,0:T(4,128)S(1)} collective-permute-done((f32[4,32]{1,0:T(4,128)S(1)}, f32[4,32]{1,0:T(4,128)S(1)}, u32[]{:S(2)}, u32[]{:S(2)}) %collective-permute-start.9) | collective-permute-done | bytes 544 | tf_op jit(solution)/shard_map/ppermute | solution.py:257
  23.4 2.7 %collective-permute-start.10 = (f32[2,32]{1,0:T(2,128)S(1)}, f32[2,32]{1,0:T(2,128)S(1)}, u32[]{:S(2)}, u32[]{:S(2)}) collective-permute-start(f32[2,32]{1,0:T(2,128)S(1)} %slice.15), channel_id=1, source_target_pairs={{0,8},{1,9},{2,10},{3,11},{4,12},{5,13},{6,14},{7,15},{8,0},{9,1},... | collective-permute-start | bytes 776 | tf_op jit(solution)/shard_map/ppermute | solution.py:257
  26.1 1.9 %collective-permute-done.10 = f32[2,32]{1,0:T(2,128)S(1)} collective-permute-done((f32[2,32]{1,0:T(2,128)S(1)}, f32[2,32]{1,0:T(2,128)S(1)}, u32[]{:S(2)}, u32[]{:S(2)}) %collective-permute-start.10) | collective-permute-done | bytes 288 | tf_op jit(solution)/shard_map/ppermute | solution.py:257
  27.9 0.6 %slice_add_fusion = f32[2,32]{1,0:T(2,128)} fusion(f32[2,32]{1,0:T(2,128)S(1)} %collective-permute-done.10, f32[4,32]{1,0:T(4,128)S(1)} %add_add_fusion), kind=kLoop, calls=%fused_computation.3 | loop fusion | flops 64 | bytes 768 | tf_op jit(solution)/shard_map/add | solution.py:343
  (13 shorter events, 0.0 us)
Async XLA Ops:
  0.0 5.3 %copy-start.4 = (bf16[2,128,256]{2,1,0:T(8,128)(2,1)S(1)}, bf16[2,128,256]{2,1,0:T(8,128)(2,1)}, u32[]{:S(2)}) copy-start(bf16[2,128,256]{2,1,0:T(8,128)(2,1)} %grads.2) | copy-start | bytes 393220
  0.0 5.3 %copy-start.3 = (bf16[2,128,256]{2,1,0:T(8,128)(2,1)S(1)}, bf16[2,128,256]{2,1,0:T(8,128)(2,1)}, u32[]{:S(2)}) copy-start(bf16[2,128,256]{2,1,0:T(8,128)(2,1)} %acts.2) | copy-start | bytes 393220
  0.0 1.0 %copy-start = (s32[2]{0:T(128)S(1)}, s32[2]{0:T(128)}, u32[]{:S(2)}) copy-start(s32[2]{0:T(128)} %param.9) | copy-start | bytes 28
  0.0 8.7 %copy-start.2 = (s32[32]{0:T(128)S(1)}, s32[32]{0:T(128)}, u32[]{:S(2)}) copy-start(s32[32]{0:T(128)} %param.11) | copy-start | bytes 388
  0.0 8.7 %copy-start.1 = (s32[2]{0:T(128)S(1)}, s32[2]{0:T(128)}, u32[]{:S(2)}) copy-start(s32[2]{0:T(128)} %layer_ids.1) | copy-start | bytes 28
  1.1 10.5 %collective-permute-start = (bf16[2,128,256]{2,1,0:T(8,128)(2,1)S(1)}, bf16[2,128,256]{2,1,0:T(8,128)(2,1)S(1)}, u32[]{:S(2)}, u32[]{:S(2)}) collective-permute-start(bf16[2,128,256]{2,1,0:T(8,128)(2,1)S(1)} %away_mask.1), channel_id=1, source_target_pairs={{0,8},{1,9},{2,10},{3,11},{4,12},{5,13},{6,14},{7,15},{8,0},{9,1},... | collective-permute-start | bytes 393224 | tf_op jit(solution)/shard_map/ppermute | solution.py:257
  5.4 6.9 %collective-permute-start.1 = (bf16[2,128,256]{2,1,0:T(8,128)(2,1)S(1)}, bf16[2,128,256]{2,1,0:T(8,128)(2,1)S(1)}, u32[]{:S(2)}, u32[]{:S(2)}) collective-permute-start(bf16[2,128,256]{2,1,0:T(8,128)(2,1)S(1)} %own.1.u0), channel_id=1, source_target_pairs={{0,1},{1,0},{2,3},{3,2},{4,5},{5,4},{6,7},{7,6},{8,9},{9,8},{10,11... | collective-permute-start | bytes 393224 | tf_op jit(solution)/shard_map/ppermute | solution.py:257
  5.5 8.0 %collective-permute-start.3 = (bf16[2,128,256]{2,1,0:T(8,128)(2,1)S(1)}, bf16[2,128,256]{2,1,0:T(8,128)(2,1)S(1)}, u32[]{:S(2)}, u32[]{:S(2)}) collective-permute-start(bf16[2,128,256]{2,1,0:T(8,128)(2,1)S(1)} %own.1.u0), channel_id=1, source_target_pairs={{0,4},{1,5},{2,7},{3,6},{4,0},{5,1},{6,3},{7,2},{8,12},{9,13},{10,... | collective-permute-start | bytes 393224 | tf_op jit(solution)/shard_map/ppermute | solution.py:257
  7.2 6.3 %collective-permute-start.2 = (bf16[2,128,256]{2,1,0:T(8,128)(2,1)S(1)}, bf16[2,128,256]{2,1,0:T(8,128)(2,1)S(1)}, u32[]{:S(2)}, u32[]{:S(2)}) collective-permute-start(bf16[2,128,256]{2,1,0:T(8,128)(2,1)S(1)} %own.1.u0), channel_id=1, source_target_pairs={{0,2},{1,3},{2,0},{3,1},{4,6},{5,7},{6,4},{7,5},{8,10},{9,11},{10,... | collective-permute-start | bytes 393224 | tf_op jit(solution)/shard_map/ppermute | solution.py:257
  11.7 5.0 %collective-permute-start.6 = (bf16[2,128,256]{2,1,0:T(8,128)(2,1)S(1)}, bf16[2,128,256]{2,1,0:T(8,128)(2,1)S(1)}, u32[]{:S(2)}, u32[]{:S(2)}) collective-permute-start(bf16[2,128,256]{2,1,0:T(8,128)(2,1)S(1)} %collective-permute-done.v), channel_id=1, source_target_pairs={{0,4},{1,5},{2,7},{3,6},{4,0},{5,1},{6,3},{7,2},{8,12},{9,13},{10,... | collective-permute-start | bytes 393224 | tf_op jit(solution)/shard_map/ppermute | solution.py:257
  12.4 5.3 %collective-permute-start.7 = (bf16[2,128,256]{2,1,0:T(8,128)(2,1)S(1)}, bf16[2,128,256]{2,1,0:T(8,128)(2,1)S(1)}, u32[]{:S(2)}, u32[]{:S(2)}) collective-permute-start(bf16[2,128,256]{2,1,0:T(8,128)(2,1)S(1)} %collective-permute-done.v), channel_id=1, source_target_pairs={{0,2},{1,3},{2,0},{3,1},{4,6},{5,7},{6,4},{7,5},{8,10},{9,11},{10,... | collective-permute-start | bytes 393224 | tf_op jit(solution)/shard_map/ppermute | solution.py:257
  14.5 1.3 %collective-permute-start.5 = (bf16[128,256]{1,0:T(8,128)(2,1)S(1)}, bf16[128,256]{1,0:T(8,128)(2,1)S(1)}, u32[]{:S(2)}, u32[]{:S(2)}) collective-permute-start(bf16[128,256]{1,0:T(8,128)(2,1)S(1)} %get-tuple-element.47), channel_id=1, source_target_pairs={{0,1},{1,0},{2,3},{3,2},{4,5},{5,4},{6,7},{7,6},{8,9},{9,8},{10,11... | collective-permute-start | bytes 196616 | tf_op jit(solution)/shard_map/ppermute | solution.py:257
  14.8 1.3 %collective-permute-start.4 = (bf16[128,256]{1,0:T(8,128)(2,1)S(1)}, bf16[128,256]{1,0:T(8,128)(2,1)S(1)}, u32[]{:S(2)}, u32[]{:S(2)}) collective-permute-start(bf16[128,256]{1,0:T(8,128)(2,1)S(1)} %get-tuple-element.48), channel_id=1, source_target_pairs={{0,1},{1,0},{2,3},{3,2},{4,5},{5,4},{6,7},{7,6},{8,9},{9,8},{10,11... | collective-permute-start | bytes 196616 | tf_op jit(solution)/shard_map/ppermute | solution.py:257
  18.3 3.6 %collective-permute-start.8 = (f32[4,32]{1,0:T(4,128)S(1)}, f32[4,32]{1,0:T(4,128)S(1)}, u32[]{:S(2)}, u32[]{:S(2)}) collective-permute-start(f32[4,32]{1,0:T(4,128)S(1)} %get-tuple-element.45), channel_id=1, source_target_pairs={{0,4},{1,5},{2,7},{3,6},{4,0},{5,1},{6,3},{7,2},{8,12},{9,13},{10,... | collective-permute-start | bytes 1544 | tf_op jit(solution)/shard_map/ppermute | solution.py:257
  19.8 3.6 %collective-permute-start.9 = (f32[4,32]{1,0:T(4,128)S(1)}, f32[4,32]{1,0:T(4,128)S(1)}, u32[]{:S(2)}, u32[]{:S(2)}) collective-permute-start(f32[4,32]{1,0:T(4,128)S(1)} %get-tuple-element.46), channel_id=1, source_target_pairs={{0,2},{1,3},{2,0},{3,1},{4,6},{5,7},{6,4},{7,5},{8,10},{9,11},{10,... | collective-permute-start | bytes 1544 | tf_op jit(solution)/shard_map/ppermute | solution.py:257
  23.4 4.5 %collective-permute-start.10 = (f32[2,32]{1,0:T(2,128)S(1)}, f32[2,32]{1,0:T(2,128)S(1)}, u32[]{:S(2)}, u32[]{:S(2)}) collective-permute-start(f32[2,32]{1,0:T(2,128)S(1)} %slice.15), channel_id=1, source_target_pairs={{0,8},{1,9},{2,10},{3,11},{4,12},{5,13},{6,14},{7,15},{8,0},{9,1},... | collective-permute-start | bytes 776 | tf_op jit(solution)/shard_map/ppermute | solution.py:257

commit v24 on v22

--- a/solution.py
+++ b/solution.py
@@ -88,10 +88,8 @@
 
 
 def whiten(x, terms):
-    total = jnp.dot(x, terms[0], preferred_element_type=jnp.float32)
-    for n in (1, 2):
-        total = total + jnp.dot(x, terms[n], preferred_element_type=jnp.float32)
-    return total.astype(jnp.bfloat16)
+    wide = jnp.concatenate([x] * 3, axis=1)
+    return jnp.dot(wide, terms[...], preferred_element_type=jnp.float32).astype(jnp.bfloat16)
 
 
 def stack(*arrays):
@@ -141,7 +139,7 @@
         rest = factor[w]
         for t in range(3):
             term = rest.astype(jnp.bfloat16)
-            terms[w, t] = term
+            terms[w, t * rest.shape[0] : (t + 1) * rest.shape[0]] = term
             rest = rest - term.astype(jnp.float32)
 
 
@@ -292,7 +290,7 @@
         51,
         (layer_ids, flagged.reshape(1, -1), act_factor, grad_factor),
         [pl.BlockSpec(memory_space=pltpu.SMEM), vmem, hbm, hbm],
-        (shape((2, 3, rank, rank), bf16), shape((8 * tokens, columns), bf16)),
+        (shape((2, 3 * rank, rank), bf16), shape((8 * tokens, columns), bf16)),
         [pltpu.VMEM((2, rank, rank), f32), pltpu.SemaphoreType.DMA((2,))],
     )
     v, terms, pick = lax.optimization_barrier((v, terms, pick))

time: 28.6 us -> 28.6 us (level)
  no operation moved by 1% of the time
where the time goes in v24:
time: 28.6 us; the launch traced here: 28.5 us
  starting transfers between devices  15.4 us (54%)
  waiting for transfers between devices  6.56 us (23%)
  Pallas kernels  5.82 us (20%)
  other arithmetic  0.57 us (2%)
    ppermute x11, starting transfers between devices, send(): return lax.ppermute(x, 'blk', [(d, to(d)) for d in range(size)])  15.4 us
    ppermute x11, waiting for transfers between devices, send(): return lax.ppermute(x, 'blk', [(d, to(d)) for d in range(size)])  6.56 us
    pallas_call x9, Pallas kernels, call(): pl.pallas_call(kernel, out_shape=out_shape, in_specs=specs + [vmem] * (le...  5.82 us
  transfers between devices with their start and end apart: 11, of which 7 were waited for; matrix products, arithmetic and copies ran while one was open for 0% of the time, Pallas kernels for 14%

profile of v24, /device:TPU:0, one launch (start us, length us, event | category | flops | bytes accessed | tf_op | source)
XLA Modules:
  0.0 28.5 jit_solution(2637578722654681771)
XLA Ops:
  0.0 1.0 %away.1.unit = bf16[2,128,256]{2,1,0:T(8,128)(2,1)S(1)} custom-call(bf16[2,128,256]{2,1,0:T(8,128)(2,1)} %acts.2, bf16[2,128,256]{2,1,0:T(8,128)(2,1)} %grads.2), custom_call_target="tpu_custom_call" | custom-call | flops 3000000000 | bytes 1000000 | tf_op jit(solution)/shard_map/away/pallas_call | solution.py:234
  1.0 0.2 away_mask.1
  1.1 4.1 %collective-permute-start = (bf16[2,128,256]{2,1,0:T(8,128)(2,1)S(1)}, bf16[2,128,256]{2,1,0:T(8,128)(2,1)S(1)}, u32[]{:S(2)}, u32[]{:S(2)}) collective-permute-start(bf16[2,128,256]{2,1,0:T(8,128)(2,1)S(1)} %away_mask.1), channel_id=1, source_target_pairs={{0,8},{1,9},{2,10},{3,11},{4,12},{5,13},{6,14},{7,15},{8,0},{9,1},... | collective-permute-start | bytes 393224 | tf_op jit(solution)/shard_map/ppermute | solution.py:255
  5.3 0.1 own.1.u0
  5.4 1.6 %collective-permute-start.1 = (bf16[2,128,256]{2,1,0:T(8,128)(2,1)S(1)}, bf16[2,128,256]{2,1,0:T(8,128)(2,1)S(1)}, u32[]{:S(2)}, u32[]{:S(2)}) collective-permute-start(bf16[2,128,256]{2,1,0:T(8,128)(2,1)S(1)} %own.1.u0), channel_id=1, source_target_pairs={{0,4},{1,5},{2,7},{3,6},{4,0},{5,1},{6,3},{7,2},{8,12},{9,13},{10,... | collective-permute-start | bytes 393224 | tf_op jit(solution)/shard_map/ppermute | solution.py:255
  7.1 0.7 %collective-permute-start.3 = (bf16[2,128,256]{2,1,0:T(8,128)(2,1)S(1)}, bf16[2,128,256]{2,1,0:T(8,128)(2,1)S(1)}, u32[]{:S(2)}, u32[]{:S(2)}) collective-permute-start(bf16[2,128,256]{2,1,0:T(8,128)(2,1)S(1)} %own.1.u0), channel_id=1, source_target_pairs={{0,2},{1,3},{2,0},{3,1},{4,6},{5,7},{6,4},{7,5},{8,10},{9,11},{10,... | collective-permute-start | bytes 393224 | tf_op jit(solution)/shard_map/ppermute | solution.py:255
  7.7 0.7 %collective-permute-start.2 = (bf16[2,128,256]{2,1,0:T(8,128)(2,1)S(1)}, bf16[2,128,256]{2,1,0:T(8,128)(2,1)S(1)}, u32[]{:S(2)}, u32[]{:S(2)}) collective-permute-start(bf16[2,128,256]{2,1,0:T(8,128)(2,1)S(1)} %own.1.u0), channel_id=1, source_target_pairs={{0,1},{1,0},{2,3},{3,2},{4,5},{5,4},{6,7},{7,6},{8,9},{9,8},{10,11... | collective-permute-start | bytes 393224 | tf_op jit(solution)/shard_map/ppermute | solution.py:255
  8.4 1.7 %factor_terms.1 = (bf16[2,768,256]{2,1,0:T(8,128)(2,1)S(1)}, bf16[1024,32]{1,0:T(8,128)(2,1)S(1)}) custom-call(s32[2]{0:T(128)S(1)} %copy-done.1, s32[1,32]{1,0:T(1,128)S(1)} %bitcast.8, f32[16,256,256]{2,1,0:T(8,128)} %act_f.1, f32[16,256,256]{2,1,0:T(8,128)} %grad_f.1), custom_call_target="tpu_custom_call" | custom-call | flops 1000000000 | bytes 1000000 | tf_op jit(solution)/shard_map/factor_terms/pallas_call | solution.py:234
  10.1 1.6 %collective-permute-done.v = bf16[2,128,256]{2,1,0:T(8,128)(2,1)S(1)} collective-permute-done((bf16[2,128,256]{2,1,0:T(8,128)(2,1)S(1)}, bf16[2,128,256]{2,1,0:T(8,128)(2,1)S(1)}, u32[]{:S(2)}, u32[]{:S(2)}) %collective-permute-start) | collective-permute-done | bytes 131104 | tf_op jit(solution)/shard_map/ppermute | solution.py:255
  11.7 0.6 %collective-permute-start.6 = (bf16[2,128,256]{2,1,0:T(8,128)(2,1)S(1)}, bf16[2,128,256]{2,1,0:T(8,128)(2,1)S(1)}, u32[]{:S(2)}, u32[]{:S(2)}) collective-permute-start(bf16[2,128,256]{2,1,0:T(8,128)(2,1)S(1)} %collective-permute-done.v), channel_id=1, source_target_pairs={{0,4},{1,5},{2,7},{3,6},{4,0},{5,1},{6,3},{7,2},{8,12},{9,13},{10,... | collective-permute-start | bytes 393224 | tf_op jit(solution)/shard_map/ppermute | solution.py:255
  12.3 0.0 collective-permute-done.1.u3
  12.3 2.0 %collective-permute-start.7 = (bf16[2,128,256]{2,1,0:T(8,128)(2,1)S(1)}, bf16[2,128,256]{2,1,0:T(8,128)(2,1)S(1)}, u32[]{:S(2)}, u32[]{:S(2)}) collective-permute-start(bf16[2,128,256]{2,1,0:T(8,128)(2,1)S(1)} %collective-permute-done.v), channel_id=1, source_target_pairs={{0,2},{1,3},{2,0},{3,1},{4,6},{5,7},{6,4},{7,5},{8,10},{9,11},{10,... | collective-permute-start | bytes 393224 | tf_op jit(solution)/shard_map/ppermute | solution.py:255
  14.4 0.0 collective-permute-done.3.u2
  14.4 0.0 collective-permute-done.2.u1
  14.4 1.0 %early_pairs.1 = (bf16[2,512,256]{2,1,0:T(8,128)(2,1)S(1)}, f32[4,1024]{1,0:T(4,128)S(1)}, f32[8,768]{1,0:T(8,128)S(1)}) custom-call(bf16[2,768,256]{2,1,0:T(8,128)(2,1)S(1)} %get-tuple-element.33.terms, bf16[2,128,256]{2,1,0:T(8,128)(2,1)S(1)} %own.1.u0, bf16[2,128,256]{2,1,0:T(8,128)(2,1)S(1)} %collective-permute-done.v, ...), custom_call_target="tpu_custom_call" | custom-call | flops 1000000000 | bytes 1000000 | tf_op jit(solution)/shard_map/early_pairs/pallas_call | solution.py:234
  15.4 0.1 collective-permute-start.5
  15.5 0.5 %collective-permute-start.4 = (bf16[128,256]{1,0:T(8,128)(2,1)S(1)}, bf16[128,256]{1,0:T(8,128)(2,1)S(1)}, u32[]{:S(2)}, u32[]{:S(2)}) collective-permute-start(bf16[128,256]{1,0:T(8,128)(2,1)S(1)} %get-tuple-element.48), channel_id=1, source_target_pairs={{0,1},{1,0},{2,3},{3,2},{4,5},{5,4},{6,7},{7,6},{8,9},{9,8},{10,11... | collective-permute-start | bytes 196616 | tf_op jit(solution)/shard_map/ppermute | solution.py:255
  16.0 0.7 %collective-permute-done.5.grads = bf16[128,256]{1,0:T(8,128)(2,1)S(1)} collective-permute-done((bf16[128,256]{1,0:T(8,128)(2,1)S(1)}, bf16[128,256]{1,0:T(8,128)(2,1)S(1)}, u32[]{:S(2)}, u32[]{:S(2)}) %collective-permute-start.5) | collective-permute-done | bytes 65568 | tf_op jit(solution)/shard_map/ppermute | solution.py:255
  16.7 0.2 collective-permute-done.4.acts
  16.9 0.3 %core_pairs.1 = (f32[4,1024]{1,0:T(4,128)S(1)}, f32[8,768]{1,0:T(8,128)S(1)}) custom-call(bf16[2,512,256]{2,1,0:T(8,128)(2,1)S(1)} %get-tuple-element.36.white, bf16[128,256]{1,0:T(8,128)(2,1)S(1)} %collective-permute-done.4.acts, bf16[128,256]{1,0:T(8,128)(2,1)S(1)} %collective-permute-done.5.grads, ...), custom_call_target="tpu_custom_call", output_to_operand_aliasing={{0}: (3, {}), {1}: (4, {})} | custom-call | flops 10000 | bytes 1000000 | tf_op jit(solution)/shard_map/core_pairs/pallas_call | solution.py:234
  17.2 0.0 collective-permute-done.6.v3
  17.2 0.5 %z_pairs.1 = (bf16[2,128,256]{2,1,0:T(8,128)(2,1)S(1)}, f32[8,768]{1,0:T(8,128)S(1)}) custom-call(bf16[2,768,256]{2,1,0:T(8,128)(2,1)S(1)} %get-tuple-element.33.terms, bf16[2,512,256]{2,1,0:T(8,128)(2,1)S(1)} %get-tuple-element.36.white, bf16[2,128,256]{2,1,0:T(8,128)(2,1)S(1)} %collective-permute-done.3.u2, ...), custom_call_target="tpu_custom_call", output_to_operand_aliasing={{1}: (7, {})} | custom-call | flops 10000 | bytes 1000000 | tf_op jit(solution)/shard_map/z_pairs/pallas_call | solution.py:234
  17.7 0.5 %collective-permute-done.7.v2 = bf16[2,128,256]{2,1,0:T(8,128)(2,1)S(1)} collective-permute-done((bf16[2,128,256]{2,1,0:T(8,128)(2,1)S(1)}, bf16[2,128,256]{2,1,0:T(8,128)(2,1)S(1)}, u32[]{:S(2)}, u32[]{:S(2)}) %collective-permute-start.7) | collective-permute-done | bytes 131104 | tf_op jit(solution)/shard_map/ppermute | solution.py:255
  18.1 0.7 %return_rows.1 = (f32[4,32]{1,0:T(4,128)S(1)}, f32[4,32]{1,0:T(4,128)S(1)}) custom-call(bf16[2,768,256]{2,1,0:T(8,128)(2,1)S(1)} %get-tuple-element.33.terms, bf16[2,512,256]{2,1,0:T(8,128)(2,1)S(1)} %get-tuple-element.36.white, bf16[2,128,256]{2,1,0:T(8,128)(2,1)S(1)} %get-tuple-element.43.white3, bf16[1024,32]{1,0:T(8,128)(2,1)S(1)} %get-tuple-element.37.pick, ...), custom_call_target="tpu_custom_call" | custom-call | flops 1000000000 | bytes 1000000 | tf_op jit(solution)/shard_map/return_rows/pallas_call | solution.py:234
  18.8 1.0 %collective-permute-start.8 = (f32[4,32]{1,0:T(4,128)S(1)}, f32[4,32]{1,0:T(4,128)S(1)}, u32[]{:S(2)}, u32[]{:S(2)}) collective-permute-start(f32[4,32]{1,0:T(4,128)S(1)} %get-tuple-element.45), channel_id=1, source_target_pairs={{0,4},{1,5},{2,7},{3,6},{4,0},{5,1},{6,3},{7,2},{8,12},{9,13},{10,... | collective-permute-start | bytes 1544 | tf_op jit(solution)/shard_map/ppermute | solution.py:255
  19.8 1.5 %collective-permute-start.9 = (f32[4,32]{1,0:T(4,128)S(1)}, f32[4,32]{1,0:T(4,128)S(1)}, u32[]{:S(2)}, u32[]{:S(2)}) collective-permute-start(f32[4,32]{1,0:T(4,128)S(1)} %get-tuple-element.46), channel_id=1, source_target_pairs={{0,2},{1,3},{2,0},{3,1},{4,6},{5,7},{6,4},{7,5},{8,10},{9,11},{10,... | collective-permute-start | bytes 1544 | tf_op jit(solution)/shard_map/ppermute | solution.py:255
  21.3 0.4 %own_rows.1 = f32[4,32]{1,0:T(4,128)S(1)} custom-call(bf16[2,512,256]{2,1,0:T(8,128)(2,1)S(1)} %get-tuple-element.36.white, bf16[1024,32]{1,0:T(8,128)(2,1)S(1)} %get-tuple-element.37.pick, f32[4,1024]{1,0:T(4,128)S(1)} %get-tuple-element.41.mine, bf16[2,128,256]{2,1,0:T(8,128)(2,1)S(1)} %collective-permute-done.6.v3, ...), custom_call_target="tpu_custom_call" | custom-call | flops 1000000000 | bytes 1000000 | tf_op jit(solution)/shard_map/own_rows/pallas_call | solution.py:234
  21.7 0.8 %collective-permute-done.8 = f32[4,32]{1,0:T(4,128)S(1)} collective-permute-done((f32[4,32]{1,0:T(4,128)S(1)}, f32[4,32]{1,0:T(4,128)S(1)}, u32[]{:S(2)}, u32[]{:S(2)}) %collective-permute-start.8) | collective-permute-done | bytes 544 | tf_op jit(solution)/shard_map/ppermute | solution.py:255
  22.5 0.9 %collective-permute-done.9 = f32[4,32]{1,0:T(4,128)S(1)} collective-permute-done((f32[4,32]{1,0:T(4,128)S(1)}, f32[4,32]{1,0:T(4,128)S(1)}, u32[]{:S(2)}, u32[]{:S(2)}) %collective-permute-start.9) | collective-permute-done | bytes 544 | tf_op jit(solution)/shard_map/ppermute | solution.py:255
  23.4 2.6 %collective-permute-start.10 = (f32[2,32]{1,0:T(2,128)S(1)}, f32[2,32]{1,0:T(2,128)S(1)}, u32[]{:S(2)}, u32[]{:S(2)}) collective-permute-start(f32[2,32]{1,0:T(2,128)S(1)} %slice.15), channel_id=1, source_target_pairs={{0,8},{1,9},{2,10},{3,11},{4,12},{5,13},{6,14},{7,15},{8,0},{9,1},... | collective-permute-start | bytes 776 | tf_op jit(solution)/shard_map/ppermute | solution.py:255
  26.0 1.9 %collective-permute-done.10 = f32[2,32]{1,0:T(2,128)S(1)} collective-permute-done((f32[2,32]{1,0:T(2,128)S(1)}, f32[2,32]{1,0:T(2,128)S(1)}, u32[]{:S(2)}, u32[]{:S(2)}) %collective-permute-start.10) | collective-permute-done | bytes 288 | tf_op jit(solution)/shard_map/ppermute | solution.py:255
  27.9 0.6 %slice_add_fusion = f32[2,32]{1,0:T(2,128)} fusion(f32[2,32]{1,0:T(2,128)S(1)} %collective-permute-done.10, f32[4,32]{1,0:T(4,128)S(1)} %add_add_fusion), kind=kLoop, calls=%fused_computation.3 | loop fusion | flops 64 | bytes 768 | tf_op jit(solution)/shard_map/add | solution.py:341
  (13 shorter events, 0.0 us)
Async XLA Ops:
  0.0 5.3 %copy-start.4 = (bf16[2,128,256]{2,1,0:T(8,128)(2,1)S(1)}, bf16[2,128,256]{2,1,0:T(8,128)(2,1)}, u32[]{:S(2)}) copy-start(bf16[2,128,256]{2,1,0:T(8,128)(2,1)} %grads.2) | copy-start | bytes 393220
  0.0 5.3 %copy-start.3 = (bf16[2,128,256]{2,1,0:T(8,128)(2,1)S(1)}, bf16[2,128,256]{2,1,0:T(8,128)(2,1)}, u32[]{:S(2)}) copy-start(bf16[2,128,256]{2,1,0:T(8,128)(2,1)} %acts.2) | copy-start | bytes 393220
  0.0 1.0 %copy-start = (s32[2]{0:T(128)S(1)}, s32[2]{0:T(128)}, u32[]{:S(2)}) copy-start(s32[2]{0:T(128)} %param.9) | copy-start | bytes 28
  0.0 8.4 %copy-start.2 = (s32[32]{0:T(128)S(1)}, s32[32]{0:T(128)}, u32[]{:S(2)}) copy-start(s32[32]{0:T(128)} %param.11) | copy-start | bytes 388
  0.0 8.4 %copy-start.1 = (s32[2]{0:T(128)S(1)}, s32[2]{0:T(128)}, u32[]{:S(2)}) copy-start(s32[2]{0:T(128)} %layer_ids.1) | copy-start | bytes 28
  1.1 10.5 %collective-permute-start = (bf16[2,128,256]{2,1,0:T(8,128)(2,1)S(1)}, bf16[2,128,256]{2,1,0:T(8,128)(2,1)S(1)}, u32[]{:S(2)}, u32[]{:S(2)}) collective-permute-start(bf16[2,128,256]{2,1,0:T(8,128)(2,1)S(1)} %away_mask.1), channel_id=1, source_target_pairs={{0,8},{1,9},{2,10},{3,11},{4,12},{5,13},{6,14},{7,15},{8,0},{9,1},... | collective-permute-start | bytes 393224 | tf_op jit(solution)/shard_map/ppermute | solution.py:255
  5.4 6.9 %collective-permute-start.1 = (bf16[2,128,256]{2,1,0:T(8,128)(2,1)S(1)}, bf16[2,128,256]{2,1,0:T(8,128)(2,1)S(1)}, u32[]{:S(2)}, u32[]{:S(2)}) collective-permute-start(bf16[2,128,256]{2,1,0:T(8,128)(2,1)S(1)} %own.1.u0), channel_id=1, source_target_pairs={{0,4},{1,5},{2,7},{3,6},{4,0},{5,1},{6,3},{7,2},{8,12},{9,13},{10,... | collective-permute-start | bytes 393224 | tf_op jit(solution)/shard_map/ppermute | solution.py:255
  7.1 7.3 %collective-permute-start.3 = (bf16[2,128,256]{2,1,0:T(8,128)(2,1)S(1)}, bf16[2,128,256]{2,1,0:T(8,128)(2,1)S(1)}, u32[]{:S(2)}, u32[]{:S(2)}) collective-permute-start(bf16[2,128,256]{2,1,0:T(8,128)(2,1)S(1)} %own.1.u0), channel_id=1, source_target_pairs={{0,2},{1,3},{2,0},{3,1},{4,6},{5,7},{6,4},{7,5},{8,10},{9,11},{10,... | collective-permute-start | bytes 393224 | tf_op jit(solution)/shard_map/ppermute | solution.py:255
  7.7 6.6 %collective-permute-start.2 = (bf16[2,128,256]{2,1,0:T(8,128)(2,1)S(1)}, bf16[2,128,256]{2,1,0:T(8,128)(2,1)S(1)}, u32[]{:S(2)}, u32[]{:S(2)}) collective-permute-start(bf16[2,128,256]{2,1,0:T(8,128)(2,1)S(1)} %own.1.u0), channel_id=1, source_target_pairs={{0,1},{1,0},{2,3},{3,2},{4,5},{5,4},{6,7},{7,6},{8,9},{9,8},{10,11... | collective-permute-start | bytes 393224 | tf_op jit(solution)/shard_map/ppermute | solution.py:255
  11.7 5.5 %collective-permute-start.6 = (bf16[2,128,256]{2,1,0:T(8,128)(2,1)S(1)}, bf16[2,128,256]{2,1,0:T(8,128)(2,1)S(1)}, u32[]{:S(2)}, u32[]{:S(2)}) collective-permute-start(bf16[2,128,256]{2,1,0:T(8,128)(2,1)S(1)} %collective-permute-done.v), channel_id=1, source_target_pairs={{0,4},{1,5},{2,7},{3,6},{4,0},{5,1},{6,3},{7,2},{8,12},{9,13},{10,... | collective-permute-start | bytes 393224 | tf_op jit(solution)/shard_map/ppermute | solution.py:255
  12.3 5.8 %collective-permute-start.7 = (bf16[2,128,256]{2,1,0:T(8,128)(2,1)S(1)}, bf16[2,128,256]{2,1,0:T(8,128)(2,1)S(1)}, u32[]{:S(2)}, u32[]{:S(2)}) collective-permute-start(bf16[2,128,256]{2,1,0:T(8,128)(2,1)S(1)} %collective-permute-done.v), channel_id=1, source_target_pairs={{0,2},{1,3},{2,0},{3,1},{4,6},{5,7},{6,4},{7,5},{8,10},{9,11},{10,... | collective-permute-start | bytes 393224 | tf_op jit(solution)/shard_map/ppermute | solution.py:255
  15.4 1.3 %collective-permute-start.5 = (bf16[128,256]{1,0:T(8,128)(2,1)S(1)}, bf16[128,256]{1,0:T(8,128)(2,1)S(1)}, u32[]{:S(2)}, u32[]{:S(2)}) collective-permute-start(bf16[128,256]{1,0:T(8,128)(2,1)S(1)} %get-tuple-element.47), channel_id=1, source_target_pairs={{0,1},{1,0},{2,3},{3,2},{4,5},{5,4},{6,7},{7,6},{8,9},{9,8},{10,11... | collective-permute-start | bytes 196616 | tf_op jit(solution)/shard_map/ppermute | solution.py:255
  15.5 1.4 %collective-permute-start.4 = (bf16[128,256]{1,0:T(8,128)(2,1)S(1)}, bf16[128,256]{1,0:T(8,128)(2,1)S(1)}, u32[]{:S(2)}, u32[]{:S(2)}) collective-permute-start(bf16[128,256]{1,0:T(8,128)(2,1)S(1)} %get-tuple-element.48), channel_id=1, source_target_pairs={{0,1},{1,0},{2,3},{3,2},{4,5},{5,4},{6,7},{7,6},{8,9},{9,8},{10,11... | collective-permute-start | bytes 196616 | tf_op jit(solution)/shard_map/ppermute | solution.py:255
  18.8 3.6 %collective-permute-start.8 = (f32[4,32]{1,0:T(4,128)S(1)}, f32[4,32]{1,0:T(4,128)S(1)}, u32[]{:S(2)}, u32[]{:S(2)}) collective-permute-start(f32[4,32]{1,0:T(4,128)S(1)} %get-tuple-element.45), channel_id=1, source_target_pairs={{0,4},{1,5},{2,7},{3,6},{4,0},{5,1},{6,3},{7,2},{8,12},{9,13},{10,... | collective-permute-start | bytes 1544 | tf_op jit(solution)/shard_map/ppermute | solution.py:255
  19.8 3.6 %collective-permute-start.9 = (f32[4,32]{1,0:T(4,128)S(1)}, f32[4,32]{1,0:T(4,128)S(1)}, u32[]{:S(2)}, u32[]{:S(2)}) collective-permute-start(f32[4,32]{1,0:T(4,128)S(1)} %get-tuple-element.46), channel_id=1, source_target_pairs={{0,2},{1,3},{2,0},{3,1},{4,6},{5,7},{6,4},{7,5},{8,10},{9,11},{10,... | collective-permute-start | bytes 1544 | tf_op jit(solution)/shard_map/ppermute | solution.py:255
  23.4 4.5 %collective-permute-start.10 = (f32[2,32]{1,0:T(2,128)S(1)}, f32[2,32]{1,0:T(2,128)S(1)}, u32[]{:S(2)}, u32[]{:S(2)}) collective-permute-start(f32[2,32]{1,0:T(2,128)S(1)} %slice.15), channel_id=1, source_target_pairs={{0,8},{1,9},{2,10},{3,11},{4,12},{5,13},{6,14},{7,15},{8,0},{9,1},... | collective-permute-start | bytes 776 | tf_op jit(solution)/shard_map/ppermute | solution.py:255

commit v25 on v22

--- a/solution.py
+++ b/solution.py
@@ -339,7 +339,7 @@
         (rows, rows),
     )
     mine = kernel(rows_kernel, "own_rows", (white, pick, mine, v3, v2), rows)
-    half_sum = mine + send(by_z, z_near) + send(by_x, lambda d: d ^ 2)
+    half_sum = mine + send(by_x, lambda d: d ^ 2) + send(by_z, z_near)
     return half_sum[:per] + send(half_sum[per:], opposite)
 
 

time: 28.6 us -> 29.5 us (1.031)
  starting transfers between devices: 15.4 us -> 16 us
    ppermute x11, starting transfers between devices: 15.4 us -> 16 us  [send(): return lax.ppermute(x, 'blk', [(d, to(d)) for d in range(size)])]
where the time goes in v25:
time: 29.5 us; the launch traced here: 29.3 us
  starting transfers between devices  16 us (54%)
  waiting for transfers between devices  6.85 us (23%)
  Pallas kernels  5.82 us (20%)
  other arithmetic  0.57 us (2%)
    ppermute x11, starting transfers between devices, send(): return lax.ppermute(x, 'blk', [(d, to(d)) for d in range(size)])  16 us
    ppermute x11, waiting for transfers between devices, send(): return lax.ppermute(x, 'blk', [(d, to(d)) for d in range(size)])  6.85 us
    pallas_call x9, Pallas kernels, call(): pl.pallas_call(kernel, out_shape=out_shape, in_specs=specs + [vmem] * (le...  5.82 us
  transfers between devices with their start and end apart: 11, of which 7 were waited for; matrix products, arithmetic and copies ran while one was open for 0% of the time, Pallas kernels for 14%

profile of v25, /device:TPU:0, one launch (start us, length us, event | category | flops | bytes accessed | tf_op | source)
XLA Modules:
  0.0 29.3 jit_solution(13995110917075705322)
XLA Ops:
  0.0 1.0 %away.1.unit = bf16[2,128,256]{2,1,0:T(8,128)(2,1)S(1)} custom-call(bf16[2,128,256]{2,1,0:T(8,128)(2,1)} %acts.2, bf16[2,128,256]{2,1,0:T(8,128)(2,1)} %grads.2), custom_call_target="tpu_custom_call" | custom-call | flops 3000000000 | bytes 1000000 | tf_op jit(solution)/shard_map/away/pallas_call | solution.py:236
  1.0 0.2 away_mask.1
  1.1 4.1 %collective-permute-start = (bf16[2,128,256]{2,1,0:T(8,128)(2,1)S(1)}, bf16[2,128,256]{2,1,0:T(8,128)(2,1)S(1)}, u32[]{:S(2)}, u32[]{:S(2)}) collective-permute-start(bf16[2,128,256]{2,1,0:T(8,128)(2,1)S(1)} %away_mask.1), channel_id=1, source_target_pairs={{0,8},{1,9},{2,10},{3,11},{4,12},{5,13},{6,14},{7,15},{8,0},{9,1},... | collective-permute-start | bytes 393224 | tf_op jit(solution)/shard_map/ppermute | solution.py:257
  5.3 0.1 own.1.u0
  5.4 1.6 %collective-permute-start.1 = (bf16[2,128,256]{2,1,0:T(8,128)(2,1)S(1)}, bf16[2,128,256]{2,1,0:T(8,128)(2,1)S(1)}, u32[]{:S(2)}, u32[]{:S(2)}) collective-permute-start(bf16[2,128,256]{2,1,0:T(8,128)(2,1)S(1)} %own.1.u0), channel_id=1, source_target_pairs={{0,4},{1,5},{2,7},{3,6},{4,0},{5,1},{6,3},{7,2},{8,12},{9,13},{10,... | collective-permute-start | bytes 393224 | tf_op jit(solution)/shard_map/ppermute | solution.py:257
  7.1 0.7 %collective-permute-start.3 = (bf16[2,128,256]{2,1,0:T(8,128)(2,1)S(1)}, bf16[2,128,256]{2,1,0:T(8,128)(2,1)S(1)}, u32[]{:S(2)}, u32[]{:S(2)}) collective-permute-start(bf16[2,128,256]{2,1,0:T(8,128)(2,1)S(1)} %own.1.u0), channel_id=1, source_target_pairs={{0,2},{1,3},{2,0},{3,1},{4,6},{5,7},{6,4},{7,5},{8,10},{9,11},{10,... | collective-permute-start | bytes 393224 | tf_op jit(solution)/shard_map/ppermute | solution.py:257
  7.7 0.7 %collective-permute-start.2 = (bf16[2,128,256]{2,1,0:T(8,128)(2,1)S(1)}, bf16[2,128,256]{2,1,0:T(8,128)(2,1)S(1)}, u32[]{:S(2)}, u32[]{:S(2)}) collective-permute-start(bf16[2,128,256]{2,1,0:T(8,128)(2,1)S(1)} %own.1.u0), channel_id=1, source_target_pairs={{0,1},{1,0},{2,3},{3,2},{4,5},{5,4},{6,7},{7,6},{8,9},{9,8},{10,11... | collective-permute-start | bytes 393224 | tf_op jit(solution)/shard_map/ppermute | solution.py:257
  8.4 1.7 %factor_terms.1 = (bf16[2,3,256,256]{3,2,1,0:T(8,128)(2,1)S(1)}, bf16[1024,32]{1,0:T(8,128)(2,1)S(1)}) custom-call(s32[2]{0:T(128)S(1)} %copy-done.1, s32[1,32]{1,0:T(1,128)S(1)} %bitcast.8, f32[16,256,256]{2,1,0:T(8,128)} %act_f.1, f32[16,256,256]{2,1,0:T(8,128)} %grad_f.1), custom_call_target="tpu_custom_call" | custom-call | flops 1000000000 | bytes 1000000 | tf_op jit(solution)/shard_map/factor_terms/pallas_call | solution.py:236
  10.1 1.6 %collective-permute-done.v = bf16[2,128,256]{2,1,0:T(8,128)(2,1)S(1)} collective-permute-done((bf16[2,128,256]{2,1,0:T(8,128)(2,1)S(1)}, bf16[2,128,256]{2,1,0:T(8,128)(2,1)S(1)}, u32[]{:S(2)}, u32[]{:S(2)}) %collective-permute-start) | collective-permute-done | bytes 131104 | tf_op jit(solution)/shard_map/ppermute | solution.py:257
  11.7 0.6 %collective-permute-start.6 = (bf16[2,128,256]{2,1,0:T(8,128)(2,1)S(1)}, bf16[2,128,256]{2,1,0:T(8,128)(2,1)S(1)}, u32[]{:S(2)}, u32[]{:S(2)}) collective-permute-start(bf16[2,128,256]{2,1,0:T(8,128)(2,1)S(1)} %collective-permute-done.v), channel_id=1, source_target_pairs={{0,4},{1,5},{2,7},{3,6},{4,0},{5,1},{6,3},{7,2},{8,12},{9,13},{10,... | collective-permute-start | bytes 393224 | tf_op jit(solution)/shard_map/ppermute | solution.py:257
  12.3 0.0 collective-permute-done.1.u3
  12.3 2.0 %collective-permute-start.7 = (bf16[2,128,256]{2,1,0:T(8,128)(2,1)S(1)}, bf16[2,128,256]{2,1,0:T(8,128)(2,1)S(1)}, u32[]{:S(2)}, u32[]{:S(2)}) collective-permute-start(bf16[2,128,256]{2,1,0:T(8,128)(2,1)S(1)} %collective-permute-done.v), channel_id=1, source_target_pairs={{0,2},{1,3},{2,0},{3,1},{4,6},{5,7},{6,4},{7,5},{8,10},{9,11},{10,... | collective-permute-start | bytes 393224 | tf_op jit(solution)/shard_map/ppermute | solution.py:257
  14.4 0.0 collective-permute-done.3.u2
  14.4 0.0 collective-permute-done.2.u1
  14.4 1.0 %early_pairs.1 = (bf16[2,512,256]{2,1,0:T(8,128)(2,1)S(1)}, f32[4,1024]{1,0:T(4,128)S(1)}, f32[8,768]{1,0:T(8,128)S(1)}) custom-call(bf16[2,3,256,256]{3,2,1,0:T(8,128)(2,1)S(1)} %get-tuple-element.33.terms, bf16[2,128,256]{2,1,0:T(8,128)(2,1)S(1)} %own.1.u0, bf16[2,128,256]{2,1,0:T(8,128)(2,1)S(1)} %collective-permute-done.v, ...), custom_call_target="tpu_custom_call" | custom-call | flops 1000000000 | bytes 1000000 | tf_op jit(solution)/shard_map/early_pairs/pallas_call | solution.py:236
  15.4 0.1 collective-permute-start.5
  15.5 0.5 %collective-permute-start.4 = (bf16[128,256]{1,0:T(8,128)(2,1)S(1)}, bf16[128,256]{1,0:T(8,128)(2,1)S(1)}, u32[]{:S(2)}, u32[]{:S(2)}) collective-permute-start(bf16[128,256]{1,0:T(8,128)(2,1)S(1)} %get-tuple-element.48), channel_id=1, source_target_pairs={{0,1},{1,0},{2,3},{3,2},{4,5},{5,4},{6,7},{7,6},{8,9},{9,8},{10,11... | collective-permute-start | bytes 196616 | tf_op jit(solution)/shard_map/ppermute | solution.py:257
  16.0 0.7 %collective-permute-done.5.grads = bf16[128,256]{1,0:T(8,128)(2,1)S(1)} collective-permute-done((bf16[128,256]{1,0:T(8,128)(2,1)S(1)}, bf16[128,256]{1,0:T(8,128)(2,1)S(1)}, u32[]{:S(2)}, u32[]{:S(2)}) %collective-permute-start.5) | collective-permute-done | bytes 65568 | tf_op jit(solution)/shard_map/ppermute | solution.py:257
  16.7 0.2 collective-permute-done.4.acts
  16.9 0.3 %core_pairs.1 = (f32[4,1024]{1,0:T(4,128)S(1)}, f32[8,768]{1,0:T(8,128)S(1)}) custom-call(bf16[2,512,256]{2,1,0:T(8,128)(2,1)S(1)} %get-tuple-element.36.white, bf16[128,256]{1,0:T(8,128)(2,1)S(1)} %collective-permute-done.4.acts, bf16[128,256]{1,0:T(8,128)(2,1)S(1)} %collective-permute-done.5.grads, ...), custom_call_target="tpu_custom_call", output_to_operand_aliasing={{0}: (3, {}), {1}: (4, {})} | custom-call | flops 10000 | bytes 1000000 | tf_op jit(solution)/shard_map/core_pairs/pallas_call | solution.py:236
  17.2 0.0 collective-permute-done.6.v3
  17.2 0.5 %z_pairs.1 = (bf16[2,128,256]{2,1,0:T(8,128)(2,1)S(1)}, f32[8,768]{1,0:T(8,128)S(1)}) custom-call(bf16[2,3,256,256]{3,2,1,0:T(8,128)(2,1)S(1)} %get-tuple-element.33.terms, bf16[2,512,256]{2,1,0:T(8,128)(2,1)S(1)} %get-tuple-element.36.white, bf16[2,128,256]{2,1,0:T(8,128)(2,1)S(1)} %collective-permute-done.3.u2, ...), custom_call_target="tpu_custom_call", output_to_operand_aliasing={{1}: (7, {})} | custom-call | flops 10000 | bytes 1000000 | tf_op jit(solution)/shard_map/z_pairs/pallas_call | solution.py:236
  17.7 0.5 %collective-permute-done.7.v2 = bf16[2,128,256]{2,1,0:T(8,128)(2,1)S(1)} collective-permute-done((bf16[2,128,256]{2,1,0:T(8,128)(2,1)S(1)}, bf16[2,128,256]{2,1,0:T(8,128)(2,1)S(1)}, u32[]{:S(2)}, u32[]{:S(2)}) %collective-permute-start.7) | collective-permute-done | bytes 131104 | tf_op jit(solution)/shard_map/ppermute | solution.py:257
  18.1 0.7 %return_rows.1 = (f32[4,32]{1,0:T(4,128)S(1)}, f32[4,32]{1,0:T(4,128)S(1)}) custom-call(bf16[2,3,256,256]{3,2,1,0:T(8,128)(2,1)S(1)} %get-tuple-element.33.terms, bf16[2,512,256]{2,1,0:T(8,128)(2,1)S(1)} %get-tuple-element.36.white, bf16[2,128,256]{2,1,0:T(8,128)(2,1)S(1)} %get-tuple-element.43.white3, bf16[1024,32]{1,0:T(8,128)(2,1)S(1)} %get-tuple-element.37.pick, ...), custom_call_target="tpu_custom_call" | custom-call | flops 1000000000 | bytes 1000000 | tf_op jit(solution)/shard_map/return_rows/pallas_call | solution.py:236
  18.8 1.8 %collective-permute-start.8 = (f32[4,32]{1,0:T(4,128)S(1)}, f32[4,32]{1,0:T(4,128)S(1)}, u32[]{:S(2)}, u32[]{:S(2)}) collective-permute-start(f32[4,32]{1,0:T(4,128)S(1)} %get-tuple-element.45), channel_id=1, source_target_pairs={{0,2},{1,3},{2,0},{3,1},{4,6},{5,7},{6,4},{7,5},{8,10},{9,11},{10,... | collective-permute-start | bytes 1544 | tf_op jit(solution)/shard_map/ppermute | solution.py:257
  20.6 0.9 %collective-permute-start.9 = (f32[4,32]{1,0:T(4,128)S(1)}, f32[4,32]{1,0:T(4,128)S(1)}, u32[]{:S(2)}, u32[]{:S(2)}) collective-permute-start(f32[4,32]{1,0:T(4,128)S(1)} %get-tuple-element.46), channel_id=1, source_target_pairs={{0,4},{1,5},{2,7},{3,6},{4,0},{5,1},{6,3},{7,2},{8,12},{9,13},{10,... | collective-permute-start | bytes 1544 | tf_op jit(solution)/shard_map/ppermute | solution.py:257
  21.5 0.4 %own_rows.1 = f32[4,32]{1,0:T(4,128)S(1)} custom-call(bf16[2,512,256]{2,1,0:T(8,128)(2,1)S(1)} %get-tuple-element.36.white, bf16[1024,32]{1,0:T(8,128)(2,1)S(1)} %get-tuple-element.37.pick, f32[4,1024]{1,0:T(4,128)S(1)} %get-tuple-element.41.mine, bf16[2,128,256]{2,1,0:T(8,128)(2,1)S(1)} %collective-permute-done.6.v3, ...), custom_call_target="tpu_custom_call" | custom-call | flops 1000000000 | bytes 1000000 | tf_op jit(solution)/shard_map/own_rows/pallas_call | solution.py:236
  21.9 0.6 %collective-permute-done.8 = f32[4,32]{1,0:T(4,128)S(1)} collective-permute-done((f32[4,32]{1,0:T(4,128)S(1)}, f32[4,32]{1,0:T(4,128)S(1)}, u32[]{:S(2)}, u32[]{:S(2)}) %collective-permute-start.8) | collective-permute-done | bytes 544 | tf_op jit(solution)/shard_map/ppermute | solution.py:257
  22.5 1.7 %collective-permute-done.9 = f32[4,32]{1,0:T(4,128)S(1)} collective-permute-done((f32[4,32]{1,0:T(4,128)S(1)}, f32[4,32]{1,0:T(4,128)S(1)}, u32[]{:S(2)}, u32[]{:S(2)}) %collective-permute-start.9) | collective-permute-done | bytes 544 | tf_op jit(solution)/shard_map/ppermute | solution.py:257
  24.2 2.9 %collective-permute-start.10 = (f32[2,32]{1,0:T(2,128)S(1)}, f32[2,32]{1,0:T(2,128)S(1)}, u32[]{:S(2)}, u32[]{:S(2)}) collective-permute-start(f32[2,32]{1,0:T(2,128)S(1)} %slice.15), channel_id=1, source_target_pairs={{0,8},{1,9},{2,10},{3,11},{4,12},{5,13},{6,14},{7,15},{8,0},{9,1},... | collective-permute-start | bytes 776 | tf_op jit(solution)/shard_map/ppermute | solution.py:257
  27.2 1.6 %collective-permute-done.10 = f32[2,32]{1,0:T(2,128)S(1)} collective-permute-done((f32[2,32]{1,0:T(2,128)S(1)}, f32[2,32]{1,0:T(2,128)S(1)}, u32[]{:S(2)}, u32[]{:S(2)}) %collective-permute-start.10) | collective-permute-done | bytes 288 | tf_op jit(solution)/shard_map/ppermute | solution.py:257
  28.8 0.6 %slice_add_fusion = f32[2,32]{1,0:T(2,128)} fusion(f32[2,32]{1,0:T(2,128)S(1)} %collective-permute-done.10, f32[4,32]{1,0:T(4,128)S(1)} %add_add_fusion), kind=kLoop, calls=%fused_computation.3 | loop fusion | flops 64 | bytes 768 | tf_op jit(solution)/shard_map/add | solution.py:343
  (13 shorter events, 0.0 us)
Async XLA Ops:
  0.0 5.3 %copy-start.4 = (bf16[2,128,256]{2,1,0:T(8,128)(2,1)S(1)}, bf16[2,128,256]{2,1,0:T(8,128)(2,1)}, u32[]{:S(2)}) copy-start(bf16[2,128,256]{2,1,0:T(8,128)(2,1)} %grads.2) | copy-start | bytes 393220
  0.0 5.3 %copy-start.3 = (bf16[2,128,256]{2,1,0:T(8,128)(2,1)S(1)}, bf16[2,128,256]{2,1,0:T(8,128)(2,1)}, u32[]{:S(2)}) copy-start(bf16[2,128,256]{2,1,0:T(8,128)(2,1)} %acts.2) | copy-start | bytes 393220
  0.0 1.0 %copy-start = (s32[2]{0:T(128)S(1)}, s32[2]{0:T(128)}, u32[]{:S(2)}) copy-start(s32[2]{0:T(128)} %param.9) | copy-start | bytes 28
  0.0 8.4 %copy-start.2 = (s32[32]{0:T(128)S(1)}, s32[32]{0:T(128)}, u32[]{:S(2)}) copy-start(s32[32]{0:T(128)} %param.11) | copy-start | bytes 388
  0.0 8.4 %copy-start.1 = (s32[2]{0:T(128)S(1)}, s32[2]{0:T(128)}, u32[]{:S(2)}) copy-start(s32[2]{0:T(128)} %layer_ids.1) | copy-start | bytes 28
  1.1 10.5 %collective-permute-start = (bf16[2,128,256]{2,1,0:T(8,128)(2,1)S(1)}, bf16[2,128,256]{2,1,0:T(8,128)(2,1)S(1)}, u32[]{:S(2)}, u32[]{:S(2)}) collective-permute-start(bf16[2,128,256]{2,1,0:T(8,128)(2,1)S(1)} %away_mask.1), channel_id=1, source_target_pairs={{0,8},{1,9},{2,10},{3,11},{4,12},{5,13},{6,14},{7,15},{8,0},{9,1},... | collective-permute-start | bytes 393224 | tf_op jit(solution)/shard_map/ppermute | solution.py:257
  5.4 6.9 %collective-permute-start.1 = (bf16[2,128,256]{2,1,0:T(8,128)(2,1)S(1)}, bf16[2,128,256]{2,1,0:T(8,128)(2,1)S(1)}, u32[]{:S(2)}, u32[]{:S(2)}) collective-permute-start(bf16[2,128,256]{2,1,0:T(8,128)(2,1)S(1)} %own.1.u0), channel_id=1, source_target_pairs={{0,4},{1,5},{2,7},{3,6},{4,0},{5,1},{6,3},{7,2},{8,12},{9,13},{10,... | collective-permute-start | bytes 393224 | tf_op jit(solution)/shard_map/ppermute | solution.py:257
  7.1 7.3 %collective-permute-start.3 = (bf16[2,128,256]{2,1,0:T(8,128)(2,1)S(1)}, bf16[2,128,256]{2,1,0:T(8,128)(2,1)S(1)}, u32[]{:S(2)}, u32[]{:S(2)}) collective-permute-start(bf16[2,128,256]{2,1,0:T(8,128)(2,1)S(1)} %own.1.u0), channel_id=1, source_target_pairs={{0,2},{1,3},{2,0},{3,1},{4,6},{5,7},{6,4},{7,5},{8,10},{9,11},{10,... | collective-permute-start | bytes 393224 | tf_op jit(solution)/shard_map/ppermute | solution.py:257
  7.7 6.6 %collective-permute-start.2 = (bf16[2,128,256]{2,1,0:T(8,128)(2,1)S(1)}, bf16[2,128,256]{2,1,0:T(8,128)(2,1)S(1)}, u32[]{:S(2)}, u32[]{:S(2)}) collective-permute-start(bf16[2,128,256]{2,1,0:T(8,128)(2,1)S(1)} %own.1.u0), channel_id=1, source_target_pairs={{0,1},{1,0},{2,3},{3,2},{4,5},{5,4},{6,7},{7,6},{8,9},{9,8},{10,11... | collective-permute-start | bytes 393224 | tf_op jit(solution)/shard_map/ppermute | solution.py:257
  11.7 5.5 %collective-permute-start.6 = (bf16[2,128,256]{2,1,0:T(8,128)(2,1)S(1)}, bf16[2,128,256]{2,1,0:T(8,128)(2,1)S(1)}, u32[]{:S(2)}, u32[]{:S(2)}) collective-permute-start(bf16[2,128,256]{2,1,0:T(8,128)(2,1)S(1)} %collective-permute-done.v), channel_id=1, source_target_pairs={{0,4},{1,5},{2,7},{3,6},{4,0},{5,1},{6,3},{7,2},{8,12},{9,13},{10,... | collective-permute-start | bytes 393224 | tf_op jit(solution)/shard_map/ppermute | solution.py:257
  12.3 5.8 %collective-permute-start.7 = (bf16[2,128,256]{2,1,0:T(8,128)(2,1)S(1)}, bf16[2,128,256]{2,1,0:T(8,128)(2,1)S(1)}, u32[]{:S(2)}, u32[]{:S(2)}) collective-permute-start(bf16[2,128,256]{2,1,0:T(8,128)(2,1)S(1)} %collective-permute-done.v), channel_id=1, source_target_pairs={{0,2},{1,3},{2,0},{3,1},{4,6},{5,7},{6,4},{7,5},{8,10},{9,11},{10,... | collective-permute-start | bytes 393224 | tf_op jit(solution)/shard_map/ppermute | solution.py:257
  15.4 1.3 %collective-permute-start.5 = (bf16[128,256]{1,0:T(8,128)(2,1)S(1)}, bf16[128,256]{1,0:T(8,128)(2,1)S(1)}, u32[]{:S(2)}, u32[]{:S(2)}) collective-permute-start(bf16[128,256]{1,0:T(8,128)(2,1)S(1)} %get-tuple-element.47), channel_id=1, source_target_pairs={{0,1},{1,0},{2,3},{3,2},{4,5},{5,4},{6,7},{7,6},{8,9},{9,8},{10,11... | collective-permute-start | bytes 196616 | tf_op jit(solution)/shard_map/ppermute | solution.py:257
  15.5 1.4 %collective-permute-start.4 = (bf16[128,256]{1,0:T(8,128)(2,1)S(1)}, bf16[128,256]{1,0:T(8,128)(2,1)S(1)}, u32[]{:S(2)}, u32[]{:S(2)}) collective-permute-start(bf16[128,256]{1,0:T(8,128)(2,1)S(1)} %get-tuple-element.48), channel_id=1, source_target_pairs={{0,1},{1,0},{2,3},{3,2},{4,5},{5,4},{6,7},{7,6},{8,9},{9,8},{10,11... | collective-permute-start | bytes 196616 | tf_op jit(solution)/shard_map/ppermute | solution.py:257
  18.8 3.7 %collective-permute-start.8 = (f32[4,32]{1,0:T(4,128)S(1)}, f32[4,32]{1,0:T(4,128)S(1)}, u32[]{:S(2)}, u32[]{:S(2)}) collective-permute-start(f32[4,32]{1,0:T(4,128)S(1)} %get-tuple-element.45), channel_id=1, source_target_pairs={{0,2},{1,3},{2,0},{3,1},{4,6},{5,7},{6,4},{7,5},{8,10},{9,11},{10,... | collective-permute-start | bytes 1544 | tf_op jit(solution)/shard_map/ppermute | solution.py:257
  20.6 3.6 %collective-permute-start.9 = (f32[4,32]{1,0:T(4,128)S(1)}, f32[4,32]{1,0:T(4,128)S(1)}, u32[]{:S(2)}, u32[]{:S(2)}) collective-permute-start(f32[4,32]{1,0:T(4,128)S(1)} %get-tuple-element.46), channel_id=1, source_target_pairs={{0,4},{1,5},{2,7},{3,6},{4,0},{5,1},{6,3},{7,2},{8,12},{9,13},{10,... | collective-permute-start | bytes 1544 | tf_op jit(solution)/shard_map/ppermute | solution.py:257
  24.2 4.5 %collective-permute-start.10 = (f32[2,32]{1,0:T(2,128)S(1)}, f32[2,32]{1,0:T(2,128)S(1)}, u32[]{:S(2)}, u32[]{:S(2)}) collective-permute-start(f32[2,32]{1,0:T(2,128)S(1)} %slice.15), channel_id=1, source_target_pairs={{0,8},{1,9},{2,10},{3,11},{4,12},{5,13},{6,14},{7,15},{8,0},{9,1},... | collective-permute-start | bytes 776 | tf_op jit(solution)/shard_map/ppermute | solution.py:257

commit v26 on v22

--- a/solution.py
+++ b/solution.py
@@ -280,21 +280,22 @@
         input_output_aliases={1: 0},
     )
     v = send(away, opposite)
-    away, lens, *data = lax.optimization_barrier((away, lens, *data))
-    own = call(
-        functools.partial(own_kernel, seq_len), "own", 10**9, 40, (lens, *data), [], unit
-    )
-    near = [send(own, to) for to in ways]
+    away, ids = lax.optimization_barrier((away, layer_ids))
     terms, pick = call(
         functools.partial(setup_kernel, seq_len, per),
         "factor_terms",
         10**9,
         51,
-        (layer_ids, flagged.reshape(1, -1), act_factor, grad_factor),
+        (ids, flagged.reshape(1, -1), act_factor, grad_factor),
         [pl.BlockSpec(memory_space=pltpu.SMEM), vmem, hbm, hbm],
         (shape((2, 3, rank, rank), bf16), shape((8 * tokens, columns), bf16)),
         [pltpu.VMEM((2, rank, rank), f32), pltpu.SemaphoreType.DMA((2,))],
     )
+    away, terms, lens, *data = lax.optimization_barrier((away, terms, lens, *data))
+    own = call(
+        functools.partial(own_kernel, seq_len), "own", 10**9, 40, (lens, *data), [], unit
+    )
+    near = [send(own, to) for to in ways]
     v, terms, pick = lax.optimization_barrier((v, terms, pick))
     v3 = send(v, ways[0])
     v, near[0] = lax.optimization_barrier((v, near[0]))

time: 28.6 us -> 29.3 us (1.024)
  waiting for transfers between devices: 6.56 us -> 7.87 us
  starting transfers between devices: 15.4 us -> 14.8 us
    ppermute x11, waiting for transfers between devices: 6.56 us -> 7.87 us  [send(): return lax.ppermute(x, 'blk', [(d, to(d)) for d in range(size)])]
    ppermute x11, starting transfers between devices: 15.4 us -> 14.8 us  [send(): return lax.ppermute(x, 'blk', [(d, to(d)) for d in range(size)])]
  transfers between devices with their start and end apart: 11 -> 11, of which waited for: 7 -> 8; matrix products, arithmetic and copies ran while one was open for 0% -> 0% of each run, Pallas kernels for 14% -> 14%
where the time goes in v26:
time: 29.3 us; the launch traced here: 29.2 us
  starting transfers between devices  14.8 us (51%)
  waiting for transfers between devices  7.87 us (27%)
  Pallas kernels  5.8 us (20%)
  other arithmetic  0.57 us (2%)
    ppermute x11, starting transfers between devices, send(): return lax.ppermute(x, 'blk', [(d, to(d)) for d in range(size)])  14.8 us
    ppermute x11, waiting for transfers between devices, send(): return lax.ppermute(x, 'blk', [(d, to(d)) for d in range(size)])  7.87 us
    pallas_call x9, Pallas kernels, call(): pl.pallas_call(kernel, out_shape=out_shape, in_specs=specs + [vmem] * (le...  5.8 us
  transfers between devices with their start and end apart: 11, of which 8 were waited for; matrix products, arithmetic and copies ran while one was open for 0% of the time, Pallas kernels for 14%

profile of v26, /device:TPU:0, one launch (start us, length us, event | category | flops | bytes accessed | tf_op | source)
XLA Modules:
  0.0 29.2 jit_solution(8018663935742521318)
XLA Ops:
  0.0 0.9 %away.1.unit = bf16[2,128,256]{2,1,0:T(8,128)(2,1)S(1)} custom-call(bf16[2,128,256]{2,1,0:T(8,128)(2,1)} %acts.2, bf16[2,128,256]{2,1,0:T(8,128)(2,1)} %grads.2), custom_call_target="tpu_custom_call" | custom-call | flops 3000000000 | bytes 1000000 | tf_op jit(solution)/shard_map/away/pallas_call | solution.py:236
  1.0 0.2 away_mask.1
  1.1 4.1 %collective-permute-start = (bf16[2,128,256]{2,1,0:T(8,128)(2,1)S(1)}, bf16[2,128,256]{2,1,0:T(8,128)(2,1)S(1)}, u32[]{:S(2)}, u32[]{:S(2)}) collective-permute-start(bf16[2,128,256]{2,1,0:T(8,128)(2,1)S(1)} %away_mask.1), channel_id=1, source_target_pairs={{0,8},{1,9},{2,10},{3,11},{4,12},{5,13},{6,14},{7,15},{8,0},{9,1},... | collective-permute-start | bytes 393224 | tf_op jit(solution)/shard_map/ppermute | solution.py:257
  5.2 1.7 %factor_terms.1 = (bf16[2,3,256,256]{3,2,1,0:T(8,128)(2,1)S(1)}, bf16[1024,32]{1,0:T(8,128)(2,1)S(1)}) custom-call(s32[2]{0:T(128)S(1)} %copy-done, s32[1,32]{1,0:T(1,128)S(1)} %bitcast.6, f32[16,256,256]{2,1,0:T(8,128)} %act_f.1, f32[16,256,256]{2,1,0:T(8,128)} %grad_f.1), custom_call_target="tpu_custom_call" | custom-call | flops 1000000000 | bytes 1000000 | tf_op jit(solution)/shard_map/factor_terms/pallas_call | solution.py:236
  6.9 0.2 own.1.u0
  7.1 1.6 %collective-permute-start.1 = (bf16[2,128,256]{2,1,0:T(8,128)(2,1)S(1)}, bf16[2,128,256]{2,1,0:T(8,128)(2,1)S(1)}, u32[]{:S(2)}, u32[]{:S(2)}) collective-permute-start(bf16[2,128,256]{2,1,0:T(8,128)(2,1)S(1)} %own.1.u0), channel_id=1, source_target_pairs={{0,4},{1,5},{2,7},{3,6},{4,0},{5,1},{6,3},{7,2},{8,12},{9,13},{10,... | collective-permute-start | bytes 393224 | tf_op jit(solution)/shard_map/ppermute | solution.py:257
  8.7 0.7 %collective-permute-start.3 = (bf16[2,128,256]{2,1,0:T(8,128)(2,1)S(1)}, bf16[2,128,256]{2,1,0:T(8,128)(2,1)S(1)}, u32[]{:S(2)}, u32[]{:S(2)}) collective-permute-start(bf16[2,128,256]{2,1,0:T(8,128)(2,1)S(1)} %own.1.u0), channel_id=1, source_target_pairs={{0,2},{1,3},{2,0},{3,1},{4,6},{5,7},{6,4},{7,5},{8,10},{9,11},{10,... | collective-permute-start | bytes 393224 | tf_op jit(solution)/shard_map/ppermute | solution.py:257
  9.4 0.7 %collective-permute-start.2 = (bf16[2,128,256]{2,1,0:T(8,128)(2,1)S(1)}, bf16[2,128,256]{2,1,0:T(8,128)(2,1)S(1)}, u32[]{:S(2)}, u32[]{:S(2)}) collective-permute-start(bf16[2,128,256]{2,1,0:T(8,128)(2,1)S(1)} %own.1.u0), channel_id=1, source_target_pairs={{0,1},{1,0},{2,3},{3,2},{4,5},{5,4},{6,7},{7,6},{8,9},{9,8},{10,11... | collective-permute-start | bytes 393224 | tf_op jit(solution)/shard_map/ppermute | solution.py:257
  10.1 1.6 %collective-permute-done.v = bf16[2,128,256]{2,1,0:T(8,128)(2,1)S(1)} collective-permute-done((bf16[2,128,256]{2,1,0:T(8,128)(2,1)S(1)}, bf16[2,128,256]{2,1,0:T(8,128)(2,1)S(1)}, u32[]{:S(2)}, u32[]{:S(2)}) %collective-permute-start) | collective-permute-done | bytes 131104 | tf_op jit(solution)/shard_map/ppermute | solution.py:257
  11.6 0.7 %collective-permute-start.6 = (bf16[2,128,256]{2,1,0:T(8,128)(2,1)S(1)}, bf16[2,128,256]{2,1,0:T(8,128)(2,1)S(1)}, u32[]{:S(2)}, u32[]{:S(2)}) collective-permute-start(bf16[2,128,256]{2,1,0:T(8,128)(2,1)S(1)} %collective-permute-done.v), channel_id=1, source_target_pairs={{0,4},{1,5},{2,7},{3,6},{4,0},{5,1},{6,3},{7,2},{8,12},{9,13},{10,... | collective-permute-start | bytes 393224 | tf_op jit(solution)/shard_map/ppermute | solution.py:257
  12.3 1.6 %collective-permute-done.1.u3 = bf16[2,128,256]{2,1,0:T(8,128)(2,1)S(1)} collective-permute-done((bf16[2,128,256]{2,1,0:T(8,128)(2,1)S(1)}, bf16[2,128,256]{2,1,0:T(8,128)(2,1)S(1)}, u32[]{:S(2)}, u32[]{:S(2)}) %collective-permute-start.1) | collective-permute-done | bytes 131104 | tf_op jit(solution)/shard_map/ppermute | solution.py:257
  13.9 2.0 %collective-permute-start.7 = (bf16[2,128,256]{2,1,0:T(8,128)(2,1)S(1)}, bf16[2,128,256]{2,1,0:T(8,128)(2,1)S(1)}, u32[]{:S(2)}, u32[]{:S(2)}) collective-permute-start(bf16[2,128,256]{2,1,0:T(8,128)(2,1)S(1)} %collective-permute-done.v), channel_id=1, source_target_pairs={{0,2},{1,3},{2,0},{3,1},{4,6},{5,7},{6,4},{7,5},{8,10},{9,11},{10,... | collective-permute-start | bytes 393224 | tf_op jit(solution)/shard_map/ppermute | solution.py:257
  15.9 0.0 collective-permute-done.3.u2
  15.9 0.0 collective-permute-done.2.u1
  15.9 1.0 %early_pairs.1 = (bf16[2,512,256]{2,1,0:T(8,128)(2,1)S(1)}, f32[4,1024]{1,0:T(4,128)S(1)}, f32[8,768]{1,0:T(8,128)S(1)}) custom-call(bf16[2,3,256,256]{3,2,1,0:T(8,128)(2,1)S(1)} %get-tuple-element.37.terms, bf16[2,128,256]{2,1,0:T(8,128)(2,1)S(1)} %own.1.u0, bf16[2,128,256]{2,1,0:T(8,128)(2,1)S(1)} %collective-permute-done.v, ...), custom_call_target="tpu_custom_call" | custom-call | flops 1000000000 | bytes 1000000 | tf_op jit(solution)/shard_map/early_pairs/pallas_call | solution.py:236
  16.9 0.1 collective-permute-start.5
  17.0 0.5 %collective-permute-start.4 = (bf16[128,256]{1,0:T(8,128)(2,1)S(1)}, bf16[128,256]{1,0:T(8,128)(2,1)S(1)}, u32[]{:S(2)}, u32[]{:S(2)}) collective-permute-start(bf16[128,256]{1,0:T(8,128)(2,1)S(1)} %get-tuple-element.52), channel_id=1, source_target_pairs={{0,1},{1,0},{2,3},{3,2},{4,5},{5,4},{6,7},{7,6},{8,9},{9,8},{10,11... | collective-permute-start | bytes 196616 | tf_op jit(solution)/shard_map/ppermute | solution.py:257
  17.5 0.7 %collective-permute-done.5.grads = bf16[128,256]{1,0:T(8,128)(2,1)S(1)} collective-permute-done((bf16[128,256]{1,0:T(8,128)(2,1)S(1)}, bf16[128,256]{1,0:T(8,128)(2,1)S(1)}, u32[]{:S(2)}, u32[]{:S(2)}) %collective-permute-start.5) | collective-permute-done | bytes 65568 | tf_op jit(solution)/shard_map/ppermute | solution.py:257
  18.2 0.2 collective-permute-done.4.acts
  18.4 0.3 %core_pairs.1 = (f32[4,1024]{1,0:T(4,128)S(1)}, f32[8,768]{1,0:T(8,128)S(1)}) custom-call(bf16[2,512,256]{2,1,0:T(8,128)(2,1)S(1)} %get-tuple-element.40.white, bf16[128,256]{1,0:T(8,128)(2,1)S(1)} %collective-permute-done.4.acts, bf16[128,256]{1,0:T(8,128)(2,1)S(1)} %collective-permute-done.5.grads, ...), custom_call_target="tpu_custom_call", output_to_operand_aliasing={{0}: (3, {}), {1}: (4, {})} | custom-call | flops 10000 | bytes 1000000 | tf_op jit(solution)/shard_map/core_pairs/pallas_call | solution.py:236
  18.7 0.0 collective-permute-done.6.v3
  18.7 0.5 %z_pairs.1 = (bf16[2,128,256]{2,1,0:T(8,128)(2,1)S(1)}, f32[8,768]{1,0:T(8,128)S(1)}) custom-call(bf16[2,3,256,256]{3,2,1,0:T(8,128)(2,1)S(1)} %get-tuple-element.37.terms, bf16[2,512,256]{2,1,0:T(8,128)(2,1)S(1)} %get-tuple-element.40.white, bf16[2,128,256]{2,1,0:T(8,128)(2,1)S(1)} %collective-permute-done.3.u2, ...), custom_call_target="tpu_custom_call", output_to_operand_aliasing={{1}: (7, {})} | custom-call | flops 10000 | bytes 1000000 | tf_op jit(solution)/shard_map/z_pairs/pallas_call | solution.py:236
  19.2 0.5 %collective-permute-done.7.v2 = bf16[2,128,256]{2,1,0:T(8,128)(2,1)S(1)} collective-permute-done((bf16[2,128,256]{2,1,0:T(8,128)(2,1)S(1)}, bf16[2,128,256]{2,1,0:T(8,128)(2,1)S(1)}, u32[]{:S(2)}, u32[]{:S(2)}) %collective-permute-start.7) | collective-permute-done | bytes 131104 | tf_op jit(solution)/shard_map/ppermute | solution.py:257
  19.6 0.7 %return_rows.1 = (f32[4,32]{1,0:T(4,128)S(1)}, f32[4,32]{1,0:T(4,128)S(1)}) custom-call(bf16[2,3,256,256]{3,2,1,0:T(8,128)(2,1)S(1)} %get-tuple-element.37.terms, bf16[2,512,256]{2,1,0:T(8,128)(2,1)S(1)} %get-tuple-element.40.white, bf16[2,128,256]{2,1,0:T(8,128)(2,1)S(1)} %get-tuple-element.47.white3, bf16[1024,32]{1,0:T(8,128)(2,1)S(1)} %get-tuple-element.41.pick, ...), custom_call_target="tpu_custom_call" | custom-call | flops 1000000000 | bytes 1000000 | tf_op jit(solution)/shard_map/return_rows/pallas_call | solution.py:236
  20.3 0.1 collective-permute-start.8
  20.4 1.8 %collective-permute-start.9 = (f32[4,32]{1,0:T(4,128)S(1)}, f32[4,32]{1,0:T(4,128)S(1)}, u32[]{:S(2)}, u32[]{:S(2)}) collective-permute-start(f32[4,32]{1,0:T(4,128)S(1)} %get-tuple-element.50), channel_id=1, source_target_pairs={{0,2},{1,3},{2,0},{3,1},{4,6},{5,7},{6,4},{7,5},{8,10},{9,11},{10,... | collective-permute-start | bytes 1544 | tf_op jit(solution)/shard_map/ppermute | solution.py:257
  22.2 0.4 %own_rows.1 = f32[4,32]{1,0:T(4,128)S(1)} custom-call(bf16[2,512,256]{2,1,0:T(8,128)(2,1)S(1)} %get-tuple-element.40.white, bf16[1024,32]{1,0:T(8,128)(2,1)S(1)} %get-tuple-element.41.pick, f32[4,1024]{1,0:T(4,128)S(1)} %get-tuple-element.45.mine, bf16[2,128,256]{2,1,0:T(8,128)(2,1)S(1)} %collective-permute-done.6.v3, ...), custom_call_target="tpu_custom_call" | custom-call | flops 1000000000 | bytes 1000000 | tf_op jit(solution)/shard_map/own_rows/pallas_call | solution.py:236
  22.6 1.4 %collective-permute-done.8 = f32[4,32]{1,0:T(4,128)S(1)} collective-permute-done((f32[4,32]{1,0:T(4,128)S(1)}, f32[4,32]{1,0:T(4,128)S(1)}, u32[]{:S(2)}, u32[]{:S(2)}) %collective-permute-start.8) | collective-permute-done | bytes 544 | tf_op jit(solution)/shard_map/ppermute | solution.py:257
  24.0 0.1 collective-permute-done.9
  24.1 2.6 %collective-permute-start.10 = (f32[2,32]{1,0:T(2,128)S(1)}, f32[2,32]{1,0:T(2,128)S(1)}, u32[]{:S(2)}, u32[]{:S(2)}) collective-permute-start(f32[2,32]{1,0:T(2,128)S(1)} %slice.15), channel_id=1, source_target_pairs={{0,8},{1,9},{2,10},{3,11},{4,12},{5,13},{6,14},{7,15},{8,0},{9,1},... | collective-permute-start | bytes 776 | tf_op jit(solution)/shard_map/ppermute | solution.py:257
  26.7 1.9 %collective-permute-done.10 = f32[2,32]{1,0:T(2,128)S(1)} collective-permute-done((f32[2,32]{1,0:T(2,128)S(1)}, f32[2,32]{1,0:T(2,128)S(1)}, u32[]{:S(2)}, u32[]{:S(2)}) %collective-permute-start.10) | collective-permute-done | bytes 288 | tf_op jit(solution)/shard_map/ppermute | solution.py:257
  28.6 0.6 %slice_add_fusion = f32[2,32]{1,0:T(2,128)} fusion(f32[2,32]{1,0:T(2,128)S(1)} %collective-permute-done.10, f32[4,32]{1,0:T(4,128)S(1)} %add_add_fusion), kind=kLoop, calls=%fused_computation.3 | loop fusion | flops 64 | bytes 768 | tf_op jit(solution)/shard_map/add | solution.py:344
  (13 shorter events, 0.0 us)
Async XLA Ops:
  0.0 0.9 %copy-start.2 = (s32[2]{0:T(128)S(1)}, s32[2]{0:T(128)}, u32[]{:S(2)}) copy-start(s32[2]{0:T(128)} %param.9) | copy-start | bytes 28
  0.0 5.2 %copy-start = (s32[2]{0:T(128)S(1)}, s32[2]{0:T(128)}, u32[]{:S(2)}) copy-start(s32[2]{0:T(128)} %layer_ids) | copy-start | bytes 28
  0.0 5.2 %copy-start.1 = (s32[32]{0:T(128)S(1)}, s32[32]{0:T(128)}, u32[]{:S(2)}) copy-start(s32[32]{0:T(128)} %param.11) | copy-start | bytes 388
  1.1 10.5 %collective-permute-start = (bf16[2,128,256]{2,1,0:T(8,128)(2,1)S(1)}, bf16[2,128,256]{2,1,0:T(8,128)(2,1)S(1)}, u32[]{:S(2)}, u32[]{:S(2)}) collective-permute-start(bf16[2,128,256]{2,1,0:T(8,128)(2,1)S(1)} %away_mask.1), channel_id=1, source_target_pairs={{0,8},{1,9},{2,10},{3,11},{4,12},{5,13},{6,14},{7,15},{8,0},{9,1},... | collective-permute-start | bytes 393224 | tf_op jit(solution)/shard_map/ppermute | solution.py:257
  5.2 1.7 %copy-start.3 = (bf16[2,128,256]{2,1,0:T(8,128)(2,1)S(1)}, bf16[2,128,256]{2,1,0:T(8,128)(2,1)}, u32[]{:S(2)}) copy-start(bf16[2,128,256]{2,1,0:T(8,128)(2,1)} %acts.2) | copy-start | bytes 393220
  5.2 1.7 %copy-start.4 = (bf16[2,128,256]{2,1,0:T(8,128)(2,1)S(1)}, bf16[2,128,256]{2,1,0:T(8,128)(2,1)}, u32[]{:S(2)}) copy-start(bf16[2,128,256]{2,1,0:T(8,128)(2,1)} %grads.2) | copy-start | bytes 393220
  7.1 6.8 %collective-permute-start.1 = (bf16[2,128,256]{2,1,0:T(8,128)(2,1)S(1)}, bf16[2,128,256]{2,1,0:T(8,128)(2,1)S(1)}, u32[]{:S(2)}, u32[]{:S(2)}) collective-permute-start(bf16[2,128,256]{2,1,0:T(8,128)(2,1)S(1)} %own.1.u0), channel_id=1, source_target_pairs={{0,4},{1,5},{2,7},{3,6},{4,0},{5,1},{6,3},{7,2},{8,12},{9,13},{10,... | collective-permute-start | bytes 393224 | tf_op jit(solution)/shard_map/ppermute | solution.py:257
  8.7 7.1 %collective-permute-start.3 = (bf16[2,128,256]{2,1,0:T(8,128)(2,1)S(1)}, bf16[2,128,256]{2,1,0:T(8,128)(2,1)S(1)}, u32[]{:S(2)}, u32[]{:S(2)}) collective-permute-start(bf16[2,128,256]{2,1,0:T(8,128)(2,1)S(1)} %own.1.u0), channel_id=1, source_target_pairs={{0,2},{1,3},{2,0},{3,1},{4,6},{5,7},{6,4},{7,5},{8,10},{9,11},{10,... | collective-permute-start | bytes 393224 | tf_op jit(solution)/shard_map/ppermute | solution.py:257
  9.4 6.5 %collective-permute-start.2 = (bf16[2,128,256]{2,1,0:T(8,128)(2,1)S(1)}, bf16[2,128,256]{2,1,0:T(8,128)(2,1)S(1)}, u32[]{:S(2)}, u32[]{:S(2)}) collective-permute-start(bf16[2,128,256]{2,1,0:T(8,128)(2,1)S(1)} %own.1.u0), channel_id=1, source_target_pairs={{0,1},{1,0},{2,3},{3,2},{4,5},{5,4},{6,7},{7,6},{8,9},{9,8},{10,11... | collective-permute-start | bytes 393224 | tf_op jit(solution)/shard_map/ppermute | solution.py:257
  11.6 7.0 %collective-permute-start.6 = (bf16[2,128,256]{2,1,0:T(8,128)(2,1)S(1)}, bf16[2,128,256]{2,1,0:T(8,128)(2,1)S(1)}, u32[]{:S(2)}, u32[]{:S(2)}) collective-permute-start(bf16[2,128,256]{2,1,0:T(8,128)(2,1)S(1)} %collective-permute-done.v), channel_id=1, source_target_pairs={{0,4},{1,5},{2,7},{3,6},{4,0},{5,1},{6,3},{7,2},{8,12},{9,13},{10,... | collective-permute-start | bytes 393224 | tf_op jit(solution)/shard_map/ppermute | solution.py:257
  13.9 5.7 %collective-permute-start.7 = (bf16[2,128,256]{2,1,0:T(8,128)(2,1)S(1)}, bf16[2,128,256]{2,1,0:T(8,128)(2,1)S(1)}, u32[]{:S(2)}, u32[]{:S(2)}) collective-permute-start(bf16[2,128,256]{2,1,0:T(8,128)(2,1)S(1)} %collective-permute-done.v), channel_id=1, source_target_pairs={{0,2},{1,3},{2,0},{3,1},{4,6},{5,7},{6,4},{7,5},{8,10},{9,11},{10,... | collective-permute-start | bytes 393224 | tf_op jit(solution)/shard_map/ppermute | solution.py:257
  16.9 1.3 %collective-permute-start.5 = (bf16[128,256]{1,0:T(8,128)(2,1)S(1)}, bf16[128,256]{1,0:T(8,128)(2,1)S(1)}, u32[]{:S(2)}, u32[]{:S(2)}) collective-permute-start(bf16[128,256]{1,0:T(8,128)(2,1)S(1)} %get-tuple-element.51), channel_id=1, source_target_pairs={{0,1},{1,0},{2,3},{3,2},{4,5},{5,4},{6,7},{7,6},{8,9},{9,8},{10,11... | collective-permute-start | bytes 196616 | tf_op jit(solution)/shard_map/ppermute | solution.py:257
  17.0 1.4 %collective-permute-start.4 = (bf16[128,256]{1,0:T(8,128)(2,1)S(1)}, bf16[128,256]{1,0:T(8,128)(2,1)S(1)}, u32[]{:S(2)}, u32[]{:S(2)}) collective-permute-start(bf16[128,256]{1,0:T(8,128)(2,1)S(1)} %get-tuple-element.52), channel_id=1, source_target_pairs={{0,1},{1,0},{2,3},{3,2},{4,5},{5,4},{6,7},{7,6},{8,9},{9,8},{10,11... | collective-permute-start | bytes 196616 | tf_op jit(solution)/shard_map/ppermute | solution.py:257
  20.3 3.6 %collective-permute-start.8 = (f32[4,32]{1,0:T(4,128)S(1)}, f32[4,32]{1,0:T(4,128)S(1)}, u32[]{:S(2)}, u32[]{:S(2)}) collective-permute-start(f32[4,32]{1,0:T(4,128)S(1)} %get-tuple-element.49), channel_id=1, source_target_pairs={{0,4},{1,5},{2,7},{3,6},{4,0},{5,1},{6,3},{7,2},{8,12},{9,13},{10,... | collective-permute-start | bytes 1544 | tf_op jit(solution)/shard_map/ppermute | solution.py:257
  20.4 3.7 %collective-permute-start.9 = (f32[4,32]{1,0:T(4,128)S(1)}, f32[4,32]{1,0:T(4,128)S(1)}, u32[]{:S(2)}, u32[]{:S(2)}) collective-permute-start(f32[4,32]{1,0:T(4,128)S(1)} %get-tuple-element.50), channel_id=1, source_target_pairs={{0,2},{1,3},{2,0},{3,1},{4,6},{5,7},{6,4},{7,5},{8,10},{9,11},{10,... | collective-permute-start | bytes 1544 | tf_op jit(solution)/shard_map/ppermute | solution.py:257
  24.1 4.5 %collective-permute-start.10 = (f32[2,32]{1,0:T(2,128)S(1)}, f32[2,32]{1,0:T(2,128)S(1)}, u32[]{:S(2)}, u32[]{:S(2)}) collective-permute-start(f32[2,32]{1,0:T(2,128)S(1)} %slice.15), channel_id=1, source_target_pairs={{0,8},{1,9},{2,10},{3,11},{4,12},{5,13},{6,14},{7,15},{8,0},{9,1},... | collective-permute-start | bytes 776 | tf_op jit(solution)/shard_map/ppermute | solution.py:257
